TPU v7x, 32 devices: a whole 2x2x4 slice. The times are simulated.
32 devices in a mesh: groups: 2 (over y), sector: 16 (over z, x, core).
Axes of the slice: x: 2, y: 2, z: 4, core: 2. Of those that a mesh axis runs over, the one named last changes fastest.
Arguments:
- wavefunction: float32 [32, 256, 256], P(('groups', 'sector')), parts along dimension 0, may hold values from -1200 to 1200
- sector_dims: int32 [32, 2], P(('groups', 'sector')), parts along dimension 0, may hold values from 64 to 256
- left_env: bfloat16 [32, 26, 256, 256], P(('groups', 'sector')), parts along dimension 0, may hold values from -2 to 2
- right_env: bfloat16 [32, 26, 256, 256], P(('groups', 'sector')), parts along dimension 0, may hold values from -2 to 2
Outputs:
- first_image: float32 [32, 256, 256], P(('groups', 'sector')), parts along dimension 0
- second_image: float32 [32, 256, 256], P(('groups', 'sector')), parts along dimension 0
There are 2 independent parts, one for each index of `groups`. A program takes and returns all parts, laid end to end along the dimension named above; each array names one. Nothing has to cross between parts.
All inputs are finite; a program needn't handle non-finite values.
Results may differ from a plain program's by a relative error of at most 0.009.
Values may be sent and summed in bfloat16 or wider, within the bound.
No kernel may reach another device: no remote copies, remote signals or barrier semaphores. Data moves between devices by JAX's collectives and lax.ppermute only.
A program may use at most 64 MiB of HBM per device.

v0:
```python
import functools

import jax
import jax.numpy as jnp
from jax import lax
from jax.experimental import pallas as pl
from jax.experimental.pallas import tpu as pltpu
from jax.sharding import PartitionSpec as P

QD = 8
SCALE = 1024.0
NT = (((1,), (1,)), ((), ()))
VM = pl.BlockSpec(memory_space=pltpu.VMEM)
HB = pl.BlockSpec(memory_space=pltpu.HBM)
AN = pl.BlockSpec(memory_space=pl.ANY)
COST = pl.CostEstimate(flops=1, bytes_accessed=1, transcendentals=0)
LONG = pl.CostEstimate(flops=4000000000, bytes_accessed=1, transcendentals=0)
PARAMS = pltpu.CompilerParams(vmem_limit_bytes=16 * 1024 * 1024)


def vmem(x):
    return pltpu.with_memory_space_constraint(x, pltpu.VMEM)


def hbm(x):
    return pltpu.with_memory_space_constraint(x, pltpu.HBM)


def call(kernel, out_shape, in_specs, out_specs, scratch=(), cost=COST, aliases={}):
    return pl.pallas_call(
        kernel, out_shape=out_shape, in_specs=in_specs, out_specs=out_specs, scratch_shapes=list(scratch),
        compiler_params=PARAMS, cost_estimate=cost, input_output_aliases=aliases,
    )


def swap(x, axis, pairs):
    to = {a: b for p in pairs for a, b in (p, p[::-1])}
    return lax.ppermute(x, axis, [(s, to.get(s, s)) for s in range(lax.axis_size(axis))])


def swap_pairs(size):
    rows = size // QD
    near = [(s, s + 1) for s in range(0, size, 2)]
    far = [(s, s + 1) for s in range(1, size - 1, 2) if s % QD != QD - 1]
    row_even = [(s, s + QD) for r in range(0, rows - 1, 2) for s in range(r * QD, r * QD + QD)]
    row_odd = [(s, s + QD) for r in range(1, rows - 1, 2) for s in range(r * QD, r * QD + QD)]
    return near, far, [p for p in (row_even, row_odd) if p]


def place(size, width):
    me = lax.axis_index("sector")
    column = lax.rem(me, QD)
    odd = lax.rem(me, 2) == 1
    row_odd = lax.rem(lax.div(me, QD), 2) == 1
    low, high, down, up = 2, 2 + width, 2 + 2 * width, 2 + 3 * width
    offsets = [jnp.where(odd, low, high), jnp.where(odd, high, low),
               jnp.where(row_odd, down, up), jnp.where(row_odd, up, down)]
    partners = [jnp.where(odd, me - 1, me + 1), jnp.where(odd, me + 1, me - 1),
                jnp.where(row_odd, me - QD, me + QD), jnp.where(row_odd, me + QD, me - QD)]
    there = [(column != 0) & (column != QD - 1),
             True if size // QD % 2 == 0 else (partners[2] >= 0) & (partners[2] < size),
             (partners[3] >= 0) & (partners[3] < size)]
    partners = [me] + [jnp.clip(p, 0, size - 1) for p in partners]
    return offsets, partners, there


def live(facts, shape):
    row_ok = lax.broadcasted_iota(jnp.int32, shape, 0).astype(jnp.float32) < facts[1:2, 0:1]
    col_ok = lax.broadcasted_iota(jnp.int32, shape, 1).astype(jnp.float32) < facts[2:3, 0:1]
    return row_ok & col_ok


def total(x):
    return jnp.sum(jnp.sum(x, axis=0, keepdims=True), axis=1, keepdims=True)


def only(there, block):
    return block if there is True else jnp.where(there, block, jnp.zeros_like(block))


def terms(src, left_ref, right_ref, first, count):
    size = src.shape[0]
    right = right_ref[pl.ds(first, count)].reshape(count * size, size)
    partial_t = lax.dot_general(right, src, NT, preferred_element_type=jnp.float32).astype(jnp.bfloat16)
    image = None
    for k in range(count):
        piece = lax.dot_general(
            left_ref[first + k], partial_t[k * size : (k + 1) * size], NT, preferred_element_type=jnp.float32
        )
        image = piece if image is None else image + piece
    return image


def fetch(left_hbm, right_hbm, left_ref, right_ref, sems, spans):
    copies = []
    at = 0
    for n, (offset, count) in enumerate(spans):
        pair = [
            pltpu.make_async_copy(source.at[0, pl.ds(offset, count)], target.at[pl.ds(at, count)], sems.at[n, e])
            for e, (source, target) in enumerate(((right_hbm, right_ref), (left_hbm, left_ref)))
        ]
        for copy in pair:
            copy.start()
        copies.append(pair)
        at += count
    return copies


def finish(copies):
    for copy in copies:
        copy.wait()


def start_kernel(wave_hbm, dims_hbm, u_ref, far_u_ref, facts_ref, wave_ref, dims_ref, sems):
    wave_copy = pltpu.make_async_copy(wave_hbm.at[0], wave_ref, sems.at[0])
    dims_copy = pltpu.make_async_copy(dims_hbm, dims_ref, sems.at[1])
    dims_copy.start()
    wave_copy.start()
    dims_copy.wait()
    lines = lax.broadcasted_iota(jnp.int32, (8, 128), 0)
    facts = jnp.where(lines == 1, dims_ref[0, 0], jnp.where(lines == 2, dims_ref[0, 1], 0)).astype(jnp.float32)
    wave_copy.wait()
    held = jnp.where(live(facts, wave_ref.shape), wave_ref[...], 0.0)
    for ref in (u_ref, far_u_ref):
        ref[...] = (held * SCALE).astype(jnp.bfloat16)
    facts_ref[...] = facts


def pass_kernel(*refs):
    pass


def after(held, first):
    return call(pass_kernel, pltpu.VMEM(held.shape, held.dtype), [AN] * 2, AN, aliases={0: 0})(vmem(held), first)


def near_kernel(size, width, rows, left_hbm, right_hbm, wave_hbm, facts_ref, self_ref, near_ref, out_ref, sums_ref,
                left_far, right_far, left_row, right_row, left_own, right_own, wave_ref, sems, far_sems, row_sems, wave_sem):
    offsets, _, _ = place(size, width)
    wave_copy = pltpu.make_async_copy(wave_hbm.at[0], wave_ref, wave_sem)
    own = fetch(left_hbm, right_hbm, left_own, right_own, sems, [(0, 2), (offsets[0], width)])
    wave_copy.start()
    later = fetch(left_hbm, right_hbm, left_far, right_far, far_sems, [(offsets[1], width)])
    later += fetch(left_hbm, right_hbm, left_row, right_row, row_sems, [(o, width) for o in offsets[2 : 2 + rows]])
    u = self_ref[...].astype(jnp.float32)
    lines = lax.broadcasted_iota(jnp.int32, (8, 128), 0)
    sums = jnp.where(lines == 1, total(u * u), 0.0)
    finish(own[0])
    out_ref[0] = terms(self_ref[...], left_own, right_own, 0, 2)
    finish(own[1])
    out_ref[1] = terms(near_ref[...], left_own, right_own, 2, width)
    wave_copy.wait()
    held = jnp.where(live(facts_ref[...], wave_ref.shape), wave_ref[...], 0.0)
    sums_ref[...] = jnp.where(lines == 0, total(held * held), sums)
    for pair in later:
        finish(pair)


def far_kernel(size, width, left_ref, right_ref, far_ref, out_ref):
    _, _, there = place(size, width)
    out_ref[...] = terms(only(there[0], far_ref[...]), left_ref, right_ref, 0, width)


def first_kernel(size, width, rows, *refs):
    near_part_ref, far_part_ref, facts_ref, sums_ref, u_ref, left_ref, right_ref = refs[:7]
    row_refs, (out_ref, w_ref, far_w_ref, sums_out_ref) = refs[7 : 7 + rows], refs[7 + rows :]
    _, _, there = place(size, width)
    image = near_part_ref[0] + near_part_ref[1] + far_part_ref[...]
    for r, source in enumerate(row_refs):
        piece = terms(only(there[1 + r], source[...]), left_ref, right_ref, r * width, width)
        out_ref[r] = piece
        image = image + piece
    image = jnp.where(live(facts_ref[...], image.shape), image, 0.0)
    u = u_ref[...].astype(jnp.float32)
    square = sums_ref[1:2, 0:1]
    cross = total(u * image)
    rho = jnp.where(square > 0.0, cross / square, 0.0)
    for ref in (w_ref, far_w_ref):
        ref[...] = (image - rho * u).astype(jnp.bfloat16)
    lines = lax.broadcasted_iota(jnp.int32, (8, 128), 0)
    sums_out_ref[...] = jnp.where(lines == 2, cross, jnp.where(lines == 4, rho, sums_ref[...]))


def spread_kernel(sums_ref, w_ref, held_in, out_ref, held_out):
    w = w_ref[...].astype(jnp.float32)
    lines = lax.broadcasted_iota(jnp.int32, (8, 128), 0)
    sums = jnp.where(lines == 3, total(w * w), sums_ref[...])
    for n in range(out_ref.shape[0]):
        out_ref[n] = sums


def image_kernel(size, width, rows, left_hbm, right_hbm, left_row, right_row, self_ref, near_ref, far_ref, *refs):
    row_refs, (out_ref, left_own, right_own, sems) = refs[:rows], refs[rows:]
    offsets, _, there = place(size, width)
    own = fetch(left_hbm, right_hbm, left_own, right_own, sems, [(0, 2)] + [(o, width) for o in offsets[:2]])
    image = None
    for r, source in enumerate(row_refs):
        piece = terms(only(there[1 + r], source[...]), left_row, right_row, r * width, width)
        image = piece if image is None else image + piece
    finish(own[0])
    image = image + terms(self_ref[...], left_own, right_own, 0, 2)
    finish(own[1])
    image = image + terms(near_ref[...], left_own, right_own, 2, width)
    finish(own[2])
    out_ref[...] = image + terms(only(there[0], far_ref[...]), left_own, right_own, 2 + width, width)


def second_kernel(size, width, rows, cells, facts_ref, stats_ref, hw_ref, near_part_ref, far_part_ref, row_part_ref,
                  first_hbm, second_hbm, first_ref, second_ref, sems):
    _, partners, _ = place(size, width)
    facts = facts_ref[...]
    stats = stats_ref[...]
    sums = jnp.sum(stats, axis=0)
    start, square, cross, inner = (sums[i : i + 1, 0:1] for i in range(4))
    scale = lax.rsqrt(start / cells + 1e-06) * (1.0 / SCALE)
    parts = [near_part_ref[0], near_part_ref[1], far_part_ref[...]] + [row_part_ref[r] for r in range(rows)]
    cell = live(facts, parts[0].shape)
    first_ref[...] = jnp.where(cell, sum(parts[1:], parts[0]), 0.0) * scale
    first_copy = pltpu.make_async_copy(first_ref, first_hbm.at[0], sems.at[0])
    first_copy.start()
    rho = cross / square
    gap = stats[:, 4:5, 0:1] - rho[None]
    residual = inner + jnp.sum(stats[:, 1:2, 0:1] * gap * gap, axis=0)
    second_scale = scale * lax.rsqrt(scale * scale * (residual / cells) + 1e-06)
    image = hw_ref[...]
    for n, part in enumerate(parts):
        image = image + (stats_ref[partners[n], 4:5, 0:1] - rho) * part
    second_ref[...] = jnp.where(cell, image, 0.0) * second_scale
    second_copy = pltpu.make_async_copy(second_ref, second_hbm.at[0], sems.at[1])
    second_copy.start()
    first_copy.wait()
    second_copy.wait()


def body(wavefunction, sector_dims, left_env, right_env):
    size = lax.axis_size("sector")
    block = wavefunction.shape[1]
    square = (block, block)
    width = (right_env.shape[1] - 2) // 4
    near, far, row_pairs = swap_pairs(size)
    rows = len(row_pairs)
    cells = float(size * block * block)
    few, every, side, last = ((n,) + square for n in (2 + width, 2 + 2 * width, width, rows * width))
    f32, bf16 = jnp.float32, jnp.bfloat16
    dma = pltpu.SemaphoreType.DMA

    u, far_u, facts = call(
        start_kernel, (pltpu.VMEM(square, bf16),) * 2 + (pltpu.VMEM((8, 128), f32),), [HB, HB], (VM,) * 3,
        [pltpu.VMEM(square, f32), pltpu.SMEM((1, 2), jnp.int32), dma((2,))],
    )(hbm(wavefunction), hbm(sector_dims))

    left_env, right_env = hbm(left_env), hbm(right_env)
    row_u = [vmem(swap(u, "sector", p)) for p in row_pairs]
    near_u = vmem(swap(u, "sector", near))
    far_u = vmem(swap(after(far_u, near_u), "sector", far))
    u, facts = vmem(u), vmem(facts)
    near_part, sums, left_far, right_far, left_row, right_row = call(
        functools.partial(near_kernel, size, width, rows),
        (pltpu.VMEM((2,) + square, f32), pltpu.VMEM((8, 128), f32)) + (pltpu.VMEM(side, bf16),) * 2 + (pltpu.VMEM(last, bf16),) * 2,
        [HB] * 3 + [VM] * 3, (VM,) * 6,
        [pltpu.VMEM(few, bf16)] * 2 + [pltpu.VMEM(square, f32), dma((2, 2)), dma((1, 2)), dma((rows, 2)), dma], LONG,
    )(left_env, right_env, hbm(wavefunction), facts, u, near_u)
    near_part, left_row, right_row = vmem(near_part), vmem(left_row), vmem(right_row)
    far_part = vmem(call(
        functools.partial(far_kernel, size, width), pltpu.VMEM(square, f32), [VM] * 3, VM, cost=LONG,
    )(vmem(left_far), vmem(right_far), far_u))
    row_part, w, far_w, sums = call(
        functools.partial(first_kernel, size, width, rows),
        (pltpu.VMEM((rows,) + square, f32),) + (pltpu.VMEM(square, bf16),) * 2 + (pltpu.VMEM((8, 128), f32),),
        [VM] * (7 + rows), (VM,) * 4,
    )(near_part, far_part, facts, vmem(sums), u, left_row, right_row, *row_u)

    row_w = [vmem(swap(w, "sector", p)) for p in row_pairs]
    near_w = vmem(swap(w, "sector", near))
    w = vmem(w)
    stats, far_w = call(
        spread_kernel, (jax.ShapeDtypeStruct((size, 8, 128), f32), pltpu.VMEM(square, bf16)), [VM] * 2 + [AN], (VM, AN),
        aliases={2: 1},
    )(vmem(sums), w, vmem(far_w))
    far_w = vmem(swap(after(far_w, near_w), "sector", far))
    stats = lax.all_to_all(stats, "sector", 0, 0, tiled=True)
    hw = call(
        functools.partial(image_kernel, size, width, rows), pltpu.VMEM(square, f32), [HB] * 2 + [VM] * (5 + rows), VM,
        [pltpu.VMEM(every, bf16)] * 2 + [dma((3, 2))],
    )(left_env, right_env, left_row, right_row, w, near_w, far_w, *row_w)
    return call(
        functools.partial(second_kernel, size, width, rows, cells),
        (jax.ShapeDtypeStruct((1,) + square, f32),) * 2, [VM] * 6, (HB, HB),
        [pltpu.VMEM(square, f32)] * 2 + [dma((2,))],
    )(facts, stats, vmem(hw), near_part, far_part, vmem(row_part))


def solution(mesh):
    placed = (
        P(("groups", "sector"), None, None),
        P(("groups", "sector"), None),
        P(("groups", "sector"), None, None, None),
        P(("groups", "sector"), None, None, None),
    )
    return jax.shard_map(
        body,
        mesh=mesh,
        in_specs=placed,
        out_specs=(P(("groups", "sector"), None, None), P(("groups", "sector"), None, None)),
        check_vma=False,
    )
```

profile of v0, /device:TPU:0, one launch (start us, length us, event | category | flops | bytes accessed | tf_op | source)
XLA Modules:
  0.0 33.9 jit_solution(12981633429969023680)
XLA Ops:
  0.6 1.0 %shard_map.59 = (bf16[256,256]{1,0:T(8,128)(2,1)S(1)}, bf16[256,256]{1,0:T(8,128)(2,1)S(1)}, f32[8,128]{1,0:T(8,128)S(1)}) custom-call(f32[1,256,256]{2,1,0:T(8,128)} %wave_hbm.3, s32[1,2]{1,0:T(1,128)} %dims_hbm.1), custom_call_target="tpu_custom_call" | custom-call | flops 1 | bytes 1 | tf_op jit(solution)/shard_map/pallas_call | solution.py:247
  1.7 0.5 %collective-permute-start = (bf16[256,256]{1,0:T(8,128)(2,1)S(1)}, bf16[256,256]{1,0:T(8,128)(2,1)S(1)}, u32[]{:S(2)}, u32[]{:S(2)}) collective-permute-start(bf16[256,256]{1,0:T(8,128)(2,1)S(1)} %get-tuple-element.18.self_ref.refs_4_), channel_id=1, source_target_pairs={{0,1},{1,0},{2,3},{3,2},{4,5},{5,4},{6,7},{7,6},{8,9},{9,8},{10,11... | collective-permute-start | bytes 393224 | tf_op jit(solution)/shard_map/ppermute | solution.py:38
  2.2 3.7 %collective-permute-start.2 = (bf16[256,256]{1,0:T(8,128)(2,1)S(1)}, bf16[256,256]{1,0:T(8,128)(2,1)S(1)}, u32[]{:S(2)}, u32[]{:S(2)}) collective-permute-start(bf16[256,256]{1,0:T(8,128)(2,1)S(1)} %get-tuple-element.18.self_ref.refs_4_), channel_id=1, source_target_pairs={{0,8},{1,9},{2,10},{3,11},{4,12},{5,13},{6,14},{7,15},{8,0},{9,1},... | collective-permute-start | bytes 393224 | tf_op jit(solution)/shard_map/ppermute | solution.py:38
  5.8 0.0 collective-permute-done.near_ref.refs_1_
  5.8 0.7 %collective-permute-start.1 = (bf16[256,256]{1,0:T(8,128)(2,1)S(1)}, bf16[256,256]{1,0:T(8,128)(2,1)S(1)}, u32[]{:S(2)}, u32[]{:S(2)}) collective-permute-start(bf16[256,256]{1,0:T(8,128)(2,1)S(1)} %shard_map.61), channel_id=1, source_target_pairs={{0,0},{1,2},{2,1},{3,4},{4,3},{5,6},{6,5},{7,7},{8,8},{9,10},{10,9... | collective-permute-start | bytes 393224 | tf_op jit(solution)/shard_map/ppermute | solution.py:38
  6.5 2.9 %shard_map.60 = (f32[2,256,256]{2,1,0:T(8,128)S(1)}, f32[8,128]{1,0:T(8,128)S(1)}, bf16[6,256,256]{2,1,0:T(8,128)(2,1)S(1)}, bf16[6,256,256]{2,1,0:T(8,128)(2,1)...) custom-call(bf16[1,26,256,256]{3,2,1,0:T(8,128)(2,1)} %left_hbm.3, ...), custom_call_target="tpu_custom_call" | custom-call | flops 4000000000 | bytes 1 | tf_op jit(solution)/shard_map/pallas_call | solution.py:257
  9.4 0.0 collective-permute-done.1.far_ref
  9.4 0.9 %shard_map.62.refs_1_.far_part_ref = f32[256,256]{1,0:T(8,128)S(1)} custom-call(bf16[6,256,256]{2,1,0:T(8,128)(2,1)S(1)} %get-tuple-element.20.left_ref, bf16[6,256,256]{2,1,0:T(8,128)(2,1)S(1)} %get-tuple-element.21.right_ref, bf16[256,256]{1,0:T(8,128)(2,1)S(1)} %collective-permute-done.1.far_ref), custom_call_target="tpu_custom_call" | custom-call | flops 4000000000 | bytes 1 | tf_op jit(solution)/shard_map/pallas_call | solution.py:264
  10.2 2.6 %collective-permute-done.2.refs_7_ = bf16[256,256]{1,0:T(8,128)(2,1)S(1)} collective-permute-done((bf16[256,256]{1,0:T(8,128)(2,1)S(1)}, bf16[256,256]{1,0:T(8,128)(2,1)S(1)}, u32[]{:S(2)}, u32[]{:S(2)}) %collective-permute-start.2) | collective-permute-done | bytes 131104 | tf_op jit(solution)/shard_map/ppermute | solution.py:38
  12.8 1.0 %shard_map.63 = (f32[1,256,256]{2,1,0:T(8,128)S(1)}, bf16[256,256]{1,0:T(8,128)(2,1)S(1)}, bf16[256,256]{1,0:T(8,128)(2,1)S(1)}, f32[8,128]{1,0:T(8,128)S(1)}) custom-call(f32[2,256,256]{2,1,0:T(8,128)S(1)} %get-tuple-element.19.refs_0_.near_part_ref, f32[256,256]{1,0:T(8,128)S(1)} %shard_map.62.refs_1_.far_part_ref, ...), custom_call_target="tpu_custom_call" | custom-call | flops 1 | bytes 1 | tf_op jit(solution)/shard_map/pallas_call | solution.py:267
  13.8 0.7 %collective-permute-start.3 = (bf16[256,256]{1,0:T(8,128)(2,1)S(1)}, bf16[256,256]{1,0:T(8,128)(2,1)S(1)}, u32[]{:S(2)}, u32[]{:S(2)}) collective-permute-start(bf16[256,256]{1,0:T(8,128)(2,1)S(1)} %get-tuple-element.27.w_ref.self_ref), channel_id=1, source_target_pairs={{0,1},{1,0},{2,3},{3,2},{4,5},{5,4},{6,7},{7,6},{8,9},{9,8},{10,11... | collective-permute-start | bytes 393224 | tf_op jit(solution)/shard_map/ppermute | solution.py:38
  14.5 1.0 %collective-permute-start.5 = (bf16[256,256]{1,0:T(8,128)(2,1)S(1)}, bf16[256,256]{1,0:T(8,128)(2,1)S(1)}, u32[]{:S(2)}, u32[]{:S(2)}) collective-permute-start(bf16[256,256]{1,0:T(8,128)(2,1)S(1)} %get-tuple-element.27.w_ref.self_ref), channel_id=1, source_target_pairs={{0,8},{1,9},{2,10},{3,11},{4,12},{5,13},{6,14},{7,15},{8,0},{9,1},... | collective-permute-start | bytes 393224 | tf_op jit(solution)/shard_map/ppermute | solution.py:38
  15.5 0.7 %shard_map.64 = (f32[16,8,128]{2,1,0:T(8,128)}, bf16[256,256]{1,0:T(8,128)(2,1)S(1)}) custom-call(f32[8,128]{1,0:T(8,128)S(1)} %get-tuple-element.26.sums_ref, bf16[256,256]{1,0:T(8,128)(2,1)S(1)} %get-tuple-element.27.w_ref.self_ref, bf16[256,256]{1,0:T(8,128)(2,1)S(1)} %get-tuple-element.28.held_in), custom_call_target="tpu_custom_call", output_to_operand_aliasing={{1}: (2, {})} | custom-call | flops 1 | bytes 1 | tf_op jit(solution)/shard_map/pallas_call | solution.py:276
  16.2 0.0 collective-permute-done.3.refs_1_.near_ref
  16.2 0.7 %collective-permute-start.4 = (bf16[256,256]{1,0:T(8,128)(2,1)S(1)}, bf16[256,256]{1,0:T(8,128)(2,1)S(1)}, u32[]{:S(2)}, u32[]{:S(2)}) collective-permute-start(bf16[256,256]{1,0:T(8,128)(2,1)S(1)} %shard_map.65), channel_id=1, source_target_pairs={{0,0},{1,2},{2,1},{3,4},{4,3},{5,6},{6,5},{7,7},{8,8},{9,10},{10,9... | collective-permute-start | bytes 393224 | tf_op jit(solution)/shard_map/ppermute | solution.py:38
  16.9 9.0 %all-to-all-start = ((f32[16,8,128]{2,1,0:T(8,128)}), f32[16,8,128]{2,1,0:T(8,128)S(1)}, u32[]{:S(2)}, u32[]{:S(2)}) async-start(f32[16,8,128]{2,1,0:T(8,128)} %get-tuple-element.29), calls=%async_computation | async-start | bytes 131072 | tf_op jit(solution)/shard_map/all_to_all | solution.py:281
  25.9 0.0 collective-permute-done.5.refs_0_
  25.9 0.0 collective-permute-done.4.far_ref
  25.9 3.5 %shard_map.66.hw_ref = f32[256,256]{1,0:T(8,128)S(1)} custom-call(bf16[1,26,256,256]{3,2,1,0:T(8,128)(2,1)} %left_hbm.3, bf16[1,26,256,256]{3,2,1,0:T(8,128)(2,1)} %right_hbm.3, bf16[6,256,256]{2,1,0:T(8,128)(2,1)S(1)} %get-tuple-element.24.refs_5_.left_row, bf16[6,256,256]{2,1,0:T(8,128)(2,1)S(1)} %get-tuple-element.25.refs_6_.right_row, ...), custom_call_target="tpu_custom_call" | custom-call | flops 1 | bytes 1 | tf_op jit(solution)/shard_map/pallas_call | solution.py:282
  29.4 3.3 %all-to-all-done.stats_ref = f32[16,8,128]{2,1,0:T(8,128)S(1)} async-done(((f32[16,8,128]{2,1,0:T(8,128)}), f32[16,8,128]{2,1,0:T(8,128)S(1)}, u32[]{:S(2)}, u32[]{:S(2)}) %all-to-all-start) | async-done | bytes 65568 | tf_op jit(solution)/shard_map/all_to_all | solution.py:281
  32.8 1.1 %shard_map.67 = (f32[1,256,256]{2,1,0:T(8,128)}, f32[1,256,256]{2,1,0:T(8,128)}) custom-call(f32[8,128]{1,0:T(8,128)S(1)} %get-tuple-element.17.facts_ref.refs_2_, f32[16,8,128]{2,1,0:T(8,128)S(1)} %all-to-all-done.stats_ref, f32[256,256]{1,0:T(8,128)S(1)} %shard_map.66.hw_ref, f32[2,256,256]{2,1,0:T(8,128)S(1)} %get-tuple-element.19.refs_0_.near_part_ref, ...), custom_call_target="tpu_custom_call" | custom-call | flops 1 | bytes 1 | tf_op jit(solution)/shard_map/pallas_call | solution.py:286
  (2 shorter events, 0.0 us)
Async XLA Ops:
  1.7 4.2 %collective-permute-start = (bf16[256,256]{1,0:T(8,128)(2,1)S(1)}, bf16[256,256]{1,0:T(8,128)(2,1)S(1)}, u32[]{:S(2)}, u32[]{:S(2)}) collective-permute-start(bf16[256,256]{1,0:T(8,128)(2,1)S(1)} %get-tuple-element.18.self_ref.refs_4_), channel_id=1, source_target_pairs={{0,1},{1,0},{2,3},{3,2},{4,5},{5,4},{6,7},{7,6},{8,9},{9,8},{10,11... | collective-permute-start | bytes 393224 | tf_op jit(solution)/shard_map/ppermute | solution.py:38
  2.2 10.6 %collective-permute-start.2 = (bf16[256,256]{1,0:T(8,128)(2,1)S(1)}, bf16[256,256]{1,0:T(8,128)(2,1)S(1)}, u32[]{:S(2)}, u32[]{:S(2)}) collective-permute-start(bf16[256,256]{1,0:T(8,128)(2,1)S(1)} %get-tuple-element.18.self_ref.refs_4_), channel_id=1, source_target_pairs={{0,8},{1,9},{2,10},{3,11},{4,12},{5,13},{6,14},{7,15},{8,0},{9,1},... | collective-permute-start | bytes 393224 | tf_op jit(solution)/shard_map/ppermute | solution.py:38
  5.8 3.5 %collective-permute-start.1 = (bf16[256,256]{1,0:T(8,128)(2,1)S(1)}, bf16[256,256]{1,0:T(8,128)(2,1)S(1)}, u32[]{:S(2)}, u32[]{:S(2)}) collective-permute-start(bf16[256,256]{1,0:T(8,128)(2,1)S(1)} %shard_map.61), channel_id=1, source_target_pairs={{0,0},{1,2},{2,1},{3,4},{4,3},{5,6},{6,5},{7,7},{8,8},{9,10},{10,9... | collective-permute-start | bytes 393224 | tf_op jit(solution)/shard_map/ppermute | solution.py:38
  13.8 2.4 %collective-permute-start.3 = (bf16[256,256]{1,0:T(8,128)(2,1)S(1)}, bf16[256,256]{1,0:T(8,128)(2,1)S(1)}, u32[]{:S(2)}, u32[]{:S(2)}) collective-permute-start(bf16[256,256]{1,0:T(8,128)(2,1)S(1)} %get-tuple-element.27.w_ref.self_ref), channel_id=1, source_target_pairs={{0,1},{1,0},{2,3},{3,2},{4,5},{5,4},{6,7},{7,6},{8,9},{9,8},{10,11... | collective-permute-start | bytes 393224 | tf_op jit(solution)/shard_map/ppermute | solution.py:38
  14.5 11.4 %collective-permute-start.5 = (bf16[256,256]{1,0:T(8,128)(2,1)S(1)}, bf16[256,256]{1,0:T(8,128)(2,1)S(1)}, u32[]{:S(2)}, u32[]{:S(2)}) collective-permute-start(bf16[256,256]{1,0:T(8,128)(2,1)S(1)} %get-tuple-element.27.w_ref.self_ref), channel_id=1, source_target_pairs={{0,8},{1,9},{2,10},{3,11},{4,12},{5,13},{6,14},{7,15},{8,0},{9,1},... | collective-permute-start | bytes 393224 | tf_op jit(solution)/shard_map/ppermute | solution.py:38
  16.2 9.7 %collective-permute-start.4 = (bf16[256,256]{1,0:T(8,128)(2,1)S(1)}, bf16[256,256]{1,0:T(8,128)(2,1)S(1)}, u32[]{:S(2)}, u32[]{:S(2)}) collective-permute-start(bf16[256,256]{1,0:T(8,128)(2,1)S(1)} %shard_map.65), channel_id=1, source_target_pairs={{0,0},{1,2},{2,1},{3,4},{4,3},{5,6},{6,5},{7,7},{8,8},{9,10},{10,9... | collective-permute-start | bytes 393224 | tf_op jit(solution)/shard_map/ppermute | solution.py:38
  16.9 15.9 %all-to-all-start = ((f32[16,8,128]{2,1,0:T(8,128)}), f32[16,8,128]{2,1,0:T(8,128)S(1)}, u32[]{:S(2)}, u32[]{:S(2)}) async-start(f32[16,8,128]{2,1,0:T(8,128)} %get-tuple-element.29), calls=%async_computation | async-start | bytes 131072 | tf_op jit(solution)/shard_map/all_to_all | solution.py:281
where the time goes:
time: 34.1 us; the launch traced here: 33.9 us
  starting transfers between devices  16.1 us (47%)
  Pallas kernels  11.1 us (33%)
  waiting for transfers between devices  5.92 us (17%)
  between operations  0.72 us (2%)
    all_to_all x1, starting transfers between devices, body(): stats = lax.all_to_all(stats, 'sector', 0, 0, tiled=True)  8.98 us
    ppermute x6, starting transfers between devices, swap(): lax.ppermute(x, axis, [(s, to.get(s, s)) for s in range(lax.axis_size(axi...  7.14 us
    pallas_call x1, Pallas kernels, body(): call(functools.partial(image_kernel, size, width, rows), pltpu.VMEM(squar...  3.52 us
    all_to_all x1, waiting for transfers between devices, body(): stats = lax.all_to_all(stats, 'sector', 0, 0, tiled=True)  3.35 us
    pallas_call x1, Pallas kernels, body(): call(functools.partial(near_kernel, size, width, rows), (pltpu.VMEM((2,)...  2.87 us
    ppermute x6, waiting for transfers between devices, swap(): lax.ppermute(x, axis, [(s, to.get(s, s)) for s in range(lax.axis_size(axi...  2.58 us
    pallas_call x1, Pallas kernels, body(): call(functools.partial(second_kernel, size, width, rows, cells), (jax.Sha...  1.1 us
    pallas_call x1, Pallas kernels, body(): call(start_kernel, (pltpu.VMEM(square, bf16),) * 2 + (pltpu.VMEM((8, 128)...  1.02 us
  transfers between devices with their start and end apart: 7, of which 2 were waited for; matrix products, arithmetic and copies ran while one was open for 0% of the time, Pallas kernels for 24%

commit v1 on v0

--- a/solution.py
+++ b/solution.py
@@ -9,6 +9,7 @@
 
 QD = 8
 SCALE = 1024.0
+QUARTERS = 4
 NT = (((1,), (1,)), ((), ()))
 VM = pl.BlockSpec(memory_space=pltpu.VMEM)
 HB = pl.BlockSpec(memory_space=pltpu.HBM)
@@ -41,7 +42,7 @@
 def swap_pairs(size):
     rows = size // QD
     near = [(s, s + 1) for s in range(0, size, 2)]
-    far = [(s, s + 1) for s in range(1, size - 1, 2) if s % QD != QD - 1]
+    far = [(s, s + 1 if s % QD != QD - 1 else s + 1 - QD) for s in range(1, size, 2)]
     row_even = [(s, s + QD) for r in range(0, rows - 1, 2) for s in range(r * QD, r * QD + QD)]
     row_odd = [(s, s + QD) for r in range(1, rows - 1, 2) for s in range(r * QD, r * QD + QD)]
     return near, far, [p for p in (row_even, row_odd) if p]
@@ -111,19 +112,31 @@
         copy.wait()
 
 
-def start_kernel(wave_hbm, dims_hbm, u_ref, far_u_ref, facts_ref, wave_ref, dims_ref, sems):
-    wave_copy = pltpu.make_async_copy(wave_hbm.at[0], wave_ref, sems.at[0])
-    dims_copy = pltpu.make_async_copy(dims_hbm, dims_ref, sems.at[1])
+def start_kernel(wave_hbm, dims_hbm, *refs):
+    u_refs, (facts_ref, wave_ref, dims_ref, sems) = refs[:3], refs[3:]
+    size = wave_ref.shape[0]
+    step = size // QUARTERS
+    dims_copy = pltpu.make_async_copy(dims_hbm, dims_ref, sems.at[QUARTERS])
     dims_copy.start()
-    wave_copy.start()
+    copies = [
+        pltpu.make_async_copy(wave_hbm.at[0, pl.ds(n * step, step)], wave_ref.at[pl.ds(n * step, step)], sems.at[n])
+        for n in range(QUARTERS)
+    ]
+    for copy in copies:
+        copy.start()
     dims_copy.wait()
+    row_count, col_count = dims_ref[0, 0], dims_ref[0, 1]
     lines = lax.broadcasted_iota(jnp.int32, (8, 128), 0)
-    facts = jnp.where(lines == 1, dims_ref[0, 0], jnp.where(lines == 2, dims_ref[0, 1], 0)).astype(jnp.float32)
-    wave_copy.wait()
-    held = jnp.where(live(facts, wave_ref.shape), wave_ref[...], 0.0)
-    for ref in (u_ref, far_u_ref):
-        ref[...] = (held * SCALE).astype(jnp.bfloat16)
-    facts_ref[...] = facts
+    facts_ref[...] = jnp.where(lines == 1, row_count, jnp.where(lines == 2, col_count, 0)).astype(jnp.float32)
+    col_ok = lax.broadcasted_iota(jnp.int32, (step, size), 1) < col_count
+    row = lax.broadcasted_iota(jnp.int32, (step, size), 0)
+    for n, copy in enumerate(copies):
+        copy.wait()
+        rows = pl.ds(n * step, step)
+        held = jnp.where((row < row_count - n * step) & col_ok, wave_ref[rows], 0.0)
+        block = (held * SCALE).astype(jnp.bfloat16)
+        for ref in u_refs:
+            ref[rows] = block
 
 
 def pass_kernel(*refs):
@@ -163,7 +176,7 @@
 
 def first_kernel(size, width, rows, *refs):
     near_part_ref, far_part_ref, facts_ref, sums_ref, u_ref, left_ref, right_ref = refs[:7]
-    row_refs, (out_ref, w_ref, far_w_ref, sums_out_ref) = refs[7 : 7 + rows], refs[7 + rows :]
+    row_refs, (out_ref, w_ref, near_w_ref, far_w_ref, stats_ref) = refs[7 : 7 + rows], refs[7 + rows :]
     _, _, there = place(size, width)
     image = near_part_ref[0] + near_part_ref[1] + far_part_ref[...]
     for r, source in enumerate(row_refs):
@@ -175,18 +188,15 @@
     square = sums_ref[1:2, 0:1]
     cross = total(u * image)
     rho = jnp.where(square > 0.0, cross / square, 0.0)
-    for ref in (w_ref, far_w_ref):
-        ref[...] = (image - rho * u).astype(jnp.bfloat16)
+    w = image - rho * u
+    for ref in (w_ref, near_w_ref, far_w_ref):
+        ref[...] = w.astype(jnp.bfloat16)
     lines = lax.broadcasted_iota(jnp.int32, (8, 128), 0)
-    sums_out_ref[...] = jnp.where(lines == 2, cross, jnp.where(lines == 4, rho, sums_ref[...]))
-
-
-def spread_kernel(sums_ref, w_ref, held_in, out_ref, held_out):
-    w = w_ref[...].astype(jnp.float32)
-    lines = lax.broadcasted_iota(jnp.int32, (8, 128), 0)
-    sums = jnp.where(lines == 3, total(w * w), sums_ref[...])
-    for n in range(out_ref.shape[0]):
-        out_ref[n] = sums
+    stats = sums_ref[...]
+    for line, value in ((2, cross), (3, total(w * w)), (4, rho)):
+        stats = jnp.where(lines == line, value, stats)
+    for n in range(stats_ref.shape[0]):
+        stats_ref[n] = stats
 
 
 def image_kernel(size, width, rows, left_hbm, right_hbm, left_row, right_row, self_ref, near_ref, far_ref, *refs):
@@ -244,16 +254,16 @@
     f32, bf16 = jnp.float32, jnp.bfloat16
     dma = pltpu.SemaphoreType.DMA
 
-    u, far_u, facts = call(
-        start_kernel, (pltpu.VMEM(square, bf16),) * 2 + (pltpu.VMEM((8, 128), f32),), [HB, HB], (VM,) * 3,
-        [pltpu.VMEM(square, f32), pltpu.SMEM((1, 2), jnp.int32), dma((2,))],
+    u, near_u, far_u, facts = call(
+        start_kernel, (pltpu.VMEM(square, bf16),) * 3 + (pltpu.VMEM((8, 128), f32),), [HB, HB], (VM,) * 4,
+        [pltpu.VMEM(square, f32), pltpu.SMEM((1, 2), jnp.int32), dma((QUARTERS + 1,))],
     )(hbm(wavefunction), hbm(sector_dims))
 
     left_env, right_env = hbm(left_env), hbm(right_env)
+    u, facts = vmem(u), vmem(facts)
     row_u = [vmem(swap(u, "sector", p)) for p in row_pairs]
-    near_u = vmem(swap(u, "sector", near))
+    near_u = vmem(swap(near_u, "sector", near))
     far_u = vmem(swap(after(far_u, near_u), "sector", far))
-    u, facts = vmem(u), vmem(facts)
     near_part, sums, left_far, right_far, left_row, right_row = call(
         functools.partial(near_kernel, size, width, rows),
         (pltpu.VMEM((2,) + square, f32), pltpu.VMEM((8, 128), f32)) + (pltpu.VMEM(side, bf16),) * 2 + (pltpu.VMEM(last, bf16),) * 2,
@@ -264,19 +274,15 @@
     far_part = vmem(call(
         functools.partial(far_kernel, size, width), pltpu.VMEM(square, f32), [VM] * 3, VM, cost=LONG,
     )(vmem(left_far), vmem(right_far), far_u))
-    row_part, w, far_w, sums = call(
+    row_part, w, near_w, far_w, stats = call(
         functools.partial(first_kernel, size, width, rows),
-        (pltpu.VMEM((rows,) + square, f32),) + (pltpu.VMEM(square, bf16),) * 2 + (pltpu.VMEM((8, 128), f32),),
-        [VM] * (7 + rows), (VM,) * 4,
+        (pltpu.VMEM((rows,) + square, f32),) + (pltpu.VMEM(square, bf16),) * 3 + (jax.ShapeDtypeStruct((size, 8, 128), f32),),
+        [VM] * (7 + rows), (VM,) * 5,
     )(near_part, far_part, facts, vmem(sums), u, left_row, right_row, *row_u)
 
+    w = vmem(w)
     row_w = [vmem(swap(w, "sector", p)) for p in row_pairs]
-    near_w = vmem(swap(w, "sector", near))
-    w = vmem(w)
-    stats, far_w = call(
-        spread_kernel, (jax.ShapeDtypeStruct((size, 8, 128), f32), pltpu.VMEM(square, bf16)), [VM] * 2 + [AN], (VM, AN),
-        aliases={2: 1},
-    )(vmem(sums), w, vmem(far_w))
+    near_w = vmem(swap(near_w, "sector", near))
     far_w = vmem(swap(after(far_w, near_w), "sector", far))
     stats = lax.all_to_all(stats, "sector", 0, 0, tiled=True)
     hw = call(

time: 34.1 us -> 31.6 us (0.927)
  waiting for transfers between devices: 5.92 us -> 4.34 us
  starting transfers between devices: 16.1 us -> 15.2 us
    all_to_all x1, starting transfers between devices: 8.98 us -> 3.5 us  [body(): stats = lax.all_to_all(stats, 'sector', 0, 0, tiled=True)]
    ppermute x6, starting transfers between devices: 7.14 us -> 11.7 us  [swap(): lax.ppermute(x, axis, [(s, to.get(s, s)) for s in range(lax.axis_size(axi...]
    all_to_all x1, waiting for transfers between devices: 3.35 us -> 2.48 us  [body(): stats = lax.all_to_all(stats, 'sector', 0, 0, tiled=True)]
    pallas_call x2 -> x1, Pallas kernels: 1.75 us -> 0.99 us  [body(): call(start_kernel, (pltpu.VMEM(square, bf16),) * 3 + (pltpu.VMEM((8, 128)...]
    pallas_call x1, Pallas kernels: 1.01 us -> 1.77 us  [body(): call(functools.partial(first_kernel, size, width, rows), (pltpu.VMEM((row...]
    ppermute x6, waiting for transfers between devices: 2.58 us -> 1.86 us  [swap(): lax.ppermute(x, axis, [(s, to.get(s, s)) for s in range(lax.axis_size(axi...]
  transfers between devices with their start and end apart: 7 -> 7, of which waited for: 2 -> 4; matrix products, arithmetic and copies ran while one was open for 0% -> 0% of each run, Pallas kernels for 24% -> 23%
where the time goes in v1:
time: 31.6 us; the launch traced here: 31.3 us
  starting transfers between devices  15.2 us (48%)
  Pallas kernels  11.1 us (35%)
  waiting for transfers between devices  4.34 us (14%)
  between operations  0.68 us (2%)
    ppermute x6, starting transfers between devices, swap(): lax.ppermute(x, axis, [(s, to.get(s, s)) for s in range(lax.axis_size(axi...  11.7 us
    pallas_call x1, Pallas kernels, body(): call(functools.partial(image_kernel, size, width, rows), pltpu.VMEM(squar...  3.52 us
    all_to_all x1, starting transfers between devices, body(): stats = lax.all_to_all(stats, 'sector', 0, 0, tiled=True)  3.5 us
    pallas_call x1, Pallas kernels, body(): call(functools.partial(near_kernel, size, width, rows), (pltpu.VMEM((2,)...  2.86 us
    all_to_all x1, waiting for transfers between devices, body(): stats = lax.all_to_all(stats, 'sector', 0, 0, tiled=True)  2.48 us
    ppermute x6, waiting for transfers between devices, swap(): lax.ppermute(x, axis, [(s, to.get(s, s)) for s in range(lax.axis_size(axi...  1.86 us
    pallas_call x1, Pallas kernels, body(): call(functools.partial(first_kernel, size, width, rows), (pltpu.VMEM((row...  1.77 us
    pallas_call x1, Pallas kernels, body(): call(functools.partial(second_kernel, size, width, rows, cells), (jax.Sha...  1.1 us
  transfers between devices with their start and end apart: 7, of which 4 were waited for; matrix products, arithmetic and copies ran while one was open for 0% of the time, Pallas kernels for 23%

profile of v1, /device:TPU:0, one launch (start us, length us, event | category | flops | bytes accessed | tf_op | source)
XLA Modules:
  0.0 31.3 jit_solution(15408676949565520878)
XLA Ops:
  0.6 1.0 %shard_map.59 = (bf16[256,256]{1,0:T(8,128)(2,1)S(1)}, bf16[256,256]{1,0:T(8,128)(2,1)S(1)}, bf16[256,256]{1,0:T(8,128)(2,1)S(1)}, f32[8,128]{1,0:T(8,128)S(1)}) custom-call(f32[1,256,256]{2,1,0:T(8,128)} %wave_hbm.3, s32[1,2]{1,0:T(1,128)} %dims_hbm.1), custom_call_target="tpu_custom_call" | custom-call | flops 1 | bytes 1 | tf_op jit(solution)/shard_map/pallas_call | solution.py:257
  1.6 0.5 %collective-permute-start = (bf16[256,256]{1,0:T(8,128)(2,1)S(1)}, bf16[256,256]{1,0:T(8,128)(2,1)S(1)}, u32[]{:S(2)}, u32[]{:S(2)}) collective-permute-start(bf16[256,256]{1,0:T(8,128)(2,1)S(1)} %get-tuple-element.19), channel_id=1, source_target_pairs={{0,1},{1,0},{2,3},{3,2},{4,5},{5,4},{6,7},{7,6},{8,9},{9,8},{10,11... | collective-permute-start | bytes 393224 | tf_op jit(solution)/shard_map/ppermute | solution.py:39
  2.1 3.7 %collective-permute-start.2 = (bf16[256,256]{1,0:T(8,128)(2,1)S(1)}, bf16[256,256]{1,0:T(8,128)(2,1)S(1)}, u32[]{:S(2)}, u32[]{:S(2)}) collective-permute-start(bf16[256,256]{1,0:T(8,128)(2,1)S(1)} %get-tuple-element.18.self_ref.refs_4_), channel_id=1, source_target_pairs={{0,8},{1,9},{2,10},{3,11},{4,12},{5,13},{6,14},{7,15},{8,0},{9,1},... | collective-permute-start | bytes 393224 | tf_op jit(solution)/shard_map/ppermute | solution.py:39
  5.8 0.0 collective-permute-done.near_ref.refs_1_
  5.8 2.3 %collective-permute-start.1 = (bf16[256,256]{1,0:T(8,128)(2,1)S(1)}, bf16[256,256]{1,0:T(8,128)(2,1)S(1)}, u32[]{:S(2)}, u32[]{:S(2)}) collective-permute-start(bf16[256,256]{1,0:T(8,128)(2,1)S(1)} %shard_map.61), channel_id=1, source_target_pairs={{0,7},{1,2},{2,1},{3,4},{4,3},{5,6},{6,5},{7,0},{8,15},{9,10},{10,... | collective-permute-start | bytes 393224 | tf_op jit(solution)/shard_map/ppermute | solution.py:39
  8.1 2.9 %shard_map.60 = (f32[2,256,256]{2,1,0:T(8,128)S(1)}, f32[8,128]{1,0:T(8,128)S(1)}, bf16[6,256,256]{2,1,0:T(8,128)(2,1)S(1)}, bf16[6,256,256]{2,1,0:T(8,128)(2,1)...) custom-call(bf16[1,26,256,256]{3,2,1,0:T(8,128)(2,1)} %left_hbm.3, ...), custom_call_target="tpu_custom_call" | custom-call | flops 4000000000 | bytes 1 | tf_op jit(solution)/shard_map/pallas_call | solution.py:267
  11.0 0.3 collective-permute-done.1.far_ref
  11.2 0.8 %shard_map.62.refs_1_.far_part_ref = f32[256,256]{1,0:T(8,128)S(1)} custom-call(bf16[6,256,256]{2,1,0:T(8,128)(2,1)S(1)} %get-tuple-element.21.left_ref, bf16[6,256,256]{2,1,0:T(8,128)(2,1)S(1)} %get-tuple-element.22.right_ref, bf16[256,256]{1,0:T(8,128)(2,1)S(1)} %collective-permute-done.1.far_ref), custom_call_target="tpu_custom_call" | custom-call | flops 4000000000 | bytes 1 | tf_op jit(solution)/shard_map/pallas_call | solution.py:274
  12.1 0.7 %collective-permute-done.2.refs_7_ = bf16[256,256]{1,0:T(8,128)(2,1)S(1)} collective-permute-done((bf16[256,256]{1,0:T(8,128)(2,1)S(1)}, bf16[256,256]{1,0:T(8,128)(2,1)S(1)}, u32[]{:S(2)}, u32[]{:S(2)}) %collective-permute-start.2) | collective-permute-done | bytes 131104 | tf_op jit(solution)/shard_map/ppermute | solution.py:39
  12.8 1.8 %shard_map.63 = (f32[1,256,256]{2,1,0:T(8,128)S(1)}, bf16[256,256]{1,0:T(8,128)(2,1)S(1)}, bf16[256,256]{1,0:T(8,128)(2,1)S(1)}, bf16[256,256]{1,0:T(8,128)(2,1)S(1)}, f32[16,8,128]{2,1,0:T(8,128)}) custom-call(f32[2,256,256]{2,1,0:T(8,128)S(1)} %get-tuple-element.20.refs_0_.near_part_ref, f32[256,256]{1,0:T(8,128)S(1)} %shard_map.62.refs_1_.far_part_ref, ...), custom_call_target="tpu_custom_call" | custom-call | flops 1 | bytes 1 | tf_op jit(solution)/shard_map/pallas_call | solution.py:277
  14.6 0.1 collective-permute-start.3
  14.7 1.8 %collective-permute-start.5 = (bf16[256,256]{1,0:T(8,128)(2,1)S(1)}, bf16[256,256]{1,0:T(8,128)(2,1)S(1)}, u32[]{:S(2)}, u32[]{:S(2)}) collective-permute-start(bf16[256,256]{1,0:T(8,128)(2,1)S(1)} %get-tuple-element.28.self_ref), channel_id=1, source_target_pairs={{0,8},{1,9},{2,10},{3,11},{4,12},{5,13},{6,14},{7,15},{8,0},{9,1},... | collective-permute-start | bytes 393224 | tf_op jit(solution)/shard_map/ppermute | solution.py:39
  16.6 0.0 collective-permute-done.3.refs_1_.near_ref
  16.6 3.3 %collective-permute-start.4 = (bf16[256,256]{1,0:T(8,128)(2,1)S(1)}, bf16[256,256]{1,0:T(8,128)(2,1)S(1)}, u32[]{:S(2)}, u32[]{:S(2)}) collective-permute-start(bf16[256,256]{1,0:T(8,128)(2,1)S(1)} %shard_map.64), channel_id=1, source_target_pairs={{0,7},{1,2},{2,1},{3,4},{4,3},{5,6},{6,5},{7,0},{8,15},{9,10},{10,... | collective-permute-start | bytes 393224 | tf_op jit(solution)/shard_map/ppermute | solution.py:39
  19.8 3.5 %all-to-all-start = ((f32[16,8,128]{2,1,0:T(8,128)}), f32[16,8,128]{2,1,0:T(8,128)S(1)}, u32[]{:S(2)}, u32[]{:S(2)}) async-start(f32[16,8,128]{2,1,0:T(8,128)} %get-tuple-element.27), calls=%async_computation | async-start | bytes 131072 | tf_op jit(solution)/shard_map/all_to_all | solution.py:287
  23.4 0.8 %collective-permute-done.5.refs_0_ = bf16[256,256]{1,0:T(8,128)(2,1)S(1)} collective-permute-done((bf16[256,256]{1,0:T(8,128)(2,1)S(1)}, bf16[256,256]{1,0:T(8,128)(2,1)S(1)}, u32[]{:S(2)}, u32[]{:S(2)}) %collective-permute-start.5) | collective-permute-done | bytes 131104 | tf_op jit(solution)/shard_map/ppermute | solution.py:39
  24.2 0.0 collective-permute-done.4.far_ref
  24.2 3.5 %shard_map.65.hw_ref = f32[256,256]{1,0:T(8,128)S(1)} custom-call(bf16[1,26,256,256]{3,2,1,0:T(8,128)(2,1)} %left_hbm.3, bf16[1,26,256,256]{3,2,1,0:T(8,128)(2,1)} %right_hbm.3, bf16[6,256,256]{2,1,0:T(8,128)(2,1)S(1)} %get-tuple-element.25.refs_5_.left_row, bf16[6,256,256]{2,1,0:T(8,128)(2,1)S(1)} %get-tuple-element.26.refs_6_.right_row, ...), custom_call_target="tpu_custom_call" | custom-call | flops 1 | bytes 1 | tf_op jit(solution)/shard_map/pallas_call | solution.py:288
  27.7 2.5 %all-to-all-done.stats_ref = f32[16,8,128]{2,1,0:T(8,128)S(1)} async-done(((f32[16,8,128]{2,1,0:T(8,128)}), f32[16,8,128]{2,1,0:T(8,128)S(1)}, u32[]{:S(2)}, u32[]{:S(2)}) %all-to-all-start) | async-done | bytes 65568 | tf_op jit(solution)/shard_map/all_to_all | solution.py:287
  30.2 1.1 %shard_map.66 = (f32[1,256,256]{2,1,0:T(8,128)}, f32[1,256,256]{2,1,0:T(8,128)}) custom-call(f32[8,128]{1,0:T(8,128)S(1)} %get-tuple-element.17.facts_ref.refs_2_, f32[16,8,128]{2,1,0:T(8,128)S(1)} %all-to-all-done.stats_ref, f32[256,256]{1,0:T(8,128)S(1)} %shard_map.65.hw_ref, f32[2,256,256]{2,1,0:T(8,128)S(1)} %get-tuple-element.20.refs_0_.near_part_ref, ...), custom_call_target="tpu_custom_call" | custom-call | flops 1 | bytes 1 | tf_op jit(solution)/shard_map/pallas_call | solution.py:292
  (2 shorter events, 0.0 us)
Async XLA Ops:
  1.6 4.2 %collective-permute-start = (bf16[256,256]{1,0:T(8,128)(2,1)S(1)}, bf16[256,256]{1,0:T(8,128)(2,1)S(1)}, u32[]{:S(2)}, u32[]{:S(2)}) collective-permute-start(bf16[256,256]{1,0:T(8,128)(2,1)S(1)} %get-tuple-element.19), channel_id=1, source_target_pairs={{0,1},{1,0},{2,3},{3,2},{4,5},{5,4},{6,7},{7,6},{8,9},{9,8},{10,11... | collective-permute-start | bytes 393224 | tf_op jit(solution)/shard_map/ppermute | solution.py:39
  2.1 10.7 %collective-permute-start.2 = (bf16[256,256]{1,0:T(8,128)(2,1)S(1)}, bf16[256,256]{1,0:T(8,128)(2,1)S(1)}, u32[]{:S(2)}, u32[]{:S(2)}) collective-permute-start(bf16[256,256]{1,0:T(8,128)(2,1)S(1)} %get-tuple-element.18.self_ref.refs_4_), channel_id=1, source_target_pairs={{0,8},{1,9},{2,10},{3,11},{4,12},{5,13},{6,14},{7,15},{8,0},{9,1},... | collective-permute-start | bytes 393224 | tf_op jit(solution)/shard_map/ppermute | solution.py:39
  5.8 5.4 %collective-permute-start.1 = (bf16[256,256]{1,0:T(8,128)(2,1)S(1)}, bf16[256,256]{1,0:T(8,128)(2,1)S(1)}, u32[]{:S(2)}, u32[]{:S(2)}) collective-permute-start(bf16[256,256]{1,0:T(8,128)(2,1)S(1)} %shard_map.61), channel_id=1, source_target_pairs={{0,7},{1,2},{2,1},{3,4},{4,3},{5,6},{6,5},{7,0},{8,15},{9,10},{10,... | collective-permute-start | bytes 393224 | tf_op jit(solution)/shard_map/ppermute | solution.py:39
  14.6 2.0 %collective-permute-start.3 = (bf16[256,256]{1,0:T(8,128)(2,1)S(1)}, bf16[256,256]{1,0:T(8,128)(2,1)S(1)}, u32[]{:S(2)}, u32[]{:S(2)}) collective-permute-start(bf16[256,256]{1,0:T(8,128)(2,1)S(1)} %get-tuple-element.29), channel_id=1, source_target_pairs={{0,1},{1,0},{2,3},{3,2},{4,5},{5,4},{6,7},{7,6},{8,9},{9,8},{10,11... | collective-permute-start | bytes 393224 | tf_op jit(solution)/shard_map/ppermute | solution.py:39
  14.7 9.5 %collective-permute-start.5 = (bf16[256,256]{1,0:T(8,128)(2,1)S(1)}, bf16[256,256]{1,0:T(8,128)(2,1)S(1)}, u32[]{:S(2)}, u32[]{:S(2)}) collective-permute-start(bf16[256,256]{1,0:T(8,128)(2,1)S(1)} %get-tuple-element.28.self_ref), channel_id=1, source_target_pairs={{0,8},{1,9},{2,10},{3,11},{4,12},{5,13},{6,14},{7,15},{8,0},{9,1},... | collective-permute-start | bytes 393224 | tf_op jit(solution)/shard_map/ppermute | solution.py:39
  16.6 7.6 %collective-permute-start.4 = (bf16[256,256]{1,0:T(8,128)(2,1)S(1)}, bf16[256,256]{1,0:T(8,128)(2,1)S(1)}, u32[]{:S(2)}, u32[]{:S(2)}) collective-permute-start(bf16[256,256]{1,0:T(8,128)(2,1)S(1)} %shard_map.64), channel_id=1, source_target_pairs={{0,7},{1,2},{2,1},{3,4},{4,3},{5,6},{6,5},{7,0},{8,15},{9,10},{10,... | collective-permute-start | bytes 393224 | tf_op jit(solution)/shard_map/ppermute | solution.py:39
  19.8 10.4 %all-to-all-start = ((f32[16,8,128]{2,1,0:T(8,128)}), f32[16,8,128]{2,1,0:T(8,128)S(1)}, u32[]{:S(2)}, u32[]{:S(2)}) async-start(f32[16,8,128]{2,1,0:T(8,128)} %get-tuple-element.27), calls=%async_computation | async-start | bytes 131072 | tf_op jit(solution)/shard_map/all_to_all | solution.py:287

commit v2 on v1

--- a/solution.py
+++ b/solution.py
@@ -42,10 +42,22 @@
 def swap_pairs(size):
     rows = size // QD
     near = [(s, s + 1) for s in range(0, size, 2)]
-    far = [(s, s + 1 if s % QD != QD - 1 else s + 1 - QD) for s in range(1, size, 2)]
     row_even = [(s, s + QD) for r in range(0, rows - 1, 2) for s in range(r * QD, r * QD + QD)]
     row_odd = [(s, s + QD) for r in range(1, rows - 1, 2) for s in range(r * QD, r * QD + QD)]
-    return near, far, [p for p in (row_even, row_odd) if p]
+    return near, [p for p in (row_even, row_odd) if p]
+
+
+def far_swap(x):
+    groups, size = lax.axis_size("groups"), lax.axis_size("sector")
+    pairs = []
+    for g in range(groups):
+        for s in range(size):
+            if s % QD == 0 or s % QD == QD - 1:
+                to, partner = (g ^ 1 if g ^ 1 < groups else g), s
+            else:
+                to, partner = g, s + 1 if s % 2 else s - 1
+            pairs.append((g * size + s, to * size + partner))
+    return lax.ppermute(x, ("groups", "sector"), pairs)
 
 
 def place(size, width):
@@ -113,7 +125,7 @@
 
 
 def start_kernel(wave_hbm, dims_hbm, *refs):
-    u_refs, (facts_ref, wave_ref, dims_ref, sems) = refs[:3], refs[3:]
+    u_refs, (facts_ref, wave_ref, dims_ref, sems) = refs[:2], refs[2:]
     size = wave_ref.shape[0]
     step = size // QUARTERS
     dims_copy = pltpu.make_async_copy(dims_hbm, dims_ref, sems.at[QUARTERS])
@@ -176,7 +188,7 @@
 
 def first_kernel(size, width, rows, *refs):
     near_part_ref, far_part_ref, facts_ref, sums_ref, u_ref, left_ref, right_ref = refs[:7]
-    row_refs, (out_ref, w_ref, near_w_ref, far_w_ref, stats_ref) = refs[7 : 7 + rows], refs[7 + rows :]
+    row_refs, (out_ref, w_ref, stats_ref) = refs[7 : 7 + rows], refs[7 + rows :]
     _, _, there = place(size, width)
     image = near_part_ref[0] + near_part_ref[1] + far_part_ref[...]
     for r, source in enumerate(row_refs):
@@ -189,8 +201,7 @@
     cross = total(u * image)
     rho = jnp.where(square > 0.0, cross / square, 0.0)
     w = image - rho * u
-    for ref in (w_ref, near_w_ref, far_w_ref):
-        ref[...] = w.astype(jnp.bfloat16)
+    w_ref[...] = w.astype(jnp.bfloat16)
     lines = lax.broadcasted_iota(jnp.int32, (8, 128), 0)
     stats = sums_ref[...]
     for line, value in ((2, cross), (3, total(w * w)), (4, rho)):
@@ -199,20 +210,22 @@
         stats_ref[n] = stats
 
 
-def image_kernel(size, width, rows, left_hbm, right_hbm, left_row, right_row, self_ref, near_ref, far_ref, *refs):
-    row_refs, (out_ref, left_own, right_own, sems) = refs[:rows], refs[rows:]
-    offsets, _, there = place(size, width)
-    own = fetch(left_hbm, right_hbm, left_own, right_own, sems, [(0, 2)] + [(o, width) for o in offsets[:2]])
+def image_kernel(size, width, rows, *refs):
+    row_refs, refs = refs[:rows], refs[rows:]
+    far_ref, near_ref, self_ref, left_row, right_row, left_hbm, right_hbm, out_ref, left_own, right_own, sems = refs
+    _, _, there = place(size, width)
+    own = fetch(left_hbm, right_hbm, left_own, right_own, sems, [(0, 2 + width), (2 + width, width)])
     image = None
     for r, source in enumerate(row_refs):
         piece = terms(only(there[1 + r], source[...]), left_row, right_row, r * width, width)
         image = piece if image is None else image + piece
+    odd = lax.rem(lax.axis_index("sector"), 2) == 1
+    near, far = near_ref[...], only(there[0], far_ref[...])
     finish(own[0])
     image = image + terms(self_ref[...], left_own, right_own, 0, 2)
+    image = image + terms(jnp.where(odd, near, far), left_own, right_own, 2, width)
     finish(own[1])
-    image = image + terms(near_ref[...], left_own, right_own, 2, width)
-    finish(own[2])
-    out_ref[...] = image + terms(only(there[0], far_ref[...]), left_own, right_own, 2 + width, width)
+    out_ref[...] = image + terms(jnp.where(odd, far, near), left_own, right_own, 2 + width, width)
 
 
 def second_kernel(size, width, rows, cells, facts_ref, stats_ref, hw_ref, near_part_ref, far_part_ref, row_part_ref,
@@ -247,23 +260,23 @@
     block = wavefunction.shape[1]
     square = (block, block)
     width = (right_env.shape[1] - 2) // 4
-    near, far, row_pairs = swap_pairs(size)
+    near, row_pairs = swap_pairs(size)
     rows = len(row_pairs)
     cells = float(size * block * block)
     few, every, side, last = ((n,) + square for n in (2 + width, 2 + 2 * width, width, rows * width))
     f32, bf16 = jnp.float32, jnp.bfloat16
     dma = pltpu.SemaphoreType.DMA
 
-    u, near_u, far_u, facts = call(
-        start_kernel, (pltpu.VMEM(square, bf16),) * 3 + (pltpu.VMEM((8, 128), f32),), [HB, HB], (VM,) * 4,
+    u, far_u, facts = call(
+        start_kernel, (pltpu.VMEM(square, bf16),) * 2 + (pltpu.VMEM((8, 128), f32),), [HB, HB], (VM,) * 3,
         [pltpu.VMEM(square, f32), pltpu.SMEM((1, 2), jnp.int32), dma((QUARTERS + 1,))],
     )(hbm(wavefunction), hbm(sector_dims))
 
     left_env, right_env = hbm(left_env), hbm(right_env)
     u, facts = vmem(u), vmem(facts)
     row_u = [vmem(swap(u, "sector", p)) for p in row_pairs]
-    near_u = vmem(swap(near_u, "sector", near))
-    far_u = vmem(swap(after(far_u, near_u), "sector", far))
+    near_u = vmem(swap(u, "sector", near))
+    far_u = vmem(far_swap(after(far_u, near_u)))
     near_part, sums, left_far, right_far, left_row, right_row = call(
         functools.partial(near_kernel, size, width, rows),
         (pltpu.VMEM((2,) + square, f32), pltpu.VMEM((8, 128), f32)) + (pltpu.VMEM(side, bf16),) * 2 + (pltpu.VMEM(last, bf16),) * 2,
@@ -274,21 +287,21 @@
     far_part = vmem(call(
         functools.partial(far_kernel, size, width), pltpu.VMEM(square, f32), [VM] * 3, VM, cost=LONG,
     )(vmem(left_far), vmem(right_far), far_u))
-    row_part, w, near_w, far_w, stats = call(
+    row_part, w, stats = call(
         functools.partial(first_kernel, size, width, rows),
-        (pltpu.VMEM((rows,) + square, f32),) + (pltpu.VMEM(square, bf16),) * 3 + (jax.ShapeDtypeStruct((size, 8, 128), f32),),
-        [VM] * (7 + rows), (VM,) * 5,
+        (pltpu.VMEM((rows,) + square, f32),) + (pltpu.VMEM(square, bf16), jax.ShapeDtypeStruct((size, 8, 128), f32)),
+        [VM] * (7 + rows), (VM,) * 3,
     )(near_part, far_part, facts, vmem(sums), u, left_row, right_row, *row_u)
 
     w = vmem(w)
     row_w = [vmem(swap(w, "sector", p)) for p in row_pairs]
-    near_w = vmem(swap(near_w, "sector", near))
-    far_w = vmem(swap(after(far_w, near_w), "sector", far))
+    near_w = vmem(swap(w, "sector", near))
+    far_w = vmem(far_swap(w))
     stats = lax.all_to_all(stats, "sector", 0, 0, tiled=True)
     hw = call(
-        functools.partial(image_kernel, size, width, rows), pltpu.VMEM(square, f32), [HB] * 2 + [VM] * (5 + rows), VM,
-        [pltpu.VMEM(every, bf16)] * 2 + [dma((3, 2))],
-    )(left_env, right_env, left_row, right_row, w, near_w, far_w, *row_w)
+        functools.partial(image_kernel, size, width, rows), pltpu.VMEM(square, f32), [VM] * (5 + rows) + [HB] * 2, VM,
+        [pltpu.VMEM(every, bf16)] * 2 + [dma((2, 2))],
+    )(*row_w, far_w, near_w, w, left_row, right_row, left_env, right_env)
     return call(
         functools.partial(second_kernel, size, width, rows, cells),
         (jax.ShapeDtypeStruct((1,) + square, f32),) * 2, [VM] * 6, (HB, HB),

time: 31.6 us -> 30.2 us (0.956)
  starting transfers between devices: 15.2 us -> 13.1 us
  waiting for transfers between devices: 4.34 us -> 5.34 us
    ppermute x6 -> x4, starting transfers between devices: 11.7 us -> 4.51 us  [swap(): lax.ppermute(x, axis, [(s, to.get(s, s)) for s in range(lax.axis_size(axi...]
    ppermute x0 -> x2, starting transfers between devices: none -> 3.04 us  [far_swap(): return lax.ppermute(x, ('groups', 'sector'), pairs)]
    all_to_all x1, starting transfers between devices: 3.5 us -> 5.56 us  [body(): stats = lax.all_to_all(stats, 'sector', 0, 0, tiled=True)]
    ppermute x6 -> x4, waiting for transfers between devices: 1.86 us -> 2.67 us  [swap(): lax.ppermute(x, axis, [(s, to.get(s, s)) for s in range(lax.axis_size(axi...]
    ppermute x0 -> x2, waiting for transfers between devices: none -> 0.58 us  [far_swap(): return lax.ppermute(x, ('groups', 'sector'), pairs)]
    all_to_all x1, waiting for transfers between devices: 2.48 us -> 2.09 us  [body(): stats = lax.all_to_all(stats, 'sector', 0, 0, tiled=True)]
where the time goes in v2:
time: 30.2 us; the launch traced here: 30 us
  starting transfers between devices  13.1 us (43%)
  Pallas kernels  10.9 us (36%)
  waiting for transfers between devices  5.34 us (18%)
  between operations  0.68 us (2%)
    all_to_all x1, starting transfers between devices, body(): stats = lax.all_to_all(stats, 'sector', 0, 0, tiled=True)  5.56 us
    ppermute x4, starting transfers between devices, swap(): lax.ppermute(x, axis, [(s, to.get(s, s)) for s in range(lax.axis_size(axi...  4.51 us
    pallas_call x1, Pallas kernels, body(): call(functools.partial(image_kernel, size, width, rows), pltpu.VMEM(squar...  3.31 us
    ppermute x2, starting transfers between devices, far_swap(): return lax.ppermute(x, ('groups', 'sector'), pairs)  3.04 us
    pallas_call x1, Pallas kernels, body(): call(functools.partial(near_kernel, size, width, rows), (pltpu.VMEM((2,)...  2.86 us
    ppermute x4, waiting for transfers between devices, swap(): lax.ppermute(x, axis, [(s, to.get(s, s)) for s in range(lax.axis_size(axi...  2.67 us
    all_to_all x1, waiting for transfers between devices, body(): stats = lax.all_to_all(stats, 'sector', 0, 0, tiled=True)  2.09 us
    pallas_call x1, Pallas kernels, body(): call(functools.partial(first_kernel, size, width, rows), (pltpu.VMEM((row...  1.75 us
  transfers between devices with their start and end apart: 7, of which 4 were waited for; matrix products, arithmetic and copies ran while one was open for 0% of the time, Pallas kernels for 23%

profile of v2, /device:TPU:0, one launch (start us, length us, event | category | flops | bytes accessed | tf_op | source)
XLA Modules:
  0.0 30.0 jit_solution(11774058412705194447)
XLA Ops:
  0.6 1.0 %shard_map.59 = (bf16[256,256]{1,0:T(8,128)(2,1)S(1)}, bf16[256,256]{1,0:T(8,128)(2,1)S(1)}, f32[8,128]{1,0:T(8,128)S(1)}) custom-call(f32[1,256,256]{2,1,0:T(8,128)} %wave_hbm.3, s32[1,2]{1,0:T(1,128)} %dims_hbm.1), custom_call_target="tpu_custom_call" | custom-call | flops 1 | bytes 1 | tf_op jit(solution)/shard_map/pallas_call | solution.py:270
  1.6 0.5 %collective-permute-start = (bf16[256,256]{1,0:T(8,128)(2,1)S(1)}, bf16[256,256]{1,0:T(8,128)(2,1)S(1)}, u32[]{:S(2)}, u32[]{:S(2)}) collective-permute-start(bf16[256,256]{1,0:T(8,128)(2,1)S(1)} %get-tuple-element.15.self_ref.refs_4_), channel_id=1, source_target_pairs={{0,1},{1,0},{2,3},{3,2},{4,5},{5,4},{6,7},{7,6},{8,9},{9,8},{10,11... | collective-permute-start | bytes 393224 | tf_op jit(solution)/shard_map/ppermute | solution.py:39
  2.1 3.7 %collective-permute-start.2 = (bf16[256,256]{1,0:T(8,128)(2,1)S(1)}, bf16[256,256]{1,0:T(8,128)(2,1)S(1)}, u32[]{:S(2)}, u32[]{:S(2)}) collective-permute-start(bf16[256,256]{1,0:T(8,128)(2,1)S(1)} %get-tuple-element.15.self_ref.refs_4_), channel_id=1, source_target_pairs={{0,8},{1,9},{2,10},{3,11},{4,12},{5,13},{6,14},{7,15},{8,0},{9,1},... | collective-permute-start | bytes 393224 | tf_op jit(solution)/shard_map/ppermute | solution.py:39
  5.8 0.0 collective-permute-done.near_ref.refs_1_
  5.8 1.5 %collective-permute-start.1 = (bf16[256,256]{1,0:T(8,128)(2,1)S(1)}, bf16[256,256]{1,0:T(8,128)(2,1)S(1)}, u32[]{:S(2)}, u32[]{:S(2)}) collective-permute-start(bf16[256,256]{1,0:T(8,128)(2,1)S(1)} %shard_map.61), channel_id=1, source_target_pairs={{0,16},{1,2},{2,1},{3,4},{4,3},{5,6},{6,5},{7,23},{8,24},{9,10},{1... | collective-permute-start | bytes 393224 | tf_op jit(solution)/shard_map/ppermute | solution.py:60
  7.3 2.9 %shard_map.60 = (f32[2,256,256]{2,1,0:T(8,128)S(1)}, f32[8,128]{1,0:T(8,128)S(1)}, bf16[6,256,256]{2,1,0:T(8,128)(2,1)S(1)}, bf16[6,256,256]{2,1,0:T(8,128)(2,1)...) custom-call(bf16[1,26,256,256]{3,2,1,0:T(8,128)(2,1)} %refs_6_.1, ...), custom_call_target="tpu_custom_call" | custom-call | flops 4000000000 | bytes 1 | tf_op jit(solution)/shard_map/pallas_call | solution.py:280
  10.2 0.6 %collective-permute-done.1.far_ref = bf16[256,256]{1,0:T(8,128)(2,1)S(1)} collective-permute-done((bf16[256,256]{1,0:T(8,128)(2,1)S(1)}, bf16[256,256]{1,0:T(8,128)(2,1)S(1)}, u32[]{:S(2)}, u32[]{:S(2)}) %collective-permute-start.1) | collective-permute-done | bytes 131104 | tf_op jit(solution)/shard_map/ppermute | solution.py:60
  10.8 0.8 %shard_map.62.refs_1_.far_part_ref = f32[256,256]{1,0:T(8,128)S(1)} custom-call(bf16[6,256,256]{2,1,0:T(8,128)(2,1)S(1)} %get-tuple-element.17.left_ref, bf16[6,256,256]{2,1,0:T(8,128)(2,1)S(1)} %get-tuple-element.18.right_ref, bf16[256,256]{1,0:T(8,128)(2,1)S(1)} %collective-permute-done.1.far_ref), custom_call_target="tpu_custom_call" | custom-call | flops 4000000000 | bytes 1 | tf_op jit(solution)/shard_map/pallas_call | solution.py:287
  11.6 1.2 %collective-permute-done.2.refs_7_ = bf16[256,256]{1,0:T(8,128)(2,1)S(1)} collective-permute-done((bf16[256,256]{1,0:T(8,128)(2,1)S(1)}, bf16[256,256]{1,0:T(8,128)(2,1)S(1)}, u32[]{:S(2)}, u32[]{:S(2)}) %collective-permute-start.2) | collective-permute-done | bytes 131104 | tf_op jit(solution)/shard_map/ppermute | solution.py:39
  12.8 1.8 %shard_map.63 = (f32[1,256,256]{2,1,0:T(8,128)S(1)}, bf16[256,256]{1,0:T(8,128)(2,1)S(1)}, f32[16,8,128]{2,1,0:T(8,128)}) custom-call(f32[2,256,256]{2,1,0:T(8,128)S(1)} %get-tuple-element.16.refs_0_.near_part_ref, f32[256,256]{1,0:T(8,128)S(1)} %shard_map.62.refs_1_.far_part_ref, f32[8,128]{1,0:T(8,128)S(1)} %get-tuple-element.14.facts_ref.refs_2_, ...), custom_call_target="tpu_custom_call" | custom-call | flops 1 | bytes 1 | tf_op jit(solution)/shard_map/pallas_call | solution.py:290
  14.6 0.1 collective-permute-start.3
  14.7 1.5 %collective-permute-start.4 = (bf16[256,256]{1,0:T(8,128)(2,1)S(1)}, bf16[256,256]{1,0:T(8,128)(2,1)S(1)}, u32[]{:S(2)}, u32[]{:S(2)}) collective-permute-start(bf16[256,256]{1,0:T(8,128)(2,1)S(1)} %get-tuple-element.24.refs_3_), channel_id=1, source_target_pairs={{0,16},{1,2},{2,1},{3,4},{4,3},{5,6},{6,5},{7,23},{8,24},{9,10},{1... | collective-permute-start | bytes 393224 | tf_op jit(solution)/shard_map/ppermute | solution.py:60
  16.2 0.2 collective-permute-start.5
  16.4 5.6 %all-to-all-start = ((f32[16,8,128]{2,1,0:T(8,128)}), f32[16,8,128]{2,1,0:T(8,128)S(1)}, u32[]{:S(2)}, u32[]{:S(2)}) async-start(f32[16,8,128]{2,1,0:T(8,128)} %get-tuple-element.23), calls=%async_computation | async-start | bytes 131072 | tf_op jit(solution)/shard_map/all_to_all | solution.py:300
  22.0 1.5 %collective-permute-done.3.refs_0_ = bf16[256,256]{1,0:T(8,128)(2,1)S(1)} collective-permute-done((bf16[256,256]{1,0:T(8,128)(2,1)S(1)}, bf16[256,256]{1,0:T(8,128)(2,1)S(1)}, u32[]{:S(2)}, u32[]{:S(2)}) %collective-permute-start.3) | collective-permute-done | bytes 131104 | tf_op jit(solution)/shard_map/ppermute | solution.py:39
  23.5 0.0 collective-permute-done.4.refs_1_
  23.5 0.0 collective-permute-done.5.refs_2_
  23.5 3.3 %shard_map.64.hw_ref = f32[256,256]{1,0:T(8,128)S(1)} custom-call(bf16[256,256]{1,0:T(8,128)(2,1)S(1)} %collective-permute-done.3.refs_0_, bf16[256,256]{1,0:T(8,128)(2,1)S(1)} %collective-permute-done.4.refs_1_, bf16[256,256]{1,0:T(8,128)(2,1)S(1)} %collective-permute-done.5.refs_2_, bf16[256,256]{1,0:T(8,128)(2,1)S(1)} %get-tuple-element.24.refs_3_, ...), custom_call_target="tpu_custom_call" | custom-call | flops 1 | bytes 1 | tf_op jit(solution)/shard_map/pallas_call | solution.py:301
  26.8 2.1 %all-to-all-done.stats_ref = f32[16,8,128]{2,1,0:T(8,128)S(1)} async-done(((f32[16,8,128]{2,1,0:T(8,128)}), f32[16,8,128]{2,1,0:T(8,128)S(1)}, u32[]{:S(2)}, u32[]{:S(2)}) %all-to-all-start) | async-done | bytes 65568 | tf_op jit(solution)/shard_map/all_to_all | solution.py:300
  28.9 1.1 %shard_map.65 = (f32[1,256,256]{2,1,0:T(8,128)}, f32[1,256,256]{2,1,0:T(8,128)}) custom-call(f32[8,128]{1,0:T(8,128)S(1)} %get-tuple-element.14.facts_ref.refs_2_, f32[16,8,128]{2,1,0:T(8,128)S(1)} %all-to-all-done.stats_ref, f32[256,256]{1,0:T(8,128)S(1)} %shard_map.64.hw_ref, f32[2,256,256]{2,1,0:T(8,128)S(1)} %get-tuple-element.16.refs_0_.near_part_ref, ...), custom_call_target="tpu_custom_call" | custom-call | flops 1 | bytes 1 | tf_op jit(solution)/shard_map/pallas_call | solution.py:305
  (1 shorter events, 0.0 us)
Async XLA Ops:
  1.6 4.2 %collective-permute-start = (bf16[256,256]{1,0:T(8,128)(2,1)S(1)}, bf16[256,256]{1,0:T(8,128)(2,1)S(1)}, u32[]{:S(2)}, u32[]{:S(2)}) collective-permute-start(bf16[256,256]{1,0:T(8,128)(2,1)S(1)} %get-tuple-element.15.self_ref.refs_4_), channel_id=1, source_target_pairs={{0,1},{1,0},{2,3},{3,2},{4,5},{5,4},{6,7},{7,6},{8,9},{9,8},{10,11... | collective-permute-start | bytes 393224 | tf_op jit(solution)/shard_map/ppermute | solution.py:39
  2.1 10.7 %collective-permute-start.2 = (bf16[256,256]{1,0:T(8,128)(2,1)S(1)}, bf16[256,256]{1,0:T(8,128)(2,1)S(1)}, u32[]{:S(2)}, u32[]{:S(2)}) collective-permute-start(bf16[256,256]{1,0:T(8,128)(2,1)S(1)} %get-tuple-element.15.self_ref.refs_4_), channel_id=1, source_target_pairs={{0,8},{1,9},{2,10},{3,11},{4,12},{5,13},{6,14},{7,15},{8,0},{9,1},... | collective-permute-start | bytes 393224 | tf_op jit(solution)/shard_map/ppermute | solution.py:39
  5.8 5.0 %collective-permute-start.1 = (bf16[256,256]{1,0:T(8,128)(2,1)S(1)}, bf16[256,256]{1,0:T(8,128)(2,1)S(1)}, u32[]{:S(2)}, u32[]{:S(2)}) collective-permute-start(bf16[256,256]{1,0:T(8,128)(2,1)S(1)} %shard_map.61), channel_id=1, source_target_pairs={{0,16},{1,2},{2,1},{3,4},{4,3},{5,6},{6,5},{7,23},{8,24},{9,10},{1... | collective-permute-start | bytes 393224 | tf_op jit(solution)/shard_map/ppermute | solution.py:60
  14.6 8.9 %collective-permute-start.3 = (bf16[256,256]{1,0:T(8,128)(2,1)S(1)}, bf16[256,256]{1,0:T(8,128)(2,1)S(1)}, u32[]{:S(2)}, u32[]{:S(2)}) collective-permute-start(bf16[256,256]{1,0:T(8,128)(2,1)S(1)} %get-tuple-element.24.refs_3_), channel_id=1, source_target_pairs={{0,8},{1,9},{2,10},{3,11},{4,12},{5,13},{6,14},{7,15},{8,0},{9,1},... | collective-permute-start | bytes 393224 | tf_op jit(solution)/shard_map/ppermute | solution.py:39
  14.7 8.8 %collective-permute-start.4 = (bf16[256,256]{1,0:T(8,128)(2,1)S(1)}, bf16[256,256]{1,0:T(8,128)(2,1)S(1)}, u32[]{:S(2)}, u32[]{:S(2)}) collective-permute-start(bf16[256,256]{1,0:T(8,128)(2,1)S(1)} %get-tuple-element.24.refs_3_), channel_id=1, source_target_pairs={{0,16},{1,2},{2,1},{3,4},{4,3},{5,6},{6,5},{7,23},{8,24},{9,10},{1... | collective-permute-start | bytes 393224 | tf_op jit(solution)/shard_map/ppermute | solution.py:60
  16.2 7.3 %collective-permute-start.5 = (bf16[256,256]{1,0:T(8,128)(2,1)S(1)}, bf16[256,256]{1,0:T(8,128)(2,1)S(1)}, u32[]{:S(2)}, u32[]{:S(2)}) collective-permute-start(bf16[256,256]{1,0:T(8,128)(2,1)S(1)} %get-tuple-element.24.refs_3_), channel_id=1, source_target_pairs={{0,1},{1,0},{2,3},{3,2},{4,5},{5,4},{6,7},{7,6},{8,9},{9,8},{10,11... | collective-permute-start | bytes 393224 | tf_op jit(solution)/shard_map/ppermute | solution.py:39
  16.4 12.5 %all-to-all-start = ((f32[16,8,128]{2,1,0:T(8,128)}), f32[16,8,128]{2,1,0:T(8,128)S(1)}, u32[]{:S(2)}, u32[]{:S(2)}) async-start(f32[16,8,128]{2,1,0:T(8,128)} %get-tuple-element.23), calls=%async_computation | async-start | bytes 131072 | tf_op jit(solution)/shard_map/all_to_all | solution.py:300

commit v3 on v2

--- a/solution.py
+++ b/solution.py
@@ -202,10 +202,10 @@
     rho = jnp.where(square > 0.0, cross / square, 0.0)
     w = image - rho * u
     w_ref[...] = w.astype(jnp.bfloat16)
-    lines = lax.broadcasted_iota(jnp.int32, (8, 128), 0)
-    stats = sums_ref[...]
-    for line, value in ((2, cross), (3, total(w * w)), (4, rho)):
-        stats = jnp.where(lines == line, value, stats)
+    lane = lax.broadcasted_iota(jnp.int32, (1, 128), 1)
+    stats = jnp.zeros((1, 128), jnp.float32)
+    for n, value in enumerate((sums_ref[0:1, 0:1], square, cross, total(w * w), rho)):
+        stats = jnp.where(lane == n, value, stats)
     for n in range(stats_ref.shape[0]):
         stats_ref[n] = stats
 
@@ -232,9 +232,9 @@
                   first_hbm, second_hbm, first_ref, second_ref, sems):
     _, partners, _ = place(size, width)
     facts = facts_ref[...]
-    stats = stats_ref[...]
-    sums = jnp.sum(stats, axis=0)
-    start, square, cross, inner = (sums[i : i + 1, 0:1] for i in range(4))
+    stats = stats_ref[:, 0, :]
+    sums = jnp.sum(stats, axis=0, keepdims=True)
+    start, square, cross, inner = (sums[:, i : i + 1] for i in range(4))
     scale = lax.rsqrt(start / cells + 1e-06) * (1.0 / SCALE)
     parts = [near_part_ref[0], near_part_ref[1], far_part_ref[...]] + [row_part_ref[r] for r in range(rows)]
     cell = live(facts, parts[0].shape)
@@ -242,12 +242,12 @@
     first_copy = pltpu.make_async_copy(first_ref, first_hbm.at[0], sems.at[0])
     first_copy.start()
     rho = cross / square
-    gap = stats[:, 4:5, 0:1] - rho[None]
-    residual = inner + jnp.sum(stats[:, 1:2, 0:1] * gap * gap, axis=0)
+    gap = stats[:, 4:5] - rho
+    residual = inner + jnp.sum(stats[:, 1:2] * gap * gap, axis=0, keepdims=True)
     second_scale = scale * lax.rsqrt(scale * scale * (residual / cells) + 1e-06)
     image = hw_ref[...]
     for n, part in enumerate(parts):
-        image = image + (stats_ref[partners[n], 4:5, 0:1] - rho) * part
+        image = image + (stats_ref[partners[n], :, 4:5] - rho) * part
     second_ref[...] = jnp.where(cell, image, 0.0) * second_scale
     second_copy = pltpu.make_async_copy(second_ref, second_hbm.at[0], sems.at[1])
     second_copy.start()
@@ -289,7 +289,7 @@
     )(vmem(left_far), vmem(right_far), far_u))
     row_part, w, stats = call(
         functools.partial(first_kernel, size, width, rows),
-        (pltpu.VMEM((rows,) + square, f32),) + (pltpu.VMEM(square, bf16), jax.ShapeDtypeStruct((size, 8, 128), f32)),
+        (pltpu.VMEM((rows,) + square, f32),) + (pltpu.VMEM(square, bf16), jax.ShapeDtypeStruct((size, 1, 128), f32)),
         [VM] * (7 + rows), (VM,) * 3,
     )(near_part, far_part, facts, vmem(sums), u, left_row, right_row, *row_u)
 

time: 30.2 us -> 29.7 us (0.983)
  waiting for transfers between devices: 5.34 us -> 4.78 us
    all_to_all x1, waiting for transfers between devices: 2.09 us -> 1.52 us  [body(): stats = lax.all_to_all(stats, 'sector', 0, 0, tiled=True)]
  transfers between devices with their start and end apart: 7 -> 7, of which waited for: 4 -> 4; matrix products, arithmetic and copies ran while one was open for 0% -> 0% of each run, Pallas kernels for 23% -> 24%
where the time goes in v3:
time: 29.7 us; the launch traced here: 29.5 us
  starting transfers between devices  13.1 us (44%)
  Pallas kernels  11 us (37%)
  waiting for transfers between devices  4.78 us (16%)
  between operations  0.68 us (2%)
    all_to_all x1, starting transfers between devices, body(): stats = lax.all_to_all(stats, 'sector', 0, 0, tiled=True)  5.56 us
    ppermute x4, starting transfers between devices, swap(): lax.ppermute(x, axis, [(s, to.get(s, s)) for s in range(lax.axis_size(axi...  4.51 us
    pallas_call x1, Pallas kernels, body(): call(functools.partial(image_kernel, size, width, rows), pltpu.VMEM(squar...  3.3 us
    ppermute x2, starting transfers between devices, far_swap(): return lax.ppermute(x, ('groups', 'sector'), pairs)  3.04 us
    pallas_call x1, Pallas kernels, body(): call(functools.partial(near_kernel, size, width, rows), (pltpu.VMEM((2,)...  2.86 us
    ppermute x4, waiting for transfers between devices, swap(): lax.ppermute(x, axis, [(s, to.get(s, s)) for s in range(lax.axis_size(axi...  2.67 us
    pallas_call x1, Pallas kernels, body(): call(functools.partial(first_kernel, size, width, rows), (pltpu.VMEM((row...  1.73 us
    all_to_all x1, waiting for transfers between devices, body(): stats = lax.all_to_all(stats, 'sector', 0, 0, tiled=True)  1.52 us
  transfers between devices with their start and end apart: 7, of which 4 were waited for; matrix products, arithmetic and copies ran while one was open for 0% of the time, Pallas kernels for 24%

profile of v3, /device:TPU:0, one launch (start us, length us, event | category | flops | bytes accessed | tf_op | source)
XLA Modules:
  0.0 29.5 jit_solution(892841999759701342)
XLA Ops:
  0.6 1.0 %shard_map.59 = (bf16[256,256]{1,0:T(8,128)(2,1)S(1)}, bf16[256,256]{1,0:T(8,128)(2,1)S(1)}, f32[8,128]{1,0:T(8,128)S(1)}) custom-call(f32[1,256,256]{2,1,0:T(8,128)} %wave_hbm.3, s32[1,2]{1,0:T(1,128)} %dims_hbm.1), custom_call_target="tpu_custom_call" | custom-call | flops 1 | bytes 1 | tf_op jit(solution)/shard_map/pallas_call | solution.py:270
  1.6 0.5 %collective-permute-start = (bf16[256,256]{1,0:T(8,128)(2,1)S(1)}, bf16[256,256]{1,0:T(8,128)(2,1)S(1)}, u32[]{:S(2)}, u32[]{:S(2)}) collective-permute-start(bf16[256,256]{1,0:T(8,128)(2,1)S(1)} %get-tuple-element.15.self_ref.refs_4_), channel_id=1, source_target_pairs={{0,1},{1,0},{2,3},{3,2},{4,5},{5,4},{6,7},{7,6},{8,9},{9,8},{10,11... | collective-permute-start | bytes 393224 | tf_op jit(solution)/shard_map/ppermute | solution.py:39
  2.1 3.7 %collective-permute-start.2 = (bf16[256,256]{1,0:T(8,128)(2,1)S(1)}, bf16[256,256]{1,0:T(8,128)(2,1)S(1)}, u32[]{:S(2)}, u32[]{:S(2)}) collective-permute-start(bf16[256,256]{1,0:T(8,128)(2,1)S(1)} %get-tuple-element.15.self_ref.refs_4_), channel_id=1, source_target_pairs={{0,8},{1,9},{2,10},{3,11},{4,12},{5,13},{6,14},{7,15},{8,0},{9,1},... | collective-permute-start | bytes 393224 | tf_op jit(solution)/shard_map/ppermute | solution.py:39
  5.8 0.0 collective-permute-done.near_ref.refs_1_
  5.8 1.5 %collective-permute-start.1 = (bf16[256,256]{1,0:T(8,128)(2,1)S(1)}, bf16[256,256]{1,0:T(8,128)(2,1)S(1)}, u32[]{:S(2)}, u32[]{:S(2)}) collective-permute-start(bf16[256,256]{1,0:T(8,128)(2,1)S(1)} %shard_map.61), channel_id=1, source_target_pairs={{0,16},{1,2},{2,1},{3,4},{4,3},{5,6},{6,5},{7,23},{8,24},{9,10},{1... | collective-permute-start | bytes 393224 | tf_op jit(solution)/shard_map/ppermute | solution.py:60
  7.3 2.9 %shard_map.60 = (f32[2,256,256]{2,1,0:T(8,128)S(1)}, f32[8,128]{1,0:T(8,128)S(1)}, bf16[6,256,256]{2,1,0:T(8,128)(2,1)S(1)}, bf16[6,256,256]{2,1,0:T(8,128)(2,1)...) custom-call(bf16[1,26,256,256]{3,2,1,0:T(8,128)(2,1)} %refs_6_.1, ...), custom_call_target="tpu_custom_call" | custom-call | flops 4000000000 | bytes 1 | tf_op jit(solution)/shard_map/pallas_call | solution.py:280
  10.2 0.6 %collective-permute-done.1.far_ref = bf16[256,256]{1,0:T(8,128)(2,1)S(1)} collective-permute-done((bf16[256,256]{1,0:T(8,128)(2,1)S(1)}, bf16[256,256]{1,0:T(8,128)(2,1)S(1)}, u32[]{:S(2)}, u32[]{:S(2)}) %collective-permute-start.1) | collective-permute-done | bytes 131104 | tf_op jit(solution)/shard_map/ppermute | solution.py:60
  10.8 0.8 %shard_map.62.refs_1_.far_part_ref = f32[256,256]{1,0:T(8,128)S(1)} custom-call(bf16[6,256,256]{2,1,0:T(8,128)(2,1)S(1)} %get-tuple-element.17.left_ref, bf16[6,256,256]{2,1,0:T(8,128)(2,1)S(1)} %get-tuple-element.18.right_ref, bf16[256,256]{1,0:T(8,128)(2,1)S(1)} %collective-permute-done.1.far_ref), custom_call_target="tpu_custom_call" | custom-call | flops 4000000000 | bytes 1 | tf_op jit(solution)/shard_map/pallas_call | solution.py:287
  11.6 1.2 %collective-permute-done.2.refs_7_ = bf16[256,256]{1,0:T(8,128)(2,1)S(1)} collective-permute-done((bf16[256,256]{1,0:T(8,128)(2,1)S(1)}, bf16[256,256]{1,0:T(8,128)(2,1)S(1)}, u32[]{:S(2)}, u32[]{:S(2)}) %collective-permute-start.2) | collective-permute-done | bytes 131104 | tf_op jit(solution)/shard_map/ppermute | solution.py:39
  12.8 1.7 %shard_map.63 = (f32[1,256,256]{2,1,0:T(8,128)S(1)}, bf16[256,256]{1,0:T(8,128)(2,1)S(1)}, f32[16,1,128]{2,1,0:T(1,128)}) custom-call(f32[2,256,256]{2,1,0:T(8,128)S(1)} %get-tuple-element.16.refs_0_.near_part_ref, f32[256,256]{1,0:T(8,128)S(1)} %shard_map.62.refs_1_.far_part_ref, f32[8,128]{1,0:T(8,128)S(1)} %get-tuple-element.14.facts_ref.refs_2_, ...), custom_call_target="tpu_custom_call" | custom-call | flops 1 | bytes 1 | tf_op jit(solution)/shard_map/pallas_call | solution.py:290
  14.5 0.1 collective-permute-start.3
  14.6 1.5 %collective-permute-start.4 = (bf16[256,256]{1,0:T(8,128)(2,1)S(1)}, bf16[256,256]{1,0:T(8,128)(2,1)S(1)}, u32[]{:S(2)}, u32[]{:S(2)}) collective-permute-start(bf16[256,256]{1,0:T(8,128)(2,1)S(1)} %get-tuple-element.24.refs_3_), channel_id=1, source_target_pairs={{0,16},{1,2},{2,1},{3,4},{4,3},{5,6},{6,5},{7,23},{8,24},{9,10},{1... | collective-permute-start | bytes 393224 | tf_op jit(solution)/shard_map/ppermute | solution.py:60
  16.2 0.2 collective-permute-start.5
  16.4 5.6 %all-to-all-start = ((f32[16,1,128]{2,1,0:T(1,128)}), f32[16,1,128]{2,1,0:T(1,128)S(1)}, u32[]{:S(2)}, u32[]{:S(2)}) async-start(f32[16,1,128]{2,1,0:T(1,128)} %get-tuple-element.23), calls=%async_computation | async-start | bytes 16384 | tf_op jit(solution)/shard_map/all_to_all | solution.py:300
  22.0 1.5 %collective-permute-done.3.refs_0_ = bf16[256,256]{1,0:T(8,128)(2,1)S(1)} collective-permute-done((bf16[256,256]{1,0:T(8,128)(2,1)S(1)}, bf16[256,256]{1,0:T(8,128)(2,1)S(1)}, u32[]{:S(2)}, u32[]{:S(2)}) %collective-permute-start.3) | collective-permute-done | bytes 131104 | tf_op jit(solution)/shard_map/ppermute | solution.py:39
  23.4 0.0 collective-permute-done.4.refs_1_
  23.4 0.0 collective-permute-done.5.refs_2_
  23.4 3.3 %shard_map.64.hw_ref = f32[256,256]{1,0:T(8,128)S(1)} custom-call(bf16[256,256]{1,0:T(8,128)(2,1)S(1)} %collective-permute-done.3.refs_0_, bf16[256,256]{1,0:T(8,128)(2,1)S(1)} %collective-permute-done.4.refs_1_, bf16[256,256]{1,0:T(8,128)(2,1)S(1)} %collective-permute-done.5.refs_2_, bf16[256,256]{1,0:T(8,128)(2,1)S(1)} %get-tuple-element.24.refs_3_, ...), custom_call_target="tpu_custom_call" | custom-call | flops 1 | bytes 1 | tf_op jit(solution)/shard_map/pallas_call | solution.py:301
  26.8 1.5 %all-to-all-done.stats_ref = f32[16,1,128]{2,1,0:T(1,128)S(1)} async-done(((f32[16,1,128]{2,1,0:T(1,128)}), f32[16,1,128]{2,1,0:T(1,128)S(1)}, u32[]{:S(2)}, u32[]{:S(2)}) %all-to-all-start) | async-done | bytes 8224 | tf_op jit(solution)/shard_map/all_to_all | solution.py:300
  28.3 1.2 %shard_map.65 = (f32[1,256,256]{2,1,0:T(8,128)}, f32[1,256,256]{2,1,0:T(8,128)}) custom-call(f32[8,128]{1,0:T(8,128)S(1)} %get-tuple-element.14.facts_ref.refs_2_, f32[16,1,128]{2,1,0:T(1,128)S(1)} %all-to-all-done.stats_ref, f32[256,256]{1,0:T(8,128)S(1)} %shard_map.64.hw_ref, f32[2,256,256]{2,1,0:T(8,128)S(1)} %get-tuple-element.16.refs_0_.near_part_ref, ...), custom_call_target="tpu_custom_call" | custom-call | flops 1 | bytes 1 | tf_op jit(solution)/shard_map/pallas_call | solution.py:305
  (1 shorter events, 0.0 us)
Async XLA Ops:
  1.6 4.2 %collective-permute-start = (bf16[256,256]{1,0:T(8,128)(2,1)S(1)}, bf16[256,256]{1,0:T(8,128)(2,1)S(1)}, u32[]{:S(2)}, u32[]{:S(2)}) collective-permute-start(bf16[256,256]{1,0:T(8,128)(2,1)S(1)} %get-tuple-element.15.self_ref.refs_4_), channel_id=1, source_target_pairs={{0,1},{1,0},{2,3},{3,2},{4,5},{5,4},{6,7},{7,6},{8,9},{9,8},{10,11... | collective-permute-start | bytes 393224 | tf_op jit(solution)/shard_map/ppermute | solution.py:39
  2.1 10.7 %collective-permute-start.2 = (bf16[256,256]{1,0:T(8,128)(2,1)S(1)}, bf16[256,256]{1,0:T(8,128)(2,1)S(1)}, u32[]{:S(2)}, u32[]{:S(2)}) collective-permute-start(bf16[256,256]{1,0:T(8,128)(2,1)S(1)} %get-tuple-element.15.self_ref.refs_4_), channel_id=1, source_target_pairs={{0,8},{1,9},{2,10},{3,11},{4,12},{5,13},{6,14},{7,15},{8,0},{9,1},... | collective-permute-start | bytes 393224 | tf_op jit(solution)/shard_map/ppermute | solution.py:39
  5.8 5.0 %collective-permute-start.1 = (bf16[256,256]{1,0:T(8,128)(2,1)S(1)}, bf16[256,256]{1,0:T(8,128)(2,1)S(1)}, u32[]{:S(2)}, u32[]{:S(2)}) collective-permute-start(bf16[256,256]{1,0:T(8,128)(2,1)S(1)} %shard_map.61), channel_id=1, source_target_pairs={{0,16},{1,2},{2,1},{3,4},{4,3},{5,6},{6,5},{7,23},{8,24},{9,10},{1... | collective-permute-start | bytes 393224 | tf_op jit(solution)/shard_map/ppermute | solution.py:60
  14.5 8.9 %collective-permute-start.3 = (bf16[256,256]{1,0:T(8,128)(2,1)S(1)}, bf16[256,256]{1,0:T(8,128)(2,1)S(1)}, u32[]{:S(2)}, u32[]{:S(2)}) collective-permute-start(bf16[256,256]{1,0:T(8,128)(2,1)S(1)} %get-tuple-element.24.refs_3_), channel_id=1, source_target_pairs={{0,8},{1,9},{2,10},{3,11},{4,12},{5,13},{6,14},{7,15},{8,0},{9,1},... | collective-permute-start | bytes 393224 | tf_op jit(solution)/shard_map/ppermute | solution.py:39
  14.6 8.8 %collective-permute-start.4 = (bf16[256,256]{1,0:T(8,128)(2,1)S(1)}, bf16[256,256]{1,0:T(8,128)(2,1)S(1)}, u32[]{:S(2)}, u32[]{:S(2)}) collective-permute-start(bf16[256,256]{1,0:T(8,128)(2,1)S(1)} %get-tuple-element.24.refs_3_), channel_id=1, source_target_pairs={{0,16},{1,2},{2,1},{3,4},{4,3},{5,6},{6,5},{7,23},{8,24},{9,10},{1... | collective-permute-start | bytes 393224 | tf_op jit(solution)/shard_map/ppermute | solution.py:60
  16.2 7.3 %collective-permute-start.5 = (bf16[256,256]{1,0:T(8,128)(2,1)S(1)}, bf16[256,256]{1,0:T(8,128)(2,1)S(1)}, u32[]{:S(2)}, u32[]{:S(2)}) collective-permute-start(bf16[256,256]{1,0:T(8,128)(2,1)S(1)} %get-tuple-element.24.refs_3_), channel_id=1, source_target_pairs={{0,1},{1,0},{2,3},{3,2},{4,5},{5,4},{6,7},{7,6},{8,9},{9,8},{10,11... | collective-permute-start | bytes 393224 | tf_op jit(solution)/shard_map/ppermute | solution.py:39
  16.4 11.9 %all-to-all-start = ((f32[16,1,128]{2,1,0:T(1,128)}), f32[16,1,128]{2,1,0:T(1,128)S(1)}, u32[]{:S(2)}, u32[]{:S(2)}) async-start(f32[16,1,128]{2,1,0:T(1,128)} %get-tuple-element.23), calls=%async_computation | async-start | bytes 16384 | tf_op jit(solution)/shard_map/all_to_all | solution.py:300

commit v4 on v3

--- a/solution.py
+++ b/solution.py
@@ -211,8 +211,9 @@
 
 
 def image_kernel(size, width, rows, *refs):
+    near_ref, far_ref, refs = refs[0], refs[1], refs[2:]
     row_refs, refs = refs[:rows], refs[rows:]
-    far_ref, near_ref, self_ref, left_row, right_row, left_hbm, right_hbm, out_ref, left_own, right_own, sems = refs
+    self_ref, left_row, right_row, left_hbm, right_hbm, out_ref, left_own, right_own, sems = refs
     _, _, there = place(size, width)
     own = fetch(left_hbm, right_hbm, left_own, right_own, sems, [(0, 2 + width), (2 + width, width)])
     image = None
@@ -301,7 +302,7 @@
     hw = call(
         functools.partial(image_kernel, size, width, rows), pltpu.VMEM(square, f32), [VM] * (5 + rows) + [HB] * 2, VM,
         [pltpu.VMEM(every, bf16)] * 2 + [dma((2, 2))],
-    )(*row_w, far_w, near_w, w, left_row, right_row, left_env, right_env)
+    )(near_w, far_w, *row_w, w, left_row, right_row, left_env, right_env)
     return call(
         functools.partial(second_kernel, size, width, rows, cells),
         (jax.ShapeDtypeStruct((1,) + square, f32),) * 2, [VM] * 6, (HB, HB),

time: 29.7 us -> 31 us (1.044)
  waiting for transfers between devices: 4.78 us -> 5.98 us
    ppermute x4, waiting for transfers between devices: 2.67 us -> 5.39 us  [swap(): lax.ppermute(x, axis, [(s, to.get(s, s)) for s in range(lax.axis_size(axi...]
    all_to_all x1, waiting for transfers between devices: 1.52 us -> 0.01 us  [body(): stats = lax.all_to_all(stats, 'sector', 0, 0, tiled=True)]
  transfers between devices with their start and end apart: 7 -> 7, of which waited for: 4 -> 3; matrix products, arithmetic and copies ran while one was open for 0% -> 0% of each run, Pallas kernels for 24% -> 23%
where the time goes in v4:
time: 31 us; the launch traced here: 30.7 us
  starting transfers between devices  13.1 us (42%)
  Pallas kernels  11 us (35%)
  waiting for transfers between devices  5.98 us (19%)
  between operations  0.7 us (2%)
    all_to_all x1, starting transfers between devices, body(): stats = lax.all_to_all(stats, 'sector', 0, 0, tiled=True)  5.78 us
    ppermute x4, waiting for transfers between devices, swap(): lax.ppermute(x, axis, [(s, to.get(s, s)) for s in range(lax.axis_size(axi...  5.39 us
    ppermute x4, starting transfers between devices, swap(): lax.ppermute(x, axis, [(s, to.get(s, s)) for s in range(lax.axis_size(axi...  4.22 us
    pallas_call x1, Pallas kernels, body(): call(functools.partial(image_kernel, size, width, rows), pltpu.VMEM(squar...  3.3 us
    ppermute x2, starting transfers between devices, far_swap(): return lax.ppermute(x, ('groups', 'sector'), pairs)  3.11 us
    pallas_call x1, Pallas kernels, body(): call(functools.partial(near_kernel, size, width, rows), (pltpu.VMEM((2,)...  2.86 us
    pallas_call x1, Pallas kernels, body(): call(functools.partial(first_kernel, size, width, rows), (pltpu.VMEM((row...  1.73 us
    pallas_call x1, Pallas kernels, body(): call(functools.partial(second_kernel, size, width, rows, cells), (jax.Sha...  1.23 us
  transfers between devices with their start and end apart: 7, of which 3 were waited for; matrix products, arithmetic and copies ran while one was open for 0% of the time, Pallas kernels for 23%

profile of v4, /device:TPU:0, one launch (start us, length us, event | category | flops | bytes accessed | tf_op | source)
XLA Modules:
  0.0 30.7 jit_solution(6146808452167060889)
XLA Ops:
  0.6 1.0 %shard_map.59 = (bf16[256,256]{1,0:T(8,128)(2,1)S(1)}, bf16[256,256]{1,0:T(8,128)(2,1)S(1)}, f32[8,128]{1,0:T(8,128)S(1)}) custom-call(f32[1,256,256]{2,1,0:T(8,128)} %wave_hbm.3, s32[1,2]{1,0:T(1,128)} %dims_hbm.1), custom_call_target="tpu_custom_call" | custom-call | flops 1 | bytes 1 | tf_op jit(solution)/shard_map/pallas_call | solution.py:271
  1.6 0.5 %collective-permute-start = (bf16[256,256]{1,0:T(8,128)(2,1)S(1)}, bf16[256,256]{1,0:T(8,128)(2,1)S(1)}, u32[]{:S(2)}, u32[]{:S(2)}) collective-permute-start(bf16[256,256]{1,0:T(8,128)(2,1)S(1)} %get-tuple-element.15.self_ref.refs_4_), channel_id=1, source_target_pairs={{0,1},{1,0},{2,3},{3,2},{4,5},{5,4},{6,7},{7,6},{8,9},{9,8},{10,11... | collective-permute-start | bytes 393224 | tf_op jit(solution)/shard_map/ppermute | solution.py:39
  2.1 3.7 %collective-permute-start.2 = (bf16[256,256]{1,0:T(8,128)(2,1)S(1)}, bf16[256,256]{1,0:T(8,128)(2,1)S(1)}, u32[]{:S(2)}, u32[]{:S(2)}) collective-permute-start(bf16[256,256]{1,0:T(8,128)(2,1)S(1)} %get-tuple-element.15.self_ref.refs_4_), channel_id=1, source_target_pairs={{0,8},{1,9},{2,10},{3,11},{4,12},{5,13},{6,14},{7,15},{8,0},{9,1},... | collective-permute-start | bytes 393224 | tf_op jit(solution)/shard_map/ppermute | solution.py:39
  5.8 0.0 collective-permute-done.near_ref.refs_1_
  5.8 1.5 %collective-permute-start.1 = (bf16[256,256]{1,0:T(8,128)(2,1)S(1)}, bf16[256,256]{1,0:T(8,128)(2,1)S(1)}, u32[]{:S(2)}, u32[]{:S(2)}) collective-permute-start(bf16[256,256]{1,0:T(8,128)(2,1)S(1)} %shard_map.61), channel_id=1, source_target_pairs={{0,16},{1,2},{2,1},{3,4},{4,3},{5,6},{6,5},{7,23},{8,24},{9,10},{1... | collective-permute-start | bytes 393224 | tf_op jit(solution)/shard_map/ppermute | solution.py:60
  7.3 2.9 %shard_map.60 = (f32[2,256,256]{2,1,0:T(8,128)S(1)}, f32[8,128]{1,0:T(8,128)S(1)}, bf16[6,256,256]{2,1,0:T(8,128)(2,1)S(1)}, bf16[6,256,256]{2,1,0:T(8,128)(2,1)...) custom-call(bf16[1,26,256,256]{3,2,1,0:T(8,128)(2,1)} %refs_6_.1, ...), custom_call_target="tpu_custom_call" | custom-call | flops 4000000000 | bytes 1 | tf_op jit(solution)/shard_map/pallas_call | solution.py:281
  10.2 0.6 %collective-permute-done.1.far_ref = bf16[256,256]{1,0:T(8,128)(2,1)S(1)} collective-permute-done((bf16[256,256]{1,0:T(8,128)(2,1)S(1)}, bf16[256,256]{1,0:T(8,128)(2,1)S(1)}, u32[]{:S(2)}, u32[]{:S(2)}) %collective-permute-start.1) | collective-permute-done | bytes 131104 | tf_op jit(solution)/shard_map/ppermute | solution.py:60
  10.8 0.8 %shard_map.62.refs_1_.far_part_ref = f32[256,256]{1,0:T(8,128)S(1)} custom-call(bf16[6,256,256]{2,1,0:T(8,128)(2,1)S(1)} %get-tuple-element.17.left_ref, bf16[6,256,256]{2,1,0:T(8,128)(2,1)S(1)} %get-tuple-element.18.right_ref, bf16[256,256]{1,0:T(8,128)(2,1)S(1)} %collective-permute-done.1.far_ref), custom_call_target="tpu_custom_call" | custom-call | flops 4000000000 | bytes 1 | tf_op jit(solution)/shard_map/pallas_call | solution.py:288
  11.6 1.2 %collective-permute-done.2.refs_7_ = bf16[256,256]{1,0:T(8,128)(2,1)S(1)} collective-permute-done((bf16[256,256]{1,0:T(8,128)(2,1)S(1)}, bf16[256,256]{1,0:T(8,128)(2,1)S(1)}, u32[]{:S(2)}, u32[]{:S(2)}) %collective-permute-start.2) | collective-permute-done | bytes 131104 | tf_op jit(solution)/shard_map/ppermute | solution.py:39
  12.8 1.7 %shard_map.63 = (f32[1,256,256]{2,1,0:T(8,128)S(1)}, bf16[256,256]{1,0:T(8,128)(2,1)S(1)}, f32[16,1,128]{2,1,0:T(1,128)}) custom-call(f32[2,256,256]{2,1,0:T(8,128)S(1)} %get-tuple-element.16.refs_0_.near_part_ref, f32[256,256]{1,0:T(8,128)S(1)} %shard_map.62.refs_1_.far_part_ref, f32[8,128]{1,0:T(8,128)S(1)} %get-tuple-element.14.facts_ref.refs_2_, ...), custom_call_target="tpu_custom_call" | custom-call | flops 1 | bytes 1 | tf_op jit(solution)/shard_map/pallas_call | solution.py:291
  14.5 0.0 collective-permute-start.3
  14.5 1.6 %collective-permute-start.4 = (bf16[256,256]{1,0:T(8,128)(2,1)S(1)}, bf16[256,256]{1,0:T(8,128)(2,1)S(1)}, u32[]{:S(2)}, u32[]{:S(2)}) collective-permute-start(bf16[256,256]{1,0:T(8,128)(2,1)S(1)} %get-tuple-element.24.refs_3_), channel_id=1, source_target_pairs={{0,16},{1,2},{2,1},{3,4},{4,3},{5,6},{6,5},{7,23},{8,24},{9,10},{1... | collective-permute-start | bytes 393224 | tf_op jit(solution)/shard_map/ppermute | solution.py:60
  16.1 0.0 collective-permute-start.5
  16.2 5.8 %all-to-all-start = ((f32[16,1,128]{2,1,0:T(1,128)}), f32[16,1,128]{2,1,0:T(1,128)S(1)}, u32[]{:S(2)}, u32[]{:S(2)}) async-start(f32[16,1,128]{2,1,0:T(1,128)} %get-tuple-element.23), calls=%async_computation | async-start | bytes 16384 | tf_op jit(solution)/shard_map/all_to_all | solution.py:301
  22.0 0.0 collective-permute-done.3.refs_0_
  22.0 0.0 collective-permute-done.4.refs_1_
  22.0 4.2 %collective-permute-done.5.refs_2_ = bf16[256,256]{1,0:T(8,128)(2,1)S(1)} collective-permute-done((bf16[256,256]{1,0:T(8,128)(2,1)S(1)}, bf16[256,256]{1,0:T(8,128)(2,1)S(1)}, u32[]{:S(2)}, u32[]{:S(2)}) %collective-permute-start.5) | collective-permute-done | bytes 131104 | tf_op jit(solution)/shard_map/ppermute | solution.py:39
  26.2 3.3 %shard_map.64.hw_ref = f32[256,256]{1,0:T(8,128)S(1)} custom-call(bf16[256,256]{1,0:T(8,128)(2,1)S(1)} %collective-permute-done.3.refs_0_, bf16[256,256]{1,0:T(8,128)(2,1)S(1)} %collective-permute-done.4.refs_1_, bf16[256,256]{1,0:T(8,128)(2,1)S(1)} %collective-permute-done.5.refs_2_, bf16[256,256]{1,0:T(8,128)(2,1)S(1)} %get-tuple-element.24.refs_3_, ...), custom_call_target="tpu_custom_call" | custom-call | flops 1 | bytes 1 | tf_op jit(solution)/shard_map/pallas_call | solution.py:302
  29.5 0.0 all-to-all-done.stats_ref
  29.5 1.2 %shard_map.65 = (f32[1,256,256]{2,1,0:T(8,128)}, f32[1,256,256]{2,1,0:T(8,128)}) custom-call(f32[8,128]{1,0:T(8,128)S(1)} %get-tuple-element.14.facts_ref.refs_2_, f32[16,1,128]{2,1,0:T(1,128)S(1)} %all-to-all-done.stats_ref, f32[256,256]{1,0:T(8,128)S(1)} %shard_map.64.hw_ref, f32[2,256,256]{2,1,0:T(8,128)S(1)} %get-tuple-element.16.refs_0_.near_part_ref, ...), custom_call_target="tpu_custom_call" | custom-call | flops 1 | bytes 1 | tf_op jit(solution)/shard_map/pallas_call | solution.py:306
  (1 shorter events, 0.0 us)
Async XLA Ops:
  1.6 4.2 %collective-permute-start = (bf16[256,256]{1,0:T(8,128)(2,1)S(1)}, bf16[256,256]{1,0:T(8,128)(2,1)S(1)}, u32[]{:S(2)}, u32[]{:S(2)}) collective-permute-start(bf16[256,256]{1,0:T(8,128)(2,1)S(1)} %get-tuple-element.15.self_ref.refs_4_), channel_id=1, source_target_pairs={{0,1},{1,0},{2,3},{3,2},{4,5},{5,4},{6,7},{7,6},{8,9},{9,8},{10,11... | collective-permute-start | bytes 393224 | tf_op jit(solution)/shard_map/ppermute | solution.py:39
  2.1 10.7 %collective-permute-start.2 = (bf16[256,256]{1,0:T(8,128)(2,1)S(1)}, bf16[256,256]{1,0:T(8,128)(2,1)S(1)}, u32[]{:S(2)}, u32[]{:S(2)}) collective-permute-start(bf16[256,256]{1,0:T(8,128)(2,1)S(1)} %get-tuple-element.15.self_ref.refs_4_), channel_id=1, source_target_pairs={{0,8},{1,9},{2,10},{3,11},{4,12},{5,13},{6,14},{7,15},{8,0},{9,1},... | collective-permute-start | bytes 393224 | tf_op jit(solution)/shard_map/ppermute | solution.py:39
  5.8 5.0 %collective-permute-start.1 = (bf16[256,256]{1,0:T(8,128)(2,1)S(1)}, bf16[256,256]{1,0:T(8,128)(2,1)S(1)}, u32[]{:S(2)}, u32[]{:S(2)}) collective-permute-start(bf16[256,256]{1,0:T(8,128)(2,1)S(1)} %shard_map.61), channel_id=1, source_target_pairs={{0,16},{1,2},{2,1},{3,4},{4,3},{5,6},{6,5},{7,23},{8,24},{9,10},{1... | collective-permute-start | bytes 393224 | tf_op jit(solution)/shard_map/ppermute | solution.py:60
  14.5 7.4 %collective-permute-start.3 = (bf16[256,256]{1,0:T(8,128)(2,1)S(1)}, bf16[256,256]{1,0:T(8,128)(2,1)S(1)}, u32[]{:S(2)}, u32[]{:S(2)}) collective-permute-start(bf16[256,256]{1,0:T(8,128)(2,1)S(1)} %get-tuple-element.24.refs_3_), channel_id=1, source_target_pairs={{0,1},{1,0},{2,3},{3,2},{4,5},{5,4},{6,7},{7,6},{8,9},{9,8},{10,11... | collective-permute-start | bytes 393224 | tf_op jit(solution)/shard_map/ppermute | solution.py:39
  14.5 7.4 %collective-permute-start.4 = (bf16[256,256]{1,0:T(8,128)(2,1)S(1)}, bf16[256,256]{1,0:T(8,128)(2,1)S(1)}, u32[]{:S(2)}, u32[]{:S(2)}) collective-permute-start(bf16[256,256]{1,0:T(8,128)(2,1)S(1)} %get-tuple-element.24.refs_3_), channel_id=1, source_target_pairs={{0,16},{1,2},{2,1},{3,4},{4,3},{5,6},{6,5},{7,23},{8,24},{9,10},{1... | collective-permute-start | bytes 393224 | tf_op jit(solution)/shard_map/ppermute | solution.py:60
  16.1 10.1 %collective-permute-start.5 = (bf16[256,256]{1,0:T(8,128)(2,1)S(1)}, bf16[256,256]{1,0:T(8,128)(2,1)S(1)}, u32[]{:S(2)}, u32[]{:S(2)}) collective-permute-start(bf16[256,256]{1,0:T(8,128)(2,1)S(1)} %get-tuple-element.24.refs_3_), channel_id=1, source_target_pairs={{0,8},{1,9},{2,10},{3,11},{4,12},{5,13},{6,14},{7,15},{8,0},{9,1},... | collective-permute-start | bytes 393224 | tf_op jit(solution)/shard_map/ppermute | solution.py:39
  16.2 13.3 %all-to-all-start = ((f32[16,1,128]{2,1,0:T(1,128)}), f32[16,1,128]{2,1,0:T(1,128)S(1)}, u32[]{:S(2)}, u32[]{:S(2)}) async-start(f32[16,1,128]{2,1,0:T(1,128)} %get-tuple-element.23), calls=%async_computation | async-start | bytes 16384 | tf_op jit(solution)/shard_map/all_to_all | solution.py:301

commit v5 on v3

--- a/solution.py
+++ b/solution.py
@@ -188,7 +188,7 @@
 
 def first_kernel(size, width, rows, *refs):
     near_part_ref, far_part_ref, facts_ref, sums_ref, u_ref, left_ref, right_ref = refs[:7]
-    row_refs, (out_ref, w_ref, stats_ref) = refs[7 : 7 + rows], refs[7 + rows :]
+    row_refs, (out_ref, w_ref, far_w_ref, sums_out_ref) = refs[7 : 7 + rows], refs[7 + rows :]
     _, _, there = place(size, width)
     image = near_part_ref[0] + near_part_ref[1] + far_part_ref[...]
     for r, source in enumerate(row_refs):
@@ -200,14 +200,22 @@
     square = sums_ref[1:2, 0:1]
     cross = total(u * image)
     rho = jnp.where(square > 0.0, cross / square, 0.0)
-    w = image - rho * u
-    w_ref[...] = w.astype(jnp.bfloat16)
+    for ref in (w_ref, far_w_ref):
+        ref[...] = (image - rho * u).astype(jnp.bfloat16)
+    lines = lax.broadcasted_iota(jnp.int32, (8, 128), 0)
+    sums_out_ref[...] = jnp.where(lines == 2, cross, jnp.where(lines == 4, rho, sums_ref[...]))
+
+
+def numbers_kernel(sums_ref, w_ref, out_ref):
+    w = w_ref[...].astype(jnp.float32)
+    values = [sums_ref[n : n + 1, 0:1] for n in range(5)]
+    values[3] = total(w * w)
     lane = lax.broadcasted_iota(jnp.int32, (1, 128), 1)
-    stats = jnp.zeros((1, 128), jnp.float32)
-    for n, value in enumerate((sums_ref[0:1, 0:1], square, cross, total(w * w), rho)):
-        stats = jnp.where(lane == n, value, stats)
-    for n in range(stats_ref.shape[0]):
-        stats_ref[n] = stats
+    numbers = jnp.zeros((1, 128), jnp.float32)
+    for n, value in enumerate(values):
+        numbers = jnp.where(lane == n, value, numbers)
+    for n in range(out_ref.shape[0]):
+        out_ref[n] = numbers
 
 
 def image_kernel(size, width, rows, *refs):
@@ -287,16 +295,17 @@
     far_part = vmem(call(
         functools.partial(far_kernel, size, width), pltpu.VMEM(square, f32), [VM] * 3, VM, cost=LONG,
     )(vmem(left_far), vmem(right_far), far_u))
-    row_part, w, stats = call(
+    row_part, w, far_w, sums = call(
         functools.partial(first_kernel, size, width, rows),
-        (pltpu.VMEM((rows,) + square, f32),) + (pltpu.VMEM(square, bf16), jax.ShapeDtypeStruct((size, 1, 128), f32)),
-        [VM] * (7 + rows), (VM,) * 3,
+        (pltpu.VMEM((rows,) + square, f32),) + (pltpu.VMEM(square, bf16),) * 2 + (pltpu.VMEM((8, 128), f32),),
+        [VM] * (7 + rows), (VM,) * 4,
     )(near_part, far_part, facts, vmem(sums), u, left_row, right_row, *row_u)
 
     w = vmem(w)
     row_w = [vmem(swap(w, "sector", p)) for p in row_pairs]
     near_w = vmem(swap(w, "sector", near))
-    far_w = vmem(far_swap(w))
+    far_w = vmem(far_swap(after(far_w, near_w)))
+    stats = call(numbers_kernel, jax.ShapeDtypeStruct((size, 1, 128), f32), [VM] * 2, VM)(vmem(sums), w)
     stats = lax.all_to_all(stats, "sector", 0, 0, tiled=True)
     hw = call(
         functools.partial(image_kernel, size, width, rows), pltpu.VMEM(square, f32), [VM] * (5 + rows) + [HB] * 2, VM,

time: 29.7 us -> 30.5 us (1.027)
  waiting for transfers between devices: 4.78 us -> 5.94 us
  starting transfers between devices: 13.1 us -> 12.7 us
    pallas_call x1, Pallas kernels: 1.73 us -> 1.01 us  [body(): call(functools.partial(first_kernel, size, width, rows), (pltpu.VMEM((row...]
    pallas_call x0 -> x1, Pallas kernels: none -> 0.71 us  [body(): call(numbers_kernel, jax.ShapeDtypeStruct((size, 1, 128), f32), [VM] * 2,...]
    all_to_all x1, waiting for transfers between devices: 1.52 us -> 2.21 us  [body(): stats = lax.all_to_all(stats, 'sector', 0, 0, tiled=True)]
    ppermute x4, waiting for transfers between devices: 2.67 us -> 3.15 us  [swap(): lax.ppermute(x, axis, [(s, to.get(s, s)) for s in range(lax.axis_size(axi...]
    all_to_all x1, starting transfers between devices: 5.56 us -> 5.17 us  [body(): stats = lax.all_to_all(stats, 'sector', 0, 0, tiled=True)]
  transfers between devices with their start and end apart: 7 -> 7, of which waited for: 4 -> 5; matrix products, arithmetic and copies ran while one was open for 0% -> 0% of each run, Pallas kernels for 24% -> 25%
where the time goes in v5:
time: 30.5 us; the launch traced here: 30.3 us
  starting transfers between devices  12.7 us (42%)
  Pallas kernels  11 us (36%)
  waiting for transfers between devices  5.94 us (19%)
  between operations  0.69 us (2%)
    all_to_all x1, starting transfers between devices, body(): stats = lax.all_to_all(stats, 'sector', 0, 0, tiled=True)  5.17 us
    ppermute x4, starting transfers between devices, swap(): lax.ppermute(x, axis, [(s, to.get(s, s)) for s in range(lax.axis_size(axi...  4.42 us
    pallas_call x1, Pallas kernels, body(): call(functools.partial(image_kernel, size, width, rows), pltpu.VMEM(squar...  3.3 us
    ppermute x4, waiting for transfers between devices, swap(): lax.ppermute(x, axis, [(s, to.get(s, s)) for s in range(lax.axis_size(axi...  3.15 us
    ppermute x2, starting transfers between devices, far_swap(): return lax.ppermute(x, ('groups', 'sector'), pairs)  3.11 us
    pallas_call x1, Pallas kernels, body(): call(functools.partial(near_kernel, size, width, rows), (pltpu.VMEM((2,)...  2.86 us
    all_to_all x1, waiting for transfers between devices, body(): stats = lax.all_to_all(stats, 'sector', 0, 0, tiled=True)  2.21 us
    pallas_call x1, Pallas kernels, body(): call(functools.partial(second_kernel, size, width, rows, cells), (jax.Sha...  1.23 us
  transfers between devices with their start and end apart: 7, of which 5 were waited for; matrix products, arithmetic and copies ran while one was open for 0% of the time, Pallas kernels for 25%

profile of v5, /device:TPU:0, one launch (start us, length us, event | category | flops | bytes accessed | tf_op | source)
XLA Modules:
  0.0 30.3 jit_solution(5022544847506717211)
XLA Ops:
  0.6 1.0 %shard_map.59 = (bf16[256,256]{1,0:T(8,128)(2,1)S(1)}, bf16[256,256]{1,0:T(8,128)(2,1)S(1)}, f32[8,128]{1,0:T(8,128)S(1)}) custom-call(f32[1,256,256]{2,1,0:T(8,128)} %wave_hbm.3, s32[1,2]{1,0:T(1,128)} %dims_hbm.1), custom_call_target="tpu_custom_call" | custom-call | flops 1 | bytes 1 | tf_op jit(solution)/shard_map/pallas_call | solution.py:278
  1.6 0.5 %collective-permute-start = (bf16[256,256]{1,0:T(8,128)(2,1)S(1)}, bf16[256,256]{1,0:T(8,128)(2,1)S(1)}, u32[]{:S(2)}, u32[]{:S(2)}) collective-permute-start(bf16[256,256]{1,0:T(8,128)(2,1)S(1)} %get-tuple-element.16.self_ref.refs_4_), channel_id=1, source_target_pairs={{0,1},{1,0},{2,3},{3,2},{4,5},{5,4},{6,7},{7,6},{8,9},{9,8},{10,11... | collective-permute-start | bytes 393224 | tf_op jit(solution)/shard_map/ppermute | solution.py:39
  2.1 3.7 %collective-permute-start.2 = (bf16[256,256]{1,0:T(8,128)(2,1)S(1)}, bf16[256,256]{1,0:T(8,128)(2,1)S(1)}, u32[]{:S(2)}, u32[]{:S(2)}) collective-permute-start(bf16[256,256]{1,0:T(8,128)(2,1)S(1)} %get-tuple-element.16.self_ref.refs_4_), channel_id=1, source_target_pairs={{0,8},{1,9},{2,10},{3,11},{4,12},{5,13},{6,14},{7,15},{8,0},{9,1},... | collective-permute-start | bytes 393224 | tf_op jit(solution)/shard_map/ppermute | solution.py:39
  5.8 0.0 collective-permute-done.near_ref.refs_1_
  5.8 1.5 %collective-permute-start.1 = (bf16[256,256]{1,0:T(8,128)(2,1)S(1)}, bf16[256,256]{1,0:T(8,128)(2,1)S(1)}, u32[]{:S(2)}, u32[]{:S(2)}) collective-permute-start(bf16[256,256]{1,0:T(8,128)(2,1)S(1)} %shard_map.61), channel_id=1, source_target_pairs={{0,16},{1,2},{2,1},{3,4},{4,3},{5,6},{6,5},{7,23},{8,24},{9,10},{1... | collective-permute-start | bytes 393224 | tf_op jit(solution)/shard_map/ppermute | solution.py:60
  7.3 2.9 %shard_map.60 = (f32[2,256,256]{2,1,0:T(8,128)S(1)}, f32[8,128]{1,0:T(8,128)S(1)}, bf16[6,256,256]{2,1,0:T(8,128)(2,1)S(1)}, bf16[6,256,256]{2,1,0:T(8,128)(2,1)...) custom-call(bf16[1,26,256,256]{3,2,1,0:T(8,128)(2,1)} %refs_6_.1, ...), custom_call_target="tpu_custom_call" | custom-call | flops 4000000000 | bytes 1 | tf_op jit(solution)/shard_map/pallas_call | solution.py:288
  10.2 0.6 %collective-permute-done.1.far_ref = bf16[256,256]{1,0:T(8,128)(2,1)S(1)} collective-permute-done((bf16[256,256]{1,0:T(8,128)(2,1)S(1)}, bf16[256,256]{1,0:T(8,128)(2,1)S(1)}, u32[]{:S(2)}, u32[]{:S(2)}) %collective-permute-start.1) | collective-permute-done | bytes 131104 | tf_op jit(solution)/shard_map/ppermute | solution.py:60
  10.8 0.8 %shard_map.62.refs_1_.far_part_ref = f32[256,256]{1,0:T(8,128)S(1)} custom-call(bf16[6,256,256]{2,1,0:T(8,128)(2,1)S(1)} %get-tuple-element.18.left_ref, bf16[6,256,256]{2,1,0:T(8,128)(2,1)S(1)} %get-tuple-element.19.right_ref, bf16[256,256]{1,0:T(8,128)(2,1)S(1)} %collective-permute-done.1.far_ref), custom_call_target="tpu_custom_call" | custom-call | flops 4000000000 | bytes 1 | tf_op jit(solution)/shard_map/pallas_call | solution.py:295
  11.6 1.2 %collective-permute-done.2.refs_7_ = bf16[256,256]{1,0:T(8,128)(2,1)S(1)} collective-permute-done((bf16[256,256]{1,0:T(8,128)(2,1)S(1)}, bf16[256,256]{1,0:T(8,128)(2,1)S(1)}, u32[]{:S(2)}, u32[]{:S(2)}) %collective-permute-start.2) | collective-permute-done | bytes 131104 | tf_op jit(solution)/shard_map/ppermute | solution.py:39
  12.8 1.0 %shard_map.63 = (f32[1,256,256]{2,1,0:T(8,128)S(1)}, bf16[256,256]{1,0:T(8,128)(2,1)S(1)}, bf16[256,256]{1,0:T(8,128)(2,1)S(1)}, f32[8,128]{1,0:T(8,128)S(1)}) custom-call(f32[2,256,256]{2,1,0:T(8,128)S(1)} %get-tuple-element.17.refs_0_.near_part_ref, f32[256,256]{1,0:T(8,128)S(1)} %shard_map.62.refs_1_.far_part_ref, ...), custom_call_target="tpu_custom_call" | custom-call | flops 1 | bytes 1 | tf_op jit(solution)/shard_map/pallas_call | solution.py:298
  13.8 0.1 collective-permute-start.4
  13.9 0.2 collective-permute-start.3
  14.1 1.2 %collective-permute-done.4.refs_1_.refs_2_ = bf16[256,256]{1,0:T(8,128)(2,1)S(1)} collective-permute-done((bf16[256,256]{1,0:T(8,128)(2,1)S(1)}, bf16[256,256]{1,0:T(8,128)(2,1)S(1)}, u32[]{:S(2)}, u32[]{:S(2)}) %collective-permute-start.4) | collective-permute-done | bytes 131104 | tf_op jit(solution)/shard_map/ppermute | solution.py:39
  15.2 1.6 %collective-permute-start.5 = (bf16[256,256]{1,0:T(8,128)(2,1)S(1)}, bf16[256,256]{1,0:T(8,128)(2,1)S(1)}, u32[]{:S(2)}, u32[]{:S(2)}) collective-permute-start(bf16[256,256]{1,0:T(8,128)(2,1)S(1)} %shard_map.65), channel_id=1, source_target_pairs={{0,16},{1,2},{2,1},{3,4},{4,3},{5,6},{6,5},{7,23},{8,24},{9,10},{1... | collective-permute-start | bytes 393224 | tf_op jit(solution)/shard_map/ppermute | solution.py:60
  16.8 0.7 %shard_map.64 = f32[16,1,128]{2,1,0:T(1,128)} custom-call(f32[8,128]{1,0:T(8,128)S(1)} %get-tuple-element.24.sums_ref, bf16[256,256]{1,0:T(8,128)(2,1)S(1)} %get-tuple-element.25.w_ref.refs_3_), custom_call_target="tpu_custom_call" | custom-call | flops 1 | bytes 1 | tf_op jit(solution)/shard_map/pallas_call | solution.py:308
  17.5 5.2 %all-to-all-start = ((f32[16,1,128]{2,1,0:T(1,128)}), f32[16,1,128]{2,1,0:T(1,128)S(1)}, u32[]{:S(2)}, u32[]{:S(2)}) async-start(f32[16,1,128]{2,1,0:T(1,128)} %shard_map.64), calls=%async_computation | async-start | bytes 16384 | tf_op jit(solution)/shard_map/all_to_all | solution.py:309
  22.7 0.8 %collective-permute-done.3.refs_0_ = bf16[256,256]{1,0:T(8,128)(2,1)S(1)} collective-permute-done((bf16[256,256]{1,0:T(8,128)(2,1)S(1)}, bf16[256,256]{1,0:T(8,128)(2,1)S(1)}, u32[]{:S(2)}, u32[]{:S(2)}) %collective-permute-start.3) | collective-permute-done | bytes 131104 | tf_op jit(solution)/shard_map/ppermute | solution.py:39
  23.5 0.0 collective-permute-done.5.refs_1_
  23.5 3.3 %shard_map.66.hw_ref = f32[256,256]{1,0:T(8,128)S(1)} custom-call(bf16[256,256]{1,0:T(8,128)(2,1)S(1)} %collective-permute-done.3.refs_0_, bf16[256,256]{1,0:T(8,128)(2,1)S(1)} %collective-permute-done.5.refs_1_, bf16[256,256]{1,0:T(8,128)(2,1)S(1)} %collective-permute-done.4.refs_1_.refs_2_, bf16[256,256]{1,0:T(8,128)(2,1)S(1)} %get-tuple-element.25.w_ref.refs_3_, ...), custom_call_target="tpu_custom_call" | custom-call | flops 1 | bytes 1 | tf_op jit(solution)/shard_map/pallas_call | solution.py:310
  26.8 2.2 %all-to-all-done.stats_ref = f32[16,1,128]{2,1,0:T(1,128)S(1)} async-done(((f32[16,1,128]{2,1,0:T(1,128)}), f32[16,1,128]{2,1,0:T(1,128)S(1)}, u32[]{:S(2)}, u32[]{:S(2)}) %all-to-all-start) | async-done | bytes 8224 | tf_op jit(solution)/shard_map/all_to_all | solution.py:309
  29.1 1.2 %shard_map.67 = (f32[1,256,256]{2,1,0:T(8,128)}, f32[1,256,256]{2,1,0:T(8,128)}) custom-call(f32[8,128]{1,0:T(8,128)S(1)} %get-tuple-element.15.facts_ref.refs_2_, f32[16,1,128]{2,1,0:T(1,128)S(1)} %all-to-all-done.stats_ref, f32[256,256]{1,0:T(8,128)S(1)} %shard_map.66.hw_ref, f32[2,256,256]{2,1,0:T(8,128)S(1)} %get-tuple-element.17.refs_0_.near_part_ref, ...), custom_call_target="tpu_custom_call" | custom-call | flops 1 | bytes 1 | tf_op jit(solution)/shard_map/pallas_call | solution.py:314
  (2 shorter events, 0.0 us)
Async XLA Ops:
  1.6 4.2 %collective-permute-start = (bf16[256,256]{1,0:T(8,128)(2,1)S(1)}, bf16[256,256]{1,0:T(8,128)(2,1)S(1)}, u32[]{:S(2)}, u32[]{:S(2)}) collective-permute-start(bf16[256,256]{1,0:T(8,128)(2,1)S(1)} %get-tuple-element.16.self_ref.refs_4_), channel_id=1, source_target_pairs={{0,1},{1,0},{2,3},{3,2},{4,5},{5,4},{6,7},{7,6},{8,9},{9,8},{10,11... | collective-permute-start | bytes 393224 | tf_op jit(solution)/shard_map/ppermute | solution.py:39
  2.1 10.7 %collective-permute-start.2 = (bf16[256,256]{1,0:T(8,128)(2,1)S(1)}, bf16[256,256]{1,0:T(8,128)(2,1)S(1)}, u32[]{:S(2)}, u32[]{:S(2)}) collective-permute-start(bf16[256,256]{1,0:T(8,128)(2,1)S(1)} %get-tuple-element.16.self_ref.refs_4_), channel_id=1, source_target_pairs={{0,8},{1,9},{2,10},{3,11},{4,12},{5,13},{6,14},{7,15},{8,0},{9,1},... | collective-permute-start | bytes 393224 | tf_op jit(solution)/shard_map/ppermute | solution.py:39
  5.8 5.0 %collective-permute-start.1 = (bf16[256,256]{1,0:T(8,128)(2,1)S(1)}, bf16[256,256]{1,0:T(8,128)(2,1)S(1)}, u32[]{:S(2)}, u32[]{:S(2)}) collective-permute-start(bf16[256,256]{1,0:T(8,128)(2,1)S(1)} %shard_map.61), channel_id=1, source_target_pairs={{0,16},{1,2},{2,1},{3,4},{4,3},{5,6},{6,5},{7,23},{8,24},{9,10},{1... | collective-permute-start | bytes 393224 | tf_op jit(solution)/shard_map/ppermute | solution.py:60
  13.8 1.4 %collective-permute-start.4 = (bf16[256,256]{1,0:T(8,128)(2,1)S(1)}, bf16[256,256]{1,0:T(8,128)(2,1)S(1)}, u32[]{:S(2)}, u32[]{:S(2)}) collective-permute-start(bf16[256,256]{1,0:T(8,128)(2,1)S(1)} %get-tuple-element.25.w_ref.refs_3_), channel_id=1, source_target_pairs={{0,1},{1,0},{2,3},{3,2},{4,5},{5,4},{6,7},{7,6},{8,9},{9,8},{10,11... | collective-permute-start | bytes 393224 | tf_op jit(solution)/shard_map/ppermute | solution.py:39
  13.9 9.6 %collective-permute-start.3 = (bf16[256,256]{1,0:T(8,128)(2,1)S(1)}, bf16[256,256]{1,0:T(8,128)(2,1)S(1)}, u32[]{:S(2)}, u32[]{:S(2)}) collective-permute-start(bf16[256,256]{1,0:T(8,128)(2,1)S(1)} %get-tuple-element.25.w_ref.refs_3_), channel_id=1, source_target_pairs={{0,8},{1,9},{2,10},{3,11},{4,12},{5,13},{6,14},{7,15},{8,0},{9,1},... | collective-permute-start | bytes 393224 | tf_op jit(solution)/shard_map/ppermute | solution.py:39
  15.2 8.3 %collective-permute-start.5 = (bf16[256,256]{1,0:T(8,128)(2,1)S(1)}, bf16[256,256]{1,0:T(8,128)(2,1)S(1)}, u32[]{:S(2)}, u32[]{:S(2)}) collective-permute-start(bf16[256,256]{1,0:T(8,128)(2,1)S(1)} %shard_map.65), channel_id=1, source_target_pairs={{0,16},{1,2},{2,1},{3,4},{4,3},{5,6},{6,5},{7,23},{8,24},{9,10},{1... | collective-permute-start | bytes 393224 | tf_op jit(solution)/shard_map/ppermute | solution.py:60
  17.5 11.5 %all-to-all-start = ((f32[16,1,128]{2,1,0:T(1,128)}), f32[16,1,128]{2,1,0:T(1,128)S(1)}, u32[]{:S(2)}, u32[]{:S(2)}) async-start(f32[16,1,128]{2,1,0:T(1,128)} %shard_map.64), calls=%async_computation | async-start | bytes 16384 | tf_op jit(solution)/shard_map/all_to_all | solution.py:309

commit v6 on v5

--- a/solution.py
+++ b/solution.py
@@ -188,7 +188,7 @@
 
 def first_kernel(size, width, rows, *refs):
     near_part_ref, far_part_ref, facts_ref, sums_ref, u_ref, left_ref, right_ref = refs[:7]
-    row_refs, (out_ref, w_ref, far_w_ref, sums_out_ref) = refs[7 : 7 + rows], refs[7 + rows :]
+    row_refs, (out_ref, w_ref, sums_out_ref, numbers_hbm, numbers_ref, sem) = refs[7 : 7 + rows], refs[7 + rows :]
     _, _, there = place(size, width)
     image = near_part_ref[0] + near_part_ref[1] + far_part_ref[...]
     for r, source in enumerate(row_refs):
@@ -200,22 +200,39 @@
     square = sums_ref[1:2, 0:1]
     cross = total(u * image)
     rho = jnp.where(square > 0.0, cross / square, 0.0)
-    for ref in (w_ref, far_w_ref):
-        ref[...] = (image - rho * u).astype(jnp.bfloat16)
+    w_ref[...] = (image - rho * u).astype(jnp.bfloat16)
     lines = lax.broadcasted_iota(jnp.int32, (8, 128), 0)
-    sums_out_ref[...] = jnp.where(lines == 2, cross, jnp.where(lines == 4, rho, sums_ref[...]))
-
-
-def numbers_kernel(sums_ref, w_ref, out_ref):
+    sums = jnp.where(lines == 2, cross, jnp.where(lines == 4, rho, sums_ref[...]))
+    sums_out_ref[...] = sums
+
+    @pl.when(even_row())
+    def _():
+        write_numbers(sums, w_ref, numbers_hbm, numbers_ref, sem)
+
+
+def even_row():
+    return lax.rem(lax.div(lax.axis_index("sector"), QD), 2) == 0
+
+
+def write_numbers(sums, w_ref, numbers_hbm, numbers_ref, sem):
     w = w_ref[...].astype(jnp.float32)
-    values = [sums_ref[n : n + 1, 0:1] for n in range(5)]
+    values = [sums[n : n + 1, 0:1] for n in range(5)]
     values[3] = total(w * w)
     lane = lax.broadcasted_iota(jnp.int32, (1, 128), 1)
     numbers = jnp.zeros((1, 128), jnp.float32)
     for n, value in enumerate(values):
         numbers = jnp.where(lane == n, value, numbers)
-    for n in range(out_ref.shape[0]):
-        out_ref[n] = numbers
+    for n in range(numbers_ref.shape[0]):
+        numbers_ref[n] = numbers
+    copy = pltpu.make_async_copy(numbers_ref, numbers_hbm, sem)
+    copy.start()
+    copy.wait()
+
+
+def numbers_kernel(held_hbm, sums_ref, w_ref, numbers_hbm, numbers_ref, sem):
+    @pl.when(jnp.logical_not(even_row()))
+    def _():
+        write_numbers(sums_ref[...], w_ref, numbers_hbm, numbers_ref, sem)
 
 
 def image_kernel(size, width, rows, *refs):
@@ -295,17 +312,19 @@
     far_part = vmem(call(
         functools.partial(far_kernel, size, width), pltpu.VMEM(square, f32), [VM] * 3, VM, cost=LONG,
     )(vmem(left_far), vmem(right_far), far_u))
-    row_part, w, far_w, sums = call(
+    table = pltpu.HBM((size, 1, 128), f32)
+    table_scratch = [pltpu.VMEM((size, 1, 128), f32), dma]
+    row_part, w, sums, stats = call(
         functools.partial(first_kernel, size, width, rows),
-        (pltpu.VMEM((rows,) + square, f32),) + (pltpu.VMEM(square, bf16),) * 2 + (pltpu.VMEM((8, 128), f32),),
-        [VM] * (7 + rows), (VM,) * 4,
+        (pltpu.VMEM((rows,) + square, f32), pltpu.VMEM(square, bf16), pltpu.VMEM((8, 128), f32), table),
+        [VM] * (7 + rows), (VM,) * 3 + (HB,), table_scratch,
     )(near_part, far_part, facts, vmem(sums), u, left_row, right_row, *row_u)
 
     w = vmem(w)
     row_w = [vmem(swap(w, "sector", p)) for p in row_pairs]
     near_w = vmem(swap(w, "sector", near))
-    far_w = vmem(far_swap(after(far_w, near_w)))
-    stats = call(numbers_kernel, jax.ShapeDtypeStruct((size, 1, 128), f32), [VM] * 2, VM)(vmem(sums), w)
+    far_w = vmem(far_swap(w))
+    stats = call(numbers_kernel, table, [HB] + [VM] * 2, HB, table_scratch, aliases={0: 0})(hbm(stats), vmem(sums), w)
     stats = lax.all_to_all(stats, "sector", 0, 0, tiled=True)
     hw = call(
         functools.partial(image_kernel, size, width, rows), pltpu.VMEM(square, f32), [VM] * (5 + rows) + [HB] * 2, VM,

time: 30.5 us -> 30.6 us (level)
  starting transfers between devices: 12.7 us -> 13.9 us
  waiting for transfers between devices: 5.94 us -> 4.77 us
    all_to_all x1, starting transfers between devices: 5.17 us -> 6.47 us  [body(): stats = lax.all_to_all(stats, 'sector', 0, 0, tiled=True)]
    ppermute x4, waiting for transfers between devices: 3.15 us -> 1.92 us  [swap(): lax.ppermute(x, axis, [(s, to.get(s, s)) for s in range(lax.axis_size(axi...]
    pallas_call x1, Pallas kernels: 1.01 us -> 1.74 us  [body(): call(functools.partial(first_kernel, size, width, rows), (pltpu.VMEM((row...]
    pallas_call x1, Pallas kernels: 0.71 us -> 0.01 us  [body(): call(numbers_kernel, table, [HB] + [VM] * 2, HB, table_scratch, aliases={...]
  transfers between devices with their start and end apart: 7 -> 7, of which waited for: 5 -> 4; matrix products, arithmetic and copies ran while one was open for 0% -> 0% of each run, Pallas kernels for 25% -> 23%
where the time goes in v6:
time: 30.6 us; the launch traced here: 30.4 us
  starting transfers between devices  13.9 us (45%)
  Pallas kernels  11 us (36%)
  waiting for transfers between devices  4.77 us (16%)
  between operations  0.7 us (2%)
    all_to_all x1, starting transfers between devices, body(): stats = lax.all_to_all(stats, 'sector', 0, 0, tiled=True)  6.47 us
    ppermute x4, starting transfers between devices, swap(): lax.ppermute(x, axis, [(s, to.get(s, s)) for s in range(lax.axis_size(axi...  4.25 us
    pallas_call x1, Pallas kernels, body(): call(functools.partial(image_kernel, size, width, rows), pltpu.VMEM(squar...  3.31 us
    ppermute x2, starting transfers between devices, far_swap(): return lax.ppermute(x, ('groups', 'sector'), pairs)  3.17 us
    pallas_call x1, Pallas kernels, body(): call(functools.partial(near_kernel, size, width, rows), (pltpu.VMEM((2,)...  2.86 us
    all_to_all x1, waiting for transfers between devices, body(): stats = lax.all_to_all(stats, 'sector', 0, 0, tiled=True)  2.27 us
    ppermute x4, waiting for transfers between devices, swap(): lax.ppermute(x, axis, [(s, to.get(s, s)) for s in range(lax.axis_size(axi...  1.92 us
    pallas_call x1, Pallas kernels, body(): call(functools.partial(first_kernel, size, width, rows), (pltpu.VMEM((row...  1.74 us
  transfers between devices with their start and end apart: 7, of which 4 were waited for; matrix products, arithmetic and copies ran while one was open for 0% of the time, Pallas kernels for 23%

profile of v6, /device:TPU:0, one launch (start us, length us, event | category | flops | bytes accessed | tf_op | source)
XLA Modules:
  0.0 30.4 jit_solution(9075530523438766234)
XLA Ops:
  0.6 1.0 %shard_map.59 = (bf16[256,256]{1,0:T(8,128)(2,1)S(1)}, bf16[256,256]{1,0:T(8,128)(2,1)S(1)}, f32[8,128]{1,0:T(8,128)S(1)}) custom-call(f32[1,256,256]{2,1,0:T(8,128)} %wave_hbm.3, s32[1,2]{1,0:T(1,128)} %dims_hbm.1), custom_call_target="tpu_custom_call" | custom-call | flops 1 | bytes 1 | tf_op jit(solution)/shard_map/pallas_call | solution.py:295
  1.6 0.5 %collective-permute-start = (bf16[256,256]{1,0:T(8,128)(2,1)S(1)}, bf16[256,256]{1,0:T(8,128)(2,1)S(1)}, u32[]{:S(2)}, u32[]{:S(2)}) collective-permute-start(bf16[256,256]{1,0:T(8,128)(2,1)S(1)} %get-tuple-element.16.self_ref.refs_4_), channel_id=1, source_target_pairs={{0,1},{1,0},{2,3},{3,2},{4,5},{5,4},{6,7},{7,6},{8,9},{9,8},{10,11... | collective-permute-start | bytes 393224 | tf_op jit(solution)/shard_map/ppermute | solution.py:39
  2.1 3.7 %collective-permute-start.2 = (bf16[256,256]{1,0:T(8,128)(2,1)S(1)}, bf16[256,256]{1,0:T(8,128)(2,1)S(1)}, u32[]{:S(2)}, u32[]{:S(2)}) collective-permute-start(bf16[256,256]{1,0:T(8,128)(2,1)S(1)} %get-tuple-element.16.self_ref.refs_4_), channel_id=1, source_target_pairs={{0,8},{1,9},{2,10},{3,11},{4,12},{5,13},{6,14},{7,15},{8,0},{9,1},... | collective-permute-start | bytes 393224 | tf_op jit(solution)/shard_map/ppermute | solution.py:39
  5.8 0.0 collective-permute-done.near_ref.refs_1_
  5.8 1.5 %collective-permute-start.1 = (bf16[256,256]{1,0:T(8,128)(2,1)S(1)}, bf16[256,256]{1,0:T(8,128)(2,1)S(1)}, u32[]{:S(2)}, u32[]{:S(2)}) collective-permute-start(bf16[256,256]{1,0:T(8,128)(2,1)S(1)} %shard_map.61), channel_id=1, source_target_pairs={{0,16},{1,2},{2,1},{3,4},{4,3},{5,6},{6,5},{7,23},{8,24},{9,10},{1... | collective-permute-start | bytes 393224 | tf_op jit(solution)/shard_map/ppermute | solution.py:60
  7.3 2.9 %shard_map.60 = (f32[2,256,256]{2,1,0:T(8,128)S(1)}, f32[8,128]{1,0:T(8,128)S(1)}, bf16[6,256,256]{2,1,0:T(8,128)(2,1)S(1)}, bf16[6,256,256]{2,1,0:T(8,128)(2,1)...) custom-call(bf16[1,26,256,256]{3,2,1,0:T(8,128)(2,1)} %refs_6_.1, ...), custom_call_target="tpu_custom_call" | custom-call | flops 4000000000 | bytes 1 | tf_op jit(solution)/shard_map/pallas_call | solution.py:305
  10.2 0.6 %collective-permute-done.1.far_ref = bf16[256,256]{1,0:T(8,128)(2,1)S(1)} collective-permute-done((bf16[256,256]{1,0:T(8,128)(2,1)S(1)}, bf16[256,256]{1,0:T(8,128)(2,1)S(1)}, u32[]{:S(2)}, u32[]{:S(2)}) %collective-permute-start.1) | collective-permute-done | bytes 131104 | tf_op jit(solution)/shard_map/ppermute | solution.py:60
  10.8 0.8 %shard_map.62.refs_1_.far_part_ref = f32[256,256]{1,0:T(8,128)S(1)} custom-call(bf16[6,256,256]{2,1,0:T(8,128)(2,1)S(1)} %get-tuple-element.18.left_ref, bf16[6,256,256]{2,1,0:T(8,128)(2,1)S(1)} %get-tuple-element.19.right_ref, bf16[256,256]{1,0:T(8,128)(2,1)S(1)} %collective-permute-done.1.far_ref), custom_call_target="tpu_custom_call" | custom-call | flops 4000000000 | bytes 1 | tf_op jit(solution)/shard_map/pallas_call | solution.py:312
  11.6 1.2 %collective-permute-done.2.refs_7_ = bf16[256,256]{1,0:T(8,128)(2,1)S(1)} collective-permute-done((bf16[256,256]{1,0:T(8,128)(2,1)S(1)}, bf16[256,256]{1,0:T(8,128)(2,1)S(1)}, u32[]{:S(2)}, u32[]{:S(2)}) %collective-permute-start.2) | collective-permute-done | bytes 131104 | tf_op jit(solution)/shard_map/ppermute | solution.py:39
  12.8 1.7 %shard_map.63 = (f32[1,256,256]{2,1,0:T(8,128)S(1)}, bf16[256,256]{1,0:T(8,128)(2,1)S(1)}, f32[8,128]{1,0:T(8,128)S(1)}, f32[16,1,128]{2,1,0:T(1,128)}) custom-call(f32[2,256,256]{2,1,0:T(8,128)S(1)} %get-tuple-element.17.refs_0_.near_part_ref, f32[256,256]{1,0:T(8,128)S(1)} %shard_map.62.refs_1_.far_part_ref, ...), custom_call_target="tpu_custom_call" | custom-call | flops 1 | bytes 1 | tf_op jit(solution)/shard_map/pallas_call | solution.py:317
  14.6 0.1 collective-permute-start.3
  14.6 1.7 %collective-permute-start.4 = (bf16[256,256]{1,0:T(8,128)(2,1)S(1)}, bf16[256,256]{1,0:T(8,128)(2,1)S(1)}, u32[]{:S(2)}, u32[]{:S(2)}) collective-permute-start(bf16[256,256]{1,0:T(8,128)(2,1)S(1)} %get-tuple-element.26.w_ref.refs_3_), channel_id=1, source_target_pairs={{0,16},{1,2},{2,1},{3,4},{4,3},{5,6},{6,5},{7,23},{8,24},{9,10},{1... | collective-permute-start | bytes 393224 | tf_op jit(solution)/shard_map/ppermute | solution.py:60
  16.3 0.0 collective-permute-start.5
  16.3 6.5 %all-to-all-start = ((f32[16,1,128]{2,1,0:T(1,128)}), f32[16,1,128]{2,1,0:T(1,128)S(1)}, u32[]{:S(2)}, u32[]{:S(2)}) async-start(f32[16,1,128]{2,1,0:T(1,128)} %shard_map.64), calls=%async_computation | async-start | bytes 16384 | tf_op jit(solution)/shard_map/all_to_all | solution.py:328
  22.8 0.7 %collective-permute-done.3.refs_0_ = bf16[256,256]{1,0:T(8,128)(2,1)S(1)} collective-permute-done((bf16[256,256]{1,0:T(8,128)(2,1)S(1)}, bf16[256,256]{1,0:T(8,128)(2,1)S(1)}, u32[]{:S(2)}, u32[]{:S(2)}) %collective-permute-start.3) | collective-permute-done | bytes 131104 | tf_op jit(solution)/shard_map/ppermute | solution.py:39
  23.5 0.0 collective-permute-done.4.refs_1_
  23.5 0.0 collective-permute-done.5.refs_2_
  23.5 3.3 %shard_map.65.hw_ref = f32[256,256]{1,0:T(8,128)S(1)} custom-call(bf16[256,256]{1,0:T(8,128)(2,1)S(1)} %collective-permute-done.3.refs_0_, bf16[256,256]{1,0:T(8,128)(2,1)S(1)} %collective-permute-done.4.refs_1_, bf16[256,256]{1,0:T(8,128)(2,1)S(1)} %collective-permute-done.5.refs_2_, bf16[256,256]{1,0:T(8,128)(2,1)S(1)} %get-tuple-element.26.w_ref.refs_3_, ...), custom_call_target="tpu_custom_call" | custom-call | flops 1 | bytes 1 | tf_op jit(solution)/shard_map/pallas_call | solution.py:329
  26.8 2.3 %all-to-all-done.stats_ref = f32[16,1,128]{2,1,0:T(1,128)S(1)} async-done(((f32[16,1,128]{2,1,0:T(1,128)}), f32[16,1,128]{2,1,0:T(1,128)S(1)}, u32[]{:S(2)}, u32[]{:S(2)}) %all-to-all-start) | async-done | bytes 8224 | tf_op jit(solution)/shard_map/all_to_all | solution.py:328
  29.1 1.2 %shard_map.66 = (f32[1,256,256]{2,1,0:T(8,128)}, f32[1,256,256]{2,1,0:T(8,128)}) custom-call(f32[8,128]{1,0:T(8,128)S(1)} %get-tuple-element.15.facts_ref.refs_2_, f32[16,1,128]{2,1,0:T(1,128)S(1)} %all-to-all-done.stats_ref, f32[256,256]{1,0:T(8,128)S(1)} %shard_map.65.hw_ref, f32[2,256,256]{2,1,0:T(8,128)S(1)} %get-tuple-element.17.refs_0_.near_part_ref, ...), custom_call_target="tpu_custom_call" | custom-call | flops 1 | bytes 1 | tf_op jit(solution)/shard_map/pallas_call | solution.py:333
  (2 shorter events, 0.0 us)
Async XLA Ops:
  1.6 4.2 %collective-permute-start = (bf16[256,256]{1,0:T(8,128)(2,1)S(1)}, bf16[256,256]{1,0:T(8,128)(2,1)S(1)}, u32[]{:S(2)}, u32[]{:S(2)}) collective-permute-start(bf16[256,256]{1,0:T(8,128)(2,1)S(1)} %get-tuple-element.16.self_ref.refs_4_), channel_id=1, source_target_pairs={{0,1},{1,0},{2,3},{3,2},{4,5},{5,4},{6,7},{7,6},{8,9},{9,8},{10,11... | collective-permute-start | bytes 393224 | tf_op jit(solution)/shard_map/ppermute | solution.py:39
  2.1 10.7 %collective-permute-start.2 = (bf16[256,256]{1,0:T(8,128)(2,1)S(1)}, bf16[256,256]{1,0:T(8,128)(2,1)S(1)}, u32[]{:S(2)}, u32[]{:S(2)}) collective-permute-start(bf16[256,256]{1,0:T(8,128)(2,1)S(1)} %get-tuple-element.16.self_ref.refs_4_), channel_id=1, source_target_pairs={{0,8},{1,9},{2,10},{3,11},{4,12},{5,13},{6,14},{7,15},{8,0},{9,1},... | collective-permute-start | bytes 393224 | tf_op jit(solution)/shard_map/ppermute | solution.py:39
  5.8 5.0 %collective-permute-start.1 = (bf16[256,256]{1,0:T(8,128)(2,1)S(1)}, bf16[256,256]{1,0:T(8,128)(2,1)S(1)}, u32[]{:S(2)}, u32[]{:S(2)}) collective-permute-start(bf16[256,256]{1,0:T(8,128)(2,1)S(1)} %shard_map.61), channel_id=1, source_target_pairs={{0,16},{1,2},{2,1},{3,4},{4,3},{5,6},{6,5},{7,23},{8,24},{9,10},{1... | collective-permute-start | bytes 393224 | tf_op jit(solution)/shard_map/ppermute | solution.py:60
  14.6 9.0 %collective-permute-start.3 = (bf16[256,256]{1,0:T(8,128)(2,1)S(1)}, bf16[256,256]{1,0:T(8,128)(2,1)S(1)}, u32[]{:S(2)}, u32[]{:S(2)}) collective-permute-start(bf16[256,256]{1,0:T(8,128)(2,1)S(1)} %get-tuple-element.26.w_ref.refs_3_), channel_id=1, source_target_pairs={{0,8},{1,9},{2,10},{3,11},{4,12},{5,13},{6,14},{7,15},{8,0},{9,1},... | collective-permute-start | bytes 393224 | tf_op jit(solution)/shard_map/ppermute | solution.py:39
  14.6 8.9 %collective-permute-start.4 = (bf16[256,256]{1,0:T(8,128)(2,1)S(1)}, bf16[256,256]{1,0:T(8,128)(2,1)S(1)}, u32[]{:S(2)}, u32[]{:S(2)}) collective-permute-start(bf16[256,256]{1,0:T(8,128)(2,1)S(1)} %get-tuple-element.26.w_ref.refs_3_), channel_id=1, source_target_pairs={{0,16},{1,2},{2,1},{3,4},{4,3},{5,6},{6,5},{7,23},{8,24},{9,10},{1... | collective-permute-start | bytes 393224 | tf_op jit(solution)/shard_map/ppermute | solution.py:60
  16.3 7.2 %collective-permute-start.5 = (bf16[256,256]{1,0:T(8,128)(2,1)S(1)}, bf16[256,256]{1,0:T(8,128)(2,1)S(1)}, u32[]{:S(2)}, u32[]{:S(2)}) collective-permute-start(bf16[256,256]{1,0:T(8,128)(2,1)S(1)} %get-tuple-element.26.w_ref.refs_3_), channel_id=1, source_target_pairs={{0,1},{1,0},{2,3},{3,2},{4,5},{5,4},{6,7},{7,6},{8,9},{9,8},{10,11... | collective-permute-start | bytes 393224 | tf_op jit(solution)/shard_map/ppermute | solution.py:39
  16.3 12.8 %all-to-all-start = ((f32[16,1,128]{2,1,0:T(1,128)}), f32[16,1,128]{2,1,0:T(1,128)S(1)}, u32[]{:S(2)}, u32[]{:S(2)}) async-start(f32[16,1,128]{2,1,0:T(1,128)} %shard_map.64), calls=%async_computation | async-start | bytes 16384 | tf_op jit(solution)/shard_map/all_to_all | solution.py:328

commit v7 on v3

--- a/solution.py
+++ b/solution.py
@@ -181,33 +181,42 @@
         finish(pair)
 
 
-def far_kernel(size, width, left_ref, right_ref, far_ref, out_ref):
+def far_kernel(size, width, left_ref, right_ref, near_part_ref, u_ref, sums_ref, far_ref, out_ref, sums_out_ref):
     _, _, there = place(size, width)
-    out_ref[...] = terms(only(there[0], far_ref[...]), left_ref, right_ref, 0, width)
+    part = terms(only(there[0], far_ref[...]), left_ref, right_ref, 0, width)
+    out_ref[...] = part
+    sums = sums_ref[...]
+    square = sums[1:2, 0:1]
+    cross = total(u_ref[...].astype(jnp.float32) * (near_part_ref[0] + near_part_ref[1] + part))
+    lines = lax.broadcasted_iota(jnp.int32, (8, 128), 0)
+    sums_out_ref[...] = jnp.where(lines == 2, jnp.where(square > 0.0, cross / square, 0.0), sums)
 
 
 def first_kernel(size, width, rows, *refs):
     near_part_ref, far_part_ref, facts_ref, sums_ref, u_ref, left_ref, right_ref = refs[:7]
-    row_refs, (out_ref, w_ref, stats_ref) = refs[7 : 7 + rows], refs[7 + rows :]
+    row_refs, (out_ref, w_ref, numbers_hbm, numbers_ref, sem) = refs[7 : 7 + rows], refs[7 + rows :]
     _, _, there = place(size, width)
     image = near_part_ref[0] + near_part_ref[1] + far_part_ref[...]
     for r, source in enumerate(row_refs):
         piece = terms(only(there[1 + r], source[...]), left_ref, right_ref, r * width, width)
         out_ref[r] = piece
         image = image + piece
-    image = jnp.where(live(facts_ref[...], image.shape), image, 0.0)
     u = u_ref[...].astype(jnp.float32)
-    square = sums_ref[1:2, 0:1]
-    cross = total(u * image)
-    rho = jnp.where(square > 0.0, cross / square, 0.0)
-    w = image - rho * u
-    w_ref[...] = w.astype(jnp.bfloat16)
+    start, square, guess = (sums_ref[n : n + 1, 0:1] for n in range(3))
+    rough = jnp.where(live(facts_ref[...], image.shape), image - guess * u, 0.0)
+    along, inner = total(u * rough), total(rough * rough)
+    shift = jnp.where(square > 0.0, along / square, 0.0)
+    rho = guess + shift
     lane = lax.broadcasted_iota(jnp.int32, (1, 128), 1)
-    stats = jnp.zeros((1, 128), jnp.float32)
-    for n, value in enumerate((sums_ref[0:1, 0:1], square, cross, total(w * w), rho)):
-        stats = jnp.where(lane == n, value, stats)
-    for n in range(stats_ref.shape[0]):
-        stats_ref[n] = stats
+    numbers = jnp.zeros((1, 128), jnp.float32)
+    for n, value in enumerate((start, square, rho * square, jnp.maximum(inner - shift * along, 0.0), rho)):
+        numbers = jnp.where(lane == n, value, numbers)
+    for n in range(numbers_ref.shape[0]):
+        numbers_ref[n] = numbers
+    copy = pltpu.make_async_copy(numbers_ref, numbers_hbm, sem)
+    copy.start()
+    w_ref[...] = (rough - shift * u).astype(jnp.bfloat16)
+    copy.wait()
 
 
 def image_kernel(size, width, rows, *refs):
@@ -284,13 +293,15 @@
         [pltpu.VMEM(few, bf16)] * 2 + [pltpu.VMEM(square, f32), dma((2, 2)), dma((1, 2)), dma((rows, 2)), dma], LONG,
     )(left_env, right_env, hbm(wavefunction), facts, u, near_u)
     near_part, left_row, right_row = vmem(near_part), vmem(left_row), vmem(right_row)
-    far_part = vmem(call(
-        functools.partial(far_kernel, size, width), pltpu.VMEM(square, f32), [VM] * 3, VM, cost=LONG,
-    )(vmem(left_far), vmem(right_far), far_u))
+    far_part, sums = call(
+        functools.partial(far_kernel, size, width), (pltpu.VMEM(square, f32), pltpu.VMEM((8, 128), f32)),
+        [VM] * 6, (VM,) * 2, cost=LONG,
+    )(vmem(left_far), vmem(right_far), near_part, u, vmem(sums), far_u)
+    far_part = vmem(far_part)
     row_part, w, stats = call(
         functools.partial(first_kernel, size, width, rows),
-        (pltpu.VMEM((rows,) + square, f32),) + (pltpu.VMEM(square, bf16), jax.ShapeDtypeStruct((size, 1, 128), f32)),
-        [VM] * (7 + rows), (VM,) * 3,
+        (pltpu.VMEM((rows,) + square, f32), pltpu.VMEM(square, bf16), pltpu.HBM((size, 1, 128), f32)),
+        [VM] * (7 + rows), (VM, VM, HB), [pltpu.VMEM((size, 1, 128), f32), dma],
     )(near_part, far_part, facts, vmem(sums), u, left_row, right_row, *row_u)
 
     w = vmem(w)

time: 29.7 us -> 29.9 us (level)
  no operation moved by 1% of the time
where the time goes in v7:
time: 29.9 us; the launch traced here: 29.6 us
  starting transfers between devices  13.3 us (44%)
  Pallas kernels  11 us (37%)
  waiting for transfers between devices  4.64 us (16%)
  between operations  0.68 us (2%)
    all_to_all x1, starting transfers between devices, body(): stats = lax.all_to_all(stats, 'sector', 0, 0, tiled=True)  5.69 us
    ppermute x4, starting transfers between devices, swap(): lax.ppermute(x, axis, [(s, to.get(s, s)) for s in range(lax.axis_size(axi...  4.57 us
    pallas_call x1, Pallas kernels, body(): call(functools.partial(image_kernel, size, width, rows), pltpu.VMEM(squar...  3.3 us
    ppermute x2, starting transfers between devices, far_swap(): return lax.ppermute(x, ('groups', 'sector'), pairs)  3.04 us
    pallas_call x1, Pallas kernels, body(): call(functools.partial(near_kernel, size, width, rows), (pltpu.VMEM((2,)...  2.86 us
    ppermute x4, waiting for transfers between devices, swap(): lax.ppermute(x, axis, [(s, to.get(s, s)) for s in range(lax.axis_size(axi...  2.41 us
    all_to_all x1, waiting for transfers between devices, body(): stats = lax.all_to_all(stats, 'sector', 0, 0, tiled=True)  1.66 us
    pallas_call x1, Pallas kernels, body(): call(functools.partial(first_kernel, size, width, rows), (pltpu.VMEM((row...  1.64 us
  transfers between devices with their start and end apart: 7, of which 4 were waited for; matrix products, arithmetic and copies ran while one was open for 0% of the time, Pallas kernels for 24%

profile of v7, /device:TPU:0, one launch (start us, length us, event | category | flops | bytes accessed | tf_op | source)
XLA Modules:
  0.0 29.6 jit_solution(7099423564512945015)
XLA Ops:
  0.6 1.0 %shard_map.59 = (bf16[256,256]{1,0:T(8,128)(2,1)S(1)}, bf16[256,256]{1,0:T(8,128)(2,1)S(1)}, f32[8,128]{1,0:T(8,128)S(1)}) custom-call(f32[1,256,256]{2,1,0:T(8,128)} %wave_hbm.3, s32[1,2]{1,0:T(1,128)} %dims_hbm.1), custom_call_target="tpu_custom_call" | custom-call | flops 1 | bytes 1 | tf_op jit(solution)/shard_map/pallas_call | solution.py:279
  1.6 0.5 %collective-permute-start = (bf16[256,256]{1,0:T(8,128)(2,1)S(1)}, bf16[256,256]{1,0:T(8,128)(2,1)S(1)}, u32[]{:S(2)}, u32[]{:S(2)}) collective-permute-start(bf16[256,256]{1,0:T(8,128)(2,1)S(1)} %get-tuple-element.17.self_ref.u_ref.refs_4_), channel_id=1, source_target_pairs={{0,1},{1,0},{2,3},{3,2},{4,5},{5,4},{6,7},{7,6},{8,9},{9,8},{10,11... | collective-permute-start | bytes 393224 | tf_op jit(solution)/shard_map/ppermute | solution.py:39
  2.1 3.7 %collective-permute-start.2 = (bf16[256,256]{1,0:T(8,128)(2,1)S(1)}, bf16[256,256]{1,0:T(8,128)(2,1)S(1)}, u32[]{:S(2)}, u32[]{:S(2)}) collective-permute-start(bf16[256,256]{1,0:T(8,128)(2,1)S(1)} %get-tuple-element.17.self_ref.u_ref.refs_4_), channel_id=1, source_target_pairs={{0,8},{1,9},{2,10},{3,11},{4,12},{5,13},{6,14},{7,15},{8,0},{9,1},... | collective-permute-start | bytes 393224 | tf_op jit(solution)/shard_map/ppermute | solution.py:39
  5.8 0.0 collective-permute-done.near_ref.refs_1_
  5.8 1.5 %collective-permute-start.1 = (bf16[256,256]{1,0:T(8,128)(2,1)S(1)}, bf16[256,256]{1,0:T(8,128)(2,1)S(1)}, u32[]{:S(2)}, u32[]{:S(2)}) collective-permute-start(bf16[256,256]{1,0:T(8,128)(2,1)S(1)} %shard_map.61), channel_id=1, source_target_pairs={{0,16},{1,2},{2,1},{3,4},{4,3},{5,6},{6,5},{7,23},{8,24},{9,10},{1... | collective-permute-start | bytes 393224 | tf_op jit(solution)/shard_map/ppermute | solution.py:60
  7.3 2.9 %shard_map.60 = (f32[2,256,256]{2,1,0:T(8,128)S(1)}, f32[8,128]{1,0:T(8,128)S(1)}, bf16[6,256,256]{2,1,0:T(8,128)(2,1)S(1)}, bf16[6,256,256]{2,1,0:T(8,128)(2,1)...) custom-call(bf16[1,26,256,256]{3,2,1,0:T(8,128)(2,1)} %refs_6_.1, ...), custom_call_target="tpu_custom_call" | custom-call | flops 4000000000 | bytes 1 | tf_op jit(solution)/shard_map/pallas_call | solution.py:289
  10.2 0.6 %collective-permute-done.1.far_ref = bf16[256,256]{1,0:T(8,128)(2,1)S(1)} collective-permute-done((bf16[256,256]{1,0:T(8,128)(2,1)S(1)}, bf16[256,256]{1,0:T(8,128)(2,1)S(1)}, u32[]{:S(2)}, u32[]{:S(2)}) %collective-permute-start.1) | collective-permute-done | bytes 131104 | tf_op jit(solution)/shard_map/ppermute | solution.py:60
  10.8 1.0 %shard_map.62 = (f32[256,256]{1,0:T(8,128)S(1)}, f32[8,128]{1,0:T(8,128)S(1)}) custom-call(bf16[6,256,256]{2,1,0:T(8,128)(2,1)S(1)} %get-tuple-element.19.left_ref, bf16[6,256,256]{2,1,0:T(8,128)(2,1)S(1)} %get-tuple-element.20.right_ref, f32[2,256,256]{2,1,0:T(8,128)S(1)} %get-tuple-element.18.near_part_ref.refs_0_, ...), custom_call_target="tpu_custom_call" | custom-call | flops 4000000000 | bytes 1 | tf_op jit(solution)/shard_map/pallas_call | solution.py:296
  11.8 1.0 %collective-permute-done.2.refs_7_ = bf16[256,256]{1,0:T(8,128)(2,1)S(1)} collective-permute-done((bf16[256,256]{1,0:T(8,128)(2,1)S(1)}, bf16[256,256]{1,0:T(8,128)(2,1)S(1)}, u32[]{:S(2)}, u32[]{:S(2)}) %collective-permute-start.2) | collective-permute-done | bytes 131104 | tf_op jit(solution)/shard_map/ppermute | solution.py:39
  12.8 1.6 %shard_map.63 = (f32[1,256,256]{2,1,0:T(8,128)S(1)}, bf16[256,256]{1,0:T(8,128)(2,1)S(1)}, f32[16,1,128]{2,1,0:T(1,128)}) custom-call(f32[2,256,256]{2,1,0:T(8,128)S(1)} %get-tuple-element.18.near_part_ref.refs_0_, f32[256,256]{1,0:T(8,128)S(1)} %get-tuple-element.23.refs_1_.far_part_ref, f32[8,128]{1,0:T(8,128)S(1)} %get-tuple-element.16.facts_ref.refs_2_, ...), custom_call_target="tpu_custom_call" | custom-call | flops 1 | bytes 1 | tf_op jit(solution)/shard_map/pallas_call | solution.py:301
  14.5 0.3 %collective-permute-start.3 = (bf16[256,256]{1,0:T(8,128)(2,1)S(1)}, bf16[256,256]{1,0:T(8,128)(2,1)S(1)}, u32[]{:S(2)}, u32[]{:S(2)}) collective-permute-start(bf16[256,256]{1,0:T(8,128)(2,1)S(1)} %get-tuple-element.28.refs_3_), channel_id=1, source_target_pairs={{0,8},{1,9},{2,10},{3,11},{4,12},{5,13},{6,14},{7,15},{8,0},{9,1},... | collective-permute-start | bytes 393224 | tf_op jit(solution)/shard_map/ppermute | solution.py:39
  14.8 1.5 %collective-permute-start.4 = (bf16[256,256]{1,0:T(8,128)(2,1)S(1)}, bf16[256,256]{1,0:T(8,128)(2,1)S(1)}, u32[]{:S(2)}, u32[]{:S(2)}) collective-permute-start(bf16[256,256]{1,0:T(8,128)(2,1)S(1)} %get-tuple-element.28.refs_3_), channel_id=1, source_target_pairs={{0,16},{1,2},{2,1},{3,4},{4,3},{5,6},{6,5},{7,23},{8,24},{9,10},{1... | collective-permute-start | bytes 393224 | tf_op jit(solution)/shard_map/ppermute | solution.py:60
  16.3 0.1 collective-permute-start.5
  16.4 5.7 %all-to-all-start = ((f32[16,1,128]{2,1,0:T(1,128)}), f32[16,1,128]{2,1,0:T(1,128)S(1)}, u32[]{:S(2)}, u32[]{:S(2)}) async-start(f32[16,1,128]{2,1,0:T(1,128)} %get-tuple-element.27), calls=%async_computation | async-start | bytes 16384 | tf_op jit(solution)/shard_map/all_to_all | solution.py:311
  22.1 1.4 %collective-permute-done.3.refs_0_ = bf16[256,256]{1,0:T(8,128)(2,1)S(1)} collective-permute-done((bf16[256,256]{1,0:T(8,128)(2,1)S(1)}, bf16[256,256]{1,0:T(8,128)(2,1)S(1)}, u32[]{:S(2)}, u32[]{:S(2)}) %collective-permute-start.3) | collective-permute-done | bytes 131104 | tf_op jit(solution)/shard_map/ppermute | solution.py:39
  23.4 0.0 collective-permute-done.4.refs_1_
  23.4 0.0 collective-permute-done.5.refs_2_
  23.4 3.3 %shard_map.64.hw_ref = f32[256,256]{1,0:T(8,128)S(1)} custom-call(bf16[256,256]{1,0:T(8,128)(2,1)S(1)} %collective-permute-done.3.refs_0_, bf16[256,256]{1,0:T(8,128)(2,1)S(1)} %collective-permute-done.4.refs_1_, bf16[256,256]{1,0:T(8,128)(2,1)S(1)} %collective-permute-done.5.refs_2_, bf16[256,256]{1,0:T(8,128)(2,1)S(1)} %get-tuple-element.28.refs_3_, ...), custom_call_target="tpu_custom_call" | custom-call | flops 1 | bytes 1 | tf_op jit(solution)/shard_map/pallas_call | solution.py:312
  26.7 1.7 %all-to-all-done.stats_ref = f32[16,1,128]{2,1,0:T(1,128)S(1)} async-done(((f32[16,1,128]{2,1,0:T(1,128)}), f32[16,1,128]{2,1,0:T(1,128)S(1)}, u32[]{:S(2)}, u32[]{:S(2)}) %all-to-all-start) | async-done | bytes 8224 | tf_op jit(solution)/shard_map/all_to_all | solution.py:311
  28.4 1.2 %shard_map.65 = (f32[1,256,256]{2,1,0:T(8,128)}, f32[1,256,256]{2,1,0:T(8,128)}) custom-call(f32[8,128]{1,0:T(8,128)S(1)} %get-tuple-element.16.facts_ref.refs_2_, f32[16,1,128]{2,1,0:T(1,128)S(1)} %all-to-all-done.stats_ref, f32[256,256]{1,0:T(8,128)S(1)} %shard_map.64.hw_ref, f32[2,256,256]{2,1,0:T(8,128)S(1)} %get-tuple-element.18.near_part_ref.refs_0_, ...), custom_call_target="tpu_custom_call" | custom-call | flops 1 | bytes 1 | tf_op jit(solution)/shard_map/pallas_call | solution.py:316
  (1 shorter events, 0.0 us)
Async XLA Ops:
  1.6 4.2 %collective-permute-start = (bf16[256,256]{1,0:T(8,128)(2,1)S(1)}, bf16[256,256]{1,0:T(8,128)(2,1)S(1)}, u32[]{:S(2)}, u32[]{:S(2)}) collective-permute-start(bf16[256,256]{1,0:T(8,128)(2,1)S(1)} %get-tuple-element.17.self_ref.u_ref.refs_4_), channel_id=1, source_target_pairs={{0,1},{1,0},{2,3},{3,2},{4,5},{5,4},{6,7},{7,6},{8,9},{9,8},{10,11... | collective-permute-start | bytes 393224 | tf_op jit(solution)/shard_map/ppermute | solution.py:39
  2.1 10.7 %collective-permute-start.2 = (bf16[256,256]{1,0:T(8,128)(2,1)S(1)}, bf16[256,256]{1,0:T(8,128)(2,1)S(1)}, u32[]{:S(2)}, u32[]{:S(2)}) collective-permute-start(bf16[256,256]{1,0:T(8,128)(2,1)S(1)} %get-tuple-element.17.self_ref.u_ref.refs_4_), channel_id=1, source_target_pairs={{0,8},{1,9},{2,10},{3,11},{4,12},{5,13},{6,14},{7,15},{8,0},{9,1},... | collective-permute-start | bytes 393224 | tf_op jit(solution)/shard_map/ppermute | solution.py:39
  5.8 5.0 %collective-permute-start.1 = (bf16[256,256]{1,0:T(8,128)(2,1)S(1)}, bf16[256,256]{1,0:T(8,128)(2,1)S(1)}, u32[]{:S(2)}, u32[]{:S(2)}) collective-permute-start(bf16[256,256]{1,0:T(8,128)(2,1)S(1)} %shard_map.61), channel_id=1, source_target_pairs={{0,16},{1,2},{2,1},{3,4},{4,3},{5,6},{6,5},{7,23},{8,24},{9,10},{1... | collective-permute-start | bytes 393224 | tf_op jit(solution)/shard_map/ppermute | solution.py:60
  14.5 9.0 %collective-permute-start.3 = (bf16[256,256]{1,0:T(8,128)(2,1)S(1)}, bf16[256,256]{1,0:T(8,128)(2,1)S(1)}, u32[]{:S(2)}, u32[]{:S(2)}) collective-permute-start(bf16[256,256]{1,0:T(8,128)(2,1)S(1)} %get-tuple-element.28.refs_3_), channel_id=1, source_target_pairs={{0,8},{1,9},{2,10},{3,11},{4,12},{5,13},{6,14},{7,15},{8,0},{9,1},... | collective-permute-start | bytes 393224 | tf_op jit(solution)/shard_map/ppermute | solution.py:39
  14.8 8.7 %collective-permute-start.4 = (bf16[256,256]{1,0:T(8,128)(2,1)S(1)}, bf16[256,256]{1,0:T(8,128)(2,1)S(1)}, u32[]{:S(2)}, u32[]{:S(2)}) collective-permute-start(bf16[256,256]{1,0:T(8,128)(2,1)S(1)} %get-tuple-element.28.refs_3_), channel_id=1, source_target_pairs={{0,16},{1,2},{2,1},{3,4},{4,3},{5,6},{6,5},{7,23},{8,24},{9,10},{1... | collective-permute-start | bytes 393224 | tf_op jit(solution)/shard_map/ppermute | solution.py:60
  16.3 7.2 %collective-permute-start.5 = (bf16[256,256]{1,0:T(8,128)(2,1)S(1)}, bf16[256,256]{1,0:T(8,128)(2,1)S(1)}, u32[]{:S(2)}, u32[]{:S(2)}) collective-permute-start(bf16[256,256]{1,0:T(8,128)(2,1)S(1)} %get-tuple-element.28.refs_3_), channel_id=1, source_target_pairs={{0,1},{1,0},{2,3},{3,2},{4,5},{5,4},{6,7},{7,6},{8,9},{9,8},{10,11... | collective-permute-start | bytes 393224 | tf_op jit(solution)/shard_map/ppermute | solution.py:39
  16.4 12.0 %all-to-all-start = ((f32[16,1,128]{2,1,0:T(1,128)}), f32[16,1,128]{2,1,0:T(1,128)S(1)}, u32[]{:S(2)}, u32[]{:S(2)}) async-start(f32[16,1,128]{2,1,0:T(1,128)} %get-tuple-element.27), calls=%async_computation | async-start | bytes 16384 | tf_op jit(solution)/shard_map/all_to_all | solution.py:311

commit v8 on v3

--- a/solution.py
+++ b/solution.py
@@ -95,13 +95,9 @@
     size = src.shape[0]
     right = right_ref[pl.ds(first, count)].reshape(count * size, size)
     partial_t = lax.dot_general(right, src, NT, preferred_element_type=jnp.float32).astype(jnp.bfloat16)
-    image = None
-    for k in range(count):
-        piece = lax.dot_general(
-            left_ref[first + k], partial_t[k * size : (k + 1) * size], NT, preferred_element_type=jnp.float32
-        )
-        image = piece if image is None else image + piece
-    return image
+    left = jnp.concatenate([left_ref[first + k] for k in range(count)], axis=1)
+    partial_t = jnp.concatenate([partial_t[k * size : (k + 1) * size] for k in range(count)], axis=1)
+    return lax.dot_general(left, partial_t, NT, preferred_element_type=jnp.float32)
 
 
 def fetch(left_hbm, right_hbm, left_ref, right_ref, sems, spans):

time: 29.7 us -> 29.6 us (level)
    all_to_all x1, waiting for transfers between devices: 1.52 us -> 1.2 us  [body(): stats = lax.all_to_all(stats, 'sector', 0, 0, tiled=True)]
where the time goes in v8:
time: 29.6 us; the launch traced here: 29.4 us
  starting transfers between devices  13.1 us (44%)
  Pallas kernels  11 us (37%)
  waiting for transfers between devices  4.64 us (16%)
  between operations  0.68 us (2%)
    all_to_all x1, starting transfers between devices, body(): stats = lax.all_to_all(stats, 'sector', 0, 0, tiled=True)  5.51 us
    ppermute x4, starting transfers between devices, swap(): lax.ppermute(x, axis, [(s, to.get(s, s)) for s in range(lax.axis_size(axi...  4.48 us
    pallas_call x1, Pallas kernels, body(): call(functools.partial(image_kernel, size, width, rows), pltpu.VMEM(squar...  3.57 us
    ppermute x2, starting transfers between devices, far_swap(): return lax.ppermute(x, ('groups', 'sector'), pairs)  3.07 us
    pallas_call x1, Pallas kernels, body(): call(functools.partial(near_kernel, size, width, rows), (pltpu.VMEM((2,)...  2.79 us
    ppermute x4, waiting for transfers between devices, swap(): lax.ppermute(x, axis, [(s, to.get(s, s)) for s in range(lax.axis_size(axi...  2.79 us
    pallas_call x1, Pallas kernels, body(): call(functools.partial(first_kernel, size, width, rows), (pltpu.VMEM((row...  1.66 us
    pallas_call x1, Pallas kernels, body(): call(functools.partial(second_kernel, size, width, rows, cells), (jax.Sha...  1.23 us
  transfers between devices with their start and end apart: 7, of which 4 were waited for; matrix products, arithmetic and copies ran while one was open for 0% of the time, Pallas kernels for 24%

profile of v8, /device:TPU:0, one launch (start us, length us, event | category | flops | bytes accessed | tf_op | source)
XLA Modules:
  0.0 29.4 jit_solution(11418150831175412083)
XLA Ops:
  0.6 1.0 %shard_map.59 = (bf16[256,256]{1,0:T(8,128)(2,1)S(1)}, bf16[256,256]{1,0:T(8,128)(2,1)S(1)}, f32[8,128]{1,0:T(8,128)S(1)}) custom-call(f32[1,256,256]{2,1,0:T(8,128)} %wave_hbm.3, s32[1,2]{1,0:T(1,128)} %dims_hbm.1), custom_call_target="tpu_custom_call" | custom-call | flops 1 | bytes 1 | tf_op jit(solution)/shard_map/pallas_call | solution.py:266
  1.6 0.5 %collective-permute-start = (bf16[256,256]{1,0:T(8,128)(2,1)S(1)}, bf16[256,256]{1,0:T(8,128)(2,1)S(1)}, u32[]{:S(2)}, u32[]{:S(2)}) collective-permute-start(bf16[256,256]{1,0:T(8,128)(2,1)S(1)} %get-tuple-element.15.self_ref.refs_4_), channel_id=1, source_target_pairs={{0,1},{1,0},{2,3},{3,2},{4,5},{5,4},{6,7},{7,6},{8,9},{9,8},{10,11... | collective-permute-start | bytes 393224 | tf_op jit(solution)/shard_map/ppermute | solution.py:39
  2.1 3.7 %collective-permute-start.2 = (bf16[256,256]{1,0:T(8,128)(2,1)S(1)}, bf16[256,256]{1,0:T(8,128)(2,1)S(1)}, u32[]{:S(2)}, u32[]{:S(2)}) collective-permute-start(bf16[256,256]{1,0:T(8,128)(2,1)S(1)} %get-tuple-element.15.self_ref.refs_4_), channel_id=1, source_target_pairs={{0,8},{1,9},{2,10},{3,11},{4,12},{5,13},{6,14},{7,15},{8,0},{9,1},... | collective-permute-start | bytes 393224 | tf_op jit(solution)/shard_map/ppermute | solution.py:39
  5.8 0.0 collective-permute-done.near_ref.refs_1_
  5.8 1.5 %collective-permute-start.1 = (bf16[256,256]{1,0:T(8,128)(2,1)S(1)}, bf16[256,256]{1,0:T(8,128)(2,1)S(1)}, u32[]{:S(2)}, u32[]{:S(2)}) collective-permute-start(bf16[256,256]{1,0:T(8,128)(2,1)S(1)} %shard_map.61), channel_id=1, source_target_pairs={{0,16},{1,2},{2,1},{3,4},{4,3},{5,6},{6,5},{7,23},{8,24},{9,10},{1... | collective-permute-start | bytes 393224 | tf_op jit(solution)/shard_map/ppermute | solution.py:60
  7.3 2.8 %shard_map.60 = (f32[2,256,256]{2,1,0:T(8,128)S(1)}, f32[8,128]{1,0:T(8,128)S(1)}, bf16[6,256,256]{2,1,0:T(8,128)(2,1)S(1)}, bf16[6,256,256]{2,1,0:T(8,128)(2,1)...) custom-call(bf16[1,26,256,256]{3,2,1,0:T(8,128)(2,1)} %refs_6_.1, ...), custom_call_target="tpu_custom_call" | custom-call | flops 4000000000 | bytes 1 | tf_op jit(solution)/shard_map/pallas_call | solution.py:276
  10.1 0.6 %collective-permute-done.1.far_ref = bf16[256,256]{1,0:T(8,128)(2,1)S(1)} collective-permute-done((bf16[256,256]{1,0:T(8,128)(2,1)S(1)}, bf16[256,256]{1,0:T(8,128)(2,1)S(1)}, u32[]{:S(2)}, u32[]{:S(2)}) %collective-permute-start.1) | collective-permute-done | bytes 131104 | tf_op jit(solution)/shard_map/ppermute | solution.py:60
  10.8 0.8 %shard_map.62.refs_1_.far_part_ref = f32[256,256]{1,0:T(8,128)S(1)} custom-call(bf16[6,256,256]{2,1,0:T(8,128)(2,1)S(1)} %get-tuple-element.17.left_ref, bf16[6,256,256]{2,1,0:T(8,128)(2,1)S(1)} %get-tuple-element.18.right_ref, bf16[256,256]{1,0:T(8,128)(2,1)S(1)} %collective-permute-done.1.far_ref), custom_call_target="tpu_custom_call" | custom-call | flops 4000000000 | bytes 1 | tf_op jit(solution)/shard_map/pallas_call | solution.py:283
  11.6 1.2 %collective-permute-done.2.refs_7_ = bf16[256,256]{1,0:T(8,128)(2,1)S(1)} collective-permute-done((bf16[256,256]{1,0:T(8,128)(2,1)S(1)}, bf16[256,256]{1,0:T(8,128)(2,1)S(1)}, u32[]{:S(2)}, u32[]{:S(2)}) %collective-permute-start.2) | collective-permute-done | bytes 131104 | tf_op jit(solution)/shard_map/ppermute | solution.py:39
  12.8 1.7 %shard_map.63 = (f32[1,256,256]{2,1,0:T(8,128)S(1)}, bf16[256,256]{1,0:T(8,128)(2,1)S(1)}, f32[16,1,128]{2,1,0:T(1,128)}) custom-call(f32[2,256,256]{2,1,0:T(8,128)S(1)} %get-tuple-element.16.refs_0_.near_part_ref, f32[256,256]{1,0:T(8,128)S(1)} %shard_map.62.refs_1_.far_part_ref, f32[8,128]{1,0:T(8,128)S(1)} %get-tuple-element.14.facts_ref.refs_2_, ...), custom_call_target="tpu_custom_call" | custom-call | flops 1 | bytes 1 | tf_op jit(solution)/shard_map/pallas_call | solution.py:286
  14.5 0.0 collective-permute-start.3
  14.5 1.6 %collective-permute-start.4 = (bf16[256,256]{1,0:T(8,128)(2,1)S(1)}, bf16[256,256]{1,0:T(8,128)(2,1)S(1)}, u32[]{:S(2)}, u32[]{:S(2)}) collective-permute-start(bf16[256,256]{1,0:T(8,128)(2,1)S(1)} %get-tuple-element.24.refs_3_), channel_id=1, source_target_pairs={{0,16},{1,2},{2,1},{3,4},{4,3},{5,6},{6,5},{7,23},{8,24},{9,10},{1... | collective-permute-start | bytes 393224 | tf_op jit(solution)/shard_map/ppermute | solution.py:60
  16.1 0.3 collective-permute-start.5
  16.3 5.5 %all-to-all-start = ((f32[16,1,128]{2,1,0:T(1,128)}), f32[16,1,128]{2,1,0:T(1,128)S(1)}, u32[]{:S(2)}, u32[]{:S(2)}) async-start(f32[16,1,128]{2,1,0:T(1,128)} %get-tuple-element.23), calls=%async_computation | async-start | bytes 16384 | tf_op jit(solution)/shard_map/all_to_all | solution.py:296
  21.8 1.5 %collective-permute-done.3.refs_0_ = bf16[256,256]{1,0:T(8,128)(2,1)S(1)} collective-permute-done((bf16[256,256]{1,0:T(8,128)(2,1)S(1)}, bf16[256,256]{1,0:T(8,128)(2,1)S(1)}, u32[]{:S(2)}, u32[]{:S(2)}) %collective-permute-start.3) | collective-permute-done | bytes 131104 | tf_op jit(solution)/shard_map/ppermute | solution.py:39
  23.4 0.0 collective-permute-done.4.refs_1_
  23.4 0.0 collective-permute-done.5.refs_2_
  23.4 3.6 %shard_map.64.hw_ref = f32[256,256]{1,0:T(8,128)S(1)} custom-call(bf16[256,256]{1,0:T(8,128)(2,1)S(1)} %collective-permute-done.3.refs_0_, bf16[256,256]{1,0:T(8,128)(2,1)S(1)} %collective-permute-done.4.refs_1_, bf16[256,256]{1,0:T(8,128)(2,1)S(1)} %collective-permute-done.5.refs_2_, bf16[256,256]{1,0:T(8,128)(2,1)S(1)} %get-tuple-element.24.refs_3_, ...), custom_call_target="tpu_custom_call" | custom-call | flops 1 | bytes 1 | tf_op jit(solution)/shard_map/pallas_call | solution.py:297
  27.0 1.2 %all-to-all-done.stats_ref = f32[16,1,128]{2,1,0:T(1,128)S(1)} async-done(((f32[16,1,128]{2,1,0:T(1,128)}), f32[16,1,128]{2,1,0:T(1,128)S(1)}, u32[]{:S(2)}, u32[]{:S(2)}) %all-to-all-start) | async-done | bytes 8224 | tf_op jit(solution)/shard_map/all_to_all | solution.py:296
  28.2 1.2 %shard_map.65 = (f32[1,256,256]{2,1,0:T(8,128)}, f32[1,256,256]{2,1,0:T(8,128)}) custom-call(f32[8,128]{1,0:T(8,128)S(1)} %get-tuple-element.14.facts_ref.refs_2_, f32[16,1,128]{2,1,0:T(1,128)S(1)} %all-to-all-done.stats_ref, f32[256,256]{1,0:T(8,128)S(1)} %shard_map.64.hw_ref, f32[2,256,256]{2,1,0:T(8,128)S(1)} %get-tuple-element.16.refs_0_.near_part_ref, ...), custom_call_target="tpu_custom_call" | custom-call | flops 1 | bytes 1 | tf_op jit(solution)/shard_map/pallas_call | solution.py:301
  (1 shorter events, 0.0 us)
Async XLA Ops:
  1.6 4.2 %collective-permute-start = (bf16[256,256]{1,0:T(8,128)(2,1)S(1)}, bf16[256,256]{1,0:T(8,128)(2,1)S(1)}, u32[]{:S(2)}, u32[]{:S(2)}) collective-permute-start(bf16[256,256]{1,0:T(8,128)(2,1)S(1)} %get-tuple-element.15.self_ref.refs_4_), channel_id=1, source_target_pairs={{0,1},{1,0},{2,3},{3,2},{4,5},{5,4},{6,7},{7,6},{8,9},{9,8},{10,11... | collective-permute-start | bytes 393224 | tf_op jit(solution)/shard_map/ppermute | solution.py:39
  2.1 10.7 %collective-permute-start.2 = (bf16[256,256]{1,0:T(8,128)(2,1)S(1)}, bf16[256,256]{1,0:T(8,128)(2,1)S(1)}, u32[]{:S(2)}, u32[]{:S(2)}) collective-permute-start(bf16[256,256]{1,0:T(8,128)(2,1)S(1)} %get-tuple-element.15.self_ref.refs_4_), channel_id=1, source_target_pairs={{0,8},{1,9},{2,10},{3,11},{4,12},{5,13},{6,14},{7,15},{8,0},{9,1},... | collective-permute-start | bytes 393224 | tf_op jit(solution)/shard_map/ppermute | solution.py:39
  5.8 5.0 %collective-permute-start.1 = (bf16[256,256]{1,0:T(8,128)(2,1)S(1)}, bf16[256,256]{1,0:T(8,128)(2,1)S(1)}, u32[]{:S(2)}, u32[]{:S(2)}) collective-permute-start(bf16[256,256]{1,0:T(8,128)(2,1)S(1)} %shard_map.61), channel_id=1, source_target_pairs={{0,16},{1,2},{2,1},{3,4},{4,3},{5,6},{6,5},{7,23},{8,24},{9,10},{1... | collective-permute-start | bytes 393224 | tf_op jit(solution)/shard_map/ppermute | solution.py:60
  14.5 8.9 %collective-permute-start.3 = (bf16[256,256]{1,0:T(8,128)(2,1)S(1)}, bf16[256,256]{1,0:T(8,128)(2,1)S(1)}, u32[]{:S(2)}, u32[]{:S(2)}) collective-permute-start(bf16[256,256]{1,0:T(8,128)(2,1)S(1)} %get-tuple-element.24.refs_3_), channel_id=1, source_target_pairs={{0,8},{1,9},{2,10},{3,11},{4,12},{5,13},{6,14},{7,15},{8,0},{9,1},... | collective-permute-start | bytes 393224 | tf_op jit(solution)/shard_map/ppermute | solution.py:39
  14.5 8.9 %collective-permute-start.4 = (bf16[256,256]{1,0:T(8,128)(2,1)S(1)}, bf16[256,256]{1,0:T(8,128)(2,1)S(1)}, u32[]{:S(2)}, u32[]{:S(2)}) collective-permute-start(bf16[256,256]{1,0:T(8,128)(2,1)S(1)} %get-tuple-element.24.refs_3_), channel_id=1, source_target_pairs={{0,16},{1,2},{2,1},{3,4},{4,3},{5,6},{6,5},{7,23},{8,24},{9,10},{1... | collective-permute-start | bytes 393224 | tf_op jit(solution)/shard_map/ppermute | solution.py:60
  16.1 7.3 %collective-permute-start.5 = (bf16[256,256]{1,0:T(8,128)(2,1)S(1)}, bf16[256,256]{1,0:T(8,128)(2,1)S(1)}, u32[]{:S(2)}, u32[]{:S(2)}) collective-permute-start(bf16[256,256]{1,0:T(8,128)(2,1)S(1)} %get-tuple-element.24.refs_3_), channel_id=1, source_target_pairs={{0,1},{1,0},{2,3},{3,2},{4,5},{5,4},{6,7},{7,6},{8,9},{9,8},{10,11... | collective-permute-start | bytes 393224 | tf_op jit(solution)/shard_map/ppermute | solution.py:39
  16.3 11.8 %all-to-all-start = ((f32[16,1,128]{2,1,0:T(1,128)}), f32[16,1,128]{2,1,0:T(1,128)S(1)}, u32[]{:S(2)}, u32[]{:S(2)}) async-start(f32[16,1,128]{2,1,0:T(1,128)} %get-tuple-element.23), calls=%async_computation | async-start | bytes 16384 | tf_op jit(solution)/shard_map/all_to_all | solution.py:296

commit v9 on v6

--- a/solution.py
+++ b/solution.py
@@ -95,13 +95,9 @@
     size = src.shape[0]
     right = right_ref[pl.ds(first, count)].reshape(count * size, size)
     partial_t = lax.dot_general(right, src, NT, preferred_element_type=jnp.float32).astype(jnp.bfloat16)
-    image = None
-    for k in range(count):
-        piece = lax.dot_general(
-            left_ref[first + k], partial_t[k * size : (k + 1) * size], NT, preferred_element_type=jnp.float32
-        )
-        image = piece if image is None else image + piece
-    return image
+    left = jnp.concatenate([left_ref[first + k] for k in range(count)], axis=1)
+    partial_t = jnp.concatenate([partial_t[k * size : (k + 1) * size] for k in range(count)], axis=1)
+    return lax.dot_general(left, partial_t, NT, preferred_element_type=jnp.float32)
 
 
 def fetch(left_hbm, right_hbm, left_ref, right_ref, sems, spans):
@@ -188,7 +184,7 @@
 
 def first_kernel(size, width, rows, *refs):
     near_part_ref, far_part_ref, facts_ref, sums_ref, u_ref, left_ref, right_ref = refs[:7]
-    row_refs, (out_ref, w_ref, sums_out_ref, numbers_hbm, numbers_ref, sem) = refs[7 : 7 + rows], refs[7 + rows :]
+    row_refs, (out_ref, w_ref, far_w_ref, sums_out_ref, numbers_hbm, numbers_ref, sem) = refs[7 : 7 + rows], refs[7 + rows :]
     _, _, there = place(size, width)
     image = near_part_ref[0] + near_part_ref[1] + far_part_ref[...]
     for r, source in enumerate(row_refs):
@@ -200,7 +196,8 @@
     square = sums_ref[1:2, 0:1]
     cross = total(u * image)
     rho = jnp.where(square > 0.0, cross / square, 0.0)
-    w_ref[...] = (image - rho * u).astype(jnp.bfloat16)
+    for ref in (w_ref, far_w_ref):
+        ref[...] = (image - rho * u).astype(jnp.bfloat16)
     lines = lax.broadcasted_iota(jnp.int32, (8, 128), 0)
     sums = jnp.where(lines == 2, cross, jnp.where(lines == 4, rho, sums_ref[...]))
     sums_out_ref[...] = sums
@@ -229,7 +226,7 @@
     copy.wait()
 
 
-def numbers_kernel(held_hbm, sums_ref, w_ref, numbers_hbm, numbers_ref, sem):
+def numbers_kernel(held_hbm, sums_ref, w_ref, far_w_in, near_w, numbers_hbm, far_w_out, numbers_ref, sem):
     @pl.when(jnp.logical_not(even_row()))
     def _():
         write_numbers(sums_ref[...], w_ref, numbers_hbm, numbers_ref, sem)
@@ -314,17 +311,19 @@
     )(vmem(left_far), vmem(right_far), far_u))
     table = pltpu.HBM((size, 1, 128), f32)
     table_scratch = [pltpu.VMEM((size, 1, 128), f32), dma]
-    row_part, w, sums, stats = call(
+    row_part, w, far_w, sums, stats = call(
         functools.partial(first_kernel, size, width, rows),
-        (pltpu.VMEM((rows,) + square, f32), pltpu.VMEM(square, bf16), pltpu.VMEM((8, 128), f32), table),
-        [VM] * (7 + rows), (VM,) * 3 + (HB,), table_scratch,
+        (pltpu.VMEM((rows,) + square, f32),) + (pltpu.VMEM(square, bf16),) * 2 + (pltpu.VMEM((8, 128), f32), table),
+        [VM] * (7 + rows), (VM,) * 4 + (HB,), table_scratch,
     )(near_part, far_part, facts, vmem(sums), u, left_row, right_row, *row_u)
 
     w = vmem(w)
     row_w = [vmem(swap(w, "sector", p)) for p in row_pairs]
     near_w = vmem(swap(w, "sector", near))
-    far_w = vmem(far_swap(w))
-    stats = call(numbers_kernel, table, [HB] + [VM] * 2, HB, table_scratch, aliases={0: 0})(hbm(stats), vmem(sums), w)
+    stats, far_w = call(
+        numbers_kernel, (table, pltpu.VMEM(square, bf16)), [HB] + [VM] * 2 + [AN] * 2, (HB, AN), table_scratch, aliases={0: 0, 3: 1},
+    )(hbm(stats), vmem(sums), w, vmem(far_w), near_w)
+    far_w = vmem(far_swap(far_w))
     stats = lax.all_to_all(stats, "sector", 0, 0, tiled=True)
     hw = call(
         functools.partial(image_kernel, size, width, rows), pltpu.VMEM(square, f32), [VM] * (5 + rows) + [HB] * 2, VM,

time: 30.6 us -> 30.6 us (level)
  starting transfers between devices: 13.9 us -> 12.7 us
  waiting for transfers between devices: 4.77 us -> 5.9 us
    ppermute x4, waiting for transfers between devices: 1.92 us -> 3.94 us  [swap(): lax.ppermute(x, axis, [(s, to.get(s, s)) for s in range(lax.axis_size(axi...]
    all_to_all x1, starting transfers between devices: 6.47 us -> 5.17 us  [body(): stats = lax.all_to_all(stats, 'sector', 0, 0, tiled=True)]
    all_to_all x1, waiting for transfers between devices: 2.27 us -> 1.31 us  [body(): stats = lax.all_to_all(stats, 'sector', 0, 0, tiled=True)]
  transfers between devices with their start and end apart: 7 -> 7, of which waited for: 4 -> 5; matrix products, arithmetic and copies ran while one was open for 0% -> 0% of each run, Pallas kernels for 23% -> 24%
where the time goes in v9:
time: 30.6 us; the launch traced here: 30.3 us
  starting transfers between devices  12.7 us (42%)
  Pallas kernels  11.1 us (36%)
  waiting for transfers between devices  5.9 us (19%)
  between operations  0.71 us (2%)
    all_to_all x1, starting transfers between devices, body(): stats = lax.all_to_all(stats, 'sector', 0, 0, tiled=True)  5.17 us
    ppermute x4, starting transfers between devices, swap(): lax.ppermute(x, axis, [(s, to.get(s, s)) for s in range(lax.axis_size(axi...  4.32 us
    ppermute x4, waiting for transfers between devices, swap(): lax.ppermute(x, axis, [(s, to.get(s, s)) for s in range(lax.axis_size(axi...  3.94 us
    pallas_call x1, Pallas kernels, body(): call(functools.partial(image_kernel, size, width, rows), pltpu.VMEM(squar...  3.57 us
    ppermute x2, starting transfers between devices, far_swap(): return lax.ppermute(x, ('groups', 'sector'), pairs)  3.17 us
    pallas_call x1, Pallas kernels, body(): call(functools.partial(near_kernel, size, width, rows), (pltpu.VMEM((2,)...  2.79 us
    pallas_call x1, Pallas kernels, body(): call(functools.partial(first_kernel, size, width, rows), (pltpu.VMEM((row...  1.67 us
    all_to_all x1, waiting for transfers between devices, body(): stats = lax.all_to_all(stats, 'sector', 0, 0, tiled=True)  1.31 us
  transfers between devices with their start and end apart: 7, of which 5 were waited for; matrix products, arithmetic and copies ran while one was open for 0% of the time, Pallas kernels for 24%

profile of v9, /device:TPU:0, one launch (start us, length us, event | category | flops | bytes accessed | tf_op | source)
XLA Modules:
  0.0 30.3 jit_solution(16777750223230113326)
XLA Ops:
  0.6 1.0 %shard_map.59 = (bf16[256,256]{1,0:T(8,128)(2,1)S(1)}, bf16[256,256]{1,0:T(8,128)(2,1)S(1)}, f32[8,128]{1,0:T(8,128)S(1)}) custom-call(f32[1,256,256]{2,1,0:T(8,128)} %wave_hbm.3, s32[1,2]{1,0:T(1,128)} %dims_hbm.1), custom_call_target="tpu_custom_call" | custom-call | flops 1 | bytes 1 | tf_op jit(solution)/shard_map/pallas_call | solution.py:292
  1.6 0.5 %collective-permute-start = (bf16[256,256]{1,0:T(8,128)(2,1)S(1)}, bf16[256,256]{1,0:T(8,128)(2,1)S(1)}, u32[]{:S(2)}, u32[]{:S(2)}) collective-permute-start(bf16[256,256]{1,0:T(8,128)(2,1)S(1)} %get-tuple-element.19.self_ref.refs_4_), channel_id=1, source_target_pairs={{0,1},{1,0},{2,3},{3,2},{4,5},{5,4},{6,7},{7,6},{8,9},{9,8},{10,11... | collective-permute-start | bytes 393224 | tf_op jit(solution)/shard_map/ppermute | solution.py:39
  2.1 3.7 %collective-permute-start.2 = (bf16[256,256]{1,0:T(8,128)(2,1)S(1)}, bf16[256,256]{1,0:T(8,128)(2,1)S(1)}, u32[]{:S(2)}, u32[]{:S(2)}) collective-permute-start(bf16[256,256]{1,0:T(8,128)(2,1)S(1)} %get-tuple-element.19.self_ref.refs_4_), channel_id=1, source_target_pairs={{0,8},{1,9},{2,10},{3,11},{4,12},{5,13},{6,14},{7,15},{8,0},{9,1},... | collective-permute-start | bytes 393224 | tf_op jit(solution)/shard_map/ppermute | solution.py:39
  5.8 0.0 collective-permute-done.near_ref.refs_1_
  5.8 1.5 %collective-permute-start.1 = (bf16[256,256]{1,0:T(8,128)(2,1)S(1)}, bf16[256,256]{1,0:T(8,128)(2,1)S(1)}, u32[]{:S(2)}, u32[]{:S(2)}) collective-permute-start(bf16[256,256]{1,0:T(8,128)(2,1)S(1)} %shard_map.61), channel_id=1, source_target_pairs={{0,16},{1,2},{2,1},{3,4},{4,3},{5,6},{6,5},{7,23},{8,24},{9,10},{1... | collective-permute-start | bytes 393224 | tf_op jit(solution)/shard_map/ppermute | solution.py:60
  7.3 2.8 %shard_map.60 = (f32[2,256,256]{2,1,0:T(8,128)S(1)}, f32[8,128]{1,0:T(8,128)S(1)}, bf16[6,256,256]{2,1,0:T(8,128)(2,1)S(1)}, bf16[6,256,256]{2,1,0:T(8,128)(2,1)...) custom-call(bf16[1,26,256,256]{3,2,1,0:T(8,128)(2,1)} %refs_6_.1, ...), custom_call_target="tpu_custom_call" | custom-call | flops 4000000000 | bytes 1 | tf_op jit(solution)/shard_map/pallas_call | solution.py:302
  10.1 0.6 %collective-permute-done.1.far_ref = bf16[256,256]{1,0:T(8,128)(2,1)S(1)} collective-permute-done((bf16[256,256]{1,0:T(8,128)(2,1)S(1)}, bf16[256,256]{1,0:T(8,128)(2,1)S(1)}, u32[]{:S(2)}, u32[]{:S(2)}) %collective-permute-start.1) | collective-permute-done | bytes 131104 | tf_op jit(solution)/shard_map/ppermute | solution.py:60
  10.8 0.8 %shard_map.62.refs_1_.far_part_ref = f32[256,256]{1,0:T(8,128)S(1)} custom-call(bf16[6,256,256]{2,1,0:T(8,128)(2,1)S(1)} %get-tuple-element.21.left_ref, bf16[6,256,256]{2,1,0:T(8,128)(2,1)S(1)} %get-tuple-element.22.right_ref, bf16[256,256]{1,0:T(8,128)(2,1)S(1)} %collective-permute-done.1.far_ref), custom_call_target="tpu_custom_call" | custom-call | flops 4000000000 | bytes 1 | tf_op jit(solution)/shard_map/pallas_call | solution.py:309
  11.6 1.2 %collective-permute-done.2.refs_7_ = bf16[256,256]{1,0:T(8,128)(2,1)S(1)} collective-permute-done((bf16[256,256]{1,0:T(8,128)(2,1)S(1)}, bf16[256,256]{1,0:T(8,128)(2,1)S(1)}, u32[]{:S(2)}, u32[]{:S(2)}) %collective-permute-start.2) | collective-permute-done | bytes 131104 | tf_op jit(solution)/shard_map/ppermute | solution.py:39
  12.8 1.7 %shard_map.63 = (f32[1,256,256]{2,1,0:T(8,128)S(1)}, bf16[256,256]{1,0:T(8,128)(2,1)S(1)}, bf16[256,256]{1,0:T(8,128)(2,1)S(1)}, f32[8,128]{1,0:T(8,128)S(1)}, f32[16,1,128]{2,1,0:T(1,128)}) custom-call(f32[2,256,256]{2,1,0:T(8,128)S(1)} %get-tuple-element.20.refs_0_.near_part_ref, f32[256,256]{1,0:T(8,128)S(1)} %shard_map.62.refs_1_.far_part_ref, ...), custom_call_target="tpu_custom_call" | custom-call | flops 1 | bytes 1 | tf_op jit(solution)/shard_map/pallas_call | solution.py:314
  14.5 0.1 collective-permute-start.3
  14.6 0.1 collective-permute-start.4
  14.6 1.3 %collective-permute-done.3.near_w.refs_2_ = bf16[256,256]{1,0:T(8,128)(2,1)S(1)} collective-permute-done((bf16[256,256]{1,0:T(8,128)(2,1)S(1)}, bf16[256,256]{1,0:T(8,128)(2,1)S(1)}, u32[]{:S(2)}, u32[]{:S(2)}) %collective-permute-start.3) | collective-permute-done | bytes 131104 | tf_op jit(solution)/shard_map/ppermute | solution.py:39
  15.9 1.7 %collective-permute-start.5 = (bf16[256,256]{1,0:T(8,128)(2,1)S(1)}, bf16[256,256]{1,0:T(8,128)(2,1)S(1)}, u32[]{:S(2)}, u32[]{:S(2)}) collective-permute-start(bf16[256,256]{1,0:T(8,128)(2,1)S(1)} %get-tuple-element.32), channel_id=1, source_target_pairs={{0,16},{1,2},{2,1},{3,4},{4,3},{5,6},{6,5},{7,23},{8,24},{9,10},{1... | collective-permute-start | bytes 393224 | tf_op jit(solution)/shard_map/ppermute | solution.py:60
  17.6 5.2 %all-to-all-start = ((f32[16,1,128]{2,1,0:T(1,128)}), f32[16,1,128]{2,1,0:T(1,128)S(1)}, u32[]{:S(2)}, u32[]{:S(2)}) async-start(f32[16,1,128]{2,1,0:T(1,128)} %get-tuple-element.31), calls=%async_computation | async-start | bytes 16384 | tf_op jit(solution)/shard_map/all_to_all | solution.py:327
  22.8 1.4 %collective-permute-done.4.refs_0_ = bf16[256,256]{1,0:T(8,128)(2,1)S(1)} collective-permute-done((bf16[256,256]{1,0:T(8,128)(2,1)S(1)}, bf16[256,256]{1,0:T(8,128)(2,1)S(1)}, u32[]{:S(2)}, u32[]{:S(2)}) %collective-permute-start.4) | collective-permute-done | bytes 131104 | tf_op jit(solution)/shard_map/ppermute | solution.py:39
  24.2 0.0 collective-permute-done.5.refs_1_
  24.2 3.6 %shard_map.65.hw_ref = f32[256,256]{1,0:T(8,128)S(1)} custom-call(bf16[256,256]{1,0:T(8,128)(2,1)S(1)} %collective-permute-done.4.refs_0_, bf16[256,256]{1,0:T(8,128)(2,1)S(1)} %collective-permute-done.5.refs_1_, bf16[256,256]{1,0:T(8,128)(2,1)S(1)} %collective-permute-done.3.near_w.refs_2_, bf16[256,256]{1,0:T(8,128)(2,1)S(1)} %get-tuple-element.29.w_ref.refs_3_, ...), custom_call_target="tpu_custom_call" | custom-call | flops 1 | bytes 1 | tf_op jit(solution)/shard_map/pallas_call | solution.py:328
  27.8 1.3 %all-to-all-done.stats_ref = f32[16,1,128]{2,1,0:T(1,128)S(1)} async-done(((f32[16,1,128]{2,1,0:T(1,128)}), f32[16,1,128]{2,1,0:T(1,128)S(1)}, u32[]{:S(2)}, u32[]{:S(2)}) %all-to-all-start) | async-done | bytes 8224 | tf_op jit(solution)/shard_map/all_to_all | solution.py:327
  29.1 1.2 %shard_map.66 = (f32[1,256,256]{2,1,0:T(8,128)}, f32[1,256,256]{2,1,0:T(8,128)}) custom-call(f32[8,128]{1,0:T(8,128)S(1)} %get-tuple-element.18.facts_ref.refs_2_, f32[16,1,128]{2,1,0:T(1,128)S(1)} %all-to-all-done.stats_ref, f32[256,256]{1,0:T(8,128)S(1)} %shard_map.65.hw_ref, f32[2,256,256]{2,1,0:T(8,128)S(1)} %get-tuple-element.20.refs_0_.near_part_ref, ...), custom_call_target="tpu_custom_call" | custom-call | flops 1 | bytes 1 | tf_op jit(solution)/shard_map/pallas_call | solution.py:332
  (2 shorter events, 0.0 us)
Async XLA Ops:
  1.6 4.2 %collective-permute-start = (bf16[256,256]{1,0:T(8,128)(2,1)S(1)}, bf16[256,256]{1,0:T(8,128)(2,1)S(1)}, u32[]{:S(2)}, u32[]{:S(2)}) collective-permute-start(bf16[256,256]{1,0:T(8,128)(2,1)S(1)} %get-tuple-element.19.self_ref.refs_4_), channel_id=1, source_target_pairs={{0,1},{1,0},{2,3},{3,2},{4,5},{5,4},{6,7},{7,6},{8,9},{9,8},{10,11... | collective-permute-start | bytes 393224 | tf_op jit(solution)/shard_map/ppermute | solution.py:39
  2.1 10.7 %collective-permute-start.2 = (bf16[256,256]{1,0:T(8,128)(2,1)S(1)}, bf16[256,256]{1,0:T(8,128)(2,1)S(1)}, u32[]{:S(2)}, u32[]{:S(2)}) collective-permute-start(bf16[256,256]{1,0:T(8,128)(2,1)S(1)} %get-tuple-element.19.self_ref.refs_4_), channel_id=1, source_target_pairs={{0,8},{1,9},{2,10},{3,11},{4,12},{5,13},{6,14},{7,15},{8,0},{9,1},... | collective-permute-start | bytes 393224 | tf_op jit(solution)/shard_map/ppermute | solution.py:39
  5.8 5.0 %collective-permute-start.1 = (bf16[256,256]{1,0:T(8,128)(2,1)S(1)}, bf16[256,256]{1,0:T(8,128)(2,1)S(1)}, u32[]{:S(2)}, u32[]{:S(2)}) collective-permute-start(bf16[256,256]{1,0:T(8,128)(2,1)S(1)} %shard_map.61), channel_id=1, source_target_pairs={{0,16},{1,2},{2,1},{3,4},{4,3},{5,6},{6,5},{7,23},{8,24},{9,10},{1... | collective-permute-start | bytes 393224 | tf_op jit(solution)/shard_map/ppermute | solution.py:60
  14.5 1.4 %collective-permute-start.3 = (bf16[256,256]{1,0:T(8,128)(2,1)S(1)}, bf16[256,256]{1,0:T(8,128)(2,1)S(1)}, u32[]{:S(2)}, u32[]{:S(2)}) collective-permute-start(bf16[256,256]{1,0:T(8,128)(2,1)S(1)} %get-tuple-element.29.w_ref.refs_3_), channel_id=1, source_target_pairs={{0,1},{1,0},{2,3},{3,2},{4,5},{5,4},{6,7},{7,6},{8,9},{9,8},{10,11... | collective-permute-start | bytes 393224 | tf_op jit(solution)/shard_map/ppermute | solution.py:39
  14.6 9.6 %collective-permute-start.4 = (bf16[256,256]{1,0:T(8,128)(2,1)S(1)}, bf16[256,256]{1,0:T(8,128)(2,1)S(1)}, u32[]{:S(2)}, u32[]{:S(2)}) collective-permute-start(bf16[256,256]{1,0:T(8,128)(2,1)S(1)} %get-tuple-element.29.w_ref.refs_3_), channel_id=1, source_target_pairs={{0,8},{1,9},{2,10},{3,11},{4,12},{5,13},{6,14},{7,15},{8,0},{9,1},... | collective-permute-start | bytes 393224 | tf_op jit(solution)/shard_map/ppermute | solution.py:39
  15.9 8.3 %collective-permute-start.5 = (bf16[256,256]{1,0:T(8,128)(2,1)S(1)}, bf16[256,256]{1,0:T(8,128)(2,1)S(1)}, u32[]{:S(2)}, u32[]{:S(2)}) collective-permute-start(bf16[256,256]{1,0:T(8,128)(2,1)S(1)} %get-tuple-element.32), channel_id=1, source_target_pairs={{0,16},{1,2},{2,1},{3,4},{4,3},{5,6},{6,5},{7,23},{8,24},{9,10},{1... | collective-permute-start | bytes 393224 | tf_op jit(solution)/shard_map/ppermute | solution.py:60
  17.6 11.5 %all-to-all-start = ((f32[16,1,128]{2,1,0:T(1,128)}), f32[16,1,128]{2,1,0:T(1,128)S(1)}, u32[]{:S(2)}, u32[]{:S(2)}) async-start(f32[16,1,128]{2,1,0:T(1,128)} %get-tuple-element.31), calls=%async_computation | async-start | bytes 16384 | tf_op jit(solution)/shard_map/all_to_all | solution.py:327

commit v10 on v8

--- a/solution.py
+++ b/solution.py
@@ -208,7 +208,7 @@
 
 def image_kernel(size, width, rows, *refs):
     row_refs, refs = refs[:rows], refs[rows:]
-    far_ref, near_ref, self_ref, left_row, right_row, left_hbm, right_hbm, out_ref, left_own, right_own, sems = refs
+    near_ref, far_ref, self_ref, left_row, right_row, left_hbm, right_hbm, out_ref, left_own, right_own, sems = refs
     _, _, there = place(size, width)
     own = fetch(left_hbm, right_hbm, left_own, right_own, sems, [(0, 2 + width), (2 + width, width)])
     image = None
@@ -297,7 +297,7 @@
     hw = call(
         functools.partial(image_kernel, size, width, rows), pltpu.VMEM(square, f32), [VM] * (5 + rows) + [HB] * 2, VM,
         [pltpu.VMEM(every, bf16)] * 2 + [dma((2, 2))],
-    )(*row_w, far_w, near_w, w, left_row, right_row, left_env, right_env)
+    )(*row_w, near_w, far_w, w, left_row, right_row, left_env, right_env)
     return call(
         functools.partial(second_kernel, size, width, rows, cells),
         (jax.ShapeDtypeStruct((1,) + square, f32),) * 2, [VM] * 6, (HB, HB),

time: 29.6 us -> 30 us (1.014)
  starting transfers between devices: 13.1 us -> 13.4 us
    all_to_all x1, starting transfers between devices: 5.51 us -> 6.09 us  [body(): stats = lax.all_to_all(stats, 'sector', 0, 0, tiled=True)]
    ppermute x4, waiting for transfers between devices: 2.79 us -> 2.46 us  [swap(): lax.ppermute(x, axis, [(s, to.get(s, s)) for s in range(lax.axis_size(axi...]
    all_to_all x1, waiting for transfers between devices: 1.2 us -> 1.53 us  [body(): stats = lax.all_to_all(stats, 'sector', 0, 0, tiled=True)]
where the time goes in v10:
time: 30 us; the launch traced here: 29.7 us
  starting transfers between devices  13.4 us (45%)
  Pallas kernels  11 us (37%)
  waiting for transfers between devices  4.64 us (15%)
  between operations  0.68 us (2%)
    all_to_all x1, starting transfers between devices, body(): stats = lax.all_to_all(stats, 'sector', 0, 0, tiled=True)  6.09 us
    ppermute x4, starting transfers between devices, swap(): lax.ppermute(x, axis, [(s, to.get(s, s)) for s in range(lax.axis_size(axi...  4.22 us
    pallas_call x1, Pallas kernels, body(): call(functools.partial(image_kernel, size, width, rows), pltpu.VMEM(squar...  3.57 us
    ppermute x2, starting transfers between devices, far_swap(): return lax.ppermute(x, ('groups', 'sector'), pairs)  3.07 us
    pallas_call x1, Pallas kernels, body(): call(functools.partial(near_kernel, size, width, rows), (pltpu.VMEM((2,)...  2.79 us
    ppermute x4, waiting for transfers between devices, swap(): lax.ppermute(x, axis, [(s, to.get(s, s)) for s in range(lax.axis_size(axi...  2.46 us
    pallas_call x1, Pallas kernels, body(): call(functools.partial(first_kernel, size, width, rows), (pltpu.VMEM((row...  1.66 us
    all_to_all x1, waiting for transfers between devices, body(): stats = lax.all_to_all(stats, 'sector', 0, 0, tiled=True)  1.53 us
  transfers between devices with their start and end apart: 7, of which 4 were waited for; matrix products, arithmetic and copies ran while one was open for 0% of the time, Pallas kernels for 24%

profile of v10, /device:TPU:0, one launch (start us, length us, event | category | flops | bytes accessed | tf_op | source)
XLA Modules:
  0.0 29.7 jit_solution(3656646783835500212)
XLA Ops:
  0.6 1.0 %shard_map.59 = (bf16[256,256]{1,0:T(8,128)(2,1)S(1)}, bf16[256,256]{1,0:T(8,128)(2,1)S(1)}, f32[8,128]{1,0:T(8,128)S(1)}) custom-call(f32[1,256,256]{2,1,0:T(8,128)} %wave_hbm.3, s32[1,2]{1,0:T(1,128)} %dims_hbm.1), custom_call_target="tpu_custom_call" | custom-call | flops 1 | bytes 1 | tf_op jit(solution)/shard_map/pallas_call | solution.py:266
  1.6 0.5 %collective-permute-start = (bf16[256,256]{1,0:T(8,128)(2,1)S(1)}, bf16[256,256]{1,0:T(8,128)(2,1)S(1)}, u32[]{:S(2)}, u32[]{:S(2)}) collective-permute-start(bf16[256,256]{1,0:T(8,128)(2,1)S(1)} %get-tuple-element.15.self_ref.refs_4_), channel_id=1, source_target_pairs={{0,1},{1,0},{2,3},{3,2},{4,5},{5,4},{6,7},{7,6},{8,9},{9,8},{10,11... | collective-permute-start | bytes 393224 | tf_op jit(solution)/shard_map/ppermute | solution.py:39
  2.1 3.7 %collective-permute-start.2 = (bf16[256,256]{1,0:T(8,128)(2,1)S(1)}, bf16[256,256]{1,0:T(8,128)(2,1)S(1)}, u32[]{:S(2)}, u32[]{:S(2)}) collective-permute-start(bf16[256,256]{1,0:T(8,128)(2,1)S(1)} %get-tuple-element.15.self_ref.refs_4_), channel_id=1, source_target_pairs={{0,8},{1,9},{2,10},{3,11},{4,12},{5,13},{6,14},{7,15},{8,0},{9,1},... | collective-permute-start | bytes 393224 | tf_op jit(solution)/shard_map/ppermute | solution.py:39
  5.8 0.0 collective-permute-done.near_ref.refs_1_
  5.8 1.5 %collective-permute-start.1 = (bf16[256,256]{1,0:T(8,128)(2,1)S(1)}, bf16[256,256]{1,0:T(8,128)(2,1)S(1)}, u32[]{:S(2)}, u32[]{:S(2)}) collective-permute-start(bf16[256,256]{1,0:T(8,128)(2,1)S(1)} %shard_map.61), channel_id=1, source_target_pairs={{0,16},{1,2},{2,1},{3,4},{4,3},{5,6},{6,5},{7,23},{8,24},{9,10},{1... | collective-permute-start | bytes 393224 | tf_op jit(solution)/shard_map/ppermute | solution.py:60
  7.3 2.8 %shard_map.60 = (f32[2,256,256]{2,1,0:T(8,128)S(1)}, f32[8,128]{1,0:T(8,128)S(1)}, bf16[6,256,256]{2,1,0:T(8,128)(2,1)S(1)}, bf16[6,256,256]{2,1,0:T(8,128)(2,1)...) custom-call(bf16[1,26,256,256]{3,2,1,0:T(8,128)(2,1)} %refs_6_.1, ...), custom_call_target="tpu_custom_call" | custom-call | flops 4000000000 | bytes 1 | tf_op jit(solution)/shard_map/pallas_call | solution.py:276
  10.1 0.6 %collective-permute-done.1.far_ref = bf16[256,256]{1,0:T(8,128)(2,1)S(1)} collective-permute-done((bf16[256,256]{1,0:T(8,128)(2,1)S(1)}, bf16[256,256]{1,0:T(8,128)(2,1)S(1)}, u32[]{:S(2)}, u32[]{:S(2)}) %collective-permute-start.1) | collective-permute-done | bytes 131104 | tf_op jit(solution)/shard_map/ppermute | solution.py:60
  10.8 0.8 %shard_map.62.refs_1_.far_part_ref = f32[256,256]{1,0:T(8,128)S(1)} custom-call(bf16[6,256,256]{2,1,0:T(8,128)(2,1)S(1)} %get-tuple-element.17.left_ref, bf16[6,256,256]{2,1,0:T(8,128)(2,1)S(1)} %get-tuple-element.18.right_ref, bf16[256,256]{1,0:T(8,128)(2,1)S(1)} %collective-permute-done.1.far_ref), custom_call_target="tpu_custom_call" | custom-call | flops 4000000000 | bytes 1 | tf_op jit(solution)/shard_map/pallas_call | solution.py:283
  11.6 1.2 %collective-permute-done.2.refs_7_ = bf16[256,256]{1,0:T(8,128)(2,1)S(1)} collective-permute-done((bf16[256,256]{1,0:T(8,128)(2,1)S(1)}, bf16[256,256]{1,0:T(8,128)(2,1)S(1)}, u32[]{:S(2)}, u32[]{:S(2)}) %collective-permute-start.2) | collective-permute-done | bytes 131104 | tf_op jit(solution)/shard_map/ppermute | solution.py:39
  12.8 1.7 %shard_map.63 = (f32[1,256,256]{2,1,0:T(8,128)S(1)}, bf16[256,256]{1,0:T(8,128)(2,1)S(1)}, f32[16,1,128]{2,1,0:T(1,128)}) custom-call(f32[2,256,256]{2,1,0:T(8,128)S(1)} %get-tuple-element.16.refs_0_.near_part_ref, f32[256,256]{1,0:T(8,128)S(1)} %shard_map.62.refs_1_.far_part_ref, f32[8,128]{1,0:T(8,128)S(1)} %get-tuple-element.14.facts_ref.refs_2_, ...), custom_call_target="tpu_custom_call" | custom-call | flops 1 | bytes 1 | tf_op jit(solution)/shard_map/pallas_call | solution.py:286
  14.5 0.0 collective-permute-start.3
  14.5 0.0 collective-permute-start.4
  14.5 1.6 %collective-permute-start.5 = (bf16[256,256]{1,0:T(8,128)(2,1)S(1)}, bf16[256,256]{1,0:T(8,128)(2,1)S(1)}, u32[]{:S(2)}, u32[]{:S(2)}) collective-permute-start(bf16[256,256]{1,0:T(8,128)(2,1)S(1)} %get-tuple-element.24.refs_3_), channel_id=1, source_target_pairs={{0,16},{1,2},{2,1},{3,4},{4,3},{5,6},{6,5},{7,23},{8,24},{9,10},{1... | collective-permute-start | bytes 393224 | tf_op jit(solution)/shard_map/ppermute | solution.py:60
  16.1 6.1 %all-to-all-start = ((f32[16,1,128]{2,1,0:T(1,128)}), f32[16,1,128]{2,1,0:T(1,128)S(1)}, u32[]{:S(2)}, u32[]{:S(2)}) async-start(f32[16,1,128]{2,1,0:T(1,128)} %get-tuple-element.23), calls=%async_computation | async-start | bytes 16384 | tf_op jit(solution)/shard_map/all_to_all | solution.py:296
  22.2 1.2 %collective-permute-done.3.refs_0_ = bf16[256,256]{1,0:T(8,128)(2,1)S(1)} collective-permute-done((bf16[256,256]{1,0:T(8,128)(2,1)S(1)}, bf16[256,256]{1,0:T(8,128)(2,1)S(1)}, u32[]{:S(2)}, u32[]{:S(2)}) %collective-permute-start.3) | collective-permute-done | bytes 131104 | tf_op jit(solution)/shard_map/ppermute | solution.py:39
  23.4 0.0 collective-permute-done.4.refs_1_
  23.4 0.0 collective-permute-done.5.refs_2_
  23.4 3.6 %shard_map.64.hw_ref = f32[256,256]{1,0:T(8,128)S(1)} custom-call(bf16[256,256]{1,0:T(8,128)(2,1)S(1)} %collective-permute-done.3.refs_0_, bf16[256,256]{1,0:T(8,128)(2,1)S(1)} %collective-permute-done.4.refs_1_, bf16[256,256]{1,0:T(8,128)(2,1)S(1)} %collective-permute-done.5.refs_2_, bf16[256,256]{1,0:T(8,128)(2,1)S(1)} %get-tuple-element.24.refs_3_, ...), custom_call_target="tpu_custom_call" | custom-call | flops 1 | bytes 1 | tf_op jit(solution)/shard_map/pallas_call | solution.py:297
  27.0 1.5 %all-to-all-done.stats_ref = f32[16,1,128]{2,1,0:T(1,128)S(1)} async-done(((f32[16,1,128]{2,1,0:T(1,128)}), f32[16,1,128]{2,1,0:T(1,128)S(1)}, u32[]{:S(2)}, u32[]{:S(2)}) %all-to-all-start) | async-done | bytes 8224 | tf_op jit(solution)/shard_map/all_to_all | solution.py:296
  28.5 1.2 %shard_map.65 = (f32[1,256,256]{2,1,0:T(8,128)}, f32[1,256,256]{2,1,0:T(8,128)}) custom-call(f32[8,128]{1,0:T(8,128)S(1)} %get-tuple-element.14.facts_ref.refs_2_, f32[16,1,128]{2,1,0:T(1,128)S(1)} %all-to-all-done.stats_ref, f32[256,256]{1,0:T(8,128)S(1)} %shard_map.64.hw_ref, f32[2,256,256]{2,1,0:T(8,128)S(1)} %get-tuple-element.16.refs_0_.near_part_ref, ...), custom_call_target="tpu_custom_call" | custom-call | flops 1 | bytes 1 | tf_op jit(solution)/shard_map/pallas_call | solution.py:301
  (1 shorter events, 0.0 us)
Async XLA Ops:
  1.6 4.2 %collective-permute-start = (bf16[256,256]{1,0:T(8,128)(2,1)S(1)}, bf16[256,256]{1,0:T(8,128)(2,1)S(1)}, u32[]{:S(2)}, u32[]{:S(2)}) collective-permute-start(bf16[256,256]{1,0:T(8,128)(2,1)S(1)} %get-tuple-element.15.self_ref.refs_4_), channel_id=1, source_target_pairs={{0,1},{1,0},{2,3},{3,2},{4,5},{5,4},{6,7},{7,6},{8,9},{9,8},{10,11... | collective-permute-start | bytes 393224 | tf_op jit(solution)/shard_map/ppermute | solution.py:39
  2.1 10.7 %collective-permute-start.2 = (bf16[256,256]{1,0:T(8,128)(2,1)S(1)}, bf16[256,256]{1,0:T(8,128)(2,1)S(1)}, u32[]{:S(2)}, u32[]{:S(2)}) collective-permute-start(bf16[256,256]{1,0:T(8,128)(2,1)S(1)} %get-tuple-element.15.self_ref.refs_4_), channel_id=1, source_target_pairs={{0,8},{1,9},{2,10},{3,11},{4,12},{5,13},{6,14},{7,15},{8,0},{9,1},... | collective-permute-start | bytes 393224 | tf_op jit(solution)/shard_map/ppermute | solution.py:39
  5.8 5.0 %collective-permute-start.1 = (bf16[256,256]{1,0:T(8,128)(2,1)S(1)}, bf16[256,256]{1,0:T(8,128)(2,1)S(1)}, u32[]{:S(2)}, u32[]{:S(2)}) collective-permute-start(bf16[256,256]{1,0:T(8,128)(2,1)S(1)} %shard_map.61), channel_id=1, source_target_pairs={{0,16},{1,2},{2,1},{3,4},{4,3},{5,6},{6,5},{7,23},{8,24},{9,10},{1... | collective-permute-start | bytes 393224 | tf_op jit(solution)/shard_map/ppermute | solution.py:60
  14.5 8.9 %collective-permute-start.3 = (bf16[256,256]{1,0:T(8,128)(2,1)S(1)}, bf16[256,256]{1,0:T(8,128)(2,1)S(1)}, u32[]{:S(2)}, u32[]{:S(2)}) collective-permute-start(bf16[256,256]{1,0:T(8,128)(2,1)S(1)} %get-tuple-element.24.refs_3_), channel_id=1, source_target_pairs={{0,8},{1,9},{2,10},{3,11},{4,12},{5,13},{6,14},{7,15},{8,0},{9,1},... | collective-permute-start | bytes 393224 | tf_op jit(solution)/shard_map/ppermute | solution.py:39
  14.5 8.9 %collective-permute-start.4 = (bf16[256,256]{1,0:T(8,128)(2,1)S(1)}, bf16[256,256]{1,0:T(8,128)(2,1)S(1)}, u32[]{:S(2)}, u32[]{:S(2)}) collective-permute-start(bf16[256,256]{1,0:T(8,128)(2,1)S(1)} %get-tuple-element.24.refs_3_), channel_id=1, source_target_pairs={{0,1},{1,0},{2,3},{3,2},{4,5},{5,4},{6,7},{7,6},{8,9},{9,8},{10,11... | collective-permute-start | bytes 393224 | tf_op jit(solution)/shard_map/ppermute | solution.py:39
  14.5 8.9 %collective-permute-start.5 = (bf16[256,256]{1,0:T(8,128)(2,1)S(1)}, bf16[256,256]{1,0:T(8,128)(2,1)S(1)}, u32[]{:S(2)}, u32[]{:S(2)}) collective-permute-start(bf16[256,256]{1,0:T(8,128)(2,1)S(1)} %get-tuple-element.24.refs_3_), channel_id=1, source_target_pairs={{0,16},{1,2},{2,1},{3,4},{4,3},{5,6},{6,5},{7,23},{8,24},{9,10},{1... | collective-permute-start | bytes 393224 | tf_op jit(solution)/shard_map/ppermute | solution.py:60
  16.1 12.4 %all-to-all-start = ((f32[16,1,128]{2,1,0:T(1,128)}), f32[16,1,128]{2,1,0:T(1,128)S(1)}, u32[]{:S(2)}, u32[]{:S(2)}) async-start(f32[16,1,128]{2,1,0:T(1,128)} %get-tuple-element.23), calls=%async_computation | async-start | bytes 16384 | tf_op jit(solution)/shard_map/all_to_all | solution.py:296

commit v11 on v8

--- a/solution.py
+++ b/solution.py
@@ -184,7 +184,7 @@
 
 def first_kernel(size, width, rows, *refs):
     near_part_ref, far_part_ref, facts_ref, sums_ref, u_ref, left_ref, right_ref = refs[:7]
-    row_refs, (out_ref, w_ref, stats_ref) = refs[7 : 7 + rows], refs[7 + rows :]
+    row_refs, (out_ref, w_ref, far_w_ref, line_ref) = refs[7 : 7 + rows], refs[7 + rows :]
     _, _, there = place(size, width)
     image = near_part_ref[0] + near_part_ref[1] + far_part_ref[...]
     for r, source in enumerate(row_refs):
@@ -197,13 +197,19 @@
     cross = total(u * image)
     rho = jnp.where(square > 0.0, cross / square, 0.0)
     w = image - rho * u
-    w_ref[...] = w.astype(jnp.bfloat16)
-    lane = lax.broadcasted_iota(jnp.int32, (1, 128), 1)
-    stats = jnp.zeros((1, 128), jnp.float32)
+    for ref in (w_ref, far_w_ref):
+        ref[...] = w.astype(jnp.bfloat16)
+    lane = lax.broadcasted_iota(jnp.int32, (1, 128), 1) - 8 * lax.rem(lax.axis_index("sector"), 2)
+    line = jnp.zeros((1, 128), jnp.float32)
     for n, value in enumerate((sums_ref[0:1, 0:1], square, cross, total(w * w), rho)):
-        stats = jnp.where(lane == n, value, stats)
-    for n in range(stats_ref.shape[0]):
-        stats_ref[n] = stats
+        line = jnp.where(lane == n, value, line)
+    line_ref[...] = jnp.broadcast_to(line, line_ref.shape)
+
+
+def merge_kernel(one_ref, other_ref, held_in, out_ref, held_out):
+    line = one_ref[0:1] + other_ref[0:1]
+    for n in range(out_ref.shape[0]):
+        out_ref[n] = line
 
 
 def image_kernel(size, width, rows, *refs):
@@ -230,7 +236,7 @@
     facts = facts_ref[...]
     stats = stats_ref[:, 0, :]
     sums = jnp.sum(stats, axis=0, keepdims=True)
-    start, square, cross, inner = (sums[:, i : i + 1] for i in range(4))
+    start, square, cross, inner = (sums[:, i : i + 1] + sums[:, i + 8 : i + 9] for i in range(4))
     scale = lax.rsqrt(start / cells + 1e-06) * (1.0 / SCALE)
     parts = [near_part_ref[0], near_part_ref[1], far_part_ref[...]] + [row_part_ref[r] for r in range(rows)]
     cell = live(facts, parts[0].shape)
@@ -238,12 +244,15 @@
     first_copy = pltpu.make_async_copy(first_ref, first_hbm.at[0], sems.at[0])
     first_copy.start()
     rho = cross / square
-    gap = stats[:, 4:5] - rho
-    residual = inner + jnp.sum(stats[:, 1:2] * gap * gap, axis=0, keepdims=True)
+    gaps = [stats[:, 8 * core + 4 : 8 * core + 5] - rho for core in range(2)]
+    spread = [stats[:, 8 * core + 1 : 8 * core + 2] * gap * gap for core, gap in enumerate(gaps)]
+    residual = inner + jnp.sum(spread[0] + spread[1], axis=0, keepdims=True)
     second_scale = scale * lax.rsqrt(scale * scale * (residual / cells) + 1e-06)
     image = hw_ref[...]
     for n, part in enumerate(parts):
-        image = image + (stats_ref[partners[n], :, 4:5] - rho) * part
+        chip, core = lax.div(partners[n], 2), lax.rem(partners[n], 2)
+        line = stats_ref[chip]
+        image = image + (jnp.where(core == 0, line[:, 4:5], line[:, 12:13]) - rho) * part
     second_ref[...] = jnp.where(cell, image, 0.0) * second_scale
     second_copy = pltpu.make_async_copy(second_ref, second_hbm.at[0], sems.at[1])
     second_copy.start()
@@ -283,17 +292,23 @@
     far_part = vmem(call(
         functools.partial(far_kernel, size, width), pltpu.VMEM(square, f32), [VM] * 3, VM, cost=LONG,
     )(vmem(left_far), vmem(right_far), far_u))
-    row_part, w, stats = call(
+    row_part, w, far_w, line = call(
         functools.partial(first_kernel, size, width, rows),
-        (pltpu.VMEM((rows,) + square, f32),) + (pltpu.VMEM(square, bf16), jax.ShapeDtypeStruct((size, 1, 128), f32)),
-        [VM] * (7 + rows), (VM,) * 3,
+        (pltpu.VMEM((rows,) + square, f32),) + (pltpu.VMEM(square, bf16),) * 2 + (pltpu.VMEM((8, 128), f32),),
+        [VM] * (7 + rows), (VM,) * 4,
     )(near_part, far_part, facts, vmem(sums), u, left_row, right_row, *row_u)
 
     w = vmem(w)
     row_w = [vmem(swap(w, "sector", p)) for p in row_pairs]
     near_w = vmem(swap(w, "sector", near))
-    far_w = vmem(far_swap(w))
-    stats = lax.all_to_all(stats, "sector", 0, 0, tiled=True)
+    line = vmem(line)
+    stats, far_w = call(
+        merge_kernel, (jax.ShapeDtypeStruct((size // 2, 1, 128), f32), pltpu.VMEM(square, bf16)), [VM] * 2 + [AN], (VM, AN),
+        aliases={2: 1},
+    )(line, vmem(swap(line, "sector", near)), vmem(far_w))
+    far_w = vmem(far_swap(far_w))
+    chips = [list(range(core, size, 2)) for core in range(2)]
+    stats = lax.all_to_all(stats, "sector", 0, 0, tiled=True, axis_index_groups=chips)
     hw = call(
         functools.partial(image_kernel, size, width, rows), pltpu.VMEM(square, f32), [VM] * (5 + rows) + [HB] * 2, VM,
         [pltpu.VMEM(every, bf16)] * 2 + [dma((2, 2))],

time: 29.6 us -> 30 us (1.014)
  waiting for transfers between devices: 4.64 us -> 5.35 us
  starting transfers between devices: 13.1 us -> 12.7 us
    all_to_all x1, starting transfers between devices: 5.51 us -> 4.89 us  [body(): lax.all_to_all(stats, 'sector', 0, 0, tiled=True, axis_index_groups=chips)]
    pallas_call x1, Pallas kernels: 1.66 us -> 1.05 us  [body(): call(functools.partial(first_kernel, size, width, rows), (pltpu.VMEM((row...]
    pallas_call x0 -> x1, Pallas kernels: none -> 0.6 us  [body(): call(merge_kernel, (jax.ShapeDtypeStruct((size // 2, 1, 128), f32), pltpu...]
    ppermute x4 -> x5, waiting for transfers between devices: 2.79 us -> 3.28 us  [swap(): lax.ppermute(x, axis, [(s, to.get(s, s)) for s in range(lax.axis_size(axi...]
    ppermute x4 -> x5, starting transfers between devices: 4.48 us -> 4.7 us  [swap(): lax.ppermute(x, axis, [(s, to.get(s, s)) for s in range(lax.axis_size(axi...]
  transfers between devices with their start and end apart: 7 -> 8, of which waited for: 4 -> 5; matrix products, arithmetic and copies ran while one was open for 0% -> 0% of each run, Pallas kernels for 24% -> 26%
where the time goes in v11:
time: 30 us; the launch traced here: 29.7 us
  starting transfers between devices  12.7 us (42%)
  Pallas kernels  11 us (37%)
  waiting for transfers between devices  5.35 us (18%)
  between operations  0.68 us (2%)
    all_to_all x1, starting transfers between devices, body(): lax.all_to_all(stats, 'sector', 0, 0, tiled=True, axis_index_groups=chips)  4.89 us
    ppermute x5, starting transfers between devices, swap(): lax.ppermute(x, axis, [(s, to.get(s, s)) for s in range(lax.axis_size(axi...  4.7 us
    pallas_call x1, Pallas kernels, body(): call(functools.partial(image_kernel, size, width, rows), pltpu.VMEM(squar...  3.57 us
    ppermute x5, waiting for transfers between devices, swap(): lax.ppermute(x, axis, [(s, to.get(s, s)) for s in range(lax.axis_size(axi...  3.28 us
    ppermute x2, starting transfers between devices, far_swap(): return lax.ppermute(x, ('groups', 'sector'), pairs)  3.11 us
    pallas_call x1, Pallas kernels, body(): call(functools.partial(near_kernel, size, width, rows), (pltpu.VMEM((2,)...  2.79 us
    all_to_all x1, waiting for transfers between devices, body(): lax.all_to_all(stats, 'sector', 0, 0, tiled=True, axis_index_groups=chips)  1.42 us
    pallas_call x1, Pallas kernels, body(): call(functools.partial(second_kernel, size, width, rows, cells), (jax.Sha...  1.23 us
  transfers between devices with their start and end apart: 8, of which 5 were waited for; matrix products, arithmetic and copies ran while one was open for 0% of the time, Pallas kernels for 26%

profile of v11, /device:TPU:0, one launch (start us, length us, event | category | flops | bytes accessed | tf_op | source)
XLA Modules:
  0.0 29.7 jit_solution(949335995160804067)
XLA Ops:
  0.6 1.0 %shard_map.59 = (bf16[256,256]{1,0:T(8,128)(2,1)S(1)}, bf16[256,256]{1,0:T(8,128)(2,1)S(1)}, f32[8,128]{1,0:T(8,128)S(1)}) custom-call(f32[1,256,256]{2,1,0:T(8,128)} %wave_hbm.3, s32[1,2]{1,0:T(1,128)} %dims_hbm.1), custom_call_target="tpu_custom_call" | custom-call | flops 1 | bytes 1 | tf_op jit(solution)/shard_map/pallas_call | solution.py:275
  1.6 0.5 %collective-permute-start = (bf16[256,256]{1,0:T(8,128)(2,1)S(1)}, bf16[256,256]{1,0:T(8,128)(2,1)S(1)}, u32[]{:S(2)}, u32[]{:S(2)}) collective-permute-start(bf16[256,256]{1,0:T(8,128)(2,1)S(1)} %get-tuple-element.18.self_ref.refs_4_), channel_id=1, source_target_pairs={{0,1},{1,0},{2,3},{3,2},{4,5},{5,4},{6,7},{7,6},{8,9},{9,8},{10,11... | collective-permute-start | bytes 393224 | tf_op jit(solution)/shard_map/ppermute | solution.py:39
  2.1 3.7 %collective-permute-start.2 = (bf16[256,256]{1,0:T(8,128)(2,1)S(1)}, bf16[256,256]{1,0:T(8,128)(2,1)S(1)}, u32[]{:S(2)}, u32[]{:S(2)}) collective-permute-start(bf16[256,256]{1,0:T(8,128)(2,1)S(1)} %get-tuple-element.18.self_ref.refs_4_), channel_id=1, source_target_pairs={{0,8},{1,9},{2,10},{3,11},{4,12},{5,13},{6,14},{7,15},{8,0},{9,1},... | collective-permute-start | bytes 393224 | tf_op jit(solution)/shard_map/ppermute | solution.py:39
  5.8 0.0 collective-permute-done.near_ref.refs_1_
  5.8 1.5 %collective-permute-start.1 = (bf16[256,256]{1,0:T(8,128)(2,1)S(1)}, bf16[256,256]{1,0:T(8,128)(2,1)S(1)}, u32[]{:S(2)}, u32[]{:S(2)}) collective-permute-start(bf16[256,256]{1,0:T(8,128)(2,1)S(1)} %shard_map.61), channel_id=1, source_target_pairs={{0,16},{1,2},{2,1},{3,4},{4,3},{5,6},{6,5},{7,23},{8,24},{9,10},{1... | collective-permute-start | bytes 393224 | tf_op jit(solution)/shard_map/ppermute | solution.py:60
  7.3 2.8 %shard_map.60 = (f32[2,256,256]{2,1,0:T(8,128)S(1)}, f32[8,128]{1,0:T(8,128)S(1)}, bf16[6,256,256]{2,1,0:T(8,128)(2,1)S(1)}, bf16[6,256,256]{2,1,0:T(8,128)(2,1)...) custom-call(bf16[1,26,256,256]{3,2,1,0:T(8,128)(2,1)} %refs_6_.1, ...), custom_call_target="tpu_custom_call" | custom-call | flops 4000000000 | bytes 1 | tf_op jit(solution)/shard_map/pallas_call | solution.py:285
  10.1 0.6 %collective-permute-done.1.far_ref = bf16[256,256]{1,0:T(8,128)(2,1)S(1)} collective-permute-done((bf16[256,256]{1,0:T(8,128)(2,1)S(1)}, bf16[256,256]{1,0:T(8,128)(2,1)S(1)}, u32[]{:S(2)}, u32[]{:S(2)}) %collective-permute-start.1) | collective-permute-done | bytes 131104 | tf_op jit(solution)/shard_map/ppermute | solution.py:60
  10.8 0.8 %shard_map.62.refs_1_.far_part_ref = f32[256,256]{1,0:T(8,128)S(1)} custom-call(bf16[6,256,256]{2,1,0:T(8,128)(2,1)S(1)} %get-tuple-element.20.left_ref, bf16[6,256,256]{2,1,0:T(8,128)(2,1)S(1)} %get-tuple-element.21.right_ref, bf16[256,256]{1,0:T(8,128)(2,1)S(1)} %collective-permute-done.1.far_ref), custom_call_target="tpu_custom_call" | custom-call | flops 4000000000 | bytes 1 | tf_op jit(solution)/shard_map/pallas_call | solution.py:292
  11.6 1.2 %collective-permute-done.2.refs_7_ = bf16[256,256]{1,0:T(8,128)(2,1)S(1)} collective-permute-done((bf16[256,256]{1,0:T(8,128)(2,1)S(1)}, bf16[256,256]{1,0:T(8,128)(2,1)S(1)}, u32[]{:S(2)}, u32[]{:S(2)}) %collective-permute-start.2) | collective-permute-done | bytes 131104 | tf_op jit(solution)/shard_map/ppermute | solution.py:39
  12.8 1.1 %shard_map.63 = (f32[1,256,256]{2,1,0:T(8,128)S(1)}, bf16[256,256]{1,0:T(8,128)(2,1)S(1)}, bf16[256,256]{1,0:T(8,128)(2,1)S(1)}, f32[8,128]{1,0:T(8,128)S(1)}) custom-call(f32[2,256,256]{2,1,0:T(8,128)S(1)} %get-tuple-element.19.refs_0_.near_part_ref, f32[256,256]{1,0:T(8,128)S(1)} %shard_map.62.refs_1_.far_part_ref, ...), custom_call_target="tpu_custom_call" | custom-call | flops 1 | bytes 1 | tf_op jit(solution)/shard_map/pallas_call | solution.py:295
  13.9 0.0 collective-permute-start.3
  13.9 0.1 collective-permute-start.4
  14.0 0.4 %collective-permute-start.6 = (bf16[256,256]{1,0:T(8,128)(2,1)S(1)}, bf16[256,256]{1,0:T(8,128)(2,1)S(1)}, u32[]{:S(2)}, u32[]{:S(2)}) collective-permute-start(bf16[256,256]{1,0:T(8,128)(2,1)S(1)} %get-tuple-element.29.refs_3_), channel_id=1, source_target_pairs={{0,1},{1,0},{2,3},{3,2},{4,5},{5,4},{6,7},{7,6},{8,9},{9,8},{10,11... | collective-permute-start | bytes 393224 | tf_op jit(solution)/shard_map/ppermute | solution.py:39
  14.4 0.7 %collective-permute-done.3.other_ref = f32[8,128]{1,0:T(8,128)S(1)} collective-permute-done((f32[8,128]{1,0:T(8,128)S(1)}, f32[8,128]{1,0:T(8,128)S(1)}, u32[]{:S(2)}, u32[]{:S(2)}) %collective-permute-start.3) | collective-permute-done | bytes 4128 | tf_op jit(solution)/shard_map/ppermute | solution.py:39
  15.0 0.6 %shard_map.64 = (f32[8,1,128]{2,1,0:T(1,128)}, bf16[256,256]{1,0:T(8,128)(2,1)S(1)}) custom-call(f32[8,128]{1,0:T(8,128)S(1)} %get-tuple-element.26.one_ref, f32[8,128]{1,0:T(8,128)S(1)} %collective-permute-done.3.other_ref, bf16[256,256]{1,0:T(8,128)(2,1)S(1)} %get-tuple-element.27.held_in), custom_call_target="tpu_custom_call", output_to_operand_aliasing={{1}: (2, {})} | custom-call | flops 1 | bytes 1 | tf_op jit(solution)/shard_map/pallas_call | solution.py:305
  15.6 1.6 %collective-permute-start.5 = (bf16[256,256]{1,0:T(8,128)(2,1)S(1)}, bf16[256,256]{1,0:T(8,128)(2,1)S(1)}, u32[]{:S(2)}, u32[]{:S(2)}) collective-permute-start(bf16[256,256]{1,0:T(8,128)(2,1)S(1)} %get-tuple-element.30), channel_id=1, source_target_pairs={{0,16},{1,2},{2,1},{3,4},{4,3},{5,6},{6,5},{7,23},{8,24},{9,10},{1... | collective-permute-start | bytes 393224 | tf_op jit(solution)/shard_map/ppermute | solution.py:60
  17.2 4.9 %all-to-all-start = ((f32[8,1,128]{2,1,0:T(1,128)}), f32[8,1,128]{2,1,0:T(1,128)S(1)}, u32[]{:S(2)}, u32[]{:S(2)}) async-start(f32[8,1,128]{2,1,0:T(1,128)} %get-tuple-element.28), calls=%async_computation | async-start | bytes 8192 | tf_op jit(solution)/shard_map/all_to_all | solution.py:311
  22.1 1.4 %collective-permute-done.4.refs_0_ = bf16[256,256]{1,0:T(8,128)(2,1)S(1)} collective-permute-done((bf16[256,256]{1,0:T(8,128)(2,1)S(1)}, bf16[256,256]{1,0:T(8,128)(2,1)S(1)}, u32[]{:S(2)}, u32[]{:S(2)}) %collective-permute-start.4) | collective-permute-done | bytes 131104 | tf_op jit(solution)/shard_map/ppermute | solution.py:39
  23.5 0.0 collective-permute-done.6.refs_2_
  23.5 0.0 collective-permute-done.5.refs_1_
  23.5 3.6 %shard_map.65.hw_ref = f32[256,256]{1,0:T(8,128)S(1)} custom-call(bf16[256,256]{1,0:T(8,128)(2,1)S(1)} %collective-permute-done.4.refs_0_, bf16[256,256]{1,0:T(8,128)(2,1)S(1)} %collective-permute-done.5.refs_1_, bf16[256,256]{1,0:T(8,128)(2,1)S(1)} %collective-permute-done.6.refs_2_, bf16[256,256]{1,0:T(8,128)(2,1)S(1)} %get-tuple-element.29.refs_3_, ...), custom_call_target="tpu_custom_call" | custom-call | flops 1 | bytes 1 | tf_op jit(solution)/shard_map/pallas_call | solution.py:312
  27.1 1.4 %all-to-all-done.stats_ref = f32[8,1,128]{2,1,0:T(1,128)S(1)} async-done(((f32[8,1,128]{2,1,0:T(1,128)}), f32[8,1,128]{2,1,0:T(1,128)S(1)}, u32[]{:S(2)}, u32[]{:S(2)}) %all-to-all-start) | async-done | bytes 4128 | tf_op jit(solution)/shard_map/all_to_all | solution.py:311
  28.5 1.2 %shard_map.66 = (f32[1,256,256]{2,1,0:T(8,128)}, f32[1,256,256]{2,1,0:T(8,128)}) custom-call(f32[8,128]{1,0:T(8,128)S(1)} %get-tuple-element.17.facts_ref.refs_2_, f32[8,1,128]{2,1,0:T(1,128)S(1)} %all-to-all-done.stats_ref, f32[256,256]{1,0:T(8,128)S(1)} %shard_map.65.hw_ref, f32[2,256,256]{2,1,0:T(8,128)S(1)} %get-tuple-element.19.refs_0_.near_part_ref, ...), custom_call_target="tpu_custom_call" | custom-call | flops 1 | bytes 1 | tf_op jit(solution)/shard_map/pallas_call | solution.py:316
  (1 shorter events, 0.0 us)
Async XLA Ops:
  1.6 4.2 %collective-permute-start = (bf16[256,256]{1,0:T(8,128)(2,1)S(1)}, bf16[256,256]{1,0:T(8,128)(2,1)S(1)}, u32[]{:S(2)}, u32[]{:S(2)}) collective-permute-start(bf16[256,256]{1,0:T(8,128)(2,1)S(1)} %get-tuple-element.18.self_ref.refs_4_), channel_id=1, source_target_pairs={{0,1},{1,0},{2,3},{3,2},{4,5},{5,4},{6,7},{7,6},{8,9},{9,8},{10,11... | collective-permute-start | bytes 393224 | tf_op jit(solution)/shard_map/ppermute | solution.py:39
  2.1 10.7 %collective-permute-start.2 = (bf16[256,256]{1,0:T(8,128)(2,1)S(1)}, bf16[256,256]{1,0:T(8,128)(2,1)S(1)}, u32[]{:S(2)}, u32[]{:S(2)}) collective-permute-start(bf16[256,256]{1,0:T(8,128)(2,1)S(1)} %get-tuple-element.18.self_ref.refs_4_), channel_id=1, source_target_pairs={{0,8},{1,9},{2,10},{3,11},{4,12},{5,13},{6,14},{7,15},{8,0},{9,1},... | collective-permute-start | bytes 393224 | tf_op jit(solution)/shard_map/ppermute | solution.py:39
  5.8 5.0 %collective-permute-start.1 = (bf16[256,256]{1,0:T(8,128)(2,1)S(1)}, bf16[256,256]{1,0:T(8,128)(2,1)S(1)}, u32[]{:S(2)}, u32[]{:S(2)}) collective-permute-start(bf16[256,256]{1,0:T(8,128)(2,1)S(1)} %shard_map.61), channel_id=1, source_target_pairs={{0,16},{1,2},{2,1},{3,4},{4,3},{5,6},{6,5},{7,23},{8,24},{9,10},{1... | collective-permute-start | bytes 393224 | tf_op jit(solution)/shard_map/ppermute | solution.py:60
  13.9 1.2 %collective-permute-start.3 = (f32[8,128]{1,0:T(8,128)S(1)}, f32[8,128]{1,0:T(8,128)S(1)}, u32[]{:S(2)}, u32[]{:S(2)}) collective-permute-start(f32[8,128]{1,0:T(8,128)S(1)} %get-tuple-element.26.one_ref), channel_id=1, source_target_pairs={{0,1},{1,0},{2,3},{3,2},{4,5},{5,4},{6,7},{7,6},{8,9},{9,8},{10,11... | collective-permute-start | bytes 12296 | tf_op jit(solution)/shard_map/ppermute | solution.py:39
  13.9 9.6 %collective-permute-start.4 = (bf16[256,256]{1,0:T(8,128)(2,1)S(1)}, bf16[256,256]{1,0:T(8,128)(2,1)S(1)}, u32[]{:S(2)}, u32[]{:S(2)}) collective-permute-start(bf16[256,256]{1,0:T(8,128)(2,1)S(1)} %get-tuple-element.29.refs_3_), channel_id=1, source_target_pairs={{0,8},{1,9},{2,10},{3,11},{4,12},{5,13},{6,14},{7,15},{8,0},{9,1},... | collective-permute-start | bytes 393224 | tf_op jit(solution)/shard_map/ppermute | solution.py:39
  14.0 9.5 %collective-permute-start.6 = (bf16[256,256]{1,0:T(8,128)(2,1)S(1)}, bf16[256,256]{1,0:T(8,128)(2,1)S(1)}, u32[]{:S(2)}, u32[]{:S(2)}) collective-permute-start(bf16[256,256]{1,0:T(8,128)(2,1)S(1)} %get-tuple-element.29.refs_3_), channel_id=1, source_target_pairs={{0,1},{1,0},{2,3},{3,2},{4,5},{5,4},{6,7},{7,6},{8,9},{9,8},{10,11... | collective-permute-start | bytes 393224 | tf_op jit(solution)/shard_map/ppermute | solution.py:39
  15.6 7.9 %collective-permute-start.5 = (bf16[256,256]{1,0:T(8,128)(2,1)S(1)}, bf16[256,256]{1,0:T(8,128)(2,1)S(1)}, u32[]{:S(2)}, u32[]{:S(2)}) collective-permute-start(bf16[256,256]{1,0:T(8,128)(2,1)S(1)} %get-tuple-element.30), channel_id=1, source_target_pairs={{0,16},{1,2},{2,1},{3,4},{4,3},{5,6},{6,5},{7,23},{8,24},{9,10},{1... | collective-permute-start | bytes 393224 | tf_op jit(solution)/shard_map/ppermute | solution.py:60
  17.2 11.3 %all-to-all-start = ((f32[8,1,128]{2,1,0:T(1,128)}), f32[8,1,128]{2,1,0:T(1,128)S(1)}, u32[]{:S(2)}, u32[]{:S(2)}) async-start(f32[8,1,128]{2,1,0:T(1,128)} %get-tuple-element.28), calls=%async_computation | async-start | bytes 8192 | tf_op jit(solution)/shard_map/all_to_all | solution.py:311

commit v12 on v8

--- a/solution.py
+++ b/solution.py
@@ -10,6 +10,7 @@
 QD = 8
 SCALE = 1024.0
 QUARTERS = 4
+HALVES = 2
 NT = (((1,), (1,)), ((), ()))
 VM = pl.BlockSpec(memory_space=pltpu.VMEM)
 HB = pl.BlockSpec(memory_space=pltpu.HBM)
@@ -177,16 +178,18 @@
         finish(pair)
 
 
-def far_kernel(size, width, left_ref, right_ref, far_ref, out_ref):
+def far_kernel(size, width, left_ref, right_ref, near_part_ref, far_ref, out_ref, sum_ref):
     _, _, there = place(size, width)
-    out_ref[...] = terms(only(there[0], far_ref[...]), left_ref, right_ref, 0, width)
+    part = terms(only(there[0], far_ref[...]), left_ref, right_ref, 0, width)
+    out_ref[...] = part
+    sum_ref[...] = near_part_ref[0] + near_part_ref[1] + part
 
 
 def first_kernel(size, width, rows, *refs):
-    near_part_ref, far_part_ref, facts_ref, sums_ref, u_ref, left_ref, right_ref = refs[:7]
-    row_refs, (out_ref, w_ref, stats_ref) = refs[7 : 7 + rows], refs[7 + rows :]
+    part_ref, facts_ref, sums_ref, u_ref, left_ref, right_ref = refs[:6]
+    row_refs, (out_ref, w_ref, stats_ref) = refs[6 : 6 + rows], refs[6 + rows :]
     _, _, there = place(size, width)
-    image = near_part_ref[0] + near_part_ref[1] + far_part_ref[...]
+    image = part_ref[...]
     for r, source in enumerate(row_refs):
         piece = terms(only(there[1 + r], source[...]), left_ref, right_ref, r * width, width)
         out_ref[r] = piece
@@ -232,23 +235,30 @@
     sums = jnp.sum(stats, axis=0, keepdims=True)
     start, square, cross, inner = (sums[:, i : i + 1] for i in range(4))
     scale = lax.rsqrt(start / cells + 1e-06) * (1.0 / SCALE)
-    parts = [near_part_ref[0], near_part_ref[1], far_part_ref[...]] + [row_part_ref[r] for r in range(rows)]
-    cell = live(facts, parts[0].shape)
-    first_ref[...] = jnp.where(cell, sum(parts[1:], parts[0]), 0.0) * scale
-    first_copy = pltpu.make_async_copy(first_ref, first_hbm.at[0], sems.at[0])
-    first_copy.start()
     rho = cross / square
     gap = stats[:, 4:5] - rho
     residual = inner + jnp.sum(stats[:, 1:2] * gap * gap, axis=0, keepdims=True)
     second_scale = scale * lax.rsqrt(scale * scale * (residual / cells) + 1e-06)
-    image = hw_ref[...]
-    for n, part in enumerate(parts):
-        image = image + (stats_ref[partners[n], :, 4:5] - rho) * part
-    second_ref[...] = jnp.where(cell, image, 0.0) * second_scale
-    second_copy = pltpu.make_async_copy(second_ref, second_hbm.at[0], sems.at[1])
-    second_copy.start()
-    first_copy.wait()
-    second_copy.wait()
+    gaps = [stats_ref[partner, :, 4:5] - rho for partner in partners[: 3 + rows]]
+    block = hw_ref.shape[0]
+    step = block // HALVES
+    col_ok = lax.broadcasted_iota(jnp.int32, (step, block), 1).astype(jnp.float32) < facts[2:3, 0:1]
+    row = lax.broadcasted_iota(jnp.int32, (step, block), 0).astype(jnp.float32)
+    copies = []
+    for n in range(HALVES):
+        lines = pl.ds(n * step, step)
+        parts = [near_part_ref[0, lines], near_part_ref[1, lines], far_part_ref[lines]]
+        parts += [row_part_ref[r, lines] for r in range(rows)]
+        cell = (row + n * step < facts[1:2, 0:1]) & col_ok
+        image = hw_ref[lines]
+        for gap, part in zip(gaps, parts):
+            image = image + gap * part
+        second_ref[lines] = jnp.where(cell, image, 0.0) * second_scale
+        first_ref[lines] = jnp.where(cell, sum(parts[1:], parts[0]), 0.0) * scale
+        for e, (source, target) in enumerate(((second_ref, second_hbm), (first_ref, first_hbm))):
+            copies.append(pltpu.make_async_copy(source.at[lines], target.at[0, lines], sems.at[n, e]))
+            copies[-1].start()
+    finish(copies)
 
 
 def body(wavefunction, sector_dims, left_env, right_env):
@@ -280,14 +290,15 @@
         [pltpu.VMEM(few, bf16)] * 2 + [pltpu.VMEM(square, f32), dma((2, 2)), dma((1, 2)), dma((rows, 2)), dma], LONG,
     )(left_env, right_env, hbm(wavefunction), facts, u, near_u)
     near_part, left_row, right_row = vmem(near_part), vmem(left_row), vmem(right_row)
-    far_part = vmem(call(
-        functools.partial(far_kernel, size, width), pltpu.VMEM(square, f32), [VM] * 3, VM, cost=LONG,
-    )(vmem(left_far), vmem(right_far), far_u))
+    far_part, part = call(
+        functools.partial(far_kernel, size, width), (pltpu.VMEM(square, f32),) * 2, [VM] * 4, (VM,) * 2, cost=LONG,
+    )(vmem(left_far), vmem(right_far), near_part, far_u)
+    far_part = vmem(far_part)
     row_part, w, stats = call(
         functools.partial(first_kernel, size, width, rows),
-        (pltpu.VMEM((rows,) + square, f32),) + (pltpu.VMEM(square, bf16), jax.ShapeDtypeStruct((size, 1, 128), f32)),
-        [VM] * (7 + rows), (VM,) * 3,
-    )(near_part, far_part, facts, vmem(sums), u, left_row, right_row, *row_u)
+        (pltpu.VMEM((rows,) + square, f32), pltpu.VMEM(square, bf16), jax.ShapeDtypeStruct((size, 1, 128), f32)),
+        [VM] * (6 + rows), (VM,) * 3,
+    )(vmem(part), facts, vmem(sums), u, left_row, right_row, *row_u)
 
     w = vmem(w)
     row_w = [vmem(swap(w, "sector", p)) for p in row_pairs]
@@ -301,7 +312,7 @@
     return call(
         functools.partial(second_kernel, size, width, rows, cells),
         (jax.ShapeDtypeStruct((1,) + square, f32),) * 2, [VM] * 6, (HB, HB),
-        [pltpu.VMEM(square, f32)] * 2 + [dma((2,))],
+        [pltpu.VMEM(square, f32)] * 2 + [dma((HALVES, 2))],
     )(facts, stats, vmem(hw), near_part, far_part, vmem(row_part))
 
 

time: 29.6 us -> 29.5 us (level)
  no operation moved by 1% of the time
where the time goes in v12:
time: 29.5 us; the launch traced here: 29.3 us
  starting transfers between devices  13.1 us (44%)
  Pallas kernels  10.9 us (37%)
  waiting for transfers between devices  4.63 us (16%)
  between operations  0.68 us (2%)
    all_to_all x1, starting transfers between devices, body(): stats = lax.all_to_all(stats, 'sector', 0, 0, tiled=True)  5.51 us
    ppermute x4, starting transfers between devices, swap(): lax.ppermute(x, axis, [(s, to.get(s, s)) for s in range(lax.axis_size(axi...  4.48 us
    pallas_call x1, Pallas kernels, body(): call(functools.partial(image_kernel, size, width, rows), pltpu.VMEM(squar...  3.58 us
    ppermute x2, starting transfers between devices, far_swap(): return lax.ppermute(x, ('groups', 'sector'), pairs)  3.07 us
    pallas_call x1, Pallas kernels, body(): call(functools.partial(near_kernel, size, width, rows), (pltpu.VMEM((2,)...  2.79 us
    ppermute x4, waiting for transfers between devices, swap(): lax.ppermute(x, axis, [(s, to.get(s, s)) for s in range(lax.axis_size(axi...  2.79 us
    pallas_call x1, Pallas kernels, body(): call(functools.partial(first_kernel, size, width, rows), (pltpu.VMEM((row...  1.66 us
    all_to_all x1, waiting for transfers between devices, body(): stats = lax.all_to_all(stats, 'sector', 0, 0, tiled=True)  1.2 us
  transfers between devices with their start and end apart: 7, of which 4 were waited for; matrix products, arithmetic and copies ran while one was open for 0% of the time, Pallas kernels for 24%

profile of v12, /device:TPU:0, one launch (start us, length us, event | category | flops | bytes accessed | tf_op | source)
XLA Modules:
  0.0 29.3 jit_solution(6507600025930670426)
XLA Ops:
  0.6 1.0 %shard_map.59 = (bf16[256,256]{1,0:T(8,128)(2,1)S(1)}, bf16[256,256]{1,0:T(8,128)(2,1)S(1)}, f32[8,128]{1,0:T(8,128)S(1)}) custom-call(f32[1,256,256]{2,1,0:T(8,128)} %wave_hbm.3, s32[1,2]{1,0:T(1,128)} %dims_hbm.1), custom_call_target="tpu_custom_call" | custom-call | flops 1 | bytes 1 | tf_op jit(solution)/shard_map/pallas_call | solution.py:276
  1.6 0.5 %collective-permute-start = (bf16[256,256]{1,0:T(8,128)(2,1)S(1)}, bf16[256,256]{1,0:T(8,128)(2,1)S(1)}, u32[]{:S(2)}, u32[]{:S(2)}) collective-permute-start(bf16[256,256]{1,0:T(8,128)(2,1)S(1)} %get-tuple-element.17.self_ref.refs_3_), channel_id=1, source_target_pairs={{0,1},{1,0},{2,3},{3,2},{4,5},{5,4},{6,7},{7,6},{8,9},{9,8},{10,11... | collective-permute-start | bytes 393224 | tf_op jit(solution)/shard_map/ppermute | solution.py:40
  2.1 3.7 %collective-permute-start.2 = (bf16[256,256]{1,0:T(8,128)(2,1)S(1)}, bf16[256,256]{1,0:T(8,128)(2,1)S(1)}, u32[]{:S(2)}, u32[]{:S(2)}) collective-permute-start(bf16[256,256]{1,0:T(8,128)(2,1)S(1)} %get-tuple-element.17.self_ref.refs_3_), channel_id=1, source_target_pairs={{0,8},{1,9},{2,10},{3,11},{4,12},{5,13},{6,14},{7,15},{8,0},{9,1},... | collective-permute-start | bytes 393224 | tf_op jit(solution)/shard_map/ppermute | solution.py:40
  5.8 0.0 collective-permute-done.near_ref.refs_1_
  5.8 1.5 %collective-permute-start.1 = (bf16[256,256]{1,0:T(8,128)(2,1)S(1)}, bf16[256,256]{1,0:T(8,128)(2,1)S(1)}, u32[]{:S(2)}, u32[]{:S(2)}) collective-permute-start(bf16[256,256]{1,0:T(8,128)(2,1)S(1)} %shard_map.61), channel_id=1, source_target_pairs={{0,16},{1,2},{2,1},{3,4},{4,3},{5,6},{6,5},{7,23},{8,24},{9,10},{1... | collective-permute-start | bytes 393224 | tf_op jit(solution)/shard_map/ppermute | solution.py:61
  7.3 2.8 %shard_map.60 = (f32[2,256,256]{2,1,0:T(8,128)S(1)}, f32[8,128]{1,0:T(8,128)S(1)}, bf16[6,256,256]{2,1,0:T(8,128)(2,1)S(1)}, bf16[6,256,256]{2,1,0:T(8,128)(2,1)...) custom-call(bf16[1,26,256,256]{3,2,1,0:T(8,128)(2,1)} %refs_6_.1, ...), custom_call_target="tpu_custom_call" | custom-call | flops 4000000000 | bytes 1 | tf_op jit(solution)/shard_map/pallas_call | solution.py:286
  10.1 0.6 %collective-permute-done.1.far_ref = bf16[256,256]{1,0:T(8,128)(2,1)S(1)} collective-permute-done((bf16[256,256]{1,0:T(8,128)(2,1)S(1)}, bf16[256,256]{1,0:T(8,128)(2,1)S(1)}, u32[]{:S(2)}, u32[]{:S(2)}) %collective-permute-start.1) | collective-permute-done | bytes 131104 | tf_op jit(solution)/shard_map/ppermute | solution.py:61
  10.8 0.8 %shard_map.62 = (f32[256,256]{1,0:T(8,128)S(1)}, f32[256,256]{1,0:T(8,128)S(1)}) custom-call(bf16[6,256,256]{2,1,0:T(8,128)(2,1)S(1)} %get-tuple-element.18.left_ref, bf16[6,256,256]{2,1,0:T(8,128)(2,1)S(1)} %get-tuple-element.19.right_ref, f32[2,256,256]{2,1,0:T(8,128)S(1)} %get-tuple-element.20.near_part_ref, ...), custom_call_target="tpu_custom_call" | custom-call | flops 4000000000 | bytes 1 | tf_op jit(solution)/shard_map/pallas_call | solution.py:293
  11.6 1.2 %collective-permute-done.2.refs_6_ = bf16[256,256]{1,0:T(8,128)(2,1)S(1)} collective-permute-done((bf16[256,256]{1,0:T(8,128)(2,1)S(1)}, bf16[256,256]{1,0:T(8,128)(2,1)S(1)}, u32[]{:S(2)}, u32[]{:S(2)}) %collective-permute-start.2) | collective-permute-done | bytes 131104 | tf_op jit(solution)/shard_map/ppermute | solution.py:40
  12.8 1.7 %shard_map.63 = (f32[1,256,256]{2,1,0:T(8,128)S(1)}, bf16[256,256]{1,0:T(8,128)(2,1)S(1)}, f32[16,1,128]{2,1,0:T(1,128)}) custom-call(f32[256,256]{1,0:T(8,128)S(1)} %get-tuple-element.22.refs_0_, f32[8,128]{1,0:T(8,128)S(1)} %get-tuple-element.16.facts_ref.refs_1_, f32[8,128]{1,0:T(8,128)S(1)} %get-tuple-element.23.refs_2_, ...), custom_call_target="tpu_custom_call" | custom-call | flops 1 | bytes 1 | tf_op jit(solution)/shard_map/pallas_call | solution.py:297
  14.5 0.0 collective-permute-start.3
  14.5 1.5 %collective-permute-start.4 = (bf16[256,256]{1,0:T(8,128)(2,1)S(1)}, bf16[256,256]{1,0:T(8,128)(2,1)S(1)}, u32[]{:S(2)}, u32[]{:S(2)}) collective-permute-start(bf16[256,256]{1,0:T(8,128)(2,1)S(1)} %get-tuple-element.27.refs_3_), channel_id=1, source_target_pairs={{0,16},{1,2},{2,1},{3,4},{4,3},{5,6},{6,5},{7,23},{8,24},{9,10},{1... | collective-permute-start | bytes 393224 | tf_op jit(solution)/shard_map/ppermute | solution.py:61
  16.1 0.3 collective-permute-start.5
  16.3 5.5 %all-to-all-start = ((f32[16,1,128]{2,1,0:T(1,128)}), f32[16,1,128]{2,1,0:T(1,128)S(1)}, u32[]{:S(2)}, u32[]{:S(2)}) async-start(f32[16,1,128]{2,1,0:T(1,128)} %get-tuple-element.26), calls=%async_computation | async-start | bytes 16384 | tf_op jit(solution)/shard_map/all_to_all | solution.py:307
  21.8 1.5 %collective-permute-done.3.refs_0_ = bf16[256,256]{1,0:T(8,128)(2,1)S(1)} collective-permute-done((bf16[256,256]{1,0:T(8,128)(2,1)S(1)}, bf16[256,256]{1,0:T(8,128)(2,1)S(1)}, u32[]{:S(2)}, u32[]{:S(2)}) %collective-permute-start.3) | collective-permute-done | bytes 131104 | tf_op jit(solution)/shard_map/ppermute | solution.py:40
  23.4 0.0 collective-permute-done.4.refs_1_
  23.4 0.0 collective-permute-done.5.refs_2_
  23.4 3.6 %shard_map.64.hw_ref = f32[256,256]{1,0:T(8,128)S(1)} custom-call(bf16[256,256]{1,0:T(8,128)(2,1)S(1)} %collective-permute-done.3.refs_0_, bf16[256,256]{1,0:T(8,128)(2,1)S(1)} %collective-permute-done.4.refs_1_, bf16[256,256]{1,0:T(8,128)(2,1)S(1)} %collective-permute-done.5.refs_2_, bf16[256,256]{1,0:T(8,128)(2,1)S(1)} %get-tuple-element.27.refs_3_, ...), custom_call_target="tpu_custom_call" | custom-call | flops 1 | bytes 1 | tf_op jit(solution)/shard_map/pallas_call | solution.py:308
  27.0 1.2 %all-to-all-done.stats_ref = f32[16,1,128]{2,1,0:T(1,128)S(1)} async-done(((f32[16,1,128]{2,1,0:T(1,128)}), f32[16,1,128]{2,1,0:T(1,128)S(1)}, u32[]{:S(2)}, u32[]{:S(2)}) %all-to-all-start) | async-done | bytes 8224 | tf_op jit(solution)/shard_map/all_to_all | solution.py:307
  28.2 1.1 %shard_map.65 = (f32[1,256,256]{2,1,0:T(8,128)}, f32[1,256,256]{2,1,0:T(8,128)}) custom-call(f32[8,128]{1,0:T(8,128)S(1)} %get-tuple-element.16.facts_ref.refs_1_, f32[16,1,128]{2,1,0:T(1,128)S(1)} %all-to-all-done.stats_ref, f32[256,256]{1,0:T(8,128)S(1)} %shard_map.64.hw_ref, f32[2,256,256]{2,1,0:T(8,128)S(1)} %get-tuple-element.20.near_part_ref, ...), custom_call_target="tpu_custom_call" | custom-call | flops 1 | bytes 1 | tf_op jit(solution)/shard_map/pallas_call | solution.py:312
  (1 shorter events, 0.0 us)
Async XLA Ops:
  1.6 4.2 %collective-permute-start = (bf16[256,256]{1,0:T(8,128)(2,1)S(1)}, bf16[256,256]{1,0:T(8,128)(2,1)S(1)}, u32[]{:S(2)}, u32[]{:S(2)}) collective-permute-start(bf16[256,256]{1,0:T(8,128)(2,1)S(1)} %get-tuple-element.17.self_ref.refs_3_), channel_id=1, source_target_pairs={{0,1},{1,0},{2,3},{3,2},{4,5},{5,4},{6,7},{7,6},{8,9},{9,8},{10,11... | collective-permute-start | bytes 393224 | tf_op jit(solution)/shard_map/ppermute | solution.py:40
  2.1 10.7 %collective-permute-start.2 = (bf16[256,256]{1,0:T(8,128)(2,1)S(1)}, bf16[256,256]{1,0:T(8,128)(2,1)S(1)}, u32[]{:S(2)}, u32[]{:S(2)}) collective-permute-start(bf16[256,256]{1,0:T(8,128)(2,1)S(1)} %get-tuple-element.17.self_ref.refs_3_), channel_id=1, source_target_pairs={{0,8},{1,9},{2,10},{3,11},{4,12},{5,13},{6,14},{7,15},{8,0},{9,1},... | collective-permute-start | bytes 393224 | tf_op jit(solution)/shard_map/ppermute | solution.py:40
  5.8 5.0 %collective-permute-start.1 = (bf16[256,256]{1,0:T(8,128)(2,1)S(1)}, bf16[256,256]{1,0:T(8,128)(2,1)S(1)}, u32[]{:S(2)}, u32[]{:S(2)}) collective-permute-start(bf16[256,256]{1,0:T(8,128)(2,1)S(1)} %shard_map.61), channel_id=1, source_target_pairs={{0,16},{1,2},{2,1},{3,4},{4,3},{5,6},{6,5},{7,23},{8,24},{9,10},{1... | collective-permute-start | bytes 393224 | tf_op jit(solution)/shard_map/ppermute | solution.py:61
  14.5 8.9 %collective-permute-start.3 = (bf16[256,256]{1,0:T(8,128)(2,1)S(1)}, bf16[256,256]{1,0:T(8,128)(2,1)S(1)}, u32[]{:S(2)}, u32[]{:S(2)}) collective-permute-start(bf16[256,256]{1,0:T(8,128)(2,1)S(1)} %get-tuple-element.27.refs_3_), channel_id=1, source_target_pairs={{0,8},{1,9},{2,10},{3,11},{4,12},{5,13},{6,14},{7,15},{8,0},{9,1},... | collective-permute-start | bytes 393224 | tf_op jit(solution)/shard_map/ppermute | solution.py:40
  14.5 8.9 %collective-permute-start.4 = (bf16[256,256]{1,0:T(8,128)(2,1)S(1)}, bf16[256,256]{1,0:T(8,128)(2,1)S(1)}, u32[]{:S(2)}, u32[]{:S(2)}) collective-permute-start(bf16[256,256]{1,0:T(8,128)(2,1)S(1)} %get-tuple-element.27.refs_3_), channel_id=1, source_target_pairs={{0,16},{1,2},{2,1},{3,4},{4,3},{5,6},{6,5},{7,23},{8,24},{9,10},{1... | collective-permute-start | bytes 393224 | tf_op jit(solution)/shard_map/ppermute | solution.py:61
  16.1 7.3 %collective-permute-start.5 = (bf16[256,256]{1,0:T(8,128)(2,1)S(1)}, bf16[256,256]{1,0:T(8,128)(2,1)S(1)}, u32[]{:S(2)}, u32[]{:S(2)}) collective-permute-start(bf16[256,256]{1,0:T(8,128)(2,1)S(1)} %get-tuple-element.27.refs_3_), channel_id=1, source_target_pairs={{0,1},{1,0},{2,3},{3,2},{4,5},{5,4},{6,7},{7,6},{8,9},{9,8},{10,11... | collective-permute-start | bytes 393224 | tf_op jit(solution)/shard_map/ppermute | solution.py:40
  16.3 11.8 %all-to-all-start = ((f32[16,1,128]{2,1,0:T(1,128)}), f32[16,1,128]{2,1,0:T(1,128)S(1)}, u32[]{:S(2)}, u32[]{:S(2)}) async-start(f32[16,1,128]{2,1,0:T(1,128)} %get-tuple-element.26), calls=%async_computation | async-start | bytes 16384 | tf_op jit(solution)/shard_map/all_to_all | solution.py:307

commit v13 on v12

--- a/solution.py
+++ b/solution.py
@@ -101,7 +101,7 @@
     return lax.dot_general(left, partial_t, NT, preferred_element_type=jnp.float32)
 
 
-def fetch(left_hbm, right_hbm, left_ref, right_ref, sems, spans):
+def fetch(left_hbm, right_hbm, left_ref, right_ref, sems, spans, start=True):
     copies = []
     at = 0
     for n, (offset, count) in enumerate(spans):
@@ -109,7 +109,7 @@
             pltpu.make_async_copy(source.at[0, pl.ds(offset, count)], target.at[pl.ds(at, count)], sems.at[n, e])
             for e, (source, target) in enumerate(((right_hbm, right_ref), (left_hbm, left_ref)))
         ]
-        for copy in pair:
+        for copy in pair if start else ():
             copy.start()
         copies.append(pair)
         at += count
@@ -213,15 +213,23 @@
     row_refs, refs = refs[:rows], refs[rows:]
     far_ref, near_ref, self_ref, left_row, right_row, left_hbm, right_hbm, out_ref, left_own, right_own, sems = refs
     _, _, there = place(size, width)
-    own = fetch(left_hbm, right_hbm, left_own, right_own, sems, [(0, 2 + width), (2 + width, width)])
+    own = fetch(left_hbm, right_hbm, left_own, right_own, sems, [(0, 2 + width), (2 + width, width)], False)
     image = None
     for r, source in enumerate(row_refs):
         piece = terms(only(there[1 + r], source[...]), left_row, right_row, r * width, width)
         image = piece if image is None else image + piece
+    out_ref[...] = image
+
+    @pl.when(lax.axis_index("sector") >= 0)
+    def _():
+        for pair in own:
+            for copy in pair:
+                copy.start()
+
     odd = lax.rem(lax.axis_index("sector"), 2) == 1
     near, far = near_ref[...], only(there[0], far_ref[...])
     finish(own[0])
-    image = image + terms(self_ref[...], left_own, right_own, 0, 2)
+    image = out_ref[...] + terms(self_ref[...], left_own, right_own, 0, 2)
     image = image + terms(jnp.where(odd, near, far), left_own, right_own, 2, width)
     finish(own[1])
     out_ref[...] = image + terms(jnp.where(odd, far, near), left_own, right_own, 2 + width, width)

time: 29.5 us -> 29.5 us (level)
  transfers between devices with their start and end apart: 7 -> 7, of which waited for: 4 -> 4; matrix products, arithmetic and copies ran while one was open for 0% -> 0% of each run, Pallas kernels for 24% -> 25%
where the time goes in v13:
time: 29.5 us; the launch traced here: 29.3 us
  starting transfers between devices  13.1 us (44%)
  Pallas kernels  11 us (37%)
  waiting for transfers between devices  4.6 us (16%)
  between operations  0.68 us (2%)
    all_to_all x1, starting transfers between devices, body(): stats = lax.all_to_all(stats, 'sector', 0, 0, tiled=True)  5.51 us
    ppermute x4, starting transfers between devices, swap(): lax.ppermute(x, axis, [(s, to.get(s, s)) for s in range(lax.axis_size(axi...  4.48 us
    pallas_call x1, Pallas kernels, body(): call(functools.partial(image_kernel, size, width, rows), pltpu.VMEM(squar...  3.6 us
    ppermute x2, starting transfers between devices, far_swap(): return lax.ppermute(x, ('groups', 'sector'), pairs)  3.07 us
    pallas_call x1, Pallas kernels, body(): call(functools.partial(near_kernel, size, width, rows), (pltpu.VMEM((2,)...  2.79 us
    ppermute x4, waiting for transfers between devices, swap(): lax.ppermute(x, axis, [(s, to.get(s, s)) for s in range(lax.axis_size(axi...  2.79 us
    pallas_call x1, Pallas kernels, body(): call(functools.partial(first_kernel, size, width, rows), (pltpu.VMEM((row...  1.66 us
    all_to_all x1, waiting for transfers between devices, body(): stats = lax.all_to_all(stats, 'sector', 0, 0, tiled=True)  1.17 us
  transfers between devices with their start and end apart: 7, of which 4 were waited for; matrix products, arithmetic and copies ran while one was open for 0% of the time, Pallas kernels for 25%

profile of v13, /device:TPU:0, one launch (start us, length us, event | category | flops | bytes accessed | tf_op | source)
XLA Modules:
  0.0 29.3 jit_solution(6384815161167703740)
XLA Ops:
  0.6 1.0 %shard_map.59 = (bf16[256,256]{1,0:T(8,128)(2,1)S(1)}, bf16[256,256]{1,0:T(8,128)(2,1)S(1)}, f32[8,128]{1,0:T(8,128)S(1)}) custom-call(f32[1,256,256]{2,1,0:T(8,128)} %wave_hbm.3, s32[1,2]{1,0:T(1,128)} %dims_hbm.1), custom_call_target="tpu_custom_call" | custom-call | flops 1 | bytes 1 | tf_op jit(solution)/shard_map/pallas_call | solution.py:284
  1.6 0.5 %collective-permute-start = (bf16[256,256]{1,0:T(8,128)(2,1)S(1)}, bf16[256,256]{1,0:T(8,128)(2,1)S(1)}, u32[]{:S(2)}, u32[]{:S(2)}) collective-permute-start(bf16[256,256]{1,0:T(8,128)(2,1)S(1)} %get-tuple-element.17.self_ref.refs_3_), channel_id=1, source_target_pairs={{0,1},{1,0},{2,3},{3,2},{4,5},{5,4},{6,7},{7,6},{8,9},{9,8},{10,11... | collective-permute-start | bytes 393224 | tf_op jit(solution)/shard_map/ppermute | solution.py:40
  2.1 3.7 %collective-permute-start.2 = (bf16[256,256]{1,0:T(8,128)(2,1)S(1)}, bf16[256,256]{1,0:T(8,128)(2,1)S(1)}, u32[]{:S(2)}, u32[]{:S(2)}) collective-permute-start(bf16[256,256]{1,0:T(8,128)(2,1)S(1)} %get-tuple-element.17.self_ref.refs_3_), channel_id=1, source_target_pairs={{0,8},{1,9},{2,10},{3,11},{4,12},{5,13},{6,14},{7,15},{8,0},{9,1},... | collective-permute-start | bytes 393224 | tf_op jit(solution)/shard_map/ppermute | solution.py:40
  5.8 0.0 collective-permute-done.near_ref.refs_1_
  5.8 1.5 %collective-permute-start.1 = (bf16[256,256]{1,0:T(8,128)(2,1)S(1)}, bf16[256,256]{1,0:T(8,128)(2,1)S(1)}, u32[]{:S(2)}, u32[]{:S(2)}) collective-permute-start(bf16[256,256]{1,0:T(8,128)(2,1)S(1)} %shard_map.61), channel_id=1, source_target_pairs={{0,16},{1,2},{2,1},{3,4},{4,3},{5,6},{6,5},{7,23},{8,24},{9,10},{1... | collective-permute-start | bytes 393224 | tf_op jit(solution)/shard_map/ppermute | solution.py:61
  7.3 2.8 %shard_map.60 = (f32[2,256,256]{2,1,0:T(8,128)S(1)}, f32[8,128]{1,0:T(8,128)S(1)}, bf16[6,256,256]{2,1,0:T(8,128)(2,1)S(1)}, bf16[6,256,256]{2,1,0:T(8,128)(2,1)...) custom-call(bf16[1,26,256,256]{3,2,1,0:T(8,128)(2,1)} %refs_6_.1, ...), custom_call_target="tpu_custom_call" | custom-call | flops 4000000000 | bytes 1 | tf_op jit(solution)/shard_map/pallas_call | solution.py:294
  10.1 0.6 %collective-permute-done.1.far_ref = bf16[256,256]{1,0:T(8,128)(2,1)S(1)} collective-permute-done((bf16[256,256]{1,0:T(8,128)(2,1)S(1)}, bf16[256,256]{1,0:T(8,128)(2,1)S(1)}, u32[]{:S(2)}, u32[]{:S(2)}) %collective-permute-start.1) | collective-permute-done | bytes 131104 | tf_op jit(solution)/shard_map/ppermute | solution.py:61
  10.8 0.8 %shard_map.62 = (f32[256,256]{1,0:T(8,128)S(1)}, f32[256,256]{1,0:T(8,128)S(1)}) custom-call(bf16[6,256,256]{2,1,0:T(8,128)(2,1)S(1)} %get-tuple-element.18.left_ref, bf16[6,256,256]{2,1,0:T(8,128)(2,1)S(1)} %get-tuple-element.19.right_ref, f32[2,256,256]{2,1,0:T(8,128)S(1)} %get-tuple-element.20.near_part_ref, ...), custom_call_target="tpu_custom_call" | custom-call | flops 4000000000 | bytes 1 | tf_op jit(solution)/shard_map/pallas_call | solution.py:301
  11.6 1.2 %collective-permute-done.2.refs_6_ = bf16[256,256]{1,0:T(8,128)(2,1)S(1)} collective-permute-done((bf16[256,256]{1,0:T(8,128)(2,1)S(1)}, bf16[256,256]{1,0:T(8,128)(2,1)S(1)}, u32[]{:S(2)}, u32[]{:S(2)}) %collective-permute-start.2) | collective-permute-done | bytes 131104 | tf_op jit(solution)/shard_map/ppermute | solution.py:40
  12.8 1.7 %shard_map.63 = (f32[1,256,256]{2,1,0:T(8,128)S(1)}, bf16[256,256]{1,0:T(8,128)(2,1)S(1)}, f32[16,1,128]{2,1,0:T(1,128)}) custom-call(f32[256,256]{1,0:T(8,128)S(1)} %get-tuple-element.22.refs_0_, f32[8,128]{1,0:T(8,128)S(1)} %get-tuple-element.16.facts_ref.refs_1_, f32[8,128]{1,0:T(8,128)S(1)} %get-tuple-element.23.refs_2_, ...), custom_call_target="tpu_custom_call" | custom-call | flops 1 | bytes 1 | tf_op jit(solution)/shard_map/pallas_call | solution.py:305
  14.5 0.0 collective-permute-start.3
  14.5 1.5 %collective-permute-start.4 = (bf16[256,256]{1,0:T(8,128)(2,1)S(1)}, bf16[256,256]{1,0:T(8,128)(2,1)S(1)}, u32[]{:S(2)}, u32[]{:S(2)}) collective-permute-start(bf16[256,256]{1,0:T(8,128)(2,1)S(1)} %get-tuple-element.27.refs_3_), channel_id=1, source_target_pairs={{0,16},{1,2},{2,1},{3,4},{4,3},{5,6},{6,5},{7,23},{8,24},{9,10},{1... | collective-permute-start | bytes 393224 | tf_op jit(solution)/shard_map/ppermute | solution.py:61
  16.1 0.3 collective-permute-start.5
  16.3 5.5 %all-to-all-start = ((f32[16,1,128]{2,1,0:T(1,128)}), f32[16,1,128]{2,1,0:T(1,128)S(1)}, u32[]{:S(2)}, u32[]{:S(2)}) async-start(f32[16,1,128]{2,1,0:T(1,128)} %get-tuple-element.26), calls=%async_computation | async-start | bytes 16384 | tf_op jit(solution)/shard_map/all_to_all | solution.py:315
  21.8 1.5 %collective-permute-done.3.refs_0_ = bf16[256,256]{1,0:T(8,128)(2,1)S(1)} collective-permute-done((bf16[256,256]{1,0:T(8,128)(2,1)S(1)}, bf16[256,256]{1,0:T(8,128)(2,1)S(1)}, u32[]{:S(2)}, u32[]{:S(2)}) %collective-permute-start.3) | collective-permute-done | bytes 131104 | tf_op jit(solution)/shard_map/ppermute | solution.py:40
  23.4 0.0 collective-permute-done.4.refs_1_
  23.4 0.0 collective-permute-done.5.refs_2_
  23.4 3.6 %shard_map.64.hw_ref = f32[256,256]{1,0:T(8,128)S(1)} custom-call(bf16[256,256]{1,0:T(8,128)(2,1)S(1)} %collective-permute-done.3.refs_0_, bf16[256,256]{1,0:T(8,128)(2,1)S(1)} %collective-permute-done.4.refs_1_, bf16[256,256]{1,0:T(8,128)(2,1)S(1)} %collective-permute-done.5.refs_2_, bf16[256,256]{1,0:T(8,128)(2,1)S(1)} %get-tuple-element.27.refs_3_, ...), custom_call_target="tpu_custom_call" | custom-call | flops 1 | bytes 1 | tf_op jit(solution)/shard_map/pallas_call | solution.py:316
  27.0 1.2 %all-to-all-done.stats_ref = f32[16,1,128]{2,1,0:T(1,128)S(1)} async-done(((f32[16,1,128]{2,1,0:T(1,128)}), f32[16,1,128]{2,1,0:T(1,128)S(1)}, u32[]{:S(2)}, u32[]{:S(2)}) %all-to-all-start) | async-done | bytes 8224 | tf_op jit(solution)/shard_map/all_to_all | solution.py:315
  28.2 1.1 %shard_map.65 = (f32[1,256,256]{2,1,0:T(8,128)}, f32[1,256,256]{2,1,0:T(8,128)}) custom-call(f32[8,128]{1,0:T(8,128)S(1)} %get-tuple-element.16.facts_ref.refs_1_, f32[16,1,128]{2,1,0:T(1,128)S(1)} %all-to-all-done.stats_ref, f32[256,256]{1,0:T(8,128)S(1)} %shard_map.64.hw_ref, f32[2,256,256]{2,1,0:T(8,128)S(1)} %get-tuple-element.20.near_part_ref, ...), custom_call_target="tpu_custom_call" | custom-call | flops 1 | bytes 1 | tf_op jit(solution)/shard_map/pallas_call | solution.py:320
  (1 shorter events, 0.0 us)
Async XLA Ops:
  1.6 4.2 %collective-permute-start = (bf16[256,256]{1,0:T(8,128)(2,1)S(1)}, bf16[256,256]{1,0:T(8,128)(2,1)S(1)}, u32[]{:S(2)}, u32[]{:S(2)}) collective-permute-start(bf16[256,256]{1,0:T(8,128)(2,1)S(1)} %get-tuple-element.17.self_ref.refs_3_), channel_id=1, source_target_pairs={{0,1},{1,0},{2,3},{3,2},{4,5},{5,4},{6,7},{7,6},{8,9},{9,8},{10,11... | collective-permute-start | bytes 393224 | tf_op jit(solution)/shard_map/ppermute | solution.py:40
  2.1 10.7 %collective-permute-start.2 = (bf16[256,256]{1,0:T(8,128)(2,1)S(1)}, bf16[256,256]{1,0:T(8,128)(2,1)S(1)}, u32[]{:S(2)}, u32[]{:S(2)}) collective-permute-start(bf16[256,256]{1,0:T(8,128)(2,1)S(1)} %get-tuple-element.17.self_ref.refs_3_), channel_id=1, source_target_pairs={{0,8},{1,9},{2,10},{3,11},{4,12},{5,13},{6,14},{7,15},{8,0},{9,1},... | collective-permute-start | bytes 393224 | tf_op jit(solution)/shard_map/ppermute | solution.py:40
  5.8 5.0 %collective-permute-start.1 = (bf16[256,256]{1,0:T(8,128)(2,1)S(1)}, bf16[256,256]{1,0:T(8,128)(2,1)S(1)}, u32[]{:S(2)}, u32[]{:S(2)}) collective-permute-start(bf16[256,256]{1,0:T(8,128)(2,1)S(1)} %shard_map.61), channel_id=1, source_target_pairs={{0,16},{1,2},{2,1},{3,4},{4,3},{5,6},{6,5},{7,23},{8,24},{9,10},{1... | collective-permute-start | bytes 393224 | tf_op jit(solution)/shard_map/ppermute | solution.py:61
  14.5 8.9 %collective-permute-start.3 = (bf16[256,256]{1,0:T(8,128)(2,1)S(1)}, bf16[256,256]{1,0:T(8,128)(2,1)S(1)}, u32[]{:S(2)}, u32[]{:S(2)}) collective-permute-start(bf16[256,256]{1,0:T(8,128)(2,1)S(1)} %get-tuple-element.27.refs_3_), channel_id=1, source_target_pairs={{0,8},{1,9},{2,10},{3,11},{4,12},{5,13},{6,14},{7,15},{8,0},{9,1},... | collective-permute-start | bytes 393224 | tf_op jit(solution)/shard_map/ppermute | solution.py:40
  14.5 8.9 %collective-permute-start.4 = (bf16[256,256]{1,0:T(8,128)(2,1)S(1)}, bf16[256,256]{1,0:T(8,128)(2,1)S(1)}, u32[]{:S(2)}, u32[]{:S(2)}) collective-permute-start(bf16[256,256]{1,0:T(8,128)(2,1)S(1)} %get-tuple-element.27.refs_3_), channel_id=1, source_target_pairs={{0,16},{1,2},{2,1},{3,4},{4,3},{5,6},{6,5},{7,23},{8,24},{9,10},{1... | collective-permute-start | bytes 393224 | tf_op jit(solution)/shard_map/ppermute | solution.py:61
  16.1 7.3 %collective-permute-start.5 = (bf16[256,256]{1,0:T(8,128)(2,1)S(1)}, bf16[256,256]{1,0:T(8,128)(2,1)S(1)}, u32[]{:S(2)}, u32[]{:S(2)}) collective-permute-start(bf16[256,256]{1,0:T(8,128)(2,1)S(1)} %get-tuple-element.27.refs_3_), channel_id=1, source_target_pairs={{0,1},{1,0},{2,3},{3,2},{4,5},{5,4},{6,7},{7,6},{8,9},{9,8},{10,11... | collective-permute-start | bytes 393224 | tf_op jit(solution)/shard_map/ppermute | solution.py:40
  16.3 11.8 %all-to-all-start = ((f32[16,1,128]{2,1,0:T(1,128)}), f32[16,1,128]{2,1,0:T(1,128)S(1)}, u32[]{:S(2)}, u32[]{:S(2)}) async-start(f32[16,1,128]{2,1,0:T(1,128)} %get-tuple-element.26), calls=%async_computation | async-start | bytes 16384 | tf_op jit(solution)/shard_map/all_to_all | solution.py:315

commit v14 on v12

--- a/solution.py
+++ b/solution.py
@@ -157,7 +157,7 @@
 
 
 def near_kernel(size, width, rows, left_hbm, right_hbm, wave_hbm, facts_ref, self_ref, near_ref, out_ref, sums_ref,
-                left_far, right_far, left_row, right_row, left_own, right_own, wave_ref, sems, far_sems, row_sems, wave_sem):
+                left_own, right_own, left_far, right_far, left_row, right_row, wave_ref, sems, far_sems, row_sems, wave_sem):
     offsets, _, _ = place(size, width)
     wave_copy = pltpu.make_async_copy(wave_hbm.at[0], wave_ref, wave_sem)
     own = fetch(left_hbm, right_hbm, left_own, right_own, sems, [(0, 2), (offsets[0], width)])
@@ -210,21 +210,16 @@
 
 
 def image_kernel(size, width, rows, *refs):
+    near_ref, far_ref, refs = refs[0], refs[1], refs[2:]
     row_refs, refs = refs[:rows], refs[rows:]
-    far_ref, near_ref, self_ref, left_row, right_row, left_hbm, right_hbm, out_ref, left_own, right_own, sems = refs
+    self_ref, left_row, right_row, left_far, right_far, left_own, right_own, _, out_ref = refs
     _, _, there = place(size, width)
-    own = fetch(left_hbm, right_hbm, left_own, right_own, sems, [(0, 2 + width), (2 + width, width)])
-    image = None
+    image = terms(self_ref[...], left_own, right_own, 0, 2)
+    image = image + terms(near_ref[...], left_own, right_own, 2, width)
+    image = image + terms(only(there[0], far_ref[...]), left_far, right_far, 0, width)
     for r, source in enumerate(row_refs):
-        piece = terms(only(there[1 + r], source[...]), left_row, right_row, r * width, width)
-        image = piece if image is None else image + piece
-    odd = lax.rem(lax.axis_index("sector"), 2) == 1
-    near, far = near_ref[...], only(there[0], far_ref[...])
-    finish(own[0])
-    image = image + terms(self_ref[...], left_own, right_own, 0, 2)
-    image = image + terms(jnp.where(odd, near, far), left_own, right_own, 2, width)
-    finish(own[1])
-    out_ref[...] = image + terms(jnp.where(odd, far, near), left_own, right_own, 2 + width, width)
+        image = image + terms(only(there[1 + r], source[...]), left_row, right_row, r * width, width)
+    out_ref[...] = image
 
 
 def second_kernel(size, width, rows, cells, facts_ref, stats_ref, hw_ref, near_part_ref, far_part_ref, row_part_ref,
@@ -269,7 +264,7 @@
     near, row_pairs = swap_pairs(size)
     rows = len(row_pairs)
     cells = float(size * block * block)
-    few, every, side, last = ((n,) + square for n in (2 + width, 2 + 2 * width, width, rows * width))
+    few, side, last = ((n,) + square for n in (2 + width, width, rows * width))
     f32, bf16 = jnp.float32, jnp.bfloat16
     dma = pltpu.SemaphoreType.DMA
 
@@ -283,16 +278,18 @@
     row_u = [vmem(swap(u, "sector", p)) for p in row_pairs]
     near_u = vmem(swap(u, "sector", near))
     far_u = vmem(far_swap(after(far_u, near_u)))
-    near_part, sums, left_far, right_far, left_row, right_row = call(
+    near_part, sums, left_own, right_own, left_far, right_far, left_row, right_row = call(
         functools.partial(near_kernel, size, width, rows),
-        (pltpu.VMEM((2,) + square, f32), pltpu.VMEM((8, 128), f32)) + (pltpu.VMEM(side, bf16),) * 2 + (pltpu.VMEM(last, bf16),) * 2,
-        [HB] * 3 + [VM] * 3, (VM,) * 6,
-        [pltpu.VMEM(few, bf16)] * 2 + [pltpu.VMEM(square, f32), dma((2, 2)), dma((1, 2)), dma((rows, 2)), dma], LONG,
+        (pltpu.VMEM((2,) + square, f32), pltpu.VMEM((8, 128), f32))
+        + (pltpu.VMEM(few, bf16),) * 2 + (pltpu.VMEM(side, bf16),) * 2 + (pltpu.VMEM(last, bf16),) * 2,
+        [HB] * 3 + [VM] * 3, (VM,) * 8,
+        [pltpu.VMEM(square, f32), dma((2, 2)), dma((1, 2)), dma((rows, 2)), dma], LONG,
     )(left_env, right_env, hbm(wavefunction), facts, u, near_u)
     near_part, left_row, right_row = vmem(near_part), vmem(left_row), vmem(right_row)
+    left_own, right_own, left_far, right_far = map(vmem, (left_own, right_own, left_far, right_far))
     far_part, part = call(
         functools.partial(far_kernel, size, width), (pltpu.VMEM(square, f32),) * 2, [VM] * 4, (VM,) * 2, cost=LONG,
-    )(vmem(left_far), vmem(right_far), near_part, far_u)
+    )(left_far, right_far, near_part, far_u)
     far_part = vmem(far_part)
     row_part, w, stats = call(
         functools.partial(first_kernel, size, width, rows),
@@ -306,9 +303,8 @@
     far_w = vmem(far_swap(w))
     stats = lax.all_to_all(stats, "sector", 0, 0, tiled=True)
     hw = call(
-        functools.partial(image_kernel, size, width, rows), pltpu.VMEM(square, f32), [VM] * (5 + rows) + [HB] * 2, VM,
-        [pltpu.VMEM(every, bf16)] * 2 + [dma((2, 2))],
-    )(*row_w, far_w, near_w, w, left_row, right_row, left_env, right_env)
+        functools.partial(image_kernel, size, width, rows), pltpu.VMEM(square, f32), [VM] * (9 + rows) + [AN], VM,
+    )(near_w, far_w, *row_w, w, left_row, right_row, left_far, right_far, left_own, right_own, stats)
     return call(
         functools.partial(second_kernel, size, width, rows, cells),
         (jax.ShapeDtypeStruct((1,) + square, f32),) * 2, [VM] * 6, (HB, HB),

time: 29.5 us -> 30.7 us (1.041)
  blocking collectives: 0 us -> 11.7 us
  starting transfers between devices: 13.1 us -> 7.56 us
  waiting for transfers between devices: 4.63 us -> 1.66 us
  Pallas kernels: 10.9 us -> 8.86 us
    all_to_all x0 -> x1, blocking collectives: none -> 11.7 us  [body(): stats = lax.all_to_all(stats, 'sector', 0, 0, tiled=True)]
    all_to_all x1 -> x0, starting transfers between devices: 5.51 us -> none  [body(): stats = lax.all_to_all(stats, 'sector', 0, 0, tiled=True)]
    pallas_call x1, Pallas kernels: 3.58 us -> 1.88 us  [body(): call(functools.partial(image_kernel, size, width, rows), pltpu.VMEM(squar...]
    ppermute x4, waiting for transfers between devices: 2.79 us -> 1.25 us  [swap(): lax.ppermute(x, axis, [(s, to.get(s, s)) for s in range(lax.axis_size(axi...]
    all_to_all x1 -> x0, waiting for transfers between devices: 1.2 us -> none  [body(): stats = lax.all_to_all(stats, 'sector', 0, 0, tiled=True)]
    pallas_call x1, Pallas kernels: 1.66 us -> 1.05 us  [body(): call(functools.partial(first_kernel, size, width, rows), (pltpu.VMEM((row...]
  transfers between devices with their start and end apart: 7 -> 6, of which waited for: 4 -> 2; matrix products, arithmetic and copies ran while one was open for 0% -> 0% of each run, Pallas kernels for 24% -> 13%
where the time goes in v14:
time: 30.7 us; the launch traced here: 30.4 us
  blocking collectives  11.7 us (38%)
  Pallas kernels  8.86 us (29%)
  starting transfers between devices  7.56 us (25%)
  waiting for transfers between devices  1.66 us (5%)
  between operations  0.67 us (2%)
    all_to_all x1, blocking collectives, body(): stats = lax.all_to_all(stats, 'sector', 0, 0, tiled=True)  11.7 us
    ppermute x4, starting transfers between devices, swap(): lax.ppermute(x, axis, [(s, to.get(s, s)) for s in range(lax.axis_size(axi...  4.42 us
    ppermute x2, starting transfers between devices, far_swap(): return lax.ppermute(x, ('groups', 'sector'), pairs)  3.13 us
    pallas_call x1, Pallas kernels, body(): call(functools.partial(near_kernel, size, width, rows), (pltpu.VMEM((2,)...  3.03 us
    pallas_call x1, Pallas kernels, body(): call(functools.partial(image_kernel, size, width, rows), pltpu.VMEM(squar...  1.88 us
    ppermute x4, waiting for transfers between devices, swap(): lax.ppermute(x, axis, [(s, to.get(s, s)) for s in range(lax.axis_size(axi...  1.25 us
    pallas_call x1, Pallas kernels, body(): call(functools.partial(second_kernel, size, width, rows, cells), (jax.Sha...  1.13 us
    pallas_call x1, Pallas kernels, body(): call(functools.partial(first_kernel, size, width, rows), (pltpu.VMEM((row...  1.05 us
  transfers between devices with their start and end apart: 6, of which 2 were waited for; matrix products, arithmetic and copies ran while one was open for 0% of the time, Pallas kernels for 13%

profile of v14, /device:TPU:0, one launch (start us, length us, event | category | flops | bytes accessed | tf_op | source)
XLA Modules:
  0.0 30.4 jit_solution(391558399237951299)
XLA Ops:
  0.6 1.0 %shard_map.59 = (bf16[256,256]{1,0:T(8,128)(2,1)S(1)}, bf16[256,256]{1,0:T(8,128)(2,1)S(1)}, f32[8,128]{1,0:T(8,128)S(1)}) custom-call(f32[1,256,256]{2,1,0:T(8,128)} %wave_hbm.3, s32[1,2]{1,0:T(1,128)} %dims_hbm.1), custom_call_target="tpu_custom_call" | custom-call | flops 1 | bytes 1 | tf_op jit(solution)/shard_map/pallas_call | solution.py:271
  1.6 0.5 %collective-permute-start = (bf16[256,256]{1,0:T(8,128)(2,1)S(1)}, bf16[256,256]{1,0:T(8,128)(2,1)S(1)}, u32[]{:S(2)}, u32[]{:S(2)}) collective-permute-start(bf16[256,256]{1,0:T(8,128)(2,1)S(1)} %get-tuple-element.19.self_ref.refs_3_), channel_id=1, source_target_pairs={{0,1},{1,0},{2,3},{3,2},{4,5},{5,4},{6,7},{7,6},{8,9},{9,8},{10,11... | collective-permute-start | bytes 393224 | tf_op jit(solution)/shard_map/ppermute | solution.py:40
  2.1 3.7 %collective-permute-start.2 = (bf16[256,256]{1,0:T(8,128)(2,1)S(1)}, bf16[256,256]{1,0:T(8,128)(2,1)S(1)}, u32[]{:S(2)}, u32[]{:S(2)}) collective-permute-start(bf16[256,256]{1,0:T(8,128)(2,1)S(1)} %get-tuple-element.19.self_ref.refs_3_), channel_id=1, source_target_pairs={{0,8},{1,9},{2,10},{3,11},{4,12},{5,13},{6,14},{7,15},{8,0},{9,1},... | collective-permute-start | bytes 393224 | tf_op jit(solution)/shard_map/ppermute | solution.py:40
  5.8 0.0 collective-permute-done.near_ref.refs_1_
  5.8 1.5 %collective-permute-start.1 = (bf16[256,256]{1,0:T(8,128)(2,1)S(1)}, bf16[256,256]{1,0:T(8,128)(2,1)S(1)}, u32[]{:S(2)}, u32[]{:S(2)}) collective-permute-start(bf16[256,256]{1,0:T(8,128)(2,1)S(1)} %shard_map.61), channel_id=1, source_target_pairs={{0,16},{1,2},{2,1},{3,4},{4,3},{5,6},{6,5},{7,23},{8,24},{9,10},{1... | collective-permute-start | bytes 393224 | tf_op jit(solution)/shard_map/ppermute | solution.py:61
  7.3 3.0 %shard_map.60 = (f32[2,256,256]{2,1,0:T(8,128)S(1)}, f32[8,128]{1,0:T(8,128)S(1)}, bf16[8,256,256]{2,1,0:T(8,128)(2,1)S(1)}, bf16[8,256,256]{2,1,0:T(8,128)(2,1)...) custom-call(bf16[1,26,256,256]{3,2,1,0:T(8,128)(2,1)} %left_hbm.1, ...), custom_call_target="tpu_custom_call" | custom-call | flops 4000000000 | bytes 1 | tf_op jit(solution)/shard_map/pallas_call | solution.py:281
  10.4 0.4 %collective-permute-done.1.far_ref = bf16[256,256]{1,0:T(8,128)(2,1)S(1)} collective-permute-done((bf16[256,256]{1,0:T(8,128)(2,1)S(1)}, bf16[256,256]{1,0:T(8,128)(2,1)S(1)}, u32[]{:S(2)}, u32[]{:S(2)}) %collective-permute-start.1) | collective-permute-done | bytes 131104 | tf_op jit(solution)/shard_map/ppermute | solution.py:61
  10.8 0.8 %shard_map.62 = (f32[256,256]{1,0:T(8,128)S(1)}, f32[256,256]{1,0:T(8,128)S(1)}) custom-call(bf16[6,256,256]{2,1,0:T(8,128)(2,1)S(1)} %get-tuple-element.20.left_ref.refs_6_, bf16[6,256,256]{2,1,0:T(8,128)(2,1)S(1)} %get-tuple-element.21.right_ref.refs_7_, f32[2,256,256]{2,1,0:T(8,128)S(1)} %get-tuple-element.22.near_part_ref, ...), custom_call_target="tpu_custom_call" | custom-call | flops 4000000000 | bytes 1 | tf_op jit(solution)/shard_map/pallas_call | solution.py:290
  11.6 1.2 %collective-permute-done.2.refs_6_ = bf16[256,256]{1,0:T(8,128)(2,1)S(1)} collective-permute-done((bf16[256,256]{1,0:T(8,128)(2,1)S(1)}, bf16[256,256]{1,0:T(8,128)(2,1)S(1)}, u32[]{:S(2)}, u32[]{:S(2)}) %collective-permute-start.2) | collective-permute-done | bytes 131104 | tf_op jit(solution)/shard_map/ppermute | solution.py:40
  12.8 1.1 %shard_map.63 = (f32[1,256,256]{2,1,0:T(8,128)S(1)}, bf16[256,256]{1,0:T(8,128)(2,1)S(1)}, f32[16,1,128]{2,1,0:T(1,128)S(1)}) custom-call(f32[256,256]{1,0:T(8,128)S(1)} %get-tuple-element.24.refs_0_, f32[8,128]{1,0:T(8,128)S(1)} %get-tuple-element.18.facts_ref.refs_1_, f32[8,128]{1,0:T(8,128)S(1)} %get-tuple-element.25.refs_2_, ...), custom_call_target="tpu_custom_call" | custom-call | flops 1 | bytes 1 | tf_op jit(solution)/shard_map/pallas_call | solution.py:294
  13.9 0.1 collective-permute-start.5
  13.9 1.6 %collective-permute-start.4 = (bf16[256,256]{1,0:T(8,128)(2,1)S(1)}, bf16[256,256]{1,0:T(8,128)(2,1)S(1)}, u32[]{:S(2)}, u32[]{:S(2)}) collective-permute-start(bf16[256,256]{1,0:T(8,128)(2,1)S(1)} %get-tuple-element.29.refs_3_), channel_id=1, source_target_pairs={{0,16},{1,2},{2,1},{3,4},{4,3},{5,6},{6,5},{7,23},{8,24},{9,10},{1... | collective-permute-start | bytes 393224 | tf_op jit(solution)/shard_map/ppermute | solution.py:61
  15.5 0.2 collective-permute-start.3
  15.7 11.7 %all_to_all.5.refs_10_.stats_ref = f32[16,1,128]{2,1,0:T(1,128)S(1)} all-to-all(f32[16,1,128]{2,1,0:T(1,128)S(1)} %get-tuple-element.28), channel_id=1, replica_groups=mesh['groups'=2,'sector'=16] {'sector'}, dimensions={0} | all-to-all | bytes 16384 | tf_op jit(solution)/shard_map/all_to_all | solution.py:304
  27.4 0.0 collective-permute-done.5.refs_2_
  27.4 0.0 collective-permute-done.4.refs_1_
  27.4 0.0 collective-permute-done.3.refs_0_
  27.4 1.9 %shard_map.64.hw_ref = f32[256,256]{1,0:T(8,128)S(1)} custom-call(bf16[256,256]{1,0:T(8,128)(2,1)S(1)} %collective-permute-done.3.refs_0_, bf16[256,256]{1,0:T(8,128)(2,1)S(1)} %collective-permute-done.4.refs_1_, bf16[256,256]{1,0:T(8,128)(2,1)S(1)} %collective-permute-done.5.refs_2_, bf16[256,256]{1,0:T(8,128)(2,1)S(1)} %get-tuple-element.29.refs_3_, ...), custom_call_target="tpu_custom_call" | custom-call | flops 1 | bytes 1 | tf_op jit(solution)/shard_map/pallas_call | solution.py:305
  29.3 1.1 %shard_map.65 = (f32[1,256,256]{2,1,0:T(8,128)}, f32[1,256,256]{2,1,0:T(8,128)}) custom-call(f32[8,128]{1,0:T(8,128)S(1)} %get-tuple-element.18.facts_ref.refs_1_, f32[16,1,128]{2,1,0:T(1,128)S(1)} %all_to_all.5.refs_10_.stats_ref, f32[256,256]{1,0:T(8,128)S(1)} %shard_map.64.hw_ref, f32[2,256,256]{2,1,0:T(8,128)S(1)} %get-tuple-element.22.near_part_ref, ...), custom_call_target="tpu_custom_call" | custom-call | flops 1 | bytes 1 | tf_op jit(solution)/shard_map/pallas_call | solution.py:308
  (1 shorter events, 0.0 us)
Async XLA Ops:
  1.6 4.2 %collective-permute-start = (bf16[256,256]{1,0:T(8,128)(2,1)S(1)}, bf16[256,256]{1,0:T(8,128)(2,1)S(1)}, u32[]{:S(2)}, u32[]{:S(2)}) collective-permute-start(bf16[256,256]{1,0:T(8,128)(2,1)S(1)} %get-tuple-element.19.self_ref.refs_3_), channel_id=1, source_target_pairs={{0,1},{1,0},{2,3},{3,2},{4,5},{5,4},{6,7},{7,6},{8,9},{9,8},{10,11... | collective-permute-start | bytes 393224 | tf_op jit(solution)/shard_map/ppermute | solution.py:40
  2.1 10.7 %collective-permute-start.2 = (bf16[256,256]{1,0:T(8,128)(2,1)S(1)}, bf16[256,256]{1,0:T(8,128)(2,1)S(1)}, u32[]{:S(2)}, u32[]{:S(2)}) collective-permute-start(bf16[256,256]{1,0:T(8,128)(2,1)S(1)} %get-tuple-element.19.self_ref.refs_3_), channel_id=1, source_target_pairs={{0,8},{1,9},{2,10},{3,11},{4,12},{5,13},{6,14},{7,15},{8,0},{9,1},... | collective-permute-start | bytes 393224 | tf_op jit(solution)/shard_map/ppermute | solution.py:40
  5.8 5.0 %collective-permute-start.1 = (bf16[256,256]{1,0:T(8,128)(2,1)S(1)}, bf16[256,256]{1,0:T(8,128)(2,1)S(1)}, u32[]{:S(2)}, u32[]{:S(2)}) collective-permute-start(bf16[256,256]{1,0:T(8,128)(2,1)S(1)} %shard_map.61), channel_id=1, source_target_pairs={{0,16},{1,2},{2,1},{3,4},{4,3},{5,6},{6,5},{7,23},{8,24},{9,10},{1... | collective-permute-start | bytes 393224 | tf_op jit(solution)/shard_map/ppermute | solution.py:61
  13.9 13.6 %collective-permute-start.5 = (bf16[256,256]{1,0:T(8,128)(2,1)S(1)}, bf16[256,256]{1,0:T(8,128)(2,1)S(1)}, u32[]{:S(2)}, u32[]{:S(2)}) collective-permute-start(bf16[256,256]{1,0:T(8,128)(2,1)S(1)} %get-tuple-element.29.refs_3_), channel_id=1, source_target_pairs={{0,8},{1,9},{2,10},{3,11},{4,12},{5,13},{6,14},{7,15},{8,0},{9,1},... | collective-permute-start | bytes 393224 | tf_op jit(solution)/shard_map/ppermute | solution.py:40
  13.9 13.5 %collective-permute-start.4 = (bf16[256,256]{1,0:T(8,128)(2,1)S(1)}, bf16[256,256]{1,0:T(8,128)(2,1)S(1)}, u32[]{:S(2)}, u32[]{:S(2)}) collective-permute-start(bf16[256,256]{1,0:T(8,128)(2,1)S(1)} %get-tuple-element.29.refs_3_), channel_id=1, source_target_pairs={{0,16},{1,2},{2,1},{3,4},{4,3},{5,6},{6,5},{7,23},{8,24},{9,10},{1... | collective-permute-start | bytes 393224 | tf_op jit(solution)/shard_map/ppermute | solution.py:61
  15.5 11.9 %collective-permute-start.3 = (bf16[256,256]{1,0:T(8,128)(2,1)S(1)}, bf16[256,256]{1,0:T(8,128)(2,1)S(1)}, u32[]{:S(2)}, u32[]{:S(2)}) collective-permute-start(bf16[256,256]{1,0:T(8,128)(2,1)S(1)} %get-tuple-element.29.refs_3_), channel_id=1, source_target_pairs={{0,1},{1,0},{2,3},{3,2},{4,5},{5,4},{6,7},{7,6},{8,9},{9,8},{10,11... | collective-permute-start | bytes 393224 | tf_op jit(solution)/shard_map/ppermute | solution.py:40

commit v15 on v12

--- a/solution.py
+++ b/solution.py
@@ -209,22 +209,25 @@
         stats_ref[n] = stats
 
 
-def image_kernel(size, width, rows, *refs):
-    row_refs, refs = refs[:rows], refs[rows:]
-    far_ref, near_ref, self_ref, left_row, right_row, left_hbm, right_hbm, out_ref, left_own, right_own, sems = refs
+def image_kernel(size, width, near_ref, far_ref, self_ref, left_hbm, right_hbm, out_ref, left_own, right_own, sems):
     _, _, there = place(size, width)
     own = fetch(left_hbm, right_hbm, left_own, right_own, sems, [(0, 2 + width), (2 + width, width)])
-    image = None
-    for r, source in enumerate(row_refs):
-        piece = terms(only(there[1 + r], source[...]), left_row, right_row, r * width, width)
-        image = piece if image is None else image + piece
     odd = lax.rem(lax.axis_index("sector"), 2) == 1
     near, far = near_ref[...], only(there[0], far_ref[...])
     finish(own[0])
-    image = image + terms(self_ref[...], left_own, right_own, 0, 2)
+    image = terms(self_ref[...], left_own, right_own, 0, 2)
     image = image + terms(jnp.where(odd, near, far), left_own, right_own, 2, width)
     finish(own[1])
     out_ref[...] = image + terms(jnp.where(odd, far, near), left_own, right_own, 2 + width, width)
+
+
+def row_kernel(size, width, rows, part_ref, left_row, right_row, *refs):
+    row_refs, (out_ref,) = refs[:rows], refs[rows:]
+    _, _, there = place(size, width)
+    image = part_ref[...]
+    for r, source in enumerate(row_refs):
+        image = image + terms(only(there[1 + r], source[...]), left_row, right_row, r * width, width)
+    out_ref[...] = image
 
 
 def second_kernel(size, width, rows, cells, facts_ref, stats_ref, hw_ref, near_part_ref, far_part_ref, row_part_ref,
@@ -306,9 +309,12 @@
     far_w = vmem(far_swap(w))
     stats = lax.all_to_all(stats, "sector", 0, 0, tiled=True)
     hw = call(
-        functools.partial(image_kernel, size, width, rows), pltpu.VMEM(square, f32), [VM] * (5 + rows) + [HB] * 2, VM,
+        functools.partial(image_kernel, size, width), pltpu.VMEM(square, f32), [VM] * 3 + [HB] * 2, VM,
         [pltpu.VMEM(every, bf16)] * 2 + [dma((2, 2))],
-    )(*row_w, far_w, near_w, w, left_row, right_row, left_env, right_env)
+    )(near_w, far_w, w, left_env, right_env)
+    hw = call(
+        functools.partial(row_kernel, size, width, rows), pltpu.VMEM(square, f32), [VM] * (3 + rows), VM,
+    )(vmem(hw), left_row, right_row, *row_w)
     return call(
         functools.partial(second_kernel, size, width, rows, cells),
         (jax.ShapeDtypeStruct((1,) + square, f32),) * 2, [VM] * 6, (HB, HB),

time: 29.5 us -> 29.6 us (level)
  waiting for transfers between devices: 4.63 us -> 4.12 us
  Pallas kernels: 10.9 us -> 11.4 us
    ppermute x4, waiting for transfers between devices: 2.79 us -> 2.18 us  [swap(): lax.ppermute(x, axis, [(s, to.get(s, s)) for s in range(lax.axis_size(axi...]
    pallas_call x1 -> x2, Pallas kernels: 3.58 us -> 4.06 us  [the longest x1 3.29 us: body(): call(functools.partial(image_kernel, size, width), pltpu.VMEM(square, f32...]
    all_to_all x1, starting transfers between devices: 5.51 us -> 5.81 us  [body(): stats = lax.all_to_all(stats, 'sector', 0, 0, tiled=True)]
  transfers between devices with their start and end apart: 7 -> 7, of which waited for: 4 -> 4; matrix products, arithmetic and copies ran while one was open for 0% -> 0% of each run, Pallas kernels for 24% -> 26%
where the time goes in v15:
time: 29.6 us; the launch traced here: 29.3 us
  starting transfers between devices  13.1 us (44%)
  Pallas kernels  11.4 us (39%)
  waiting for transfers between devices  4.12 us (14%)
  between operations  0.7 us (2%)
    all_to_all x1, starting transfers between devices, body(): stats = lax.all_to_all(stats, 'sector', 0, 0, tiled=True)  5.81 us
    ppermute x4, starting transfers between devices, swap(): lax.ppermute(x, axis, [(s, to.get(s, s)) for s in range(lax.axis_size(axi...  4.19 us
    pallas_call x1, Pallas kernels, body(): call(functools.partial(image_kernel, size, width), pltpu.VMEM(square, f32...  3.29 us
    ppermute x2, starting transfers between devices, far_swap(): return lax.ppermute(x, ('groups', 'sector'), pairs)  3.11 us
    pallas_call x1, Pallas kernels, body(): call(functools.partial(near_kernel, size, width, rows), (pltpu.VMEM((2,)...  2.79 us
    ppermute x4, waiting for transfers between devices, swap(): lax.ppermute(x, axis, [(s, to.get(s, s)) for s in range(lax.axis_size(axi...  2.18 us
    pallas_call x1, Pallas kernels, body(): call(functools.partial(first_kernel, size, width, rows), (pltpu.VMEM((row...  1.66 us
    all_to_all x1, waiting for transfers between devices, body(): stats = lax.all_to_all(stats, 'sector', 0, 0, tiled=True)  1.3 us
  transfers between devices with their start and end apart: 7, of which 4 were waited for; matrix products, arithmetic and copies ran while one was open for 0% of the time, Pallas kernels for 26%

profile of v15, /device:TPU:0, one launch (start us, length us, event | category | flops | bytes accessed | tf_op | source)
XLA Modules:
  0.0 29.3 jit_solution(15005791290749640364)
XLA Ops:
  0.6 1.0 %shard_map.59 = (bf16[256,256]{1,0:T(8,128)(2,1)S(1)}, bf16[256,256]{1,0:T(8,128)(2,1)S(1)}, f32[8,128]{1,0:T(8,128)S(1)}) custom-call(f32[1,256,256]{2,1,0:T(8,128)} %wave_hbm.3, s32[1,2]{1,0:T(1,128)} %dims_hbm.1), custom_call_target="tpu_custom_call" | custom-call | flops 1 | bytes 1 | tf_op jit(solution)/shard_map/pallas_call | solution.py:279
  1.6 0.5 %collective-permute-start = (bf16[256,256]{1,0:T(8,128)(2,1)S(1)}, bf16[256,256]{1,0:T(8,128)(2,1)S(1)}, u32[]{:S(2)}, u32[]{:S(2)}) collective-permute-start(bf16[256,256]{1,0:T(8,128)(2,1)S(1)} %get-tuple-element.17.self_ref.refs_3_), channel_id=1, source_target_pairs={{0,1},{1,0},{2,3},{3,2},{4,5},{5,4},{6,7},{7,6},{8,9},{9,8},{10,11... | collective-permute-start | bytes 393224 | tf_op jit(solution)/shard_map/ppermute | solution.py:40
  2.1 3.7 %collective-permute-start.2 = (bf16[256,256]{1,0:T(8,128)(2,1)S(1)}, bf16[256,256]{1,0:T(8,128)(2,1)S(1)}, u32[]{:S(2)}, u32[]{:S(2)}) collective-permute-start(bf16[256,256]{1,0:T(8,128)(2,1)S(1)} %get-tuple-element.17.self_ref.refs_3_), channel_id=1, source_target_pairs={{0,8},{1,9},{2,10},{3,11},{4,12},{5,13},{6,14},{7,15},{8,0},{9,1},... | collective-permute-start | bytes 393224 | tf_op jit(solution)/shard_map/ppermute | solution.py:40
  5.8 0.0 collective-permute-done.near_ref.refs_1_
  5.8 1.5 %collective-permute-start.1 = (bf16[256,256]{1,0:T(8,128)(2,1)S(1)}, bf16[256,256]{1,0:T(8,128)(2,1)S(1)}, u32[]{:S(2)}, u32[]{:S(2)}) collective-permute-start(bf16[256,256]{1,0:T(8,128)(2,1)S(1)} %shard_map.61), channel_id=1, source_target_pairs={{0,16},{1,2},{2,1},{3,4},{4,3},{5,6},{6,5},{7,23},{8,24},{9,10},{1... | collective-permute-start | bytes 393224 | tf_op jit(solution)/shard_map/ppermute | solution.py:61
  7.3 2.8 %shard_map.60 = (f32[2,256,256]{2,1,0:T(8,128)S(1)}, f32[8,128]{1,0:T(8,128)S(1)}, bf16[6,256,256]{2,1,0:T(8,128)(2,1)S(1)}, bf16[6,256,256]{2,1,0:T(8,128)(2,1)...) custom-call(bf16[1,26,256,256]{3,2,1,0:T(8,128)(2,1)} %left_hbm.3, ...), custom_call_target="tpu_custom_call" | custom-call | flops 4000000000 | bytes 1 | tf_op jit(solution)/shard_map/pallas_call | solution.py:289
  10.1 0.6 %collective-permute-done.1.far_ref = bf16[256,256]{1,0:T(8,128)(2,1)S(1)} collective-permute-done((bf16[256,256]{1,0:T(8,128)(2,1)S(1)}, bf16[256,256]{1,0:T(8,128)(2,1)S(1)}, u32[]{:S(2)}, u32[]{:S(2)}) %collective-permute-start.1) | collective-permute-done | bytes 131104 | tf_op jit(solution)/shard_map/ppermute | solution.py:61
  10.8 0.8 %shard_map.62 = (f32[256,256]{1,0:T(8,128)S(1)}, f32[256,256]{1,0:T(8,128)S(1)}) custom-call(bf16[6,256,256]{2,1,0:T(8,128)(2,1)S(1)} %get-tuple-element.18.left_ref, bf16[6,256,256]{2,1,0:T(8,128)(2,1)S(1)} %get-tuple-element.19.right_ref, f32[2,256,256]{2,1,0:T(8,128)S(1)} %get-tuple-element.20.near_part_ref, ...), custom_call_target="tpu_custom_call" | custom-call | flops 4000000000 | bytes 1 | tf_op jit(solution)/shard_map/pallas_call | solution.py:296
  11.6 1.2 %collective-permute-done.2.refs_6_ = bf16[256,256]{1,0:T(8,128)(2,1)S(1)} collective-permute-done((bf16[256,256]{1,0:T(8,128)(2,1)S(1)}, bf16[256,256]{1,0:T(8,128)(2,1)S(1)}, u32[]{:S(2)}, u32[]{:S(2)}) %collective-permute-start.2) | collective-permute-done | bytes 131104 | tf_op jit(solution)/shard_map/ppermute | solution.py:40
  12.8 1.7 %shard_map.63 = (f32[1,256,256]{2,1,0:T(8,128)S(1)}, bf16[256,256]{1,0:T(8,128)(2,1)S(1)}, f32[16,1,128]{2,1,0:T(1,128)}) custom-call(f32[256,256]{1,0:T(8,128)S(1)} %get-tuple-element.22.refs_0_, f32[8,128]{1,0:T(8,128)S(1)} %get-tuple-element.16.facts_ref.refs_1_, f32[8,128]{1,0:T(8,128)S(1)} %get-tuple-element.23.refs_2_, ...), custom_call_target="tpu_custom_call" | custom-call | flops 1 | bytes 1 | tf_op jit(solution)/shard_map/pallas_call | solution.py:300
  14.5 0.0 collective-permute-start.3
  14.5 1.6 %collective-permute-start.4 = (bf16[256,256]{1,0:T(8,128)(2,1)S(1)}, bf16[256,256]{1,0:T(8,128)(2,1)S(1)}, u32[]{:S(2)}, u32[]{:S(2)}) collective-permute-start(bf16[256,256]{1,0:T(8,128)(2,1)S(1)} %get-tuple-element.27.self_ref), channel_id=1, source_target_pairs={{0,16},{1,2},{2,1},{3,4},{4,3},{5,6},{6,5},{7,23},{8,24},{9,10},{1... | collective-permute-start | bytes 393224 | tf_op jit(solution)/shard_map/ppermute | solution.py:61
  16.1 0.0 collective-permute-start.5
  16.1 5.8 %all-to-all-start = ((f32[16,1,128]{2,1,0:T(1,128)}), f32[16,1,128]{2,1,0:T(1,128)S(1)}, u32[]{:S(2)}, u32[]{:S(2)}) async-start(f32[16,1,128]{2,1,0:T(1,128)} %get-tuple-element.26), calls=%async_computation | async-start | bytes 16384 | tf_op jit(solution)/shard_map/all_to_all | solution.py:310
  21.9 0.0 collective-permute-done.3.near_ref
  21.9 0.0 collective-permute-done.4.far_ref
  21.9 3.3 %shard_map.64.part_ref = f32[256,256]{1,0:T(8,128)S(1)} custom-call(bf16[256,256]{1,0:T(8,128)(2,1)S(1)} %collective-permute-done.3.near_ref, bf16[256,256]{1,0:T(8,128)(2,1)S(1)} %collective-permute-done.4.far_ref, bf16[256,256]{1,0:T(8,128)(2,1)S(1)} %get-tuple-element.27.self_ref, bf16[1,26,256,256]{3,2,1,0:T(8,128)(2,1)} %left_hbm.3, ...), custom_call_target="tpu_custom_call" | custom-call | flops 1 | bytes 1 | tf_op jit(solution)/shard_map/pallas_call | solution.py:311
  25.2 0.9 %collective-permute-done.5.refs_0_ = bf16[256,256]{1,0:T(8,128)(2,1)S(1)} collective-permute-done((bf16[256,256]{1,0:T(8,128)(2,1)S(1)}, bf16[256,256]{1,0:T(8,128)(2,1)S(1)}, u32[]{:S(2)}, u32[]{:S(2)}) %collective-permute-start.5) | collective-permute-done | bytes 131104 | tf_op jit(solution)/shard_map/ppermute | solution.py:40
  26.1 0.8 %shard_map.65.hw_ref = f32[256,256]{1,0:T(8,128)S(1)} custom-call(f32[256,256]{1,0:T(8,128)S(1)} %shard_map.64.part_ref, bf16[6,256,256]{2,1,0:T(8,128)(2,1)S(1)} %get-tuple-element.24.refs_4_.left_row, bf16[6,256,256]{2,1,0:T(8,128)(2,1)S(1)} %get-tuple-element.25.refs_5_.right_row, bf16[256,256]{1,0:T(8,128)(2,1)S(1)} %collective-permute-done.5.refs_0_), custom_call_target="tpu_custom_call" | custom-call | flops 1 | bytes 1 | tf_op jit(solution)/shard_map/pallas_call | solution.py:315
  26.9 1.3 %all-to-all-done.stats_ref = f32[16,1,128]{2,1,0:T(1,128)S(1)} async-done(((f32[16,1,128]{2,1,0:T(1,128)}), f32[16,1,128]{2,1,0:T(1,128)S(1)}, u32[]{:S(2)}, u32[]{:S(2)}) %all-to-all-start) | async-done | bytes 8224 | tf_op jit(solution)/shard_map/all_to_all | solution.py:310
  28.2 1.1 %shard_map.66 = (f32[1,256,256]{2,1,0:T(8,128)}, f32[1,256,256]{2,1,0:T(8,128)}) custom-call(f32[8,128]{1,0:T(8,128)S(1)} %get-tuple-element.16.facts_ref.refs_1_, f32[16,1,128]{2,1,0:T(1,128)S(1)} %all-to-all-done.stats_ref, f32[256,256]{1,0:T(8,128)S(1)} %shard_map.65.hw_ref, f32[2,256,256]{2,1,0:T(8,128)S(1)} %get-tuple-element.20.near_part_ref, ...), custom_call_target="tpu_custom_call" | custom-call | flops 1 | bytes 1 | tf_op jit(solution)/shard_map/pallas_call | solution.py:318
  (1 shorter events, 0.0 us)
Async XLA Ops:
  1.6 4.2 %collective-permute-start = (bf16[256,256]{1,0:T(8,128)(2,1)S(1)}, bf16[256,256]{1,0:T(8,128)(2,1)S(1)}, u32[]{:S(2)}, u32[]{:S(2)}) collective-permute-start(bf16[256,256]{1,0:T(8,128)(2,1)S(1)} %get-tuple-element.17.self_ref.refs_3_), channel_id=1, source_target_pairs={{0,1},{1,0},{2,3},{3,2},{4,5},{5,4},{6,7},{7,6},{8,9},{9,8},{10,11... | collective-permute-start | bytes 393224 | tf_op jit(solution)/shard_map/ppermute | solution.py:40
  2.1 10.7 %collective-permute-start.2 = (bf16[256,256]{1,0:T(8,128)(2,1)S(1)}, bf16[256,256]{1,0:T(8,128)(2,1)S(1)}, u32[]{:S(2)}, u32[]{:S(2)}) collective-permute-start(bf16[256,256]{1,0:T(8,128)(2,1)S(1)} %get-tuple-element.17.self_ref.refs_3_), channel_id=1, source_target_pairs={{0,8},{1,9},{2,10},{3,11},{4,12},{5,13},{6,14},{7,15},{8,0},{9,1},... | collective-permute-start | bytes 393224 | tf_op jit(solution)/shard_map/ppermute | solution.py:40
  5.8 5.0 %collective-permute-start.1 = (bf16[256,256]{1,0:T(8,128)(2,1)S(1)}, bf16[256,256]{1,0:T(8,128)(2,1)S(1)}, u32[]{:S(2)}, u32[]{:S(2)}) collective-permute-start(bf16[256,256]{1,0:T(8,128)(2,1)S(1)} %shard_map.61), channel_id=1, source_target_pairs={{0,16},{1,2},{2,1},{3,4},{4,3},{5,6},{6,5},{7,23},{8,24},{9,10},{1... | collective-permute-start | bytes 393224 | tf_op jit(solution)/shard_map/ppermute | solution.py:61
  14.5 7.4 %collective-permute-start.3 = (bf16[256,256]{1,0:T(8,128)(2,1)S(1)}, bf16[256,256]{1,0:T(8,128)(2,1)S(1)}, u32[]{:S(2)}, u32[]{:S(2)}) collective-permute-start(bf16[256,256]{1,0:T(8,128)(2,1)S(1)} %get-tuple-element.27.self_ref), channel_id=1, source_target_pairs={{0,1},{1,0},{2,3},{3,2},{4,5},{5,4},{6,7},{7,6},{8,9},{9,8},{10,11... | collective-permute-start | bytes 393224 | tf_op jit(solution)/shard_map/ppermute | solution.py:40
  14.5 7.4 %collective-permute-start.4 = (bf16[256,256]{1,0:T(8,128)(2,1)S(1)}, bf16[256,256]{1,0:T(8,128)(2,1)S(1)}, u32[]{:S(2)}, u32[]{:S(2)}) collective-permute-start(bf16[256,256]{1,0:T(8,128)(2,1)S(1)} %get-tuple-element.27.self_ref), channel_id=1, source_target_pairs={{0,16},{1,2},{2,1},{3,4},{4,3},{5,6},{6,5},{7,23},{8,24},{9,10},{1... | collective-permute-start | bytes 393224 | tf_op jit(solution)/shard_map/ppermute | solution.py:61
  16.1 10.1 %collective-permute-start.5 = (bf16[256,256]{1,0:T(8,128)(2,1)S(1)}, bf16[256,256]{1,0:T(8,128)(2,1)S(1)}, u32[]{:S(2)}, u32[]{:S(2)}) collective-permute-start(bf16[256,256]{1,0:T(8,128)(2,1)S(1)} %get-tuple-element.27.self_ref), channel_id=1, source_target_pairs={{0,8},{1,9},{2,10},{3,11},{4,12},{5,13},{6,14},{7,15},{8,0},{9,1},... | collective-permute-start | bytes 393224 | tf_op jit(solution)/shard_map/ppermute | solution.py:40
  16.1 12.1 %all-to-all-start = ((f32[16,1,128]{2,1,0:T(1,128)}), f32[16,1,128]{2,1,0:T(1,128)S(1)}, u32[]{:S(2)}, u32[]{:S(2)}) async-start(f32[16,1,128]{2,1,0:T(1,128)} %get-tuple-element.26), calls=%async_computation | async-start | bytes 16384 | tf_op jit(solution)/shard_map/all_to_all | solution.py:310

commit v16 on v15

--- a/solution.py
+++ b/solution.py
@@ -48,13 +48,16 @@
     return near, [p for p in (row_even, row_odd) if p]
 
 
-def far_swap(x):
+def far_swap(x, across):
     groups, size = lax.axis_size("groups"), lax.axis_size("sector")
     pairs = []
     for g in range(groups):
         for s in range(size):
-            if s % QD == 0 or s % QD == QD - 1:
+            end = s % QD == 0 or s % QD == QD - 1
+            if end and across:
                 to, partner = (g ^ 1 if g ^ 1 < groups else g), s
+            elif end:
+                to, partner = g, s + QD - 1 if s % QD == 0 else s + 1 - QD
             else:
                 to, partner = g, s + 1 if s % 2 else s - 1
             pairs.append((g * size + s, to * size + partner))
@@ -285,7 +288,7 @@
     u, facts = vmem(u), vmem(facts)
     row_u = [vmem(swap(u, "sector", p)) for p in row_pairs]
     near_u = vmem(swap(u, "sector", near))
-    far_u = vmem(far_swap(after(far_u, near_u)))
+    far_u = vmem(far_swap(after(far_u, near_u), True))
     near_part, sums, left_far, right_far, left_row, right_row = call(
         functools.partial(near_kernel, size, width, rows),
         (pltpu.VMEM((2,) + square, f32), pltpu.VMEM((8, 128), f32)) + (pltpu.VMEM(side, bf16),) * 2 + (pltpu.VMEM(last, bf16),) * 2,
@@ -306,7 +309,7 @@
     w = vmem(w)
     row_w = [vmem(swap(w, "sector", p)) for p in row_pairs]
     near_w = vmem(swap(w, "sector", near))
-    far_w = vmem(far_swap(w))
+    far_w = vmem(far_swap(w, False))
     stats = lax.all_to_all(stats, "sector", 0, 0, tiled=True)
     hw = call(
         functools.partial(image_kernel, size, width), pltpu.VMEM(square, f32), [VM] * 3 + [HB] * 2, VM,

time: 29.6 us -> 30.7 us (1.037)
  starting transfers between devices: 13.1 us -> 14.2 us
    ppermute x4, starting transfers between devices: 4.19 us -> 7.55 us  [swap(): lax.ppermute(x, axis, [(s, to.get(s, s)) for s in range(lax.axis_size(axi...]
    all_to_all x1, starting transfers between devices: 5.81 us -> 3.47 us  [body(): stats = lax.all_to_all(stats, 'sector', 0, 0, tiled=True)]
    ppermute x4, waiting for transfers between devices: 2.18 us -> 1.25 us  [swap(): lax.ppermute(x, axis, [(s, to.get(s, s)) for s in range(lax.axis_size(axi...]
    all_to_all x1, waiting for transfers between devices: 1.3 us -> 2.18 us  [body(): stats = lax.all_to_all(stats, 'sector', 0, 0, tiled=True)]
  transfers between devices with their start and end apart: 7 -> 7, of which waited for: 4 -> 3; matrix products, arithmetic and copies ran while one was open for 0% -> 0% of each run, Pallas kernels for 26% -> 25%
where the time goes in v16:
time: 30.7 us; the launch traced here: 30.4 us
  starting transfers between devices  14.2 us (46%)
  Pallas kernels  11.4 us (37%)
  waiting for transfers between devices  4.07 us (13%)
  between operations  0.7 us (2%)
    ppermute x4, starting transfers between devices, swap(): lax.ppermute(x, axis, [(s, to.get(s, s)) for s in range(lax.axis_size(axi...  7.55 us
    all_to_all x1, starting transfers between devices, body(): stats = lax.all_to_all(stats, 'sector', 0, 0, tiled=True)  3.47 us
    pallas_call x1, Pallas kernels, body(): call(functools.partial(image_kernel, size, width), pltpu.VMEM(square, f32...  3.29 us
    ppermute x2, starting transfers between devices, far_swap(): return lax.ppermute(x, ('groups', 'sector'), pairs)  3.22 us
    pallas_call x1, Pallas kernels, body(): call(functools.partial(near_kernel, size, width, rows), (pltpu.VMEM((2,)...  2.79 us
    all_to_all x1, waiting for transfers between devices, body(): stats = lax.all_to_all(stats, 'sector', 0, 0, tiled=True)  2.18 us
    pallas_call x1, Pallas kernels, body(): call(functools.partial(first_kernel, size, width, rows), (pltpu.VMEM((row...  1.66 us
    ppermute x4, waiting for transfers between devices, swap(): lax.ppermute(x, axis, [(s, to.get(s, s)) for s in range(lax.axis_size(axi...  1.25 us
  transfers between devices with their start and end apart: 7, of which 3 were waited for; matrix products, arithmetic and copies ran while one was open for 0% of the time, Pallas kernels for 25%

profile of v16, /device:TPU:0, one launch (start us, length us, event | category | flops | bytes accessed | tf_op | source)
XLA Modules:
  0.0 30.4 jit_solution(3122864783486239077)
XLA Ops:
  0.6 1.0 %shard_map.59 = (bf16[256,256]{1,0:T(8,128)(2,1)S(1)}, bf16[256,256]{1,0:T(8,128)(2,1)S(1)}, f32[8,128]{1,0:T(8,128)S(1)}) custom-call(f32[1,256,256]{2,1,0:T(8,128)} %wave_hbm.3, s32[1,2]{1,0:T(1,128)} %dims_hbm.1), custom_call_target="tpu_custom_call" | custom-call | flops 1 | bytes 1 | tf_op jit(solution)/shard_map/pallas_call | solution.py:282
  1.6 0.5 %collective-permute-start = (bf16[256,256]{1,0:T(8,128)(2,1)S(1)}, bf16[256,256]{1,0:T(8,128)(2,1)S(1)}, u32[]{:S(2)}, u32[]{:S(2)}) collective-permute-start(bf16[256,256]{1,0:T(8,128)(2,1)S(1)} %get-tuple-element.17.self_ref.refs_3_), channel_id=1, source_target_pairs={{0,1},{1,0},{2,3},{3,2},{4,5},{5,4},{6,7},{7,6},{8,9},{9,8},{10,11... | collective-permute-start | bytes 393224 | tf_op jit(solution)/shard_map/ppermute | solution.py:40
  2.1 3.7 %collective-permute-start.2 = (bf16[256,256]{1,0:T(8,128)(2,1)S(1)}, bf16[256,256]{1,0:T(8,128)(2,1)S(1)}, u32[]{:S(2)}, u32[]{:S(2)}) collective-permute-start(bf16[256,256]{1,0:T(8,128)(2,1)S(1)} %get-tuple-element.17.self_ref.refs_3_), channel_id=1, source_target_pairs={{0,8},{1,9},{2,10},{3,11},{4,12},{5,13},{6,14},{7,15},{8,0},{9,1},... | collective-permute-start | bytes 393224 | tf_op jit(solution)/shard_map/ppermute | solution.py:40
  5.8 0.0 collective-permute-done.near_ref.refs_1_
  5.8 1.5 %collective-permute-start.1 = (bf16[256,256]{1,0:T(8,128)(2,1)S(1)}, bf16[256,256]{1,0:T(8,128)(2,1)S(1)}, u32[]{:S(2)}, u32[]{:S(2)}) collective-permute-start(bf16[256,256]{1,0:T(8,128)(2,1)S(1)} %shard_map.61), channel_id=1, source_target_pairs={{0,16},{1,2},{2,1},{3,4},{4,3},{5,6},{6,5},{7,23},{8,24},{9,10},{1... | collective-permute-start | bytes 393224 | tf_op jit(solution)/shard_map/ppermute | solution.py:64
  7.3 2.8 %shard_map.60 = (f32[2,256,256]{2,1,0:T(8,128)S(1)}, f32[8,128]{1,0:T(8,128)S(1)}, bf16[6,256,256]{2,1,0:T(8,128)(2,1)S(1)}, bf16[6,256,256]{2,1,0:T(8,128)(2,1)...) custom-call(bf16[1,26,256,256]{3,2,1,0:T(8,128)(2,1)} %left_hbm.3, ...), custom_call_target="tpu_custom_call" | custom-call | flops 4000000000 | bytes 1 | tf_op jit(solution)/shard_map/pallas_call | solution.py:292
  10.1 0.6 %collective-permute-done.1.far_ref = bf16[256,256]{1,0:T(8,128)(2,1)S(1)} collective-permute-done((bf16[256,256]{1,0:T(8,128)(2,1)S(1)}, bf16[256,256]{1,0:T(8,128)(2,1)S(1)}, u32[]{:S(2)}, u32[]{:S(2)}) %collective-permute-start.1) | collective-permute-done | bytes 131104 | tf_op jit(solution)/shard_map/ppermute | solution.py:64
  10.8 0.8 %shard_map.62 = (f32[256,256]{1,0:T(8,128)S(1)}, f32[256,256]{1,0:T(8,128)S(1)}) custom-call(bf16[6,256,256]{2,1,0:T(8,128)(2,1)S(1)} %get-tuple-element.18.left_ref, bf16[6,256,256]{2,1,0:T(8,128)(2,1)S(1)} %get-tuple-element.19.right_ref, f32[2,256,256]{2,1,0:T(8,128)S(1)} %get-tuple-element.20.near_part_ref, ...), custom_call_target="tpu_custom_call" | custom-call | flops 4000000000 | bytes 1 | tf_op jit(solution)/shard_map/pallas_call | solution.py:299
  11.6 1.2 %collective-permute-done.2.refs_6_ = bf16[256,256]{1,0:T(8,128)(2,1)S(1)} collective-permute-done((bf16[256,256]{1,0:T(8,128)(2,1)S(1)}, bf16[256,256]{1,0:T(8,128)(2,1)S(1)}, u32[]{:S(2)}, u32[]{:S(2)}) %collective-permute-start.2) | collective-permute-done | bytes 131104 | tf_op jit(solution)/shard_map/ppermute | solution.py:40
  12.8 1.7 %shard_map.63 = (f32[1,256,256]{2,1,0:T(8,128)S(1)}, bf16[256,256]{1,0:T(8,128)(2,1)S(1)}, f32[16,1,128]{2,1,0:T(1,128)}) custom-call(f32[256,256]{1,0:T(8,128)S(1)} %get-tuple-element.22.refs_0_, f32[8,128]{1,0:T(8,128)S(1)} %get-tuple-element.16.facts_ref.refs_1_, f32[8,128]{1,0:T(8,128)S(1)} %get-tuple-element.23.refs_2_, ...), custom_call_target="tpu_custom_call" | custom-call | flops 1 | bytes 1 | tf_op jit(solution)/shard_map/pallas_call | solution.py:303
  14.5 0.0 collective-permute-start.3
  14.5 1.7 %collective-permute-start.4 = (bf16[256,256]{1,0:T(8,128)(2,1)S(1)}, bf16[256,256]{1,0:T(8,128)(2,1)S(1)}, u32[]{:S(2)}, u32[]{:S(2)}) collective-permute-start(bf16[256,256]{1,0:T(8,128)(2,1)S(1)} %get-tuple-element.27.self_ref), channel_id=1, source_target_pairs={{0,7},{1,2},{2,1},{3,4},{4,3},{5,6},{6,5},{7,0},{8,15},{9,10},{10,... | collective-permute-start | bytes 393224 | tf_op jit(solution)/shard_map/ppermute | solution.py:64
  16.2 3.4 %collective-permute-start.5 = (bf16[256,256]{1,0:T(8,128)(2,1)S(1)}, bf16[256,256]{1,0:T(8,128)(2,1)S(1)}, u32[]{:S(2)}, u32[]{:S(2)}) collective-permute-start(bf16[256,256]{1,0:T(8,128)(2,1)S(1)} %get-tuple-element.27.self_ref), channel_id=1, source_target_pairs={{0,8},{1,9},{2,10},{3,11},{4,12},{5,13},{6,14},{7,15},{8,0},{9,1},... | collective-permute-start | bytes 393224 | tf_op jit(solution)/shard_map/ppermute | solution.py:40
  19.5 3.5 %all-to-all-start = ((f32[16,1,128]{2,1,0:T(1,128)}), f32[16,1,128]{2,1,0:T(1,128)S(1)}, u32[]{:S(2)}, u32[]{:S(2)}) async-start(f32[16,1,128]{2,1,0:T(1,128)} %get-tuple-element.26), calls=%async_computation | async-start | bytes 16384 | tf_op jit(solution)/shard_map/all_to_all | solution.py:313
  23.0 0.0 collective-permute-done.3.near_ref
  23.0 0.0 collective-permute-done.4.far_ref
  23.0 3.3 %shard_map.64.part_ref = f32[256,256]{1,0:T(8,128)S(1)} custom-call(bf16[256,256]{1,0:T(8,128)(2,1)S(1)} %collective-permute-done.3.near_ref, bf16[256,256]{1,0:T(8,128)(2,1)S(1)} %collective-permute-done.4.far_ref, bf16[256,256]{1,0:T(8,128)(2,1)S(1)} %get-tuple-element.27.self_ref, bf16[1,26,256,256]{3,2,1,0:T(8,128)(2,1)} %left_hbm.3, ...), custom_call_target="tpu_custom_call" | custom-call | flops 1 | bytes 1 | tf_op jit(solution)/shard_map/pallas_call | solution.py:314
  26.3 0.0 collective-permute-done.5.refs_0_
  26.3 0.8 %shard_map.65.hw_ref = f32[256,256]{1,0:T(8,128)S(1)} custom-call(f32[256,256]{1,0:T(8,128)S(1)} %shard_map.64.part_ref, bf16[6,256,256]{2,1,0:T(8,128)(2,1)S(1)} %get-tuple-element.24.refs_4_.left_row, bf16[6,256,256]{2,1,0:T(8,128)(2,1)S(1)} %get-tuple-element.25.refs_5_.right_row, bf16[256,256]{1,0:T(8,128)(2,1)S(1)} %collective-permute-done.5.refs_0_), custom_call_target="tpu_custom_call" | custom-call | flops 1 | bytes 1 | tf_op jit(solution)/shard_map/pallas_call | solution.py:318
  27.1 2.2 %all-to-all-done.stats_ref = f32[16,1,128]{2,1,0:T(1,128)S(1)} async-done(((f32[16,1,128]{2,1,0:T(1,128)}), f32[16,1,128]{2,1,0:T(1,128)S(1)}, u32[]{:S(2)}, u32[]{:S(2)}) %all-to-all-start) | async-done | bytes 8224 | tf_op jit(solution)/shard_map/all_to_all | solution.py:313
  29.3 1.1 %shard_map.66 = (f32[1,256,256]{2,1,0:T(8,128)}, f32[1,256,256]{2,1,0:T(8,128)}) custom-call(f32[8,128]{1,0:T(8,128)S(1)} %get-tuple-element.16.facts_ref.refs_1_, f32[16,1,128]{2,1,0:T(1,128)S(1)} %all-to-all-done.stats_ref, f32[256,256]{1,0:T(8,128)S(1)} %shard_map.65.hw_ref, f32[2,256,256]{2,1,0:T(8,128)S(1)} %get-tuple-element.20.near_part_ref, ...), custom_call_target="tpu_custom_call" | custom-call | flops 1 | bytes 1 | tf_op jit(solution)/shard_map/pallas_call | solution.py:321
  (1 shorter events, 0.0 us)
Async XLA Ops:
  1.6 4.2 %collective-permute-start = (bf16[256,256]{1,0:T(8,128)(2,1)S(1)}, bf16[256,256]{1,0:T(8,128)(2,1)S(1)}, u32[]{:S(2)}, u32[]{:S(2)}) collective-permute-start(bf16[256,256]{1,0:T(8,128)(2,1)S(1)} %get-tuple-element.17.self_ref.refs_3_), channel_id=1, source_target_pairs={{0,1},{1,0},{2,3},{3,2},{4,5},{5,4},{6,7},{7,6},{8,9},{9,8},{10,11... | collective-permute-start | bytes 393224 | tf_op jit(solution)/shard_map/ppermute | solution.py:40
  2.1 10.7 %collective-permute-start.2 = (bf16[256,256]{1,0:T(8,128)(2,1)S(1)}, bf16[256,256]{1,0:T(8,128)(2,1)S(1)}, u32[]{:S(2)}, u32[]{:S(2)}) collective-permute-start(bf16[256,256]{1,0:T(8,128)(2,1)S(1)} %get-tuple-element.17.self_ref.refs_3_), channel_id=1, source_target_pairs={{0,8},{1,9},{2,10},{3,11},{4,12},{5,13},{6,14},{7,15},{8,0},{9,1},... | collective-permute-start | bytes 393224 | tf_op jit(solution)/shard_map/ppermute | solution.py:40
  5.8 5.0 %collective-permute-start.1 = (bf16[256,256]{1,0:T(8,128)(2,1)S(1)}, bf16[256,256]{1,0:T(8,128)(2,1)S(1)}, u32[]{:S(2)}, u32[]{:S(2)}) collective-permute-start(bf16[256,256]{1,0:T(8,128)(2,1)S(1)} %shard_map.61), channel_id=1, source_target_pairs={{0,16},{1,2},{2,1},{3,4},{4,3},{5,6},{6,5},{7,23},{8,24},{9,10},{1... | collective-permute-start | bytes 393224 | tf_op jit(solution)/shard_map/ppermute | solution.py:64
  14.5 8.5 %collective-permute-start.3 = (bf16[256,256]{1,0:T(8,128)(2,1)S(1)}, bf16[256,256]{1,0:T(8,128)(2,1)S(1)}, u32[]{:S(2)}, u32[]{:S(2)}) collective-permute-start(bf16[256,256]{1,0:T(8,128)(2,1)S(1)} %get-tuple-element.27.self_ref), channel_id=1, source_target_pairs={{0,1},{1,0},{2,3},{3,2},{4,5},{5,4},{6,7},{7,6},{8,9},{9,8},{10,11... | collective-permute-start | bytes 393224 | tf_op jit(solution)/shard_map/ppermute | solution.py:40
  14.5 8.6 %collective-permute-start.4 = (bf16[256,256]{1,0:T(8,128)(2,1)S(1)}, bf16[256,256]{1,0:T(8,128)(2,1)S(1)}, u32[]{:S(2)}, u32[]{:S(2)}) collective-permute-start(bf16[256,256]{1,0:T(8,128)(2,1)S(1)} %get-tuple-element.27.self_ref), channel_id=1, source_target_pairs={{0,7},{1,2},{2,1},{3,4},{4,3},{5,6},{6,5},{7,0},{8,15},{9,10},{10,... | collective-permute-start | bytes 393224 | tf_op jit(solution)/shard_map/ppermute | solution.py:64
  16.2 10.2 %collective-permute-start.5 = (bf16[256,256]{1,0:T(8,128)(2,1)S(1)}, bf16[256,256]{1,0:T(8,128)(2,1)S(1)}, u32[]{:S(2)}, u32[]{:S(2)}) collective-permute-start(bf16[256,256]{1,0:T(8,128)(2,1)S(1)} %get-tuple-element.27.self_ref), channel_id=1, source_target_pairs={{0,8},{1,9},{2,10},{3,11},{4,12},{5,13},{6,14},{7,15},{8,0},{9,1},... | collective-permute-start | bytes 393224 | tf_op jit(solution)/shard_map/ppermute | solution.py:40
  19.5 9.8 %all-to-all-start = ((f32[16,1,128]{2,1,0:T(1,128)}), f32[16,1,128]{2,1,0:T(1,128)S(1)}, u32[]{:S(2)}, u32[]{:S(2)}) async-start(f32[16,1,128]{2,1,0:T(1,128)} %get-tuple-element.26), calls=%async_computation | async-start | bytes 16384 | tf_op jit(solution)/shard_map/all_to_all | solution.py:313

commit v17 on v15

--- a/solution.py
+++ b/solution.py
@@ -187,7 +187,7 @@
 
 def first_kernel(size, width, rows, *refs):
     part_ref, facts_ref, sums_ref, u_ref, left_ref, right_ref = refs[:6]
-    row_refs, (out_ref, w_ref, stats_ref) = refs[6 : 6 + rows], refs[6 + rows :]
+    row_refs, (out_ref, w_ref, sums_out_ref, numbers_hbm, numbers_ref, sem) = refs[6 : 6 + rows], refs[6 + rows :]
     _, _, there = place(size, width)
     image = part_ref[...]
     for r, source in enumerate(row_refs):
@@ -199,14 +199,39 @@
     square = sums_ref[1:2, 0:1]
     cross = total(u * image)
     rho = jnp.where(square > 0.0, cross / square, 0.0)
-    w = image - rho * u
-    w_ref[...] = w.astype(jnp.bfloat16)
+    w_ref[...] = (image - rho * u).astype(jnp.bfloat16)
+    lines = lax.broadcasted_iota(jnp.int32, (8, 128), 0)
+    sums = jnp.where(lines == 2, cross, jnp.where(lines == 4, rho, sums_ref[...]))
+    sums_out_ref[...] = sums
+
+    @pl.when(even_row())
+    def _():
+        write_numbers(sums, w_ref, numbers_hbm, numbers_ref, sem)
+
+
+def even_row():
+    return lax.rem(lax.div(lax.axis_index("sector"), QD), 2) == 0
+
+
+def write_numbers(sums, w_ref, numbers_hbm, numbers_ref, sem):
+    w = w_ref[...].astype(jnp.float32)
+    values = [sums[n : n + 1, 0:1] for n in range(5)]
+    values[3] = total(w * w)
     lane = lax.broadcasted_iota(jnp.int32, (1, 128), 1)
-    stats = jnp.zeros((1, 128), jnp.float32)
-    for n, value in enumerate((sums_ref[0:1, 0:1], square, cross, total(w * w), rho)):
-        stats = jnp.where(lane == n, value, stats)
-    for n in range(stats_ref.shape[0]):
-        stats_ref[n] = stats
+    numbers = jnp.zeros((1, 128), jnp.float32)
+    for n, value in enumerate(values):
+        numbers = jnp.where(lane == n, value, numbers)
+    for n in range(numbers_ref.shape[0]):
+        numbers_ref[n] = numbers
+    copy = pltpu.make_async_copy(numbers_ref, numbers_hbm, sem)
+    copy.start()
+    copy.wait()
+
+
+def numbers_kernel(held_hbm, sums_ref, w_ref, numbers_hbm, numbers_ref, sem):
+    @pl.when(jnp.logical_not(even_row()))
+    def _():
+        write_numbers(sums_ref[...], w_ref, numbers_hbm, numbers_ref, sem)
 
 
 def image_kernel(size, width, near_ref, far_ref, self_ref, left_hbm, right_hbm, out_ref, left_own, right_own, sems):
@@ -297,16 +322,19 @@
         functools.partial(far_kernel, size, width), (pltpu.VMEM(square, f32),) * 2, [VM] * 4, (VM,) * 2, cost=LONG,
     )(vmem(left_far), vmem(right_far), near_part, far_u)
     far_part = vmem(far_part)
-    row_part, w, stats = call(
+    table = pltpu.HBM((size, 1, 128), f32)
+    table_scratch = [pltpu.VMEM((size, 1, 128), f32), dma]
+    row_part, w, sums, stats = call(
         functools.partial(first_kernel, size, width, rows),
-        (pltpu.VMEM((rows,) + square, f32), pltpu.VMEM(square, bf16), jax.ShapeDtypeStruct((size, 1, 128), f32)),
-        [VM] * (6 + rows), (VM,) * 3,
+        (pltpu.VMEM((rows,) + square, f32), pltpu.VMEM(square, bf16), pltpu.VMEM((8, 128), f32), table),
+        [VM] * (6 + rows), (VM,) * 3 + (HB,), table_scratch,
     )(vmem(part), facts, vmem(sums), u, left_row, right_row, *row_u)
 
     w = vmem(w)
     row_w = [vmem(swap(w, "sector", p)) for p in row_pairs]
     near_w = vmem(swap(w, "sector", near))
     far_w = vmem(far_swap(w))
+    stats = call(numbers_kernel, table, [HB] + [VM] * 2, HB, table_scratch, aliases={0: 0})(hbm(stats), vmem(sums), w)
     stats = lax.all_to_all(stats, "sector", 0, 0, tiled=True)
     hw = call(
         functools.partial(image_kernel, size, width), pltpu.VMEM(square, f32), [VM] * 3 + [HB] * 2, VM,

time: 29.6 us -> 30.3 us (1.024)
  starting transfers between devices: 13.1 us -> 13.8 us
    ppermute x4, waiting for transfers between devices: 2.18 us -> 1.25 us  [swap(): lax.ppermute(x, axis, [(s, to.get(s, s)) for s in range(lax.axis_size(axi...]
    all_to_all x1, waiting for transfers between devices: 1.3 us -> 2.22 us  [body(): stats = lax.all_to_all(stats, 'sector', 0, 0, tiled=True)]
    all_to_all x1, starting transfers between devices: 5.81 us -> 6.4 us  [body(): stats = lax.all_to_all(stats, 'sector', 0, 0, tiled=True)]
  transfers between devices with their start and end apart: 7 -> 7, of which waited for: 4 -> 3; matrix products, arithmetic and copies ran while one was open for 0% -> 0% of each run, Pallas kernels for 26% -> 25%
where the time goes in v17:
time: 30.3 us; the launch traced here: 30.1 us
  starting transfers between devices  13.8 us (46%)
  Pallas kernels  11.4 us (38%)
  waiting for transfers between devices  4.11 us (14%)
  between operations  0.73 us (2%)
    all_to_all x1, starting transfers between devices, body(): stats = lax.all_to_all(stats, 'sector', 0, 0, tiled=True)  6.4 us
    ppermute x4, starting transfers between devices, swap(): lax.ppermute(x, axis, [(s, to.get(s, s)) for s in range(lax.axis_size(axi...  4.25 us
    pallas_call x1, Pallas kernels, body(): call(functools.partial(image_kernel, size, width), pltpu.VMEM(square, f32...  3.29 us
    ppermute x2, starting transfers between devices, far_swap(): return lax.ppermute(x, ('groups', 'sector'), pairs)  3.17 us
    pallas_call x1, Pallas kernels, body(): call(functools.partial(near_kernel, size, width, rows), (pltpu.VMEM((2,)...  2.79 us
    all_to_all x1, waiting for transfers between devices, body(): stats = lax.all_to_all(stats, 'sector', 0, 0, tiled=True)  2.22 us
    pallas_call x1, Pallas kernels, body(): call(functools.partial(first_kernel, size, width, rows), (pltpu.VMEM((row...  1.67 us
    ppermute x4, waiting for transfers between devices, swap(): lax.ppermute(x, axis, [(s, to.get(s, s)) for s in range(lax.axis_size(axi...  1.25 us
  transfers between devices with their start and end apart: 7, of which 3 were waited for; matrix products, arithmetic and copies ran while one was open for 0% of the time, Pallas kernels for 25%

profile of v17, /device:TPU:0, one launch (start us, length us, event | category | flops | bytes accessed | tf_op | source)
XLA Modules:
  0.0 30.1 jit_solution(5931599812336475435)
XLA Ops:
  0.6 1.0 %shard_map.59 = (bf16[256,256]{1,0:T(8,128)(2,1)S(1)}, bf16[256,256]{1,0:T(8,128)(2,1)S(1)}, f32[8,128]{1,0:T(8,128)S(1)}) custom-call(f32[1,256,256]{2,1,0:T(8,128)} %wave_hbm.3, s32[1,2]{1,0:T(1,128)} %dims_hbm.1), custom_call_target="tpu_custom_call" | custom-call | flops 1 | bytes 1 | tf_op jit(solution)/shard_map/pallas_call | solution.py:304
  1.6 0.5 %collective-permute-start = (bf16[256,256]{1,0:T(8,128)(2,1)S(1)}, bf16[256,256]{1,0:T(8,128)(2,1)S(1)}, u32[]{:S(2)}, u32[]{:S(2)}) collective-permute-start(bf16[256,256]{1,0:T(8,128)(2,1)S(1)} %get-tuple-element.18.self_ref.refs_3_), channel_id=1, source_target_pairs={{0,1},{1,0},{2,3},{3,2},{4,5},{5,4},{6,7},{7,6},{8,9},{9,8},{10,11... | collective-permute-start | bytes 393224 | tf_op jit(solution)/shard_map/ppermute | solution.py:40
  2.1 3.7 %collective-permute-start.2 = (bf16[256,256]{1,0:T(8,128)(2,1)S(1)}, bf16[256,256]{1,0:T(8,128)(2,1)S(1)}, u32[]{:S(2)}, u32[]{:S(2)}) collective-permute-start(bf16[256,256]{1,0:T(8,128)(2,1)S(1)} %get-tuple-element.18.self_ref.refs_3_), channel_id=1, source_target_pairs={{0,8},{1,9},{2,10},{3,11},{4,12},{5,13},{6,14},{7,15},{8,0},{9,1},... | collective-permute-start | bytes 393224 | tf_op jit(solution)/shard_map/ppermute | solution.py:40
  5.8 0.0 collective-permute-done.near_ref.refs_1_
  5.8 1.5 %collective-permute-start.1 = (bf16[256,256]{1,0:T(8,128)(2,1)S(1)}, bf16[256,256]{1,0:T(8,128)(2,1)S(1)}, u32[]{:S(2)}, u32[]{:S(2)}) collective-permute-start(bf16[256,256]{1,0:T(8,128)(2,1)S(1)} %shard_map.61), channel_id=1, source_target_pairs={{0,16},{1,2},{2,1},{3,4},{4,3},{5,6},{6,5},{7,23},{8,24},{9,10},{1... | collective-permute-start | bytes 393224 | tf_op jit(solution)/shard_map/ppermute | solution.py:61
  7.3 2.8 %shard_map.60 = (f32[2,256,256]{2,1,0:T(8,128)S(1)}, f32[8,128]{1,0:T(8,128)S(1)}, bf16[6,256,256]{2,1,0:T(8,128)(2,1)S(1)}, bf16[6,256,256]{2,1,0:T(8,128)(2,1)...) custom-call(bf16[1,26,256,256]{3,2,1,0:T(8,128)(2,1)} %left_hbm.3, ...), custom_call_target="tpu_custom_call" | custom-call | flops 4000000000 | bytes 1 | tf_op jit(solution)/shard_map/pallas_call | solution.py:314
  10.1 0.6 %collective-permute-done.1.far_ref = bf16[256,256]{1,0:T(8,128)(2,1)S(1)} collective-permute-done((bf16[256,256]{1,0:T(8,128)(2,1)S(1)}, bf16[256,256]{1,0:T(8,128)(2,1)S(1)}, u32[]{:S(2)}, u32[]{:S(2)}) %collective-permute-start.1) | collective-permute-done | bytes 131104 | tf_op jit(solution)/shard_map/ppermute | solution.py:61
  10.8 0.8 %shard_map.62 = (f32[256,256]{1,0:T(8,128)S(1)}, f32[256,256]{1,0:T(8,128)S(1)}) custom-call(bf16[6,256,256]{2,1,0:T(8,128)(2,1)S(1)} %get-tuple-element.19.left_ref, bf16[6,256,256]{2,1,0:T(8,128)(2,1)S(1)} %get-tuple-element.20.right_ref, f32[2,256,256]{2,1,0:T(8,128)S(1)} %get-tuple-element.21.near_part_ref, ...), custom_call_target="tpu_custom_call" | custom-call | flops 4000000000 | bytes 1 | tf_op jit(solution)/shard_map/pallas_call | solution.py:321
  11.6 1.2 %collective-permute-done.2.refs_6_ = bf16[256,256]{1,0:T(8,128)(2,1)S(1)} collective-permute-done((bf16[256,256]{1,0:T(8,128)(2,1)S(1)}, bf16[256,256]{1,0:T(8,128)(2,1)S(1)}, u32[]{:S(2)}, u32[]{:S(2)}) %collective-permute-start.2) | collective-permute-done | bytes 131104 | tf_op jit(solution)/shard_map/ppermute | solution.py:40
  12.8 1.7 %shard_map.63 = (f32[1,256,256]{2,1,0:T(8,128)S(1)}, bf16[256,256]{1,0:T(8,128)(2,1)S(1)}, f32[8,128]{1,0:T(8,128)S(1)}, f32[16,1,128]{2,1,0:T(1,128)}) custom-call(f32[256,256]{1,0:T(8,128)S(1)} %get-tuple-element.23.refs_0_, f32[8,128]{1,0:T(8,128)S(1)} %get-tuple-element.17.facts_ref.refs_1_, f32[8,128]{1,0:T(8,128)S(1)} %get-tuple-element.24.refs_2_, ...), custom_call_target="tpu_custom_call" | custom-call | flops 1 | bytes 1 | tf_op jit(solution)/shard_map/pallas_call | solution.py:327
  14.5 0.1 collective-permute-start.3
  14.6 1.7 %collective-permute-start.4 = (bf16[256,256]{1,0:T(8,128)(2,1)S(1)}, bf16[256,256]{1,0:T(8,128)(2,1)S(1)}, u32[]{:S(2)}, u32[]{:S(2)}) collective-permute-start(bf16[256,256]{1,0:T(8,128)(2,1)S(1)} %get-tuple-element.29.w_ref.self_ref), channel_id=1, source_target_pairs={{0,16},{1,2},{2,1},{3,4},{4,3},{5,6},{6,5},{7,23},{8,24},{9,10},{1... | collective-permute-start | bytes 393224 | tf_op jit(solution)/shard_map/ppermute | solution.py:61
  16.2 0.0 collective-permute-start.5
  16.2 6.4 %all-to-all-start = ((f32[16,1,128]{2,1,0:T(1,128)}), f32[16,1,128]{2,1,0:T(1,128)S(1)}, u32[]{:S(2)}, u32[]{:S(2)}) async-start(f32[16,1,128]{2,1,0:T(1,128)} %shard_map.64), calls=%async_computation | async-start | bytes 16384 | tf_op jit(solution)/shard_map/all_to_all | solution.py:338
  22.6 0.0 collective-permute-done.3.near_ref
  22.7 0.0 collective-permute-done.4.far_ref
  22.7 3.3 %shard_map.65.part_ref = f32[256,256]{1,0:T(8,128)S(1)} custom-call(bf16[256,256]{1,0:T(8,128)(2,1)S(1)} %collective-permute-done.3.near_ref, bf16[256,256]{1,0:T(8,128)(2,1)S(1)} %collective-permute-done.4.far_ref, bf16[256,256]{1,0:T(8,128)(2,1)S(1)} %get-tuple-element.29.w_ref.self_ref, bf16[1,26,256,256]{3,2,1,0:T(8,128)(2,1)} %left_hbm.3, ...), custom_call_target="tpu_custom_call" | custom-call | flops 1 | bytes 1 | tf_op jit(solution)/shard_map/pallas_call | solution.py:339
  26.0 0.0 collective-permute-done.5.refs_0_
  26.0 0.8 %shard_map.66.hw_ref = f32[256,256]{1,0:T(8,128)S(1)} custom-call(f32[256,256]{1,0:T(8,128)S(1)} %shard_map.65.part_ref, bf16[6,256,256]{2,1,0:T(8,128)(2,1)S(1)} %get-tuple-element.25.refs_4_.left_row, bf16[6,256,256]{2,1,0:T(8,128)(2,1)S(1)} %get-tuple-element.26.refs_5_.right_row, bf16[256,256]{1,0:T(8,128)(2,1)S(1)} %collective-permute-done.5.refs_0_), custom_call_target="tpu_custom_call" | custom-call | flops 1 | bytes 1 | tf_op jit(solution)/shard_map/pallas_call | solution.py:343
  26.8 2.2 %all-to-all-done.stats_ref = f32[16,1,128]{2,1,0:T(1,128)S(1)} async-done(((f32[16,1,128]{2,1,0:T(1,128)}), f32[16,1,128]{2,1,0:T(1,128)S(1)}, u32[]{:S(2)}, u32[]{:S(2)}) %all-to-all-start) | async-done | bytes 8224 | tf_op jit(solution)/shard_map/all_to_all | solution.py:338
  29.0 1.1 %shard_map.67 = (f32[1,256,256]{2,1,0:T(8,128)}, f32[1,256,256]{2,1,0:T(8,128)}) custom-call(f32[8,128]{1,0:T(8,128)S(1)} %get-tuple-element.17.facts_ref.refs_1_, f32[16,1,128]{2,1,0:T(1,128)S(1)} %all-to-all-done.stats_ref, f32[256,256]{1,0:T(8,128)S(1)} %shard_map.66.hw_ref, f32[2,256,256]{2,1,0:T(8,128)S(1)} %get-tuple-element.21.near_part_ref, ...), custom_call_target="tpu_custom_call" | custom-call | flops 1 | bytes 1 | tf_op jit(solution)/shard_map/pallas_call | solution.py:346
  (2 shorter events, 0.0 us)
Async XLA Ops:
  1.6 4.2 %collective-permute-start = (bf16[256,256]{1,0:T(8,128)(2,1)S(1)}, bf16[256,256]{1,0:T(8,128)(2,1)S(1)}, u32[]{:S(2)}, u32[]{:S(2)}) collective-permute-start(bf16[256,256]{1,0:T(8,128)(2,1)S(1)} %get-tuple-element.18.self_ref.refs_3_), channel_id=1, source_target_pairs={{0,1},{1,0},{2,3},{3,2},{4,5},{5,4},{6,7},{7,6},{8,9},{9,8},{10,11... | collective-permute-start | bytes 393224 | tf_op jit(solution)/shard_map/ppermute | solution.py:40
  2.1 10.7 %collective-permute-start.2 = (bf16[256,256]{1,0:T(8,128)(2,1)S(1)}, bf16[256,256]{1,0:T(8,128)(2,1)S(1)}, u32[]{:S(2)}, u32[]{:S(2)}) collective-permute-start(bf16[256,256]{1,0:T(8,128)(2,1)S(1)} %get-tuple-element.18.self_ref.refs_3_), channel_id=1, source_target_pairs={{0,8},{1,9},{2,10},{3,11},{4,12},{5,13},{6,14},{7,15},{8,0},{9,1},... | collective-permute-start | bytes 393224 | tf_op jit(solution)/shard_map/ppermute | solution.py:40
  5.8 5.0 %collective-permute-start.1 = (bf16[256,256]{1,0:T(8,128)(2,1)S(1)}, bf16[256,256]{1,0:T(8,128)(2,1)S(1)}, u32[]{:S(2)}, u32[]{:S(2)}) collective-permute-start(bf16[256,256]{1,0:T(8,128)(2,1)S(1)} %shard_map.61), channel_id=1, source_target_pairs={{0,16},{1,2},{2,1},{3,4},{4,3},{5,6},{6,5},{7,23},{8,24},{9,10},{1... | collective-permute-start | bytes 393224 | tf_op jit(solution)/shard_map/ppermute | solution.py:61
  14.5 8.2 %collective-permute-start.3 = (bf16[256,256]{1,0:T(8,128)(2,1)S(1)}, bf16[256,256]{1,0:T(8,128)(2,1)S(1)}, u32[]{:S(2)}, u32[]{:S(2)}) collective-permute-start(bf16[256,256]{1,0:T(8,128)(2,1)S(1)} %get-tuple-element.29.w_ref.self_ref), channel_id=1, source_target_pairs={{0,1},{1,0},{2,3},{3,2},{4,5},{5,4},{6,7},{7,6},{8,9},{9,8},{10,11... | collective-permute-start | bytes 393224 | tf_op jit(solution)/shard_map/ppermute | solution.py:40
  14.6 8.1 %collective-permute-start.4 = (bf16[256,256]{1,0:T(8,128)(2,1)S(1)}, bf16[256,256]{1,0:T(8,128)(2,1)S(1)}, u32[]{:S(2)}, u32[]{:S(2)}) collective-permute-start(bf16[256,256]{1,0:T(8,128)(2,1)S(1)} %get-tuple-element.29.w_ref.self_ref), channel_id=1, source_target_pairs={{0,16},{1,2},{2,1},{3,4},{4,3},{5,6},{6,5},{7,23},{8,24},{9,10},{1... | collective-permute-start | bytes 393224 | tf_op jit(solution)/shard_map/ppermute | solution.py:61
  16.2 9.8 %collective-permute-start.5 = (bf16[256,256]{1,0:T(8,128)(2,1)S(1)}, bf16[256,256]{1,0:T(8,128)(2,1)S(1)}, u32[]{:S(2)}, u32[]{:S(2)}) collective-permute-start(bf16[256,256]{1,0:T(8,128)(2,1)S(1)} %get-tuple-element.29.w_ref.self_ref), channel_id=1, source_target_pairs={{0,8},{1,9},{2,10},{3,11},{4,12},{5,13},{6,14},{7,15},{8,0},{9,1},... | collective-permute-start | bytes 393224 | tf_op jit(solution)/shard_map/ppermute | solution.py:40
  16.2 12.7 %all-to-all-start = ((f32[16,1,128]{2,1,0:T(1,128)}), f32[16,1,128]{2,1,0:T(1,128)S(1)}, u32[]{:S(2)}, u32[]{:S(2)}) async-start(f32[16,1,128]{2,1,0:T(1,128)} %shard_map.64), calls=%async_computation | async-start | bytes 16384 | tf_op jit(solution)/shard_map/all_to_all | solution.py:338

commit v18 on v15

--- a/solution.py
+++ b/solution.py
@@ -9,7 +9,7 @@
 
 QD = 8
 SCALE = 1024.0
-QUARTERS = 4
+QUARTERS = 2
 HALVES = 2
 NT = (((1,), (1,)), ((), ()))
 VM = pl.BlockSpec(memory_space=pltpu.VMEM)
@@ -178,35 +178,44 @@
         finish(pair)
 
 
-def far_kernel(size, width, left_ref, right_ref, near_part_ref, far_ref, out_ref, sum_ref):
+def far_kernel(size, width, left_ref, right_ref, near_part_ref, u_ref, sums_ref, far_ref, out_ref, sum_ref, sums_out_ref):
     _, _, there = place(size, width)
     part = terms(only(there[0], far_ref[...]), left_ref, right_ref, 0, width)
     out_ref[...] = part
-    sum_ref[...] = near_part_ref[0] + near_part_ref[1] + part
+    part = near_part_ref[0] + near_part_ref[1] + part
+    sum_ref[...] = part
+    sums = sums_ref[...]
+    square = sums[1:2, 0:1]
+    cross = total(u_ref[...].astype(jnp.float32) * part)
+    lines = lax.broadcasted_iota(jnp.int32, (8, 128), 0)
+    sums_out_ref[...] = jnp.where(lines == 2, jnp.where(square > 0.0, cross / square, 0.0), sums)
 
 
 def first_kernel(size, width, rows, *refs):
     part_ref, facts_ref, sums_ref, u_ref, left_ref, right_ref = refs[:6]
-    row_refs, (out_ref, w_ref, stats_ref) = refs[6 : 6 + rows], refs[6 + rows :]
+    row_refs, (out_ref, w_ref, numbers_hbm, numbers_ref, sem) = refs[6 : 6 + rows], refs[6 + rows :]
     _, _, there = place(size, width)
     image = part_ref[...]
     for r, source in enumerate(row_refs):
         piece = terms(only(there[1 + r], source[...]), left_ref, right_ref, r * width, width)
         out_ref[r] = piece
         image = image + piece
-    image = jnp.where(live(facts_ref[...], image.shape), image, 0.0)
     u = u_ref[...].astype(jnp.float32)
-    square = sums_ref[1:2, 0:1]
-    cross = total(u * image)
-    rho = jnp.where(square > 0.0, cross / square, 0.0)
-    w = image - rho * u
-    w_ref[...] = w.astype(jnp.bfloat16)
+    start, square, guess = (sums_ref[n : n + 1, 0:1] for n in range(3))
+    rough = jnp.where(live(facts_ref[...], image.shape), image - guess * u, 0.0)
+    along, inner = total(u * rough), total(rough * rough)
+    shift = jnp.where(square > 0.0, along / square, 0.0)
+    rho = guess + shift
     lane = lax.broadcasted_iota(jnp.int32, (1, 128), 1)
-    stats = jnp.zeros((1, 128), jnp.float32)
-    for n, value in enumerate((sums_ref[0:1, 0:1], square, cross, total(w * w), rho)):
-        stats = jnp.where(lane == n, value, stats)
-    for n in range(stats_ref.shape[0]):
-        stats_ref[n] = stats
+    numbers = jnp.zeros((1, 128), jnp.float32)
+    for n, value in enumerate((start, square, rho * square, jnp.maximum(inner - shift * along, 0.0), rho)):
+        numbers = jnp.where(lane == n, value, numbers)
+    for n in range(numbers_ref.shape[0]):
+        numbers_ref[n] = numbers
+    copy = pltpu.make_async_copy(numbers_ref, numbers_hbm, sem)
+    copy.start()
+    w_ref[...] = (rough - shift * u).astype(jnp.bfloat16)
+    copy.wait()
 
 
 def image_kernel(size, width, near_ref, far_ref, self_ref, left_hbm, right_hbm, out_ref, left_own, right_own, sems):
@@ -293,14 +302,15 @@
         [pltpu.VMEM(few, bf16)] * 2 + [pltpu.VMEM(square, f32), dma((2, 2)), dma((1, 2)), dma((rows, 2)), dma], LONG,
     )(left_env, right_env, hbm(wavefunction), facts, u, near_u)
     near_part, left_row, right_row = vmem(near_part), vmem(left_row), vmem(right_row)
-    far_part, part = call(
-        functools.partial(far_kernel, size, width), (pltpu.VMEM(square, f32),) * 2, [VM] * 4, (VM,) * 2, cost=LONG,
-    )(vmem(left_far), vmem(right_far), near_part, far_u)
+    far_part, part, sums = call(
+        functools.partial(far_kernel, size, width), (pltpu.VMEM(square, f32),) * 2 + (pltpu.VMEM((8, 128), f32),),
+        [VM] * 6, (VM,) * 3, cost=LONG,
+    )(vmem(left_far), vmem(right_far), near_part, u, vmem(sums), far_u)
     far_part = vmem(far_part)
     row_part, w, stats = call(
         functools.partial(first_kernel, size, width, rows),
-        (pltpu.VMEM((rows,) + square, f32), pltpu.VMEM(square, bf16), jax.ShapeDtypeStruct((size, 1, 128), f32)),
-        [VM] * (6 + rows), (VM,) * 3,
+        (pltpu.VMEM((rows,) + square, f32), pltpu.VMEM(square, bf16), pltpu.HBM((size, 1, 128), f32)),
+        [VM] * (6 + rows), (VM, VM, HB), [pltpu.VMEM((size, 1, 128), f32), dma],
     )(vmem(part), facts, vmem(sums), u, left_row, right_row, *row_u)
 
     w = vmem(w)

time: 29.6 us -> 29.6 us (level)
  no operation moved by 1% of the time
where the time goes in v18:
time: 29.6 us; the launch traced here: 29.4 us
  starting transfers between devices  13.2 us (45%)
  Pallas kernels  11.5 us (39%)
  waiting for transfers between devices  3.99 us (13%)
  between operations  0.71 us (2%)
    all_to_all x1, starting transfers between devices, body(): stats = lax.all_to_all(stats, 'sector', 0, 0, tiled=True)  5.71 us
    ppermute x4, starting transfers between devices, swap(): lax.ppermute(x, axis, [(s, to.get(s, s)) for s in range(lax.axis_size(axi...  4.35 us
    pallas_call x1, Pallas kernels, body(): call(functools.partial(image_kernel, size, width), pltpu.VMEM(square, f32...  3.29 us
    ppermute x2, starting transfers between devices, far_swap(): return lax.ppermute(x, ('groups', 'sector'), pairs)  3.17 us
    pallas_call x1, Pallas kernels, body(): call(functools.partial(near_kernel, size, width, rows), (pltpu.VMEM((2,)...  2.8 us
    ppermute x4, waiting for transfers between devices, swap(): lax.ppermute(x, axis, [(s, to.get(s, s)) for s in range(lax.axis_size(axi...  2.01 us
    pallas_call x1, Pallas kernels, body(): call(functools.partial(first_kernel, size, width, rows), (pltpu.VMEM((row...  1.57 us
    all_to_all x1, waiting for transfers between devices, body(): stats = lax.all_to_all(stats, 'sector', 0, 0, tiled=True)  1.34 us
  transfers between devices with their start and end apart: 7, of which 4 were waited for; matrix products, arithmetic and copies ran while one was open for 0% of the time, Pallas kernels for 26%

profile of v18, /device:TPU:0, one launch (start us, length us, event | category | flops | bytes accessed | tf_op | source)
XLA Modules:
  0.0 29.4 jit_solution(4177493311080891924)
XLA Ops:
  0.6 1.0 %shard_map.59 = (bf16[256,256]{1,0:T(8,128)(2,1)S(1)}, bf16[256,256]{1,0:T(8,128)(2,1)S(1)}, f32[8,128]{1,0:T(8,128)S(1)}) custom-call(f32[1,256,256]{2,1,0:T(8,128)} %wave_hbm.3, s32[1,2]{1,0:T(1,128)} %dims_hbm.1), custom_call_target="tpu_custom_call" | custom-call | flops 1 | bytes 1 | tf_op jit(solution)/shard_map/pallas_call | solution.py:288
  1.7 0.5 %collective-permute-start = (bf16[256,256]{1,0:T(8,128)(2,1)S(1)}, bf16[256,256]{1,0:T(8,128)(2,1)S(1)}, u32[]{:S(2)}, u32[]{:S(2)}) collective-permute-start(bf16[256,256]{1,0:T(8,128)(2,1)S(1)} %get-tuple-element.18.self_ref.u_ref.refs_3_), channel_id=1, source_target_pairs={{0,1},{1,0},{2,3},{3,2},{4,5},{5,4},{6,7},{7,6},{8,9},{9,8},{10,11... | collective-permute-start | bytes 393224 | tf_op jit(solution)/shard_map/ppermute | solution.py:40
  2.2 3.7 %collective-permute-start.2 = (bf16[256,256]{1,0:T(8,128)(2,1)S(1)}, bf16[256,256]{1,0:T(8,128)(2,1)S(1)}, u32[]{:S(2)}, u32[]{:S(2)}) collective-permute-start(bf16[256,256]{1,0:T(8,128)(2,1)S(1)} %get-tuple-element.18.self_ref.u_ref.refs_3_), channel_id=1, source_target_pairs={{0,8},{1,9},{2,10},{3,11},{4,12},{5,13},{6,14},{7,15},{8,0},{9,1},... | collective-permute-start | bytes 393224 | tf_op jit(solution)/shard_map/ppermute | solution.py:40
  5.8 0.0 collective-permute-done.near_ref.refs_1_
  5.8 1.5 %collective-permute-start.1 = (bf16[256,256]{1,0:T(8,128)(2,1)S(1)}, bf16[256,256]{1,0:T(8,128)(2,1)S(1)}, u32[]{:S(2)}, u32[]{:S(2)}) collective-permute-start(bf16[256,256]{1,0:T(8,128)(2,1)S(1)} %shard_map.61), channel_id=1, source_target_pairs={{0,16},{1,2},{2,1},{3,4},{4,3},{5,6},{6,5},{7,23},{8,24},{9,10},{1... | collective-permute-start | bytes 393224 | tf_op jit(solution)/shard_map/ppermute | solution.py:61
  7.4 2.8 %shard_map.60 = (f32[2,256,256]{2,1,0:T(8,128)S(1)}, f32[8,128]{1,0:T(8,128)S(1)}, bf16[6,256,256]{2,1,0:T(8,128)(2,1)S(1)}, bf16[6,256,256]{2,1,0:T(8,128)(2,1)...) custom-call(bf16[1,26,256,256]{3,2,1,0:T(8,128)(2,1)} %left_hbm.3, ...), custom_call_target="tpu_custom_call" | custom-call | flops 4000000000 | bytes 1 | tf_op jit(solution)/shard_map/pallas_call | solution.py:298
  10.2 0.6 %collective-permute-done.1.far_ref = bf16[256,256]{1,0:T(8,128)(2,1)S(1)} collective-permute-done((bf16[256,256]{1,0:T(8,128)(2,1)S(1)}, bf16[256,256]{1,0:T(8,128)(2,1)S(1)}, u32[]{:S(2)}, u32[]{:S(2)}) %collective-permute-start.1) | collective-permute-done | bytes 131104 | tf_op jit(solution)/shard_map/ppermute | solution.py:61
  10.8 0.9 %shard_map.62 = (f32[256,256]{1,0:T(8,128)S(1)}, f32[256,256]{1,0:T(8,128)S(1)}, f32[8,128]{1,0:T(8,128)S(1)}) custom-call(bf16[6,256,256]{2,1,0:T(8,128)(2,1)S(1)} %get-tuple-element.19.left_ref, bf16[6,256,256]{2,1,0:T(8,128)(2,1)S(1)} %get-tuple-element.20.right_ref, f32[2,256,256]{2,1,0:T(8,128)S(1)} %get-tuple-element.21.near_part_ref, ...), custom_call_target="tpu_custom_call" | custom-call | flops 4000000000 | bytes 1 | tf_op jit(solution)/shard_map/pallas_call | solution.py:305
  11.7 1.1 %collective-permute-done.2.refs_6_ = bf16[256,256]{1,0:T(8,128)(2,1)S(1)} collective-permute-done((bf16[256,256]{1,0:T(8,128)(2,1)S(1)}, bf16[256,256]{1,0:T(8,128)(2,1)S(1)}, u32[]{:S(2)}, u32[]{:S(2)}) %collective-permute-start.2) | collective-permute-done | bytes 131104 | tf_op jit(solution)/shard_map/ppermute | solution.py:40
  12.8 1.6 %shard_map.63 = (f32[1,256,256]{2,1,0:T(8,128)S(1)}, bf16[256,256]{1,0:T(8,128)(2,1)S(1)}, f32[16,1,128]{2,1,0:T(1,128)}) custom-call(f32[256,256]{1,0:T(8,128)S(1)} %get-tuple-element.24.refs_0_, f32[8,128]{1,0:T(8,128)S(1)} %get-tuple-element.17.facts_ref.refs_1_, f32[8,128]{1,0:T(8,128)S(1)} %get-tuple-element.25.refs_2_, ...), custom_call_target="tpu_custom_call" | custom-call | flops 1 | bytes 1 | tf_op jit(solution)/shard_map/pallas_call | solution.py:310
  14.4 0.1 collective-permute-start.3
  14.5 1.7 %collective-permute-start.4 = (bf16[256,256]{1,0:T(8,128)(2,1)S(1)}, bf16[256,256]{1,0:T(8,128)(2,1)S(1)}, u32[]{:S(2)}, u32[]{:S(2)}) collective-permute-start(bf16[256,256]{1,0:T(8,128)(2,1)S(1)} %get-tuple-element.29.self_ref), channel_id=1, source_target_pairs={{0,16},{1,2},{2,1},{3,4},{4,3},{5,6},{6,5},{7,23},{8,24},{9,10},{1... | collective-permute-start | bytes 393224 | tf_op jit(solution)/shard_map/ppermute | solution.py:61
  16.1 0.1 collective-permute-start.5
  16.2 5.7 %all-to-all-start = ((f32[16,1,128]{2,1,0:T(1,128)}), f32[16,1,128]{2,1,0:T(1,128)S(1)}, u32[]{:S(2)}, u32[]{:S(2)}) async-start(f32[16,1,128]{2,1,0:T(1,128)} %get-tuple-element.28), calls=%async_computation | async-start | bytes 16384 | tf_op jit(solution)/shard_map/all_to_all | solution.py:320
  22.0 0.0 collective-permute-done.3.near_ref
  22.0 0.0 collective-permute-done.4.far_ref
  22.0 3.3 %shard_map.64.part_ref = f32[256,256]{1,0:T(8,128)S(1)} custom-call(bf16[256,256]{1,0:T(8,128)(2,1)S(1)} %collective-permute-done.3.near_ref, bf16[256,256]{1,0:T(8,128)(2,1)S(1)} %collective-permute-done.4.far_ref, bf16[256,256]{1,0:T(8,128)(2,1)S(1)} %get-tuple-element.29.self_ref, bf16[1,26,256,256]{3,2,1,0:T(8,128)(2,1)} %left_hbm.3, ...), custom_call_target="tpu_custom_call" | custom-call | flops 1 | bytes 1 | tf_op jit(solution)/shard_map/pallas_call | solution.py:321
  25.3 0.9 %collective-permute-done.5.refs_0_ = bf16[256,256]{1,0:T(8,128)(2,1)S(1)} collective-permute-done((bf16[256,256]{1,0:T(8,128)(2,1)S(1)}, bf16[256,256]{1,0:T(8,128)(2,1)S(1)}, u32[]{:S(2)}, u32[]{:S(2)}) %collective-permute-start.5) | collective-permute-done | bytes 131104 | tf_op jit(solution)/shard_map/ppermute | solution.py:40
  26.2 0.8 %shard_map.65.hw_ref = f32[256,256]{1,0:T(8,128)S(1)} custom-call(f32[256,256]{1,0:T(8,128)S(1)} %shard_map.64.part_ref, bf16[6,256,256]{2,1,0:T(8,128)(2,1)S(1)} %get-tuple-element.26.refs_4_.left_row, bf16[6,256,256]{2,1,0:T(8,128)(2,1)S(1)} %get-tuple-element.27.refs_5_.right_row, bf16[256,256]{1,0:T(8,128)(2,1)S(1)} %collective-permute-done.5.refs_0_), custom_call_target="tpu_custom_call" | custom-call | flops 1 | bytes 1 | tf_op jit(solution)/shard_map/pallas_call | solution.py:325
  26.9 1.3 %all-to-all-done.stats_ref = f32[16,1,128]{2,1,0:T(1,128)S(1)} async-done(((f32[16,1,128]{2,1,0:T(1,128)}), f32[16,1,128]{2,1,0:T(1,128)S(1)}, u32[]{:S(2)}, u32[]{:S(2)}) %all-to-all-start) | async-done | bytes 8224 | tf_op jit(solution)/shard_map/all_to_all | solution.py:320
  28.3 1.1 %shard_map.66 = (f32[1,256,256]{2,1,0:T(8,128)}, f32[1,256,256]{2,1,0:T(8,128)}) custom-call(f32[8,128]{1,0:T(8,128)S(1)} %get-tuple-element.17.facts_ref.refs_1_, f32[16,1,128]{2,1,0:T(1,128)S(1)} %all-to-all-done.stats_ref, f32[256,256]{1,0:T(8,128)S(1)} %shard_map.65.hw_ref, f32[2,256,256]{2,1,0:T(8,128)S(1)} %get-tuple-element.21.near_part_ref, ...), custom_call_target="tpu_custom_call" | custom-call | flops 1 | bytes 1 | tf_op jit(solution)/shard_map/pallas_call | solution.py:328
  (1 shorter events, 0.0 us)
Async XLA Ops:
  1.7 4.2 %collective-permute-start = (bf16[256,256]{1,0:T(8,128)(2,1)S(1)}, bf16[256,256]{1,0:T(8,128)(2,1)S(1)}, u32[]{:S(2)}, u32[]{:S(2)}) collective-permute-start(bf16[256,256]{1,0:T(8,128)(2,1)S(1)} %get-tuple-element.18.self_ref.u_ref.refs_3_), channel_id=1, source_target_pairs={{0,1},{1,0},{2,3},{3,2},{4,5},{5,4},{6,7},{7,6},{8,9},{9,8},{10,11... | collective-permute-start | bytes 393224 | tf_op jit(solution)/shard_map/ppermute | solution.py:40
  2.2 10.7 %collective-permute-start.2 = (bf16[256,256]{1,0:T(8,128)(2,1)S(1)}, bf16[256,256]{1,0:T(8,128)(2,1)S(1)}, u32[]{:S(2)}, u32[]{:S(2)}) collective-permute-start(bf16[256,256]{1,0:T(8,128)(2,1)S(1)} %get-tuple-element.18.self_ref.u_ref.refs_3_), channel_id=1, source_target_pairs={{0,8},{1,9},{2,10},{3,11},{4,12},{5,13},{6,14},{7,15},{8,0},{9,1},... | collective-permute-start | bytes 393224 | tf_op jit(solution)/shard_map/ppermute | solution.py:40
  5.8 5.0 %collective-permute-start.1 = (bf16[256,256]{1,0:T(8,128)(2,1)S(1)}, bf16[256,256]{1,0:T(8,128)(2,1)S(1)}, u32[]{:S(2)}, u32[]{:S(2)}) collective-permute-start(bf16[256,256]{1,0:T(8,128)(2,1)S(1)} %shard_map.61), channel_id=1, source_target_pairs={{0,16},{1,2},{2,1},{3,4},{4,3},{5,6},{6,5},{7,23},{8,24},{9,10},{1... | collective-permute-start | bytes 393224 | tf_op jit(solution)/shard_map/ppermute | solution.py:61
  14.4 7.5 %collective-permute-start.3 = (bf16[256,256]{1,0:T(8,128)(2,1)S(1)}, bf16[256,256]{1,0:T(8,128)(2,1)S(1)}, u32[]{:S(2)}, u32[]{:S(2)}) collective-permute-start(bf16[256,256]{1,0:T(8,128)(2,1)S(1)} %get-tuple-element.29.self_ref), channel_id=1, source_target_pairs={{0,1},{1,0},{2,3},{3,2},{4,5},{5,4},{6,7},{7,6},{8,9},{9,8},{10,11... | collective-permute-start | bytes 393224 | tf_op jit(solution)/shard_map/ppermute | solution.py:40
  14.5 7.5 %collective-permute-start.4 = (bf16[256,256]{1,0:T(8,128)(2,1)S(1)}, bf16[256,256]{1,0:T(8,128)(2,1)S(1)}, u32[]{:S(2)}, u32[]{:S(2)}) collective-permute-start(bf16[256,256]{1,0:T(8,128)(2,1)S(1)} %get-tuple-element.29.self_ref), channel_id=1, source_target_pairs={{0,16},{1,2},{2,1},{3,4},{4,3},{5,6},{6,5},{7,23},{8,24},{9,10},{1... | collective-permute-start | bytes 393224 | tf_op jit(solution)/shard_map/ppermute | solution.py:61
  16.1 10.0 %collective-permute-start.5 = (bf16[256,256]{1,0:T(8,128)(2,1)S(1)}, bf16[256,256]{1,0:T(8,128)(2,1)S(1)}, u32[]{:S(2)}, u32[]{:S(2)}) collective-permute-start(bf16[256,256]{1,0:T(8,128)(2,1)S(1)} %get-tuple-element.29.self_ref), channel_id=1, source_target_pairs={{0,8},{1,9},{2,10},{3,11},{4,12},{5,13},{6,14},{7,15},{8,0},{9,1},... | collective-permute-start | bytes 393224 | tf_op jit(solution)/shard_map/ppermute | solution.py:40
  16.2 12.0 %all-to-all-start = ((f32[16,1,128]{2,1,0:T(1,128)}), f32[16,1,128]{2,1,0:T(1,128)S(1)}, u32[]{:S(2)}, u32[]{:S(2)}) async-start(f32[16,1,128]{2,1,0:T(1,128)} %get-tuple-element.28), calls=%async_computation | async-start | bytes 16384 | tf_op jit(solution)/shard_map/all_to_all | solution.py:320

commit v19 on v15

--- a/solution.py
+++ b/solution.py
@@ -285,7 +285,7 @@
     u, facts = vmem(u), vmem(facts)
     row_u = [vmem(swap(u, "sector", p)) for p in row_pairs]
     near_u = vmem(swap(u, "sector", near))
-    far_u = vmem(far_swap(after(far_u, near_u)))
+    far_u = vmem(far_swap(far_u))
     near_part, sums, left_far, right_far, left_row, right_row = call(
         functools.partial(near_kernel, size, width, rows),
         (pltpu.VMEM((2,) + square, f32), pltpu.VMEM((8, 128), f32)) + (pltpu.VMEM(side, bf16),) * 2 + (pltpu.VMEM(last, bf16),) * 2,

time: 29.6 us -> 29.6 us (level)
  no operation moved by 1% of the time
where the time goes in v19:
time: 29.6 us; the launch traced here: 29.3 us
  starting transfers between devices  13.1 us (44%)
  Pallas kernels  11.4 us (39%)
  waiting for transfers between devices  4.12 us (14%)
  between operations  0.7 us (2%)
    all_to_all x1, starting transfers between devices, body(): stats = lax.all_to_all(stats, 'sector', 0, 0, tiled=True)  5.81 us
    ppermute x4, starting transfers between devices, swap(): lax.ppermute(x, axis, [(s, to.get(s, s)) for s in range(lax.axis_size(axi...  4.19 us
    pallas_call x1, Pallas kernels, body(): call(functools.partial(image_kernel, size, width), pltpu.VMEM(square, f32...  3.29 us
    ppermute x2, starting transfers between devices, far_swap(): return lax.ppermute(x, ('groups', 'sector'), pairs)  3.11 us
    pallas_call x1, Pallas kernels, body(): call(functools.partial(near_kernel, size, width, rows), (pltpu.VMEM((2,)...  2.8 us
    ppermute x4, waiting for transfers between devices, swap(): lax.ppermute(x, axis, [(s, to.get(s, s)) for s in range(lax.axis_size(axi...  2.18 us
    pallas_call x1, Pallas kernels, body(): call(functools.partial(first_kernel, size, width, rows), (pltpu.VMEM((row...  1.66 us
    all_to_all x1, waiting for transfers between devices, body(): stats = lax.all_to_all(stats, 'sector', 0, 0, tiled=True)  1.3 us
  transfers between devices with their start and end apart: 7, of which 4 were waited for; matrix products, arithmetic and copies ran while one was open for 0% of the time, Pallas kernels for 26%

profile of v19, /device:TPU:0, one launch (start us, length us, event | category | flops | bytes accessed | tf_op | source)
XLA Modules:
  0.0 29.3 jit_solution(4154486730461784006)
XLA Ops:
  0.6 1.0 %shard_map.59 = (bf16[256,256]{1,0:T(8,128)(2,1)S(1)}, bf16[256,256]{1,0:T(8,128)(2,1)S(1)}, f32[8,128]{1,0:T(8,128)S(1)}) custom-call(f32[1,256,256]{2,1,0:T(8,128)} %wave_hbm.3, s32[1,2]{1,0:T(1,128)} %dims_hbm.1), custom_call_target="tpu_custom_call" | custom-call | flops 1 | bytes 1 | tf_op jit(solution)/shard_map/pallas_call | solution.py:279
  1.6 0.5 %collective-permute-start = (bf16[256,256]{1,0:T(8,128)(2,1)S(1)}, bf16[256,256]{1,0:T(8,128)(2,1)S(1)}, u32[]{:S(2)}, u32[]{:S(2)}) collective-permute-start(bf16[256,256]{1,0:T(8,128)(2,1)S(1)} %get-tuple-element.17.self_ref.refs_3_), channel_id=1, source_target_pairs={{0,1},{1,0},{2,3},{3,2},{4,5},{5,4},{6,7},{7,6},{8,9},{9,8},{10,11... | collective-permute-start | bytes 393224 | tf_op jit(solution)/shard_map/ppermute | solution.py:40
  2.1 3.7 %collective-permute-start.2 = (bf16[256,256]{1,0:T(8,128)(2,1)S(1)}, bf16[256,256]{1,0:T(8,128)(2,1)S(1)}, u32[]{:S(2)}, u32[]{:S(2)}) collective-permute-start(bf16[256,256]{1,0:T(8,128)(2,1)S(1)} %get-tuple-element.17.self_ref.refs_3_), channel_id=1, source_target_pairs={{0,8},{1,9},{2,10},{3,11},{4,12},{5,13},{6,14},{7,15},{8,0},{9,1},... | collective-permute-start | bytes 393224 | tf_op jit(solution)/shard_map/ppermute | solution.py:40
  5.8 1.5 %collective-permute-start.1 = (bf16[256,256]{1,0:T(8,128)(2,1)S(1)}, bf16[256,256]{1,0:T(8,128)(2,1)S(1)}, u32[]{:S(2)}, u32[]{:S(2)}) collective-permute-start(bf16[256,256]{1,0:T(8,128)(2,1)S(1)} %get-tuple-element.21), channel_id=1, source_target_pairs={{0,16},{1,2},{2,1},{3,4},{4,3},{5,6},{6,5},{7,23},{8,24},{9,10},{1... | collective-permute-start | bytes 393224 | tf_op jit(solution)/shard_map/ppermute | solution.py:61
  7.3 0.0 collective-permute-done.near_ref
  7.3 2.8 %shard_map.60 = (f32[2,256,256]{2,1,0:T(8,128)S(1)}, f32[8,128]{1,0:T(8,128)S(1)}, bf16[6,256,256]{2,1,0:T(8,128)(2,1)S(1)}, bf16[6,256,256]{2,1,0:T(8,128)(2,1)...) custom-call(bf16[1,26,256,256]{3,2,1,0:T(8,128)(2,1)} %left_hbm.3, ...), custom_call_target="tpu_custom_call" | custom-call | flops 4000000000 | bytes 1 | tf_op jit(solution)/shard_map/pallas_call | solution.py:289
  10.1 0.6 %collective-permute-done.1.far_ref = bf16[256,256]{1,0:T(8,128)(2,1)S(1)} collective-permute-done((bf16[256,256]{1,0:T(8,128)(2,1)S(1)}, bf16[256,256]{1,0:T(8,128)(2,1)S(1)}, u32[]{:S(2)}, u32[]{:S(2)}) %collective-permute-start.1) | collective-permute-done | bytes 131104 | tf_op jit(solution)/shard_map/ppermute | solution.py:61
  10.8 0.8 %shard_map.61 = (f32[256,256]{1,0:T(8,128)S(1)}, f32[256,256]{1,0:T(8,128)S(1)}) custom-call(bf16[6,256,256]{2,1,0:T(8,128)(2,1)S(1)} %get-tuple-element.18.left_ref, bf16[6,256,256]{2,1,0:T(8,128)(2,1)S(1)} %get-tuple-element.19.right_ref, f32[2,256,256]{2,1,0:T(8,128)S(1)} %get-tuple-element.20.near_part_ref, ...), custom_call_target="tpu_custom_call" | custom-call | flops 4000000000 | bytes 1 | tf_op jit(solution)/shard_map/pallas_call | solution.py:296
  11.6 1.2 %collective-permute-done.2.refs_6_ = bf16[256,256]{1,0:T(8,128)(2,1)S(1)} collective-permute-done((bf16[256,256]{1,0:T(8,128)(2,1)S(1)}, bf16[256,256]{1,0:T(8,128)(2,1)S(1)}, u32[]{:S(2)}, u32[]{:S(2)}) %collective-permute-start.2) | collective-permute-done | bytes 131104 | tf_op jit(solution)/shard_map/ppermute | solution.py:40
  12.8 1.7 %shard_map.62 = (f32[1,256,256]{2,1,0:T(8,128)S(1)}, bf16[256,256]{1,0:T(8,128)(2,1)S(1)}, f32[16,1,128]{2,1,0:T(1,128)}) custom-call(f32[256,256]{1,0:T(8,128)S(1)} %get-tuple-element.22.refs_0_, f32[8,128]{1,0:T(8,128)S(1)} %get-tuple-element.16.facts_ref.refs_1_, f32[8,128]{1,0:T(8,128)S(1)} %get-tuple-element.23.refs_2_, ...), custom_call_target="tpu_custom_call" | custom-call | flops 1 | bytes 1 | tf_op jit(solution)/shard_map/pallas_call | solution.py:300
  14.5 0.0 collective-permute-start.3
  14.5 1.6 %collective-permute-start.4 = (bf16[256,256]{1,0:T(8,128)(2,1)S(1)}, bf16[256,256]{1,0:T(8,128)(2,1)S(1)}, u32[]{:S(2)}, u32[]{:S(2)}) collective-permute-start(bf16[256,256]{1,0:T(8,128)(2,1)S(1)} %get-tuple-element.27.self_ref), channel_id=1, source_target_pairs={{0,16},{1,2},{2,1},{3,4},{4,3},{5,6},{6,5},{7,23},{8,24},{9,10},{1... | collective-permute-start | bytes 393224 | tf_op jit(solution)/shard_map/ppermute | solution.py:61
  16.1 0.0 collective-permute-start.5
  16.1 5.8 %all-to-all-start = ((f32[16,1,128]{2,1,0:T(1,128)}), f32[16,1,128]{2,1,0:T(1,128)S(1)}, u32[]{:S(2)}, u32[]{:S(2)}) async-start(f32[16,1,128]{2,1,0:T(1,128)} %get-tuple-element.26), calls=%async_computation | async-start | bytes 16384 | tf_op jit(solution)/shard_map/all_to_all | solution.py:310
  21.9 0.0 collective-permute-done.3.near_ref
  21.9 0.0 collective-permute-done.4.far_ref
  21.9 3.3 %shard_map.63.part_ref = f32[256,256]{1,0:T(8,128)S(1)} custom-call(bf16[256,256]{1,0:T(8,128)(2,1)S(1)} %collective-permute-done.3.near_ref, bf16[256,256]{1,0:T(8,128)(2,1)S(1)} %collective-permute-done.4.far_ref, bf16[256,256]{1,0:T(8,128)(2,1)S(1)} %get-tuple-element.27.self_ref, bf16[1,26,256,256]{3,2,1,0:T(8,128)(2,1)} %left_hbm.3, ...), custom_call_target="tpu_custom_call" | custom-call | flops 1 | bytes 1 | tf_op jit(solution)/shard_map/pallas_call | solution.py:311
  25.2 0.9 %collective-permute-done.5.refs_0_ = bf16[256,256]{1,0:T(8,128)(2,1)S(1)} collective-permute-done((bf16[256,256]{1,0:T(8,128)(2,1)S(1)}, bf16[256,256]{1,0:T(8,128)(2,1)S(1)}, u32[]{:S(2)}, u32[]{:S(2)}) %collective-permute-start.5) | collective-permute-done | bytes 131104 | tf_op jit(solution)/shard_map/ppermute | solution.py:40
  26.1 0.8 %shard_map.64.hw_ref = f32[256,256]{1,0:T(8,128)S(1)} custom-call(f32[256,256]{1,0:T(8,128)S(1)} %shard_map.63.part_ref, bf16[6,256,256]{2,1,0:T(8,128)(2,1)S(1)} %get-tuple-element.24.refs_4_.left_row, bf16[6,256,256]{2,1,0:T(8,128)(2,1)S(1)} %get-tuple-element.25.refs_5_.right_row, bf16[256,256]{1,0:T(8,128)(2,1)S(1)} %collective-permute-done.5.refs_0_), custom_call_target="tpu_custom_call" | custom-call | flops 1 | bytes 1 | tf_op jit(solution)/shard_map/pallas_call | solution.py:315
  26.9 1.3 %all-to-all-done.stats_ref = f32[16,1,128]{2,1,0:T(1,128)S(1)} async-done(((f32[16,1,128]{2,1,0:T(1,128)}), f32[16,1,128]{2,1,0:T(1,128)S(1)}, u32[]{:S(2)}, u32[]{:S(2)}) %all-to-all-start) | async-done | bytes 8224 | tf_op jit(solution)/shard_map/all_to_all | solution.py:310
  28.2 1.1 %shard_map.65 = (f32[1,256,256]{2,1,0:T(8,128)}, f32[1,256,256]{2,1,0:T(8,128)}) custom-call(f32[8,128]{1,0:T(8,128)S(1)} %get-tuple-element.16.facts_ref.refs_1_, f32[16,1,128]{2,1,0:T(1,128)S(1)} %all-to-all-done.stats_ref, f32[256,256]{1,0:T(8,128)S(1)} %shard_map.64.hw_ref, f32[2,256,256]{2,1,0:T(8,128)S(1)} %get-tuple-element.20.near_part_ref, ...), custom_call_target="tpu_custom_call" | custom-call | flops 1 | bytes 1 | tf_op jit(solution)/shard_map/pallas_call | solution.py:318
Async XLA Ops:
  1.6 5.7 %collective-permute-start = (bf16[256,256]{1,0:T(8,128)(2,1)S(1)}, bf16[256,256]{1,0:T(8,128)(2,1)S(1)}, u32[]{:S(2)}, u32[]{:S(2)}) collective-permute-start(bf16[256,256]{1,0:T(8,128)(2,1)S(1)} %get-tuple-element.17.self_ref.refs_3_), channel_id=1, source_target_pairs={{0,1},{1,0},{2,3},{3,2},{4,5},{5,4},{6,7},{7,6},{8,9},{9,8},{10,11... | collective-permute-start | bytes 393224 | tf_op jit(solution)/shard_map/ppermute | solution.py:40
  2.1 10.7 %collective-permute-start.2 = (bf16[256,256]{1,0:T(8,128)(2,1)S(1)}, bf16[256,256]{1,0:T(8,128)(2,1)S(1)}, u32[]{:S(2)}, u32[]{:S(2)}) collective-permute-start(bf16[256,256]{1,0:T(8,128)(2,1)S(1)} %get-tuple-element.17.self_ref.refs_3_), channel_id=1, source_target_pairs={{0,8},{1,9},{2,10},{3,11},{4,12},{5,13},{6,14},{7,15},{8,0},{9,1},... | collective-permute-start | bytes 393224 | tf_op jit(solution)/shard_map/ppermute | solution.py:40
  5.8 5.0 %collective-permute-start.1 = (bf16[256,256]{1,0:T(8,128)(2,1)S(1)}, bf16[256,256]{1,0:T(8,128)(2,1)S(1)}, u32[]{:S(2)}, u32[]{:S(2)}) collective-permute-start(bf16[256,256]{1,0:T(8,128)(2,1)S(1)} %get-tuple-element.21), channel_id=1, source_target_pairs={{0,16},{1,2},{2,1},{3,4},{4,3},{5,6},{6,5},{7,23},{8,24},{9,10},{1... | collective-permute-start | bytes 393224 | tf_op jit(solution)/shard_map/ppermute | solution.py:61
  14.5 7.4 %collective-permute-start.3 = (bf16[256,256]{1,0:T(8,128)(2,1)S(1)}, bf16[256,256]{1,0:T(8,128)(2,1)S(1)}, u32[]{:S(2)}, u32[]{:S(2)}) collective-permute-start(bf16[256,256]{1,0:T(8,128)(2,1)S(1)} %get-tuple-element.27.self_ref), channel_id=1, source_target_pairs={{0,1},{1,0},{2,3},{3,2},{4,5},{5,4},{6,7},{7,6},{8,9},{9,8},{10,11... | collective-permute-start | bytes 393224 | tf_op jit(solution)/shard_map/ppermute | solution.py:40
  14.5 7.4 %collective-permute-start.4 = (bf16[256,256]{1,0:T(8,128)(2,1)S(1)}, bf16[256,256]{1,0:T(8,128)(2,1)S(1)}, u32[]{:S(2)}, u32[]{:S(2)}) collective-permute-start(bf16[256,256]{1,0:T(8,128)(2,1)S(1)} %get-tuple-element.27.self_ref), channel_id=1, source_target_pairs={{0,16},{1,2},{2,1},{3,4},{4,3},{5,6},{6,5},{7,23},{8,24},{9,10},{1... | collective-permute-start | bytes 393224 | tf_op jit(solution)/shard_map/ppermute | solution.py:61
  16.1 10.1 %collective-permute-start.5 = (bf16[256,256]{1,0:T(8,128)(2,1)S(1)}, bf16[256,256]{1,0:T(8,128)(2,1)S(1)}, u32[]{:S(2)}, u32[]{:S(2)}) collective-permute-start(bf16[256,256]{1,0:T(8,128)(2,1)S(1)} %get-tuple-element.27.self_ref), channel_id=1, source_target_pairs={{0,8},{1,9},{2,10},{3,11},{4,12},{5,13},{6,14},{7,15},{8,0},{9,1},... | collective-permute-start | bytes 393224 | tf_op jit(solution)/shard_map/ppermute | solution.py:40
  16.1 12.1 %all-to-all-start = ((f32[16,1,128]{2,1,0:T(1,128)}), f32[16,1,128]{2,1,0:T(1,128)S(1)}, u32[]{:S(2)}, u32[]{:S(2)}) async-start(f32[16,1,128]{2,1,0:T(1,128)} %get-tuple-element.26), calls=%async_computation | async-start | bytes 16384 | tf_op jit(solution)/shard_map/all_to_all | solution.py:310
